TPU v7x, 32 devices: a whole 2x2x4 slice. The times are simulated.
32 devices in a mesh: grp: 4 (over x, core), blk: 8 (over z, y).
Axes of the slice: x: 2, y: 2, z: 4, core: 2. Of those that a mesh axis runs over, the one named last changes fastest.
Arguments:
- tokens: bfloat16 [8192, 512], P(('grp', 'blk')), may hold values from -6 to 6
- seq_len: int32 [4, 4], P('grp'), may hold values from 0 to 1024, as said below
- qkv_weight: bfloat16 [2, 512, 1536], replicated, may hold values from -0.1875 to 0.1875
- out_weight: bfloat16 [2, 512, 512], replicated, may hold values from -0.75 to 0.75
- up_weight: bfloat16 [2, 512, 2048], replicated, may hold values from -0.25 to 0.25
- up_bias: float32 [2, 2048], replicated, may hold values from -3 to 3
- down_weight: bfloat16 [2, 2048, 512], replicated, may hold values from -0.125 to 0.125
- down_bias: float32 [2, 512], replicated, may hold values from -3 to 3
- alphas: float32 [2, 2], replicated, may hold values from 0.3 to 0.7
- cotangent: bfloat16 [8192, 512], P(('grp', 'blk')), may hold values from -6 to 6
Outputs:
- output: bfloat16 [8192, 512], P(('grp', 'blk'))
- input_grad: float32 [8192, 512], P(('grp', 'blk'))
- qkv_grad: float32 [2, 512, 1536], P(None, 'blk')
- out_grad: float32 [2, 512, 512], P(None, 'blk')
- up_grad: float32 [2, 512, 2048], P(None, 'blk')
- up_bias_grad: float32 [2, 2048], P(None, 'blk')
- down_grad: float32 [2, 2048, 512], P(None, 'blk')
- down_bias_grad: float32 [2, 512], P(None, 'blk')
- alpha_grad: float32 [2, 2], replicated
Inputs may be any that keep to these rules, and one draw needn't show every extreme that they name: `seq_len`: each group's row holds k entries of 1024, then 4 - 2k entries of 512, then k zeros, for a k of 1 to 2 drawn for each group; the row sums to 2048.
All inputs are finite; a program needn't handle non-finite values.
Results may differ from a plain program's by a relative error of at most 0.023.
Values may be sent and summed in bfloat16 or wider, within the bound.
A program may use at most 192 MiB of HBM per device.

v0:
```python
import jax
import jax.numpy as jnp
from jax import lax
from jax.sharding import PartitionSpec as P

HEADS = 8
LAYERS = 2


NEGATIVE = -1e30


def layout(seq_len, local_count, cycle_size):
    piece_rows = seq_len[0] // cycle_size
    end_rows = jnp.cumsum(piece_rows)
    start_rows = end_rows - piece_rows
    local_rows = jnp.arange(local_count, dtype=jnp.int32)
    segment = jnp.sum((local_rows[:, None] >= end_rows[None, :]).astype(jnp.int32), axis=1)
    picked = segment[:, None] == jnp.arange(seq_len.shape[1], dtype=jnp.int32)[None, :]
    offset = local_rows - jnp.sum(jnp.where(picked, start_rows[None, :], 0), axis=1)
    span_rows = jnp.sum(jnp.where(picked, piece_rows[None, :], 0), axis=1)
    return (segment, offset, span_rows)


def gelu_exact(values):
    return jax.nn.gelu(values, approximate=False)


def key_block(whole, geometry, block_index, head_count):
    query_seg, query_pos, seg_all, pos_all, block_rows, score_scale = geometry
    first_row = block_index * block_rows
    key_piece = lax.dynamic_slice_in_dim(whole, first_row, block_rows, 0)
    key_seg = lax.dynamic_slice_in_dim(seg_all, first_row, block_rows, 0)
    key_pos = lax.dynamic_slice_in_dim(pos_all, first_row, block_rows, 0)
    half_width = key_piece.shape[1] // 2
    keys_part = key_piece[:, :half_width].reshape(block_rows, head_count, -1)
    values_part = key_piece[:, half_width:].reshape(block_rows, head_count, -1)
    return (keys_part, values_part, key_seg, key_pos)


def block_scores(queries, keys_part, key_seg, key_pos, geometry):
    query_seg, query_pos, seg_all, pos_all, block_rows, score_scale = geometry
    scores = (
        jnp.einsum("qhd,khd->hqk", queries, keys_part, preferred_element_type=jnp.float32)
        * score_scale
    )
    allowed = (query_seg[:, None] == key_seg[None, :]) & (key_pos[None, :] <= query_pos[:, None])
    return (scores, allowed[None])


def attend(queries, whole, geometry):
    row_count, head_count, head_dim = queries.shape
    block_count = whole.shape[0] // geometry[4]

    def statistics(running, block_index):
        largest, totals = running
        keys_part, values_part, key_seg, key_pos = key_block(
            whole, geometry, block_index, head_count
        )
        scores, allowed = block_scores(queries, keys_part, key_seg, key_pos, geometry)
        newest = jnp.maximum(largest, jnp.max(jnp.where(allowed, scores, NEGATIVE), axis=2))
        weights = jnp.where(allowed, jnp.exp(scores - newest[:, :, None]), 0.0)
        totals = totals * jnp.exp(largest - newest) + jnp.sum(weights, axis=2)
        return ((newest, totals), None)

    initial = (
        jnp.full((head_count, row_count), NEGATIVE, jnp.float32),
        jnp.zeros((head_count, row_count), jnp.float32),
    )
    (largest, totals), unused = lax.scan(statistics, initial, jnp.arange(block_count))
    log_total = largest + jnp.log(totals)

    def weighted(output_sum, block_index):
        keys_part, values_part, key_seg, key_pos = key_block(
            whole, geometry, block_index, head_count
        )
        scores, allowed = block_scores(queries, keys_part, key_seg, key_pos, geometry)
        probs = jnp.where(allowed, jnp.exp(scores - log_total[:, :, None]), 0.0).astype(
            jnp.bfloat16
        )
        output_sum = output_sum + jnp.einsum(
            "hqk,khd->qhd", probs, values_part, preferred_element_type=jnp.float32
        )
        return (output_sum, None)

    output_sum, unused = lax.scan(
        weighted, jnp.zeros((row_count, head_count, head_dim), jnp.float32), jnp.arange(block_count)
    )
    return (output_sum, log_total)


def attend_back(queries, whole, log_total, delta_sum, grad_heads, geometry):
    row_count, head_count, head_dim = queries.shape
    block_rows = geometry[4]
    score_scale = geometry[5]
    block_count = whole.shape[0] // block_rows

    def gradients(query_grad, block_index):
        keys_part, values_part, key_seg, key_pos = key_block(
            whole, geometry, block_index, head_count
        )
        scores, allowed = block_scores(queries, keys_part, key_seg, key_pos, geometry)
        probs = jnp.where(allowed, jnp.exp(scores - log_total[:, :, None]), 0.0)
        grad_probs = jnp.einsum(
            "qhd,khd->hqk", grad_heads, values_part, preferred_element_type=jnp.float32
        )
        grad_scores = (probs * (grad_probs - delta_sum[:, :, None])).astype(jnp.bfloat16)
        query_grad = (
            query_grad
            + jnp.einsum("hqk,khd->qhd", grad_scores, keys_part, preferred_element_type=jnp.float32)
            * score_scale
        )
        key_grad = (
            jnp.einsum("hqk,qhd->khd", grad_scores, queries, preferred_element_type=jnp.float32)
            * score_scale
        )
        value_grad = jnp.einsum(
            "hqk,qhd->khd",
            probs.astype(jnp.bfloat16),
            grad_heads,
            preferred_element_type=jnp.float32,
        )
        joined = jnp.concatenate(
            [key_grad.reshape(block_rows, -1), value_grad.reshape(block_rows, -1)], axis=1
        )
        return (query_grad, joined)

    query_grad, stacked = lax.scan(
        gradients,
        jnp.zeros((row_count, head_count, head_dim), jnp.float32),
        jnp.arange(block_count),
    )
    return (query_grad, stacked.reshape(whole.shape[0], -1))


def layer_forward(hidden, layer_index, weights, geometry):
    qkv_weight, out_weight, up_weight, up_bias, down_weight, down_bias, alphas = weights
    row_count, model_width = hidden.shape
    projection = qkv_weight[layer_index]
    rounded = hidden.astype(jnp.bfloat16)
    queries = (
        jnp.dot(rounded, projection[:, :model_width], preferred_element_type=jnp.float32)
        .astype(jnp.bfloat16)
        .reshape(row_count, HEADS, -1)
    )
    key_value = jnp.dot(
        rounded, projection[:, model_width:], preferred_element_type=jnp.float32
    ).astype(jnp.bfloat16)
    whole = lax.all_gather(key_value, "blk", axis=0, tiled=True)
    heads_out, log_total = attend(queries, whole, geometry)
    heads_rounded = heads_out.reshape(row_count, model_width).astype(jnp.bfloat16)
    branch = jnp.dot(heads_rounded, out_weight[layer_index], preferred_element_type=jnp.float32)
    alpha_pair = alphas[layer_index]
    middle = hidden + alpha_pair[0] * branch
    entered = middle.astype(jnp.bfloat16)
    gate_pre = (
        jnp.dot(entered, up_weight[layer_index], preferred_element_type=jnp.float32)
        + up_bias[layer_index]
    )
    activated = gelu_exact(gate_pre).astype(jnp.bfloat16)
    second = (
        jnp.dot(activated, down_weight[layer_index], preferred_element_type=jnp.float32)
        + down_bias[layer_index]
    )
    result = middle + alpha_pair[1] * second
    saved = (
        rounded,
        queries,
        key_value,
        whole,
        heads_out,
        heads_rounded,
        log_total,
        branch,
        entered,
        gate_pre,
        activated,
        second,
    )
    return (result, saved)


def layer_backward(grad_hidden, saved, layer_index, weights, geometry):
    qkv_weight, out_weight, up_weight, up_bias, down_weight, down_bias, alphas = weights
    (
        rounded,
        queries,
        key_value,
        saved_whole,
        heads_out,
        heads_rounded,
        log_total,
        branch,
        entered,
        gate_pre,
        activated,
        second,
    ) = saved
    row_count = grad_hidden.shape[0]
    alpha_pair = alphas[layer_index]
    grad_second = (alpha_pair[1] * grad_hidden).astype(jnp.bfloat16)
    alpha_second = jnp.sum(grad_hidden * second)
    bias_down = jnp.sum(grad_second.astype(jnp.float32), axis=0)
    grad_down = jnp.einsum("tf,td->fd", activated, grad_second, preferred_element_type=jnp.float32)
    grad_act = jnp.einsum(
        "td,fd->tf", grad_second, down_weight[layer_index], preferred_element_type=jnp.float32
    )
    unused, gelu_pull = jax.vjp(gelu_exact, gate_pre)
    grad_gate = gelu_pull(grad_act)[0].astype(jnp.bfloat16)
    bias_up = jnp.sum(grad_gate.astype(jnp.float32), axis=0)
    grad_up = jnp.einsum("td,tf->df", entered, grad_gate, preferred_element_type=jnp.float32)
    grad_middle = grad_hidden + jnp.einsum(
        "tf,df->td", grad_gate, up_weight[layer_index], preferred_element_type=jnp.float32
    )
    grad_branch = (alpha_pair[0] * grad_middle).astype(jnp.bfloat16)
    alpha_first = jnp.sum(grad_middle * branch)
    grad_proj_out = jnp.einsum(
        "te,td->ed", heads_rounded, grad_branch, preferred_element_type=jnp.float32
    )
    grad_heads = (
        jnp.einsum(
            "td,ed->te", grad_branch, out_weight[layer_index], preferred_element_type=jnp.float32
        )
        .astype(jnp.bfloat16)
        .reshape(queries.shape)
    )
    delta_sum = jnp.sum(grad_heads.astype(jnp.float32) * heads_out, axis=2).T
    whole = lax.all_gather(key_value, "blk", axis=0, tiled=True)
    query_grad, key_terms = attend_back(queries, whole, log_total, delta_sum, grad_heads, geometry)
    key_grads = lax.psum_scatter(
        key_terms.astype(jnp.bfloat16), "blk", scatter_dimension=0, tiled=True
    )
    grad_proj = jnp.concatenate(
        [query_grad.reshape(row_count, -1).astype(jnp.bfloat16), key_grads], axis=1
    )
    grad_qkv = jnp.einsum("td,te->de", rounded, grad_proj, preferred_element_type=jnp.float32)
    grad_input = grad_middle + jnp.einsum(
        "te,de->td", grad_proj, qkv_weight[layer_index], preferred_element_type=jnp.float32
    )
    layer_grads = (
        grad_qkv,
        grad_proj_out,
        grad_up,
        bias_up,
        grad_down,
        bias_down,
        jnp.stack([alpha_first, alpha_second]),
    )
    return (grad_input, layer_grads)


def reduce_all(layer_results, cycle_size):
    stacked = [
        jnp.stack([layer_entry[member] for layer_entry in layer_results], axis=0)
        for member in range(6)
    ]
    alpha_tiles = jnp.stack(
        [jnp.tile(layer_entry[6], cycle_size) for layer_entry in layer_results], axis=0
    )
    shares = (
        lax.psum_scatter(
            stacked[0].astype(jnp.bfloat16), "blk", scatter_dimension=1, tiled=True
        ).astype(jnp.float32),
        lax.psum_scatter(
            stacked[1].astype(jnp.bfloat16), "blk", scatter_dimension=1, tiled=True
        ).astype(jnp.float32),
        lax.psum_scatter(
            stacked[2].astype(jnp.bfloat16), "blk", scatter_dimension=1, tiled=True
        ).astype(jnp.float32),
        lax.psum_scatter(
            stacked[3].astype(jnp.bfloat16), "blk", scatter_dimension=1, tiled=True
        ).astype(jnp.float32),
        lax.psum_scatter(
            stacked[4].astype(jnp.bfloat16), "blk", scatter_dimension=1, tiled=True
        ).astype(jnp.float32),
        lax.psum_scatter(
            stacked[5].astype(jnp.bfloat16), "blk", scatter_dimension=1, tiled=True
        ).astype(jnp.float32),
        lax.psum_scatter(
            alpha_tiles.astype(jnp.bfloat16), "blk", scatter_dimension=1, tiled=True
        ).astype(jnp.float32),
    )
    return (
        lax.psum(shares[0].astype(jnp.bfloat16), "grp").astype(jnp.float32),
        lax.psum(shares[1].astype(jnp.bfloat16), "grp").astype(jnp.float32),
        lax.psum(shares[2].astype(jnp.bfloat16), "grp").astype(jnp.float32),
        lax.psum(shares[3].astype(jnp.bfloat16), "grp").astype(jnp.float32),
        lax.psum(shares[4].astype(jnp.bfloat16), "grp").astype(jnp.float32),
        lax.psum(shares[5].astype(jnp.bfloat16), "grp").astype(jnp.float32),
        lax.psum(shares[6].astype(jnp.bfloat16), "grp").astype(jnp.float32),
    )


def body(
    tokens,
    seq_len,
    qkv_weight,
    out_weight,
    up_weight,
    up_bias,
    down_weight,
    down_bias,
    alphas,
    cotangent,
):
    row_count, model_width = tokens.shape
    cycle_size = lax.axis_size("blk")
    cycle_place = lax.axis_index("blk")
    head_dim = model_width // HEADS
    total_rows = cycle_size * row_count
    block_rows = min(max(row_count, 512), total_rows)
    segment, offset, span_rows = layout(seq_len, row_count, cycle_size)
    query_pos = cycle_place * span_rows + offset
    seg_all = jnp.tile(segment, cycle_size)
    pos_all = jnp.repeat(jnp.arange(cycle_size, dtype=jnp.int32), row_count) * jnp.tile(
        span_rows, cycle_size
    ) + jnp.tile(offset, cycle_size)
    geometry = (segment, query_pos, seg_all, pos_all, block_rows, head_dim ** (-0.5))
    weights = (qkv_weight, out_weight, up_weight, up_bias, down_weight, down_bias, alphas)
    hidden = tokens.astype(jnp.float32)
    saved_layers = []
    for layer_index in range(LAYERS):
        hidden, saved = layer_forward(hidden, layer_index, weights, geometry)
        saved_layers.append(saved)
    output = hidden.astype(jnp.bfloat16)
    grad_hidden = cotangent.astype(jnp.float32)
    layer_results = []
    for layer_index in reversed(range(LAYERS)):
        grad_hidden, layer_grads = layer_backward(
            grad_hidden, saved_layers[layer_index], layer_index, weights, geometry
        )
        layer_results.insert(0, layer_grads)
    finals = reduce_all(layer_results, cycle_size)
    return (
        output,
        grad_hidden,
        finals[0],
        finals[1],
        finals[2],
        finals[3],
        finals[4],
        finals[5],
        finals[6],
    )


def solution(mesh):
    placed = (
        P(("grp", "blk"), None),
        P("grp", None),
        P(),
        P(),
        P(),
        P(),
        P(),
        P(),
        P(),
        P(("grp", "blk"), None),
    )
    return jax.shard_map(
        body,
        mesh=mesh,
        in_specs=placed,
        out_specs=(
            P(("grp", "blk"), None),
            P(("grp", "blk"), None),
            P(None, "blk", None),
            P(None, "blk", None),
            P(None, "blk", None),
            P(None, "blk"),
            P(None, "blk", None),
            P(None, "blk"),
            P(),
        ),
        check_vma=False,
    )
```

profile of v0, /device:TPU:0, one launch (start us, length us, event | category | flops | bytes accessed | tf_op | source)
XLA Modules:
  0.0 1191.1 jit_solution(18298880526505694946)
XLA Ops:
  7.2 3.3 slice_bitcast_fusion
  13.4 74.6 %all-gather.3.cloned.1.call-done = bf16[2048,1024]{1,0:T(8,128)(2,1)} async-done(((bf16[256,1024]{1,0:T(8,128)(2,1)}), bf16[2048,1024]{1,0:T(8,128)(2,1)}) %all-gather.3.cloned.1.call-update) | async-done | bytes 4194320 | tf_op jit(solution)/shard_map/all_gather | solution.py:149
  88.0 6.5 copy.126
  94.5 34.7 %while.74 = (s32[]{:T(128)}, f32[8,256]{1,0:T(8,128)S(1)}, f32[8,256]{1,0:T(8,128)S(1)}, s32[256]{0:T(256)S(1)}, s32[4]{0:T(128)S(1)}, /*index=5*/s32[2048]{0:T(...) while((s32[]{:T(128)}, f32[8,256]{1,0:T(8,128)S(1)}, ...), condition=%wide.region_7.8_spmd.clone, body=%wide.region_4.7_spmd.clone.sunk | while | flops 141961216 | bytes 10737886 | solution.py:70
  100.1 3.0 fusion.245
  108.8 3.0 fusion.245
  117.4 3.0 fusion.245
  126.1 3.0 fusion.245
  129.2 17.2 %while.75 = (s32[]{:T(128)}, f32[256,8,64]{0,2,1:T(8,128)S(1)}, s32[4]{0:T(128)S(1)}, bf16[2048,1024]{0,1:T(8,128)(2,1)}, s32[256]{0:T(256)S(1)}, /*index=5*/s32...) while((s32[]{:T(128)}, f32[256,8,64]{0,2,1:T(8,128)S(1)}, ...), condition=%wide.region_9.10_spmd.clone, body=%wide.region_8.9_spmd.clone.sunk | while | flops 273285120 | bytes 4741365 | solution.py:86
  147.6 7.9 multiply_convert_fusion.1
  155.5 2.9 multiply_add_fusion.1
  161.5 70.1 %all-gather.5.cloned.1.call-done = bf16[2048,1024]{1,0:T(8,128)(2,1)} async-done(((bf16[256,1024]{1,0:T(8,128)(2,1)}), bf16[2048,1024]{1,0:T(8,128)(2,1)}) %all-gather.5.cloned.1.call-update) | async-done | bytes 4194320 | tf_op jit(solution)/shard_map/all_gather | solution.py:149
  231.5 6.6 copy.129
  238.1 34.8 %while.76 = (s32[]{:T(128)}, f32[8,256]{1,0:T(8,128)S(1)}, f32[8,256]{1,0:T(8,128)S(1)}, s32[256]{0:T(256)S(1)}, s32[4]{0:T(128)S(1)}, /*index=5*/s32[2048]{0:T(...) while((s32[]{:T(128)}, f32[8,256]{1,0:T(8,128)S(1)}, ...), condition=%wide.region_13.14_spmd.clone, body=%wide.region_10.13_spmd.clone.sunk | while | flops 141961216 | bytes 10737886 | solution.py:70
  243.7 3.0 fusion.254
  252.4 3.0 fusion.254
  261.1 3.0 fusion.254
  269.9 3.0 fusion.254
  273.0 23.2 %while.77 = (s32[]{:T(128)}, f32[256,8,64]{0,2,1:T(8,128)}, s32[4]{0:T(128)S(1)}, bf16[2048,1024]{0,1:T(8,128)(2,1)}, s32[256]{0:T(256)S(1)}, /*index=5*/s32[204...) while((s32[]{:T(128)}, f32[256,8,64]{0,2,1:T(8,128)}, ...), condition=%wide.region_15.16_spmd.clone, body=%wide.region_14.15_spmd.clone.sunk | while | flops 273285120 | bytes 4741365 | solution.py:86
  280.9 3.2 fusion.259
  287.0 3.2 fusion.259
  293.0 3.2 fusion.259
  298.9 6.7 multiply_convert_fusion
  309.6 3.3 multiply_reduce_fusion
  318.0 54.4 %while.78 = (s32[]{:T(128)}, f32[256,8,64]{0,2,1:T(8,128)}, bf16[4,512,1024]{2,1,0:T(8,128)(2,1)}, s32[4]{0:T(128)S(1)}, bf16[2048,1024]{0,1:T(8,128)(2,1)}, /*i...) while((s32[]{:T(128)}, f32[256,8,64]{0,2,1:T(8,128)}, ...), condition=%wide.region_18.19_spmd.clone, body=%wide.region_17.18_spmd.clone.sunk | while | flops 684982272 | bytes 49289784 | solution.py:128
  325.4 3.1 fusion.274
  339.2 3.1 fusion.274
  353.0 3.1 fusion.274
  366.8 3.1 fusion.274
  373.6 85.1 %reduce-scatter.13.cloned.1.call-done = bf16[256,1024]{1,0:T(8,128)(2,1)} async-done(((bf16[2048,1024]{1,0:T(8,128)(2,1)}), bf16[256,1024]{1,0:T(8,128)(2,1)}) %reduce-scatter.13.cloned.1.call-update) | async-done | bytes 524304 | tf_op jit(solution)/shard_map/reduce_scatter | solution.py:230
  458.7 3.7 fusion.133
  462.5 4.4 fusion.142
  475.1 53.6 %while.79 = (s32[]{:T(128)}, f32[256,8,64]{0,2,1:T(8,128)S(1)}, bf16[4,512,1024]{2,1,0:T(8,128)(2,1)}, s32[4]{0:T(128)S(1)}, bf16[2048,1024]{0,1:T(8,128)(2,1)},...) while((s32[]{:T(128)}, f32[256,8,64]{0,2,1:T(8,128)S(1)}, ...), condition=%wide.region_22.23_spmd.clone, body=%wide.region_21.22_spmd.clone.sunk | while | flops 684982272 | bytes 49289784 | solution.py:128
  483.1 3.2 fusion.289
  496.4 3.2 fusion.289
  509.7 3.2 fusion.289
  523.1 3.2 fusion.289
  531.8 84.9 %reduce-scatter.15.cloned.1.call-done = bf16[256,1024]{1,0:T(8,128)(2,1)} async-done(((bf16[2048,1024]{1,0:T(8,128)(2,1)}), bf16[256,1024]{1,0:T(8,128)(2,1)}) %reduce-scatter.15.cloned.1.call-update) | async-done | bytes 524304 | tf_op jit(solution)/shard_map/reduce_scatter | solution.py:230
  618.8 6.0 copy.139
  643.4 110.2 %all-reduce.7.cloned.1.call-done = bf16[2,512,1536]{2,0,1:T(2,128)(2,1)} async-done(((bf16[2,512,1536]{2,0,1:T(2,128)(2,1)}), bf16[2,512,1536]{2,0,1:T(2,128)(2,1)}) %all-reduce.7.cloned.1.call-update) | async-done | bytes 3145744
  755.6 64.6 %reduce-scatter.17.cloned.1.call-done = bf16[2,64,512]{2,1,0:T(8,128)(2,1)} async-done(((bf16[2,512,512]{2,1,0:T(8,128)(2,1)}), bf16[2,64,512]{2,1,0:T(8,128)(2,1)}) %reduce-scatter.17.cloned.1.call-update) | async-done | bytes 131088 | tf_op jit(solution)/shard_map/reduce_scatter | solution.py:264
  820.2 90.6 %reduce-scatter.19.cloned.1.call-done = bf16[2,64,2048]{2,1,0:T(8,128)(2,1)} async-done(((bf16[2,512,2048]{2,1,0:T(8,128)(2,1)}), bf16[2,64,2048]{2,1,0:T(8,128)(2,1)}) %reduce-scatter.19.cloned.1.call-update) | async-done | bytes 524304 | tf_op jit(solution)/shard_map/reduce_scatter | solution.py:267
  910.8 91.9 %reduce-scatter.21.cloned.1.call-done = bf16[2,256,512]{2,1,0:T(8,128)(2,1)} async-done(((bf16[2,2048,512]{2,1,0:T(8,128)(2,1)}), bf16[2,256,512]{2,1,0:T(8,128)(2,1)}) %reduce-scatter.21.cloned.1.call-update) | async-done | bytes 524304 | tf_op jit(solution)/shard_map/reduce_scatter | solution.py:273
  1008.2 20.3 %all-reduce.1 = bf16[2,16]{1,0:T(2,128)(2,1)S(1)} all-reduce(bf16[2,16]{1,0:T(2,128)(2,1)S(1)} %pad_maximum_fusion.12), channel_id=10, replica_groups=mesh['grp'=4,'blk'=8] {'blk'}, use_global_device_ids=true, to_apply=%region_44.45.clone | all-reduce | flops 32 | bytes 128
  1028.5 38.8 %reduce-scatter.25.cloned.1.call-done = bf16[64,2]{1,0:T(8,128)(2,1)} async-done(((bf16[512,2]{1,0:T(8,128)(2,1)}), bf16[64,2]{1,0:T(8,128)(2,1)}) %reduce-scatter.25.cloned.1.call-update) | async-done | bytes 272
  1068.1 64.0 %reduce-scatter.23.cloned.1.call-done = bf16[256,2]{1,0:T(8,128)(2,1)} async-done(((bf16[2048,2]{1,0:T(8,128)(2,1)}), bf16[256,2]{1,0:T(8,128)(2,1)}) %reduce-scatter.23.cloned.1.call-update) | async-done | bytes 1040
  1133.0 5.7 all-reduce.2
  1142.9 34.3 %all-reduce.9.cloned.1.call-done = (bf16[2,64,1536]{2,0,1:T(2,128)(2,1)}, bf16[2,64,512]{2,1,0:T(8,128)(2,1)}, bf16[2,64,2048]{2,1,0:T(8,128)(2,1)}, bf16[2,256,512]{2,1,0:T(8,128)(2,1)}) async-done(((bf16[2,64,1536]{2,0,1:T(2,128)(2,1)}, bf16[2,64,512]{2,1,0:T(8,128)(2,1)}, bf16[2,64,2048]{2,1,0:T(8,128)(2,1)}, bf16[2,256,512]{2,1,0:T(8,128)(2,1)}), (bf16[2,64,1536]{2,0,1:T(2,128)(2,1)}, ...) | async-done | bytes 1572880 | tf_op jit(solution)/shard_map/psum | solution.py:284
  (553 shorter events, 211.5 us)
Async XLA Ops:
  7.2 3.3 copy-start.36
  7.2 80.8 %all-gather.3.cloned.1.call-start = ((), (), s32[]{:S(2)}) async-start(), calls=%async_computation.7 | async-start | bytes 4718592 | tf_op jit(solution)/shard_map/all_gather | solution.py:149
  11.8 219.7 %all-gather.5.cloned.1.call-start = ((), (), s32[]{:S(2)}) async-start(), calls=%async_computation.8 | async-start | bytes 4718592 | tf_op jit(solution)/shard_map/all_gather | solution.py:149
  129.2 17.3 %copy-start.7 = (bf16[2,512,512]{2,1,0:T(8,128)(2,1)S(1)}, bf16[2,512,512]{2,1,0:T(8,128)(2,1)}, u32[]{:S(2)}) copy-start(bf16[2,512,512]{2,1,0:T(8,128)(2,1)} %param.25) | copy-start | bytes 3145732
  129.2 17.3 %copy-start.37 = (bf16[256,512]{1,0:T(8,128)(2,1)S(1)}, bf16[256,512]{1,0:T(8,128)(2,1)}, u32[]{:S(2)}) copy-start(bf16[256,512]{1,0:T(8,128)(2,1)} %param.22) | copy-start | bytes 786436
  146.5 9.0 copy-start.21
  146.5 9.0 copy-start.53
  147.5 8.0 copy-start.26
  147.5 8.0 copy-start.45
  147.5 7.9 copy-start.38
  147.5 7.9 copy-start.65
  158.4 151.1 %copy-start.3 = (f32[256,512]{1,0:T(8,128)}, f32[256,512]{1,0:T(8,128)S(1)}, u32[]{:S(2)}) copy-start(f32[256,512]{1,0:T(8,128)S(1)} %get-tuple-element.1135) | copy-start | bytes 1572868
  159.7 299.0 %reduce-scatter.13.cloned.1.call-start = ((), (), s32[]{:S(2)}) async-start(), calls=%async_computation.9 | async-start | bytes 4718592 | tf_op jit(solution)/shard_map/reduce_scatter | solution.py:230
  296.2 9.4 copy-start.42
  296.2 9.4 copy-start.56
  298.9 6.8 copy-start.24
  298.9 6.8 copy-start.66
  309.6 3.3 copy-start.28
  318.2 3.3 copy-start.73
  331.0 3.3 copy-start.73
  344.7 3.3 copy-start.73
  358.5 3.3 copy-start.73
  372.4 86.3 %copy-start.19 = (f32[256,512]{1,0:T(8,128)S(1)}, f32[256,512]{1,0:T(8,128)}, u32[]{:S(2)}) copy-start(f32[256,512]{1,0:T(8,128)} %copy-done.18) | copy-start | bytes 1572868
  372.4 244.3 %reduce-scatter.15.cloned.1.call-start = ((), (), s32[]{:S(2)}) async-start(), calls=%async_computation.10 | async-start | bytes 4718592 | tf_op jit(solution)/shard_map/reduce_scatter | solution.py:230
  373.6 88.8 %copy-start.40 = (bf16[256,512]{1,0:T(8,128)(2,1)}, bf16[256,512]{1,0:T(8,128)(2,1)S(1)}, u32[]{:S(2)}) copy-start(bf16[256,512]{1,0:T(8,128)(2,1)S(1)} %copy.133) | copy-start | bytes 786436
  458.7 3.7 copy-start.67
  462.5 4.5 copy-start.48
  462.5 4.5 copy-start.44
  462.5 4.5 copy-start.46
  462.5 4.4 copy-start.69
  475.3 3.3 copy-start.71
  478.7 3.7 copy-start.1
  488.7 3.3 copy-start.71
  492.0 3.7 copy-start.1
  502.0 3.3 copy-start.71
  505.3 3.7 copy-start.1
  515.3 3.3 copy-start.71
  518.7 3.7 copy-start.1
  528.7 224.8 %all-reduce.7.cloned.1.call-start = ((), (), s32[]{:S(2)}) async-start(), calls=%async_computation.16 | async-start | bytes 6291456
  528.8 87.9 %copy-start.39 = (bf16[256,512]{1,0:T(8,128)(2,1)S(1)}, bf16[256,512]{1,0:T(8,128)(2,1)}, u32[]{:S(2)}) copy-start(bf16[256,512]{1,0:T(8,128)(2,1)} %param.22) | copy-start | bytes 786436
  624.8 195.4 %reduce-scatter.17.cloned.1.call-start = ((), (), s32[]{:S(2)}) async-start(), calls=%async_computation.11 | async-start | bytes 1179648 | tf_op jit(solution)/shard_map/reduce_scatter | solution.py:264
  628.9 281.9 %reduce-scatter.19.cloned.1.call-start = ((), (), s32[]{:S(2)}) async-start(), calls=%async_computation.12 | async-start | bytes 4718592 | tf_op jit(solution)/shard_map/reduce_scatter | solution.py:267
  633.4 369.4 %reduce-scatter.21.cloned.1.call-start = ((), (), s32[]{:S(2)}) async-start(), calls=%async_computation.13 | async-start | bytes 4718592 | tf_op jit(solution)/shard_map/reduce_scatter | solution.py:273
  639.2 428.1 %reduce-scatter.25.cloned.1.call-start = ((), (), s32[]{:S(2)}) async-start(), calls=%async_computation.15 | async-start | bytes 147456
  642.2 489.9 %reduce-scatter.23.cloned.1.call-start = ((), (), s32[]{:S(2)}) async-start(), calls=%async_computation.14 | async-start | bytes 589824
  643.3 497.0 %copy-start.11 = (bf16[2,512,1536]{2,1,0:T(8,128)(2,1)S(1)}, bf16[2,512,1536]{2,1,0:T(8,128)(2,1)}, u32[]{:S(2)}) copy-start(bf16[2,512,1536]{2,1,0:T(8,128)(2,1)} %param.24) | copy-start | bytes 9437188
  643.3 533.9 %all-reduce.9.cloned.1.call-start = ((), (), s32[]{:S(2)}) async-start(), calls=%async_computation.17 | async-start | bytes 3145728 | tf_op jit(solution)/shard_map/psum | solution.py:284
  1177.3 5.8 copy-start.43
  (74 other events, 128.9 us)
Sparse Core Ops, SparseCore 0:
  11.9 76.0 all-gather.2
  159.8 71.6 all-gather.4
  372.5 86.1 reduce-scatter.12
  528.9 87.7 reduce-scatter.14
  625.0 128.5 all-reduce.6
  757.8 62.3 reduce-scatter.16
  823.9 86.9 reduce-scatter.18
  914.9 87.8 reduce-scatter.20
  1006.6 60.5 reduce-scatter.24
  1071.0 60.9 reduce-scatter.22
  1134.8 42.3 all-reduce.8
where the time goes:
time: 1200 us; the launch traced here: 1190 us
  waiting for transfers between devices  809 us (67%)
  matrix products  157 us (13%)
  local copies, waits for them, and re-layouts  112 us (9%)
  other arithmetic  51.8 us (4%)
  blocking collectives  25.9 us (2%)
  loops' own time  17.7 us (1%)
  between operations  16.5 us (1%)
    unnamed x14, waiting for transfers between devices  213 us
    reduce_scatter x2, waiting for transfers between devices, layer_backward(): lax.psum_scatter(key_terms.astype(jnp.bfloat16), 'blk', scatter_dimension...  170 us
    all_gather x2, waiting for transfers between devices, layer_forward(): whole = lax.all_gather(key_value, 'blk', axis=0, tiled=True)  145 us
    reduce_scatter x1, waiting for transfers between devices, reduce_all(): lax.psum_scatter(stacked[4].astype(jnp.bfloat16), 'blk', scatter_dimensio...  91.9 us
    reduce_scatter x1, waiting for transfers between devices, reduce_all(): lax.psum_scatter(stacked[2].astype(jnp.bfloat16), 'blk', scatter_dimensio...  90.6 us
    reduce_scatter x1, waiting for transfers between devices, reduce_all(): lax.psum_scatter(stacked[1].astype(jnp.bfloat16), 'blk', scatter_dimensio...  64.6 us
    psum x1, waiting for transfers between devices, reduce_all(): lax.psum(shares[0].astype(jnp.bfloat16), 'grp').astype(jnp.float32)  34.3 us
    dot_general x16, matrix products, block_scores(): jnp.einsum('qhd,khd->hqk', queries, keys_part, preferred_element_type=jnp...  29.2 us
  transfers between devices with their start and end apart: 11, of which 11 were waited for; matrix products, arithmetic and copies ran while one was open for 3% of the time, Pallas kernels for 0%

commit v1 on v0

--- a/solution.py
+++ b/solution.py
@@ -1,13 +1,657 @@
+import functools
+
 import jax
 import jax.numpy as jnp
 from jax import lax
+from jax.experimental import pallas as pl
+from jax.experimental.pallas import tpu as pltpu
 from jax.sharding import PartitionSpec as P
 
 HEADS = 8
 LAYERS = 2
-
-
 NEGATIVE = -1e30
+MESH = pl.DeviceIdType.MESH
+F32 = jnp.float32
+BF16 = jnp.bfloat16
+
+HALF = 128
+RUNS = 8
+DIM = 64
+WIDTH = 512
+FF = 2048
+CUT = 512
+TILE = 256
+TILES = HALF * RUNS // TILE
+PACK = HALF + DIM
+CHUNK = 768
+SMALL = FF + WIDTH + 128
+EARLY = (192, 576)
+LATE = (0, 192)
+
+
+def nn(a, b):
+    return lax.dot_general(a, b, (((1,), (0,)), ((), ())), preferred_element_type=F32)
+
+
+def nt(a, b):
+    return lax.dot_general(a, b, (((1,), (1,)), ((), ())), preferred_element_type=F32)
+
+
+def layers_kernel(
+    tokens, seq_len, alphas, up_bias, down_bias, cotangent, qkv_hbm, out_hbm, up_hbm, down_hbm,
+    output, input_grad, qkv_grad, out_grad, up_grad, up_bias_grad, down_grad, down_bias_grad, alpha_grad,
+    wqkv, wout, wup, wdown,
+    hidden, grad, hid_t, attn_t, ent_t, act_t, branch, slope, second,
+    dz, du, da, dqkv,
+    pack_out, head_out, qkv_in, o_in, do_in, dqkv_in,
+    kv, kv_t, rq, ro, o_t, lse, acc, dq_t, bias,
+    parts, core_in, x_in, yz_in, final, small, small_grp, small_sum, small_blk,
+    w_sem, a2a_send, a2a_recv, core_send, core_recv, x_send, x_recv, yz_send, yz_recv, fin_send, fin_recv,
+    small_send, small_recv, wide_send, wide_recv, core_free, x_free,
+):
+    grp = lax.axis_index("grp")
+    blk = lax.axis_index("blk")
+    core = lax.rem(grp, 2)
+    side = lax.div(grp, 2)
+    lane = lax.broadcasted_iota(jnp.int32, (HALF, 128), 1)
+    low = lane < DIM
+
+    weight_copies = {}
+    for layer in range(LAYERS):
+        for number, (source, target) in enumerate(
+            ((qkv_hbm, wqkv), (out_hbm, wout), (up_hbm, wup), (down_hbm, wdown))
+        ):
+            weight_copies[layer, number] = pltpu.make_async_copy(
+                source.at[layer], target.at[layer], w_sem.at[layer, number]
+            )
+            weight_copies[layer, number].start()
+
+    barrier = pltpu.get_barrier_semaphore()
+    for step in range(1, RUNS):
+        pl.semaphore_signal(
+            barrier, inc=1, device_id=(grp, lax.rem(blk + step, RUNS)), device_id_type=MESH
+        )
+    for step in range(1, 4):
+        pl.semaphore_signal(
+            barrier, inc=1, device_id=(lax.rem(grp + step, 4), blk), device_id_type=MESH
+        )
+
+    key_row = lax.broadcasted_iota(jnp.int32, (TILE, TILE), 0)
+    query_col = lax.broadcasted_iota(jnp.int32, (TILE, TILE), 1)
+    later = key_row > query_col
+    end_second = lax.div(seq_len[0, 0] + seq_len[0, 1], RUNS)
+    key_sub = lax.rem(key_row, HALF) + HALF >= end_second
+    query_sub = lax.rem(query_col, HALF) + HALF >= end_second
+    apart = jnp.logical_xor(key_sub, query_sub)
+    bias[0, 0] = jnp.zeros((TILE, TILE), F32)
+    bias[0, 1] = jnp.where(later, NEGATIVE, 0.0)
+    bias[1, 0] = jnp.where(apart, NEGATIVE, 0.0)
+    bias[1, 1] = jnp.where(jnp.logical_or(later, apart), NEGATIVE, 0.0)
+    for layer in range(LAYERS):
+        for half in range(2):
+            rq[layer, half, DIM:, :] = jnp.zeros((DIM, HALF * RUNS), BF16)
+    ro[0:DIM, :] = jnp.zeros((DIM, HALF * RUNS), BF16)
+
+    def rows_of(half):
+        return pl.ds(pl.multiple_of(half * HALF, HALF), HALF)
+
+    def slot_of(run):
+        return lax.rem(run + RUNS - blk, RUNS)
+
+    def exchange(kind, layer, half, outgoing, incoming):
+        incoming[layer, half, 0] = outgoing[half, blk]
+        for step in range(1, RUNS):
+            peer = lax.rem(blk + step, RUNS)
+            pltpu.make_async_remote_copy(
+                src_ref=outgoing.at[half, peer],
+                dst_ref=incoming.at[layer, half, RUNS - step],
+                send_sem=a2a_send.at[kind, layer, half],
+                recv_sem=a2a_recv.at[kind, layer, half],
+                device_id=(grp, peer),
+                device_id_type=MESH,
+            ).start()
+
+    def arrived(kind, layer, half, incoming):
+        whole = incoming.at[layer, half, pl.ds(1, RUNS - 1)]
+        pltpu.make_async_copy(whole, whole, a2a_recv.at[kind, layer, half]).wait()
+
+    def left(kind, layer, half, outgoing):
+        whole = outgoing.at[half, pl.ds(1, RUNS - 1)]
+        pltpu.make_async_copy(whole, whole, a2a_send.at[kind, layer, half]).wait()
+
+    def project(layer, half):
+        rows = rows_of(half)
+        rounded = hidden[half].astype(BF16)
+        hid_t[layer, :, rows] = rounded.T
+        if layer == 1:
+            left(0, 0, half, pack_out)
+        queries = nn(rounded, wqkv[layer, :, 0:WIDTH]) * (DIM ** -0.5)
+        queries_t = queries.T.astype(BF16)
+        keys = nn(rounded, wqkv[layer, :, WIDTH : 2 * WIDTH])
+        values = nn(rounded, wqkv[layer, :, 2 * WIDTH : 3 * WIDTH])
+        for pair in range(RUNS // 2):
+            k_pair = keys[:, 128 * pair : 128 * pair + 128]
+            v_pair = values[:, 128 * pair : 128 * pair + 128]
+            first = jnp.where(low, k_pair, pltpu.roll(v_pair, DIM, 1))
+            other = jnp.where(low, pltpu.roll(k_pair, DIM, 1), v_pair)
+            pack_out[half, 2 * pair, 0:HALF, :] = first.astype(BF16)
+            pack_out[half, 2 * pair + 1, 0:HALF, :] = other.astype(BF16)
+        for head in range(RUNS):
+            pack_out[half, head, HALF:, :] = queries_t[DIM * head : DIM * head + DIM, :]
+        exchange(0, layer, half, pack_out, qkv_in)
+
+    def attend(layer, half):
+        arrived(0, layer, half, qkv_in)
+        if layer == 1:
+            left(1, 0, half, head_out)
+        for run in range(RUNS):
+            slot = slot_of(run)
+            span = slice(HALF * run, HALF * run + HALF)
+            block = qkv_in[layer, half, slot, 0:HALF, :]
+            kv[layer, half, span, :] = block
+            kv_t[layer, half, :, span] = block.T
+            rq[layer, half, 0:DIM, span] = qkv_in[layer, half, slot, HALF:, :]
+        for i in range(TILES):
+            columns = slice(TILE * i, TILE * i + TILE)
+            query_tile = rq[layer, half, :, columns]
+            scores = []
+            for j in range(i + 1):
+                tile = nn(kv[layer, half, TILE * j : TILE * j + TILE, :], query_tile)
+                scores.append(tile + bias[half, 1 if j == i else 0])
+            largest = functools.reduce(
+                jnp.maximum, [jnp.max(tile, axis=0, keepdims=True) for tile in scores]
+            )
+            total = jnp.zeros((1, TILE), F32)
+            summed = jnp.zeros((DIM, TILE), F32)
+            for j in range(i + 1):
+                weight = jnp.exp(scores[j] - largest)
+                total = total + jnp.sum(weight, axis=0, keepdims=True)
+                summed = summed + nn(
+                    kv_t[layer, half, DIM:, TILE * j : TILE * j + TILE], weight.astype(BF16)
+                )
+            summed = summed / total
+            o_t[layer, half, :, columns] = summed
+            lse[layer, half, :, columns] = largest + jnp.log(total)
+            rounded = summed.astype(BF16)
+            for run in range(2):
+                head_out[half, 2 * i + run] = rounded[:, HALF * run : HALF * run + HALF]
+        exchange(1, layer, half, head_out, o_in)
+
+    def feed(layer, half):
+        rows = rows_of(half)
+        arrived(1, layer, half, o_in)
+        for head in range(RUNS):
+            attn_t[layer, DIM * head : DIM * head + DIM, rows] = o_in[layer, half, slot_of(head)]
+        attn = attn_t[layer, :, rows].T
+        grown = nn(attn, wout[layer])
+        branch[layer, half] = grown
+        middle = hidden[half] + alphas[layer, 0] * grown
+        entered = middle.astype(BF16)
+        ent_t[layer, :, rows] = entered.T
+        total = jnp.zeros((HALF, WIDTH), F32)
+        for step in range(FF // CUT):
+            cut = slice(CUT * step, CUT * step + CUT)
+            gate = nn(entered, wup[layer, :, cut]) + up_bias[layer : layer + 1, cut]
+            risen = 0.5 * (1.0 + lax.erf(gate * (0.5 ** 0.5)))
+            slope[layer, half, :, cut] = risen + gate * jnp.exp(-0.5 * gate * gate) * 0.3989422804014327
+            active = (gate * risen).astype(BF16)
+            act_t[layer, cut, rows] = active.T
+            total = total + nn(active, wdown[layer, cut, :])
+        total = total + down_bias[layer : layer + 1, :]
+        second[layer, half] = total
+        hidden[half] = middle + alphas[layer, 1] * total
+
+    def total_of(values):
+        return jnp.sum(jnp.sum(values, axis=0, keepdims=True), axis=1, keepdims=True)
+
+    def feed_back(layer, half):
+        rows = rows_of(half)
+        start = grad[half]
+        scaled = (alphas[layer, 1] * start).astype(BF16)
+        dz[rows, :] = scaled
+        alpha_second = total_of(start * second[layer, half])
+        small[half, layer : layer + 1, FF : FF + WIDTH] = jnp.sum(scaled.astype(F32), axis=0, keepdims=True)
+        middle = start
+        for step in range(FF // CUT):
+            cut = slice(CUT * step, CUT * step + CUT)
+            gate = (nt(scaled, wdown[layer, cut, :]) * slope[layer, half, :, cut]).astype(BF16)
+            du[rows, cut] = gate
+            small[half, layer : layer + 1, cut] = jnp.sum(gate.astype(F32), axis=0, keepdims=True)
+            middle = middle + nt(gate, wup[layer, :, cut])
+        grad[half] = middle
+        alpha_first = total_of(middle * branch[layer, half])
+        column = lax.broadcasted_iota(jnp.int32, (1, 128), 1)
+        small[half, layer : layer + 1, FF + WIDTH :] = jnp.where(
+            column == 0, alpha_first, jnp.where(column == 1, alpha_second, 0.0)
+        )
+        mixed = (alphas[layer, 0] * middle).astype(BF16)
+        da[rows, :] = mixed
+        spread = nt(wout[layer], mixed).astype(BF16)
+        left(*((1, 1) if layer == 1 else (2, 1)), half, head_out)
+        for head in range(RUNS):
+            head_out[half, head] = spread[DIM * head : DIM * head + DIM, :]
+        exchange(2, layer, half, head_out, do_in)
+
+    def attend_back(layer, half):
+        arrived(2, layer, half, do_in)
+        for run in range(RUNS):
+            ro[DIM:, HALF * run : HALF * run + HALF] = do_in[layer, half, slot_of(run)]
+        for i in range(TILES):
+            columns = slice(TILE * i, TILE * i + TILE)
+            query_tile = rq[layer, half, :, columns]
+            grad_tile = ro[:, columns]
+            log_total = lse[layer, half, :, columns]
+            delta = jnp.sum(
+                ro[DIM:, columns].astype(F32) * o_t[layer, half, :, columns], axis=0, keepdims=True
+            )
+            query_grad = jnp.zeros((DIM, TILE), F32)
+            for j in range(i + 1):
+                span = slice(TILE * j, TILE * j + TILE)
+                keys = kv[layer, half, span, :]
+                weight = jnp.exp(nn(keys, query_tile) + bias[half, 1 if j == i else 0] - log_total)
+                scored = (weight * (nn(keys, grad_tile) - delta)).astype(BF16)
+                term = nt(scored, query_tile) + nt(weight.astype(BF16), grad_tile)
+                if j == i:
+                    acc[span, :] = term
+                else:
+                    acc[span, :] += term
+                query_grad = query_grad + nn(kv_t[layer, half, 0:DIM, span], scored)
+            dq_t[:, columns] = query_grad * (DIM ** -0.5)
+        left(*((0, 1) if layer == 1 else (3, 1)), half, pack_out)
+        for run in range(RUNS):
+            span = slice(HALF * run, HALF * run + HALF)
+            pack_out[half, run, 0:HALF, :] = acc[span, :].astype(BF16)
+            pack_out[half, run, HALF:, :] = dq_t[:, span].astype(BF16)
+        exchange(3, layer, half, pack_out, dqkv_in)
+
+    def project_back(layer, half):
+        rows = rows_of(half)
+        arrived(3, layer, half, dqkv_in)
+        turned = jnp.concatenate(
+            [dqkv_in[layer, half, slot_of(head), HALF:, :] for head in range(RUNS)], axis=0
+        )
+        dqkv[rows, 0:WIDTH] = turned.T
+        for pair in range(RUNS // 2):
+            first = dqkv_in[layer, half, slot_of(2 * pair), 0:HALF, :].astype(F32)
+            other = dqkv_in[layer, half, slot_of(2 * pair + 1), 0:HALF, :].astype(F32)
+            k_pair = jnp.where(low, first, pltpu.roll(other, DIM, 1))
+            v_pair = jnp.where(low, pltpu.roll(first, DIM, 1), other)
+            dqkv[rows, WIDTH + 128 * pair : WIDTH + 128 * pair + 128] = k_pair.astype(BF16)
+            dqkv[rows, 2 * WIDTH + 128 * pair : 2 * WIDTH + 128 * pair + 128] = v_pair.astype(BF16)
+        grad[half] = grad[half] + nt(dqkv[rows, :], wqkv[layer])
+
+    def scatter_rows(layer, result, first_row):
+        for place in range(RUNS):
+            for quarter in range(4):
+                parts[layer, quarter, place, first_row : first_row + DIM, :] = result[
+                    DIM * place : DIM * place + DIM, 128 * quarter : 128 * quarter + 128
+                ].astype(BF16)
+
+    def early_grads(layer):
+        scatter_rows(layer, nn(attn_t[layer], da[...]), 192)
+        for step in range(FF // CUT):
+            cut = slice(CUT * step, CUT * step + CUT)
+            scatter_rows(layer, nn(ent_t[layer], du[:, cut]), 256 + DIM * step)
+        for place in range(RUNS):
+            result = nn(act_t[layer, TILE * place : TILE * place + TILE, :], dz[...])
+            for quarter in range(4):
+                parts[layer, quarter, place, 512:768, :] = result[
+                    :, 128 * quarter : 128 * quarter + 128
+                ].astype(BF16)
+
+    def late_grads(layer):
+        for step in range(3):
+            scatter_rows(layer, nn(hid_t[layer], dqkv[:, WIDTH * step : WIDTH * step + WIDTH]), DIM * step)
+
+    def core_copy(layer, stage, across):
+        first, count = (EARLY, LATE)[stage]
+        rows = pl.ds(first, count)
+        return pltpu.make_async_remote_copy(
+            src_ref=parts.at[layer, 2 * across + 1 - core, :, rows],
+            dst_ref=core_in.at[across, :, rows],
+            send_sem=core_send.at[layer, stage, across],
+            recv_sem=core_recv.at[layer, stage, across],
+            device_id=(2 * side + 1 - core, blk),
+            device_id_type=MESH,
+        )
+
+    def x_copy(layer, stage):
+        first, count = (EARLY, LATE)[stage]
+        rows = pl.ds(first, count)
+        return pltpu.make_async_remote_copy(
+            src_ref=parts.at[layer, 2 * (1 - side) + core, :, rows],
+            dst_ref=x_in.at[:, rows],
+            send_sem=x_send.at[layer, stage],
+            recv_sem=x_recv.at[layer, stage],
+            device_id=(2 * (1 - side) + core, blk),
+            device_id_type=MESH,
+        )
+
+    def yz_copy(layer, stage, step):
+        first, count = (EARLY, LATE)[stage]
+        rows = pl.ds(first, count)
+        peer = lax.rem(blk + step, RUNS)
+        return pltpu.make_async_remote_copy(
+            src_ref=parts.at[layer, grp, peer, rows],
+            dst_ref=yz_in.at[layer, RUNS - step, rows],
+            send_sem=yz_send.at[layer, stage, step],
+            recv_sem=yz_recv.at[layer, stage, RUNS - step],
+            device_id=(grp, peer),
+            device_id_type=MESH,
+        )
+
+    def final_copy(layer, stage, step):
+        first, count = (EARLY, LATE)[stage]
+        rows = pl.ds(first, count)
+        return pltpu.make_async_remote_copy(
+            src_ref=final.at[layer, grp, rows],
+            dst_ref=final.at[layer, grp, rows],
+            send_sem=fin_send.at[layer, stage, step],
+            recv_sem=fin_recv.at[layer, stage, step],
+            device_id=(lax.rem(grp + step, 4), blk),
+            device_id_type=MESH,
+        )
+
+    def core_start(layer, stage):
+        if layer == 0:
+            pl.semaphore_wait(core_free.at[stage], 1)
+        for across in range(2):
+            core_copy(layer, stage, across).start()
+
+    def core_done(layer, stage):
+        first, count = (EARLY, LATE)[stage]
+        rows = pl.ds(first, count)
+        for across in range(2):
+            core_copy(layer, stage, across).wait()
+        for turn in range(2):
+            across = 1 - side if turn == 0 else side
+
+            def add(place, carry):
+                own = parts[layer, 2 * across + core, place, rows, :].astype(F32)
+                own = own + core_in[across, place, rows, :].astype(F32)
+                parts[layer, 2 * across + core, place, rows, :] = own.astype(BF16)
+                return carry
+
+            lax.fori_loop(0, RUNS, add, 0)
+            if turn == 0:
+                if layer == 0:
+                    pl.semaphore_wait(x_free.at[stage], 1)
+                x_copy(layer, stage).start()
+        if layer == 1:
+            pl.semaphore_signal(
+                core_free.at[stage],
+                inc=1,
+                device_id=(2 * side + 1 - core, blk),
+                device_id_type=MESH,
+            )
+
+    def x_done(layer, stage):
+        first, count = (EARLY, LATE)[stage]
+        rows = pl.ds(first, count)
+        x_copy(layer, stage).wait()
+
+        def add(place, carry):
+            own = parts[layer, grp, place, rows, :].astype(F32) + x_in[place, rows, :].astype(F32)
+            parts[layer, grp, place, rows, :] = own.astype(BF16)
+            return carry
+
+        lax.fori_loop(0, RUNS, add, 0)
+        if layer == 1:
+            pl.semaphore_signal(
+                x_free.at[stage],
+                inc=1,
+                device_id=(2 * (1 - side) + core, blk),
+                device_id_type=MESH,
+            )
+        for step in range(1, RUNS):
+            yz_copy(layer, stage, step).start()
+
+    def yz_done(layer, stage):
+        first, count = (EARLY, LATE)[stage]
+        rows = pl.ds(first, count)
+        for step in range(1, RUNS):
+            yz_copy(layer, stage, step).wait()
+        total = parts[layer, grp, blk, rows, :].astype(F32)
+        for slot in range(1, RUNS):
+            total = total + yz_in[layer, slot, rows, :].astype(F32)
+        final[layer, grp, rows, :] = total.astype(BF16)
+        for step in range(1, 4):
+            final_copy(layer, stage, step).start()
+
+    def final_done(layer, stage):
+        for step in range(1, 4):
+            final_copy(layer, stage, step).wait()
+        for quarter in range(4):
+            at = slice(128 * quarter, 128 * quarter + 128)
+
+            def block(first, count):
+                return final[layer, quarter, first : first + count, :].astype(F32)
+
+            if stage == 0:
+                out_grad[layer, :, at] = block(192, DIM)
+                for step in range(4):
+                    up_grad[layer, :, CUT * step + 128 * quarter : CUT * step + 128 * quarter + 128] = block(
+                        256 + DIM * step, DIM
+                    )
+                down_grad[layer, :, at] = block(512, 256)
+            else:
+                for step in range(3):
+                    qkv_grad[layer, :, WIDTH * step + 128 * quarter : WIDTH * step + 128 * quarter + 128] = block(
+                        DIM * step, DIM
+                    )
+
+    def small_copy(step):
+        return pltpu.make_async_remote_copy(
+            src_ref=small_grp.at[grp],
+            dst_ref=small_grp.at[grp],
+            send_sem=small_send.at[step],
+            recv_sem=small_recv.at[step],
+            device_id=(lax.rem(grp + step, 4), blk),
+            device_id_type=MESH,
+        )
+
+    def wide_copy(step):
+        return pltpu.make_async_remote_copy(
+            src_ref=small_blk.at[blk],
+            dst_ref=small_blk.at[blk],
+            send_sem=wide_send.at[step],
+            recv_sem=wide_recv.at[step],
+            device_id=(grp, lax.rem(blk + step, RUNS)),
+            device_id_type=MESH,
+        )
+
+    def small_start():
+        small_grp[grp] = small[0] + small[1]
+        for step in range(1, 4):
+            small_copy(step).start()
+
+    def small_middle():
+        for step in range(1, 4):
+            small_copy(step).wait()
+        small_blk[blk] = (small_grp[0] + small_grp[1]) + (small_grp[2] + small_grp[3])
+        for step in range(1, RUNS):
+            wide_copy(step).start()
+
+    def small_done():
+        for step in range(1, RUNS):
+            wide_copy(step).wait()
+        total = small_blk[0]
+        for place in range(1, RUNS):
+            total = total + small_blk[place]
+        small_sum[...] = total
+        up_bias_grad[...] = small_sum[:, pl.ds(pl.multiple_of(blk * 256, 256), 256)]
+        pair = small_sum[:, pl.ds(pl.multiple_of(FF + 128 * lax.div(blk, 2), 128), 128)]
+        turned = pltpu.roll(pair, DIM, 1)
+        down_bias_grad[...] = jnp.where(lax.rem(blk, 2) == 1, turned, pair)[:, 0:DIM]
+        alpha_grad[...] = small_sum[:, FF + WIDTH : FF + WIDTH + 2]
+
+    def halves(*phases):
+        def both(half, carry):
+            for phase in phases:
+                phase(half)
+            return carry
+
+        lax.fori_loop(0, 2, both, 0)
+
+    for half in range(2):
+        hidden[half] = tokens[HALF * half : HALF * half + HALF, :].astype(F32)
+    pl.semaphore_wait(barrier, RUNS - 1 + 3)
+    weight_copies[0, 0].wait()
+    halves(functools.partial(project, 0))
+    for number in range(1, 4):
+        weight_copies[0, number].wait()
+    halves(functools.partial(attend, 0))
+    weight_copies[1, 0].wait()
+    halves(functools.partial(feed, 0), functools.partial(project, 1))
+    for number in range(1, 4):
+        weight_copies[1, number].wait()
+    halves(functools.partial(attend, 1))
+    halves(functools.partial(feed, 1))
+    for half in range(2):
+        output[HALF * half : HALF * half + HALF, :] = hidden[half].astype(BF16)
+        grad[half] = cotangent[HALF * half : HALF * half + HALF, :].astype(F32)
+
+    halves(functools.partial(feed_back, 1))
+    early_grads(1)
+    core_start(1, 0)
+    halves(functools.partial(attend_back, 1))
+    core_done(1, 0)
+    halves(functools.partial(project_back, 1), functools.partial(feed_back, 0))
+    small_start()
+    late_grads(1)
+    core_start(1, 1)
+    early_grads(0)
+    core_start(0, 0)
+    x_done(1, 0)
+    core_done(1, 1)
+    halves(functools.partial(attend_back, 0))
+    small_middle()
+    core_done(0, 0)
+    halves(functools.partial(project_back, 0))
+    for half in range(2):
+        input_grad[HALF * half : HALF * half + HALF, :] = grad[half]
+    late_grads(0)
+    core_start(0, 1)
+    x_done(1, 1)
+    yz_done(1, 0)
+    core_done(0, 1)
+    small_done()
+    x_done(0, 0)
+    yz_done(1, 1)
+    x_done(0, 1)
+    final_done(1, 0)
+    final_done(1, 1)
+    yz_done(0, 0)
+    yz_done(0, 1)
+    final_done(0, 0)
+    final_done(0, 1)
+
+    for half in range(2):
+        left(2, 0, half, head_out)
+        left(3, 0, half, pack_out)
+
+
+def fast_body(
+    tokens, seq_len, qkv_weight, out_weight, up_weight, up_bias, down_weight, down_bias, alphas, cotangent
+):
+    whole = pl.BlockSpec(memory_space=pltpu.VMEM)
+    scalar = pl.BlockSpec(memory_space=pltpu.SMEM)
+    far = pl.BlockSpec(memory_space=pl.ANY)
+    shape = jax.ShapeDtypeStruct
+    rows = HALF * RUNS
+
+    def vmem(*dims):
+        return pltpu.VMEM(dims, BF16)
+
+    def wide(*dims):
+        return pltpu.VMEM(dims, F32)
+
+    dma = pltpu.SemaphoreType.DMA
+    return tuple(
+        pl.pallas_call(
+            layers_kernel,
+            out_shape=(
+                shape((2 * HALF, WIDTH), BF16),
+                shape((2 * HALF, WIDTH), F32),
+                shape((LAYERS, DIM, 3 * WIDTH), F32),
+                shape((LAYERS, DIM, WIDTH), F32),
+                shape((LAYERS, DIM, FF), F32),
+                shape((LAYERS, FF // RUNS), F32),
+                shape((LAYERS, FF // RUNS, WIDTH), F32),
+                shape((LAYERS, DIM), F32),
+                shape((LAYERS, 2), F32),
+            ),
+            in_specs=[whole, scalar, scalar, whole, whole, whole, far, far, far, far],
+            out_specs=(whole,) * 9,
+            scratch_shapes=[
+                vmem(LAYERS, WIDTH, 3 * WIDTH),
+                vmem(LAYERS, WIDTH, WIDTH),
+                vmem(LAYERS, WIDTH, FF),
+                vmem(LAYERS, FF, WIDTH),
+                wide(2, HALF, WIDTH),
+                wide(2, HALF, WIDTH),
+                vmem(LAYERS, WIDTH, 2 * HALF),
+                vmem(LAYERS, WIDTH, 2 * HALF),
+                vmem(LAYERS, WIDTH, 2 * HALF),
+                vmem(LAYERS, FF, 2 * HALF),
+                wide(LAYERS, 2, HALF, WIDTH),
+                wide(LAYERS, 2, HALF, FF),
+                wide(LAYERS, 2, HALF, WIDTH),
+                vmem(2 * HALF, WIDTH),
+                vmem(2 * HALF, FF),
+                vmem(2 * HALF, WIDTH),
+                vmem(2 * HALF, 3 * WIDTH),
+                vmem(2, RUNS, PACK, 128),
+                vmem(2, RUNS, DIM, 128),
+                vmem(LAYERS, 2, RUNS, PACK, 128),
+                vmem(LAYERS, 2, RUNS, DIM, 128),
+                vmem(LAYERS, 2, RUNS, DIM, 128),
+                vmem(LAYERS, 2, RUNS, PACK, 128),
+                vmem(LAYERS, 2, rows, 128),
+                vmem(LAYERS, 2, 128, rows),
+                vmem(LAYERS, 2, 128, rows),
+                vmem(128, rows),
+                wide(LAYERS, 2, DIM, rows),
+                wide(LAYERS, 2, 1, rows),
+                wide(rows, 128),
+                wide(DIM, rows),
+                wide(2, 2, TILE, TILE),
+                vmem(LAYERS, 4, RUNS, CHUNK, 128),
+                vmem(2, RUNS, CHUNK, 128),
+                vmem(RUNS, CHUNK, 128),
+                vmem(LAYERS, RUNS, CHUNK, 128),
+                vmem(LAYERS, 4, CHUNK, 128),
+                wide(2, LAYERS, SMALL),
+                wide(4, LAYERS, SMALL),
+                wide(LAYERS, SMALL),
+                wide(RUNS, LAYERS, SMALL),
+                dma((LAYERS, 4)),
+                dma((4, LAYERS, 2)),
+                dma((4, LAYERS, 2)),
+                dma((LAYERS, 2, 2)),
+                dma((LAYERS, 2, 2)),
+                dma((LAYERS, 2)),
+                dma((LAYERS, 2)),
+                dma((LAYERS, 2, RUNS)),
+                dma((LAYERS, 2, RUNS)),
+                dma((LAYERS, 2, 4)),
+                dma((LAYERS, 2, 4)),
+                dma((4,)),
+                dma((4,)),
+                dma((RUNS,)),
+                dma((RUNS,)),
+                pltpu.SemaphoreType.REGULAR((2,)),
+                pltpu.SemaphoreType.REGULAR((2,)),
+            ],
+            compiler_params=pltpu.CompilerParams(
+                collective_id=0, has_side_effects=True, vmem_limit_bytes=63 * 1024 * 1024
+            ),
+            name="layers",
+        )(
+            tokens, seq_len, alphas, up_bias, down_bias, cotangent,
+            qkv_weight, out_weight, up_weight, down_weight,
+        )
+    )
 
 
 def layout(seq_len, local_count, cycle_size):
@@ -357,8 +1001,9 @@
         P(),
         P(("grp", "blk"), None),
     )
+    sizes = (mesh.shape["grp"], mesh.shape["blk"])
     return jax.shard_map(
-        body,
+        fast_body if sizes == (4, RUNS) else body,
         mesh=mesh,
         in_specs=placed,
         out_specs=(

time: 1200 us -> 205 us (0.17)
  waiting for transfers between devices: 809 us -> 0 us
  Pallas kernels: 0 us -> 190 us
  matrix products: 157 us -> 0 us
  local copies, waits for them, and re-layouts: 112 us -> 11.1 us
  other arithmetic: 51.8 us -> 0 us
  blocking collectives: 25.9 us -> 0 us
  loops' own time: 17.7 us -> 0 us
  between operations: 16.5 us -> 0.7 us
    reduce_scatter x5 -> x0, waiting for transfers between devices: 417 us -> none  [the longest x2 170 us: layer_backward(): lax.psum_scatter(key_terms.astype(jnp.bfloat16), 'blk', scatter_dimension...]
    unnamed x14 -> x0, waiting for transfers between devices: 213 us -> none
    pallas_call x0 -> x1, Pallas kernels: none -> 190 us  [fast_body(): pl.pallas_call(layers_kernel, out_shape=(shape((2 * HALF, WIDTH), BF16),...]
    dot_general x82 -> x0, matrix products: 157 us -> none  [the longest x16 29.2 us: block_scores(): jnp.einsum('qhd,khd->hqk', queries, keys_part, preferred_element_type=jnp...]
    all_gather x2 -> x0, waiting for transfers between devices: 145 us -> none  [layer_forward(): whole = lax.all_gather(key_value, 'blk', axis=0, tiled=True)]
    psum x1 -> x0, waiting for transfers between devices: 34.3 us -> none  [reduce_all(): lax.psum(shares[0].astype(jnp.bfloat16), 'grp').astype(jnp.float32)]
    slice x27 -> x0, local copies, waits for them, and re-layouts: 29.7 us -> none  [the longest x16 18.9 us: key_block(): keys_part = key_piece[:, :half_width].reshape(block_rows, head_count, -1)]
    reduce_sum x14 -> x0, other arithmetic: 29.5 us -> none  [the longest x8 24.4 us: statistics(): totals = totals * jnp.exp(largest - newest) + jnp.sum(weights, axis=2)]
  transfers between devices with their start and end apart: 11 -> 0, of which waited for: 11 -> 0; matrix products, arithmetic and copies ran while one was open for 3% -> 0% of each run, Pallas kernels for 0% -> 0%
where the time goes in v1:
time: 205 us; the launch traced here: 202 us
  Pallas kernels  190 us (93%)
  local copies, waits for them, and re-layouts  11.1 us (5%)
    pallas_call x1, Pallas kernels, fast_body(): pl.pallas_call(layers_kernel, out_shape=(shape((2 * HALF, WIDTH), BF16),...  190 us
    unnamed x19, local copies, waits for them, and re-layouts  11.1 us

profile of v1, /device:TPU:0, one launch (start us, length us, event | category | flops | bytes accessed | tf_op | source)
XLA Modules:
  0.0 202.1 jit_solution(11039182320296751145)
XLA Ops:
  0.6 190.3 %layers.1 = (bf16[256,512]{1,0:T(8,128)(2,1)}, f32[256,512]{1,0:T(8,128)}, f32[2,64,1536]{2,1,0:T(8,128)}, f32[2,64,512]{2,1,0:T(8,128)}, f32[2,64,2048]{2,1,0:T...) custom-call(bf16[256,512]{1,0:T(8,128)(2,1)} %tokens.1, ...), custom_call_target="tpu_custom_call" | custom-call | tf_op jit(solution)/shard_map/layers/pallas_call | solution.py:571
  191.0 0.0 copy-start.1
  191.0 0.0 copy-start.2
  191.0 0.0 copy-start
  191.0 0.0 copy-start.4
  191.0 0.0 copy-start.3
  191.0 1.8 copy.28
  192.8 1.9 copy.29
  194.7 2.1 %copy.30 = f32[2,64,1536]{2,1,0:T(8,128)} copy(f32[2,64,1536]{2,1,0:T(8,128)} %get-tuple-element.20) | data formatting | bytes 1572864
  196.8 1.7 copy.31
  198.4 0.0 copy-done.1
  198.4 1.0 copy.32
  199.4 0.0 copy-done.2
  199.4 0.6 copy.33
  200.0 0.0 copy-done
  200.0 1.0 copy.34
  201.0 0.0 copy-done.4
  201.0 0.6 copy.35
  201.5 0.0 copy-done.3
  201.5 0.6 copy.36
Async XLA Ops:
  191.0 7.5 %copy-start.1 = (f32[2,64,2048]{2,1,0:T(8,128)S(1)}, f32[2,64,2048]{2,1,0:T(8,128)}, u32[]{:S(2)}) copy-start(f32[2,64,2048]{2,1,0:T(8,128)} %get-tuple-element.22) | copy-start | bytes 3145732
  191.0 8.4 %copy-start.2 = (f32[2,256]{1,0:T(2,128)S(1)}, f32[2,256]{1,0:T(2,128)}, u32[]{:S(2)}) copy-start(f32[2,256]{1,0:T(2,128)} %get-tuple-element.23) | copy-start | bytes 6148
  191.0 9.0 %copy-start = (f32[2,256,512]{2,1,0:T(8,128)S(1)}, f32[2,256,512]{2,1,0:T(8,128)}, u32[]{:S(2)}) copy-start(f32[2,256,512]{2,1,0:T(8,128)} %get-tuple-element.24) | copy-start | bytes 3145732
  191.0 10.0 %copy-start.4 = (f32[2,64]{1,0:T(2,128)S(1)}, f32[2,64]{1,0:T(2,128)}, u32[]{:S(2)}) copy-start(f32[2,64]{1,0:T(2,128)} %get-tuple-element.25) | copy-start | bytes 1540
  191.0 10.5 %copy-start.3 = (f32[2,2]{1,0:T(2,128)S(1)}, f32[2,2]{1,0:T(2,128)}, u32[]{:S(2)}) copy-start(f32[2,2]{1,0:T(2,128)} %get-tuple-element.26) | copy-start | bytes 52

commit v2 on v0

--- a/solution.py
+++ b/solution.py
@@ -1,13 +1,874 @@
+import functools
+
 import jax
 import jax.numpy as jnp
 from jax import lax
+from jax.experimental import pallas as pl
+from jax.experimental.pallas import tpu as pltpu
 from jax.sharding import PartitionSpec as P
 
 HEADS = 8
 LAYERS = 2
-
-
 NEGATIVE = -1e30
+MESH = pl.DeviceIdType.MESH
+F32 = jnp.float32
+BF16 = jnp.bfloat16
+
+HALF = 128
+RUNS = 8
+TEAM = 4
+OWN = RUNS // TEAM
+DIM = 64
+WIDTH = 512
+FF = 2048
+CUT = 512
+TILE = 256
+PACK = HALF + DIM
+CHUNK = 768
+SMALL = FF + WIDTH + 128
+ROWS = (((192, 288), (480, 288)), ((0, 96), (96, 96)))
+SPAN = ((192, 576), (0, 192))
+
+
+def nn(a, b):
+    return lax.dot_general(a, b, (((1,), (0,)), ((), ())), preferred_element_type=F32)
+
+
+def nt(a, b):
+    return lax.dot_general(a, b, (((1,), (1,)), ((), ())), preferred_element_type=F32)
+
+
+def layers_kernel(
+    tokens, seq_len, alphas, up_bias, down_bias, cotangent, qkv_hbm, out_hbm, up_hbm, down_hbm,
+    final_hbm, output_hbm, input_grad_hbm, small_final,
+    wqkv, wout, wup, wdown,
+    tok_in, cot_in, flag_out, flag_in, back_out, out_in, grad_in,
+    hidden, grad, hid_t, attn_t, ent_t, act_t, branch, slope, second,
+    dz, du, da, dqkv,
+    pack_out, head_out, qkv_in, o_in, do_in, dqkv_in,
+    kv, kv_t, rq, ro, o_t, lse, acc, dq_t, bias,
+    parts, core_in, x_in, y_in, z_in, final, small, small_in, small_z, small_sum,
+    w_sem, move_send, move_recv, a2a_send, a2a_recv, core_send, core_recv, x_send, x_recv, y_send, y_recv,
+    z_send, z_recv, fin_send, fin_recv, small_send, small_recv, out_sem, core_free, x_free, y_free,
+):
+    grp = lax.axis_index("grp")
+    blk = lax.axis_index("blk")
+    core = lax.rem(grp, 2)
+    side = lax.div(grp, 2)
+    yy = lax.rem(blk, 2)
+    zz = lax.div(blk, 2)
+    member = 2 * core + yy
+    far_side = 2 * (1 - side) + core
+    low = lax.broadcasted_iota(jnp.int32, (HALF, 128), 1) < DIM
+
+    def place(c, x, z, y):
+        return (2 * x + c, 2 * z + y)
+
+    core_peer = place(1 - core, side, zz, yy)
+    x_peer = place(core, 1 - side, zz, yy)
+    y_peer = place(core, side, zz, 1 - yy)
+
+    weight_copies = {}
+    for layer in range(LAYERS):
+        for number, (source, target) in enumerate(
+            ((qkv_hbm, wqkv), (out_hbm, wout), (up_hbm, wup), (down_hbm, wdown))
+        ):
+            weight_copies[layer, number] = pltpu.make_async_copy(
+                source.at[layer], target.at[layer], w_sem.at[layer, number]
+            )
+            weight_copies[layer, number].start()
+
+    barrier = pltpu.get_barrier_semaphore()
+    for step in range(1, 4):
+        pl.semaphore_signal(
+            barrier, inc=1, device_id=place(core, side, lax.rem(zz + step, 4), yy), device_id_type=MESH
+        )
+    for step in range(4):
+        pl.semaphore_signal(
+            barrier, inc=1, device_id=place(1 - core, side, lax.rem(zz + step, 4), yy), device_id_type=MESH
+        )
+    pl.semaphore_signal(barrier, inc=1, device_id=x_peer, device_id_type=MESH)
+    pl.semaphore_signal(barrier, inc=1, device_id=y_peer, device_id_type=MESH)
+    pl.semaphore_signal(
+        barrier, inc=1, device_id=place(1 - core, side, zz, 1 - yy), device_id_type=MESH
+    )
+
+    end_second = lax.div(seq_len[0, 0] + seq_len[0, 1], RUNS)
+    flag_out[...] = jnp.full((8, 128), end_second.astype(F32), F32)
+    for layer in range(LAYERS):
+        for head in range(OWN):
+            rq[layer, head, DIM:, :] = jnp.zeros((DIM, HALF * RUNS), BF16)
+    for head in range(OWN):
+        ro[head, 0:DIM, :] = jnp.zeros((DIM, HALF * RUNS), BF16)
+
+    def moved(kind, slot, source, target, at, core_at, z_at):
+        here = jnp.logical_and(core_at == core, z_at == zz)
+
+        @pl.when(here)
+        def _():
+            pltpu.make_async_copy(source, target.at[at], move_recv.at[kind, at]).start()
+
+        @pl.when(jnp.logical_not(here))
+        def _():
+            pltpu.make_async_remote_copy(
+                src_ref=source,
+                dst_ref=target.at[at],
+                send_sem=move_send.at[kind, slot],
+                recv_sem=move_recv.at[kind, at],
+                device_id=place(core_at, side, z_at, yy),
+                device_id_type=MESH,
+            ).start()
+
+    def move_left(kind, slot, source, core_at, z_at):
+        here = jnp.logical_and(core_at == core, z_at == zz)
+
+        @pl.when(jnp.logical_not(here))
+        def _():
+            pltpu.make_async_copy(source, source, move_send.at[kind, slot]).wait()
+
+    def move_arrived(kind, at, target):
+        pltpu.make_async_copy(target.at[at], target.at[at], move_recv.at[kind, at]).wait()
+
+    def to_team(kind, half, source, target):
+        moved(kind, half, source, target, lax.div(zz, 2), lax.rem(zz, 2), 2 * half + core)
+
+    def to_team_left(kind, half, source):
+        move_left(kind, half, source, lax.rem(zz, 2), 2 * half + core)
+
+    def to_owner(kind, chunk, source, target):
+        moved(kind, chunk, source, target, lax.div(zz, 2), lax.rem(zz, 2), core + 2 * chunk)
+
+    def to_owner_left(kind, chunk, source):
+        move_left(kind, chunk, source, lax.rem(zz, 2), core + 2 * chunk)
+
+    def half_of(ref, half):
+        return ref.at[pl.ds(HALF * half, HALF)]
+
+    def rows_of(half):
+        return pl.ds(pl.multiple_of(half * HALF, HALF), HALF)
+
+    def slot_of(other):
+        return lax.rem(other + TEAM - member, TEAM)
+
+    def exchange(kind, layer, half, outgoing, incoming):
+        incoming[layer, half, 0] = outgoing[half, member]
+        for step in range(1, TEAM):
+            peer = lax.rem(member + step, TEAM)
+            pltpu.make_async_remote_copy(
+                src_ref=outgoing.at[half, peer],
+                dst_ref=incoming.at[layer, half, TEAM - step],
+                send_sem=a2a_send.at[kind, layer, half],
+                recv_sem=a2a_recv.at[kind, layer, half],
+                device_id=place(lax.div(peer, 2), side, zz, lax.rem(peer, 2)),
+                device_id_type=MESH,
+            ).start()
+
+    def arrived(kind, layer, half, incoming):
+        whole = incoming.at[layer, half, pl.ds(1, TEAM - 1)]
+        pltpu.make_async_copy(whole, whole, a2a_recv.at[kind, layer, half]).wait()
+
+    def left(kind, layer, half, outgoing):
+        whole = outgoing.at[half, pl.ds(1, TEAM - 1)]
+        pltpu.make_async_copy(whole, whole, a2a_send.at[kind, layer, half]).wait()
+
+    def project(layer, half):
+        rows = rows_of(half)
+        rounded = hidden[half].astype(BF16)
+        hid_t[layer, :, rows] = rounded.T
+        if layer == 1:
+            left(0, 0, half, pack_out)
+        queries = nn(rounded, wqkv[layer, :, 0:WIDTH]) * (DIM ** -0.5)
+        queries_t = queries.T.astype(BF16)
+        keys = nn(rounded, wqkv[layer, :, WIDTH : 2 * WIDTH])
+        values = nn(rounded, wqkv[layer, :, 2 * WIDTH : 3 * WIDTH])
+        for pair in range(RUNS // 2):
+            k_pair = keys[:, 128 * pair : 128 * pair + 128]
+            v_pair = values[:, 128 * pair : 128 * pair + 128]
+            first = jnp.where(low, k_pair, pltpu.roll(v_pair, DIM, 1))
+            other = jnp.where(low, pltpu.roll(k_pair, DIM, 1), v_pair)
+            pack_out[half, pair, 0, 0:HALF, :] = first.astype(BF16)
+            pack_out[half, pair, 1, 0:HALF, :] = other.astype(BF16)
+        for head in range(RUNS):
+            pack_out[half, head // 2, head % 2, HALF:, :] = queries_t[DIM * head : DIM * head + DIM, :]
+        exchange(0, layer, half, pack_out, qkv_in)
+
+    def attend(layer, chunk):
+        arrived(0, layer, chunk, qkv_in)
+        if layer == 1:
+            left(1, 0, chunk, head_out)
+
+        def one_head(head, carry):
+            for other in range(TEAM):
+                slot = slot_of(other)
+                start = HALF * (TEAM * chunk + other)
+                span = slice(start, start + HALF)
+                block = qkv_in[layer, chunk, slot, head, 0:HALF, :]
+                kv[layer, head, span, :] = block
+                kv_t[layer, head, :, span] = block.T
+                rq[layer, head, 0:DIM, span] = qkv_in[layer, chunk, slot, head, HALF:, :]
+            for i in (2 * chunk, 2 * chunk + 1):
+                columns = slice(TILE * i, TILE * i + TILE)
+                query_tile = rq[layer, head, :, columns]
+                scores = []
+                for j in range(i + 1):
+                    tile = nn(kv[layer, head, TILE * j : TILE * j + TILE, :], query_tile)
+                    scores.append(tile + bias[1 if j == i else 0])
+                largest = functools.reduce(
+                    jnp.maximum, [jnp.max(tile, axis=0, keepdims=True) for tile in scores]
+                )
+                total = jnp.zeros((1, TILE), F32)
+                summed = jnp.zeros((DIM, TILE), F32)
+                for j in range(i + 1):
+                    weight = jnp.exp(scores[j] - largest)
+                    total = total + jnp.sum(weight, axis=0, keepdims=True)
+                    summed = summed + nn(
+                        kv_t[layer, head, DIM:, TILE * j : TILE * j + TILE], weight.astype(BF16)
+                    )
+                summed = summed / total
+                o_t[layer, head, :, columns] = summed
+                lse[layer, head, :, columns] = largest + jnp.log(total)
+                rounded = summed.astype(BF16)
+                for part in range(2):
+                    head_out[chunk, 2 * (i - 2 * chunk) + part, head] = rounded[
+                        :, HALF * part : HALF * part + HALF
+                    ]
+            return carry
+
+        lax.fori_loop(0, OWN, one_head, 0)
+        exchange(1, layer, chunk, head_out, o_in)
+
+    def feed(layer, half):
+        rows = rows_of(half)
+        arrived(1, layer, half, o_in)
+        for head in range(RUNS):
+            attn_t[layer, DIM * head : DIM * head + DIM, rows] = o_in[layer, half, slot_of(head // 2), head % 2]
+        attn = attn_t[layer, :, rows].T
+        grown = nn(attn, wout[layer])
+        branch[layer, half] = grown
+        middle = hidden[half] + alphas[layer, 0] * grown
+        entered = middle.astype(BF16)
+        ent_t[layer, :, rows] = entered.T
+        total = jnp.zeros((HALF, WIDTH), F32)
+        for step in range(FF // CUT):
+            cut = slice(CUT * step, CUT * step + CUT)
+            gate = nn(entered, wup[layer, :, cut]) + up_bias[layer : layer + 1, cut]
+            risen = 0.5 * (1.0 + lax.erf(gate * (0.5 ** 0.5)))
+            slope[layer, half, :, cut] = risen + gate * jnp.exp(-0.5 * gate * gate) * 0.3989422804014327
+            active = (gate * risen).astype(BF16)
+            act_t[layer, cut, rows] = active.T
+            total = total + nn(active, wdown[layer, cut, :])
+        total = total + down_bias[layer : layer + 1, :]
+        second[layer, half] = total
+        hidden[half] = middle + alphas[layer, 1] * total
+
+    def total_of(values):
+        return jnp.sum(jnp.sum(values, axis=0, keepdims=True), axis=1, keepdims=True)
+
+    def feed_back(layer, half):
+        rows = rows_of(half)
+        start = grad[half]
+        scaled = (alphas[layer, 1] * start).astype(BF16)
+        dz[rows, :] = scaled
+        alpha_second = total_of(start * second[layer, half])
+        small[half, layer : layer + 1, FF : FF + WIDTH] = jnp.sum(scaled.astype(F32), axis=0, keepdims=True)
+        middle = start
+        for step in range(FF // CUT):
+            cut = slice(CUT * step, CUT * step + CUT)
+            gate = (nt(scaled, wdown[layer, cut, :]) * slope[layer, half, :, cut]).astype(BF16)
+            du[rows, cut] = gate
+            small[half, layer : layer + 1, cut] = jnp.sum(gate.astype(F32), axis=0, keepdims=True)
+            middle = middle + nt(gate, wup[layer, :, cut])
+        grad[half] = middle
+        alpha_first = total_of(middle * branch[layer, half])
+        column = lax.broadcasted_iota(jnp.int32, (1, 128), 1)
+        small[half, layer : layer + 1, FF + WIDTH :] = jnp.where(
+            column == 0, alpha_first, jnp.where(column == 1, alpha_second, 0.0)
+        )
+        mixed = (alphas[layer, 0] * middle).astype(BF16)
+        da[rows, :] = mixed
+        spread = nt(wout[layer], mixed).astype(BF16)
+        left(*((1, 1) if layer == 1 else (2, 1)), half, head_out)
+        for head in range(RUNS):
+            head_out[half, head // 2, head % 2] = spread[DIM * head : DIM * head + DIM, :]
+        exchange(2, layer, half, head_out, do_in)
+
+    def attend_back(layer, chunk):
+        arrived(2, layer, chunk, do_in)
+        left(*((0, 1) if layer == 1 else (3, 1)), chunk, pack_out)
+
+        def one_head(head, carry):
+            for other in range(TEAM):
+                start = HALF * (TEAM * chunk + other)
+                ro[head, DIM:, start : start + HALF] = do_in[layer, chunk, slot_of(other), head]
+            for i in (2 * chunk, 2 * chunk + 1):
+                columns = slice(TILE * i, TILE * i + TILE)
+                query_tile = rq[layer, head, :, columns]
+                grad_tile = ro[head, :, columns]
+                log_total = lse[layer, head, :, columns]
+                delta = jnp.sum(
+                    ro[head, DIM:, columns].astype(F32) * o_t[layer, head, :, columns],
+                    axis=0,
+                    keepdims=True,
+                )
+                query_grad = jnp.zeros((DIM, TILE), F32)
+                for j in range(i + 1):
+                    span = slice(TILE * j, TILE * j + TILE)
+                    keys = kv[layer, head, span, :]
+                    weight = jnp.exp(nn(keys, query_tile) + bias[1 if j == i else 0] - log_total)
+                    scored = (weight * (nn(keys, grad_tile) - delta)).astype(BF16)
+                    term = nt(scored, query_tile) + nt(weight.astype(BF16), grad_tile)
+                    if chunk == 1 and (i == 2 or j == i):
+                        acc[head, span, :] = term
+                    else:
+                        acc[head, span, :] += term
+                    query_grad = query_grad + nn(kv_t[layer, head, 0:DIM, span], scored)
+                dq_t[:, columns] = query_grad * (DIM ** -0.5)
+            for other in range(TEAM):
+                start = HALF * (TEAM * chunk + other)
+                span = slice(start, start + HALF)
+                pack_out[chunk, other, head, 0:HALF, :] = acc[head, span, :].astype(BF16)
+                pack_out[chunk, other, head, HALF:, :] = dq_t[:, span].astype(BF16)
+            return carry
+
+        lax.fori_loop(0, OWN, one_head, 0)
+        exchange(3, layer, chunk, pack_out, dqkv_in)
+
+    def project_back(layer, half):
+        rows = rows_of(half)
+        arrived(3, layer, half, dqkv_in)
+        turned = jnp.concatenate(
+            [dqkv_in[layer, half, slot_of(head // 2), head % 2, HALF:, :] for head in range(RUNS)], axis=0
+        )
+        dqkv[rows, 0:WIDTH] = turned.T
+        for pair in range(RUNS // 2):
+            first = dqkv_in[layer, half, slot_of(pair), 0, 0:HALF, :].astype(F32)
+            other = dqkv_in[layer, half, slot_of(pair), 1, 0:HALF, :].astype(F32)
+            k_pair = jnp.where(low, first, pltpu.roll(other, DIM, 1))
+            v_pair = jnp.where(low, pltpu.roll(first, DIM, 1), other)
+            dqkv[rows, WIDTH + 128 * pair : WIDTH + 128 * pair + 128] = k_pair.astype(BF16)
+            dqkv[rows, 2 * WIDTH + 128 * pair : 2 * WIDTH + 128 * pair + 128] = v_pair.astype(BF16)
+        grad[half] = grad[half] + nt(dqkv[rows, :], wqkv[layer])
+
+    def scatter_rows(layer, result, first_row):
+        for run in range(RUNS):
+            for quarter in range(4):
+                parts[layer, quarter, run // 2, run % 2, first_row : first_row + DIM, :] = result[
+                    DIM * run : DIM * run + DIM, 128 * quarter : 128 * quarter + 128
+                ].astype(BF16)
+
+    def early_grads(layer):
+        scatter_rows(layer, nn(attn_t[layer], da[...]), 192)
+        for step in range(FF // CUT):
+            cut = slice(CUT * step, CUT * step + CUT)
+            scatter_rows(layer, nn(ent_t[layer], du[:, cut]), 256 + DIM * step)
+        for run in range(RUNS):
+            result = nn(act_t[layer, TILE * run : TILE * run + TILE, :], dz[...])
+            for quarter in range(4):
+                parts[layer, quarter, run // 2, run % 2, 512:768, :] = result[
+                    :, 128 * quarter : 128 * quarter + 128
+                ].astype(BF16)
+
+    def late_grads(layer):
+        for step in range(3):
+            scatter_rows(layer, nn(hid_t[layer], dqkv[:, WIDTH * step : WIDTH * step + WIDTH]), DIM * step)
+
+    def remote(source, target, send, recv, peer):
+        return pltpu.make_async_remote_copy(
+            src_ref=source,
+            dst_ref=target,
+            send_sem=send,
+            recv_sem=recv,
+            device_id=peer,
+            device_id_type=MESH,
+        )
+
+    def credit(semaphore, peer):
+        pl.semaphore_signal(semaphore, inc=1, device_id=peer, device_id_type=MESH)
+
+    def core_copy(layer, part, across):
+        rows = pl.ds(*SPAN[part])
+        return remote(
+            parts.at[layer, 2 * across + 1 - core, :, :, rows],
+            core_in.at[across, :, :, rows],
+            core_send.at[layer, part, across],
+            core_recv.at[layer, part, across],
+            core_peer,
+        )
+
+    def x_copy(layer, part, order):
+        rows = pl.ds(*ROWS[part][order])
+        which = (x_send.at[layer, part, order], x_recv.at[layer, part, order], x_peer)
+        if order == 0:
+            return remote(parts.at[layer, far_side, :, :, rows], x_in.at[:, :, rows], *which)
+        return remote(parts.at[layer, far_side, :, yy, rows], x_in.at[:, 0, rows], *which)
+
+    def y_copy(layer, part, order, across):
+        rows = pl.ds(*ROWS[part][order])
+        which = (y_send.at[layer, part, order, across], y_recv.at[layer, part, order, across], y_peer)
+        quarter = grp if order == 0 else 2 * across + core
+        return remote(parts.at[layer, quarter, :, 1 - yy, rows], y_in.at[across, :, rows], *which)
+
+    def z_copy(layer, part, order, step):
+        rows = pl.ds(*ROWS[part][order])
+        peer = lax.rem(zz + step, 4)
+        return remote(
+            parts.at[layer, grp, peer, yy, rows],
+            z_in.at[layer, 4 - step, rows],
+            z_send.at[layer, part, order, step],
+            z_recv.at[layer, part, order, 4 - step],
+            place(core, side, peer, yy),
+        )
+
+    def final_copy(layer, part, which):
+        rows = pl.ds(*SPAN[part])
+        quarter = far_side if which == 2 else grp
+        block = final.at[layer, quarter, rows]
+        return remote(
+            block,
+            block,
+            fin_send.at[layer, part, which],
+            fin_recv.at[layer, part, which],
+            x_peer if which == 0 else core_peer,
+        )
+
+    def core_start(layer, part):
+        if layer == 0:
+            pl.semaphore_wait(core_free.at[part], 1)
+        for across in range(2):
+            core_copy(layer, part, across).start()
+
+    def core_done(layer, part):
+        rows = pl.ds(*SPAN[part])
+        for across in range(2):
+            core_copy(layer, part, across).wait()
+        for turn in range(2):
+            across = 1 - side if turn == 0 else side
+            quarter = 2 * across + core
+
+            def add(z, carry):
+                for y in range(2):
+                    own = parts[layer, quarter, z, y, rows, :].astype(F32)
+                    own = own + core_in[across, z, y, rows, :].astype(F32)
+                    parts[layer, quarter, z, y, rows, :] = own.astype(BF16)
+                return carry
+
+            lax.fori_loop(0, 4, add, 0)
+            if turn == 0:
+                if layer == 0:
+                    pl.semaphore_wait(x_free.at[part, 0], 1)
+                x_copy(layer, part, 0).start()
+        if layer == 1:
+            credit(core_free.at[part], core_peer)
+        else:
+            pl.semaphore_wait(y_free.at[part, 1], 1)
+        for across in range(2):
+            y_copy(layer, part, 1, across).start()
+
+    def first_done(layer, part):
+        rows = pl.ds(*ROWS[part][1])
+        for across in range(2):
+            y_copy(layer, part, 1, across).wait()
+        for turn in range(2):
+            across = 1 - side if turn == 0 else side
+            quarter = 2 * across + core
+
+            def add(z, carry):
+                own = parts[layer, quarter, z, yy, rows, :].astype(F32)
+                own = own + y_in[across, z, rows, :].astype(F32)
+                parts[layer, quarter, z, yy, rows, :] = own.astype(BF16)
+                return carry
+
+            lax.fori_loop(0, 4, add, 0)
+            if turn == 0:
+                if layer == 0:
+                    pl.semaphore_wait(x_free.at[part, 1], 1)
+                x_copy(layer, part, 1).start()
+        if layer == 1:
+            credit(y_free.at[part, 1], y_peer)
+
+        rows = pl.ds(*ROWS[part][0])
+        x_copy(layer, part, 0).wait()
+        for turn in range(2):
+            y = 1 - yy if turn == 0 else yy
+
+            def add(z, carry):
+                own = parts[layer, grp, z, y, rows, :].astype(F32) + x_in[z, y, rows, :].astype(F32)
+                parts[layer, grp, z, y, rows, :] = own.astype(BF16)
+                return carry
+
+            lax.fori_loop(0, 4, add, 0)
+            if turn == 0:
+                if layer == 0:
+                    pl.semaphore_wait(y_free.at[part, 0], 1)
+                y_copy(layer, part, 0, 0).start()
+        if layer == 1:
+            credit(x_free.at[part, 0], x_peer)
+
+    def second_done(layer, part):
+        for order in (1, 0):
+            rows = pl.ds(*ROWS[part][order])
+            (y_copy(layer, part, 0, 0) if order == 0 else x_copy(layer, part, 1)).wait()
+
+            def add(z, carry):
+                arrival = y_in[0, z, rows, :] if order == 0 else x_in[z, 0, rows, :]
+                own = parts[layer, grp, z, yy, rows, :].astype(F32) + arrival.astype(F32)
+                parts[layer, grp, z, yy, rows, :] = own.astype(BF16)
+                return carry
+
+            lax.fori_loop(0, 4, add, 0)
+            if layer == 1:
+                if order == 0:
+                    credit(y_free.at[part, 0], y_peer)
+                else:
+                    credit(x_free.at[part, 1], x_peer)
+            for step in range(1, 4):
+                z_copy(layer, part, order, step).start()
+
+    def z_done(layer, part):
+        rows = pl.ds(*SPAN[part])
+        for order in (1, 0):
+            for step in range(1, 4):
+                z_copy(layer, part, order, step).wait()
+        total = parts[layer, grp, zz, yy, rows, :].astype(F32)
+        for slot in range(1, 4):
+            total = total + z_in[layer, slot, rows, :].astype(F32)
+        final[layer, grp, rows, :] = total.astype(BF16)
+        for which in range(2):
+            final_copy(layer, part, which).start()
+
+    def final_pass(layer, part):
+        final_copy(layer, part, 0).wait()
+        final_copy(layer, part, 2).start()
+
+    def final_out(layer, part):
+        rows = pl.ds(*SPAN[part])
+        return pltpu.make_async_copy(
+            final.at[layer, :, rows], final_hbm.at[layer, :, rows], out_sem.at[layer, part]
+        )
+
+    def final_done(layer, part):
+        for which in range(1, 3):
+            final_copy(layer, part, which).wait()
+        final_out(layer, part).start()
+
+    def small_copy(stage):
+        peer = (core_peer, x_peer, y_peer)[stage]
+        return remote(
+            small_sum.at[stage], small_in.at[stage], small_send.at[stage], small_recv.at[stage], peer
+        )
+
+    def small_z_copy(step):
+        return remote(
+            small_z.at[zz],
+            small_z.at[zz],
+            small_send.at[2 + step],
+            small_recv.at[2 + step],
+            place(core, side, lax.rem(zz + step, 4), yy),
+        )
+
+    def small_start():
+        small_sum[0] = small[0] + small[1]
+        small_copy(0).start()
+
+    def small_next(stage):
+        small_copy(stage).wait()
+        total = small_sum[stage] + small_in[stage]
+        if stage < 2:
+            small_sum[stage + 1] = total
+            small_copy(stage + 1).start()
+        else:
+            small_z[zz] = total
+            for step in range(1, 4):
+                small_z_copy(step).start()
+
+    def small_done():
+        for step in range(1, 4):
+            small_z_copy(step).wait()
+        small_sum[0] = (small_z[0] + small_z[1]) + (small_z[2] + small_z[3])
+        small_final[:, 0:256] = small_sum[0, :, pl.ds(pl.multiple_of(blk * 256, 256), 256)]
+        pair = small_sum[0, :, pl.ds(pl.multiple_of(FF + 128 * zz, 128), 128)]
+        small_final[:, 256:384] = jnp.where(yy == 1, pltpu.roll(pair, DIM, 1), pair)
+        small_final[:, 384:512] = small_sum[0, :, FF + WIDTH :]
+
+    def halves(*phases, backward=False):
+        def both(step, carry):
+            for phase in phases:
+                phase(1 - step if backward else step)
+            return carry
+
+        lax.fori_loop(0, 2, both, 0)
+
+    def begin(half):
+        move_arrived(0, half, tok_in)
+        hidden[half] = tok_in[half].astype(F32)
+
+    def finish(half):
+        back_out[0, half] = hidden[half].astype(BF16)
+        to_owner(3, half, back_out.at[0, half], out_in)
+
+    def turn_round(half):
+        move_arrived(2, half, cot_in)
+        grad[half] = cot_in[half].astype(F32)
+
+    def hand_back(half):
+        back_out[1, half] = grad[half].astype(BF16)
+        to_owner(4, half, back_out.at[1, half], grad_in)
+
+    pl.semaphore_wait(barrier, 10)
+    for half in range(2):
+        to_team(0, half, half_of(tokens, half), tok_in)
+    for half in range(2):
+        to_team(1, half, flag_out, flag_in)
+    for half in range(2):
+        to_team(2, half, half_of(cotangent, half), cot_in)
+    weight_copies[0, 0].wait()
+    halves(begin, functools.partial(project, 0))
+
+    move_arrived(1, 0, flag_in)
+    move_arrived(1, 1, flag_in)
+    border = jnp.concatenate([flag_in[0, 0:1, :]] * 2, axis=1) - (HALF * lax.div(zz, 2)).astype(F32)
+    key_row = lax.broadcasted_iota(jnp.int32, (TILE, TILE), 0)
+    query_col = lax.broadcasted_iota(jnp.int32, (TILE, TILE), 1)
+    later = key_row > query_col
+    key_sub = lax.rem(key_row, HALF).astype(F32) >= border
+    query_sub = lax.rem(query_col, HALF).astype(F32) >= border
+    apart = jnp.logical_xor(key_sub, query_sub)
+    bias[0] = jnp.where(apart, NEGATIVE, 0.0)
+    bias[1] = jnp.where(jnp.logical_or(later, apart), NEGATIVE, 0.0)
+
+    for number in range(1, 4):
+        weight_copies[0, number].wait()
+    attend(0, 0)
+    attend(0, 1)
+    weight_copies[1, 0].wait()
+    halves(functools.partial(feed, 0), functools.partial(project, 1))
+    for number in range(1, 4):
+        weight_copies[1, number].wait()
+    attend(1, 0)
+    attend(1, 1)
+    halves(functools.partial(feed, 1), finish)
+
+    halves(turn_round, functools.partial(feed_back, 1), backward=True)
+    early_grads(1)
+    core_start(1, 0)
+    attend_back(1, 1)
+    attend_back(1, 0)
+    core_done(1, 0)
+    halves(functools.partial(project_back, 1), functools.partial(feed_back, 0), backward=True)
+    small_start()
+    late_grads(1)
+    core_start(1, 1)
+    early_grads(0)
+    core_start(0, 0)
+    attend_back(0, 1)
+    small_next(0)
+    core_done(1, 1)
+    attend_back(0, 0)
+    small_next(1)
+    first_done(1, 0)
+    core_done(0, 0)
+    halves(functools.partial(project_back, 0), hand_back, backward=True)
+    late_grads(0)
+    core_start(0, 1)
+    small_next(2)
+    first_done(1, 1)
+    second_done(1, 0)
+    core_done(0, 1)
+    first_done(0, 0)
+    second_done(1, 1)
+    z_done(1, 0)
+    first_done(0, 1)
+    second_done(0, 0)
+    small_done()
+    z_done(1, 1)
+    final_pass(1, 0)
+    second_done(0, 1)
+    final_pass(1, 1)
+    final_done(1, 0)
+    final_done(1, 1)
+    results = []
+    for half in range(2):
+        rows = pl.ds(HALF * half, HALF)
+        move_arrived(3, half, out_in)
+        results.append(pltpu.make_async_copy(out_in.at[half], output_hbm.at[rows], out_sem.at[2, half]))
+        move_arrived(4, half, grad_in)
+        results.append(pltpu.make_async_copy(grad_in.at[half], input_grad_hbm.at[rows], out_sem.at[3, half]))
+    for copy in results:
+        copy.start()
+    z_done(0, 0)
+    z_done(0, 1)
+    final_pass(0, 0)
+    final_pass(0, 1)
+    final_done(0, 0)
+    final_done(0, 1)
+
+    for half in range(2):
+        left(2, 0, half, head_out)
+        left(3, 0, half, pack_out)
+        to_team_left(0, half, half_of(tokens, half))
+        to_team_left(1, half, flag_out)
+        to_team_left(2, half, half_of(cotangent, half))
+        to_owner_left(3, half, back_out.at[0, half])
+        to_owner_left(4, half, back_out.at[1, half])
+    for copy in results:
+        copy.wait()
+    for layer in range(LAYERS):
+        for part in range(2):
+            final_out(layer, part).wait()
+
+
+def results_kernel(
+    final, out_block, grad_block, small,
+    output, input_grad, qkv_grad, out_grad, up_grad, up_bias_grad, down_grad, down_bias_grad, alpha_grad,
+):
+    output[...] = out_block[...]
+    input_grad[...] = grad_block[...].astype(F32)
+    up_bias_grad[...] = small[:, 0:256]
+    down_bias_grad[...] = small[:, 256 : 256 + DIM]
+    alpha_grad[...] = small[:, 384:386]
+    for layer in range(LAYERS):
+        for quarter in range(4):
+
+            def block(first, count):
+                return final[layer, quarter, first : first + count, :].astype(F32)
+
+            def columns(step):
+                return slice(WIDTH * step + 128 * quarter, WIDTH * step + 128 * quarter + 128)
+
+            for step in range(3):
+                qkv_grad[layer, :, columns(step)] = block(DIM * step, DIM)
+            out_grad[layer, :, columns(0)] = block(192, DIM)
+            for step in range(4):
+                up_grad[layer, :, columns(step)] = block(256 + DIM * step, DIM)
+            down_grad[layer, :, columns(0)] = block(512, 256)
+
+
+def fast_body(
+    tokens, seq_len, qkv_weight, out_weight, up_weight, up_bias, down_weight, down_bias, alphas, cotangent
+):
+    whole = pl.BlockSpec(memory_space=pltpu.VMEM)
+    scalar = pl.BlockSpec(memory_space=pltpu.SMEM)
+    far = pl.BlockSpec(memory_space=pl.ANY)
+    shape = jax.ShapeDtypeStruct
+    rows = HALF * RUNS
+
+    def vmem(*dims):
+        return pltpu.VMEM(dims, BF16)
+
+    def wide(*dims):
+        return pltpu.VMEM(dims, F32)
+
+    dma = pltpu.SemaphoreType.DMA
+    final, out_block, grad_block, small = pl.pallas_call(
+        layers_kernel,
+        out_shape=(
+            shape((LAYERS, 4, CHUNK, 128), BF16),
+            shape((2 * HALF, WIDTH), BF16),
+            shape((2 * HALF, WIDTH), BF16),
+            shape((LAYERS, WIDTH), F32),
+        ),
+        in_specs=[whole, scalar, scalar, whole, whole, whole, far, far, far, far],
+        out_specs=(far, far, far, whole),
+        scratch_shapes=[
+            vmem(LAYERS, WIDTH, 3 * WIDTH),
+            vmem(LAYERS, WIDTH, WIDTH),
+            vmem(LAYERS, WIDTH, FF),
+            vmem(LAYERS, FF, WIDTH),
+            vmem(2, HALF, WIDTH),
+            vmem(2, HALF, WIDTH),
+            wide(8, 128),
+            wide(2, 8, 128),
+            vmem(2, 2, HALF, WIDTH),
+            vmem(2, HALF, WIDTH),
+            vmem(2, HALF, WIDTH),
+            wide(2, HALF, WIDTH),
+            wide(2, HALF, WIDTH),
+            vmem(LAYERS, WIDTH, 2 * HALF),
+            vmem(LAYERS, WIDTH, 2 * HALF),
+            vmem(LAYERS, WIDTH, 2 * HALF),
+            vmem(LAYERS, FF, 2 * HALF),
+            wide(LAYERS, 2, HALF, WIDTH),
+            wide(LAYERS, 2, HALF, FF),
+            wide(LAYERS, 2, HALF, WIDTH),
+            vmem(2 * HALF, WIDTH),
+            vmem(2 * HALF, FF),
+            vmem(2 * HALF, WIDTH),
+            vmem(2 * HALF, 3 * WIDTH),
+            vmem(2, TEAM, OWN, PACK, 128),
+            vmem(2, TEAM, OWN, DIM, 128),
+            vmem(LAYERS, 2, TEAM, OWN, PACK, 128),
+            vmem(LAYERS, 2, TEAM, OWN, DIM, 128),
+            vmem(LAYERS, 2, TEAM, OWN, DIM, 128),
+            vmem(LAYERS, 2, TEAM, OWN, PACK, 128),
+            vmem(LAYERS, OWN, rows, 128),
+            vmem(LAYERS, OWN, 128, rows),
+            vmem(LAYERS, OWN, 128, rows),
+            vmem(OWN, 128, rows),
+            wide(LAYERS, OWN, DIM, rows),
+            wide(LAYERS, OWN, 1, rows),
+            wide(OWN, rows, 128),
+            wide(DIM, rows),
+            wide(2, TILE, TILE),
+            vmem(LAYERS, 4, 4, 2, CHUNK, 128),
+            vmem(2, 4, 2, CHUNK, 128),
+            vmem(4, 2, CHUNK, 128),
+            vmem(2, 4, CHUNK, 128),
+            vmem(LAYERS, 4, CHUNK, 128),
+            vmem(LAYERS, 4, CHUNK, 128),
+            wide(2, LAYERS, SMALL),
+            wide(3, LAYERS, SMALL),
+            wide(4, LAYERS, SMALL),
+            wide(3, LAYERS, SMALL),
+            dma((LAYERS, 4)),
+            dma((5, 2)),
+            dma((5, 2)),
+            dma((4, LAYERS, 2)),
+            dma((4, LAYERS, 2)),
+            dma((LAYERS, 2, 2)),
+            dma((LAYERS, 2, 2)),
+            dma((LAYERS, 2, 2)),
+            dma((LAYERS, 2, 2)),
+            dma((LAYERS, 2, 2, 2)),
+            dma((LAYERS, 2, 2, 2)),
+            dma((LAYERS, 2, 2, 4)),
+            dma((LAYERS, 2, 2, 4)),
+            dma((LAYERS, 2, 3)),
+            dma((LAYERS, 2, 3)),
+            dma((6,)),
+            dma((6,)),
+            dma((4, 2)),
+            pltpu.SemaphoreType.REGULAR((2,)),
+            pltpu.SemaphoreType.REGULAR((2, 2)),
+            pltpu.SemaphoreType.REGULAR((2, 2)),
+        ],
+        compiler_params=pltpu.CompilerParams(
+            collective_id=0, has_side_effects=True, vmem_limit_bytes=63 * 1024 * 1024
+        ),
+        name="layers",
+    )(
+        tokens, seq_len, alphas, up_bias, down_bias, cotangent,
+        qkv_weight, out_weight, up_weight, down_weight,
+    )
+    return tuple(
+        pl.pallas_call(
+            results_kernel,
+            out_shape=(
+                shape((2 * HALF, WIDTH), BF16),
+                shape((2 * HALF, WIDTH), F32),
+                shape((LAYERS, DIM, 3 * WIDTH), F32),
+                shape((LAYERS, DIM, WIDTH), F32),
+                shape((LAYERS, DIM, FF), F32),
+                shape((LAYERS, FF // RUNS), F32),
+                shape((LAYERS, FF // RUNS, WIDTH), F32),
+                shape((LAYERS, DIM), F32),
+                shape((LAYERS, 2), F32),
+            ),
+            in_specs=[whole] * 4,
+            out_specs=(whole,) * 9,
+            compiler_params=pltpu.CompilerParams(vmem_limit_bytes=24 * 1024 * 1024),
+            name="results",
+        )(final, out_block, grad_block, small)
+    )
 
 
 def layout(seq_len, local_count, cycle_size):
@@ -357,8 +1218,9 @@
         P(),
         P(("grp", "blk"), None),
     )
+    sizes = (mesh.shape["grp"], mesh.shape["blk"])
     return jax.shard_map(
-        body,
+        fast_body if sizes == (4, RUNS) else body,
         mesh=mesh,
         in_specs=placed,
         out_specs=(

time: 1200 us -> 159 us (0.13)
  waiting for transfers between devices: 809 us -> 0 us
  matrix products: 157 us -> 0 us
  Pallas kernels: 0 us -> 154 us
  local copies, waits for them, and re-layouts: 112 us -> 3.97 us
  other arithmetic: 51.8 us -> 0 us
  blocking collectives: 25.9 us -> 0 us
  loops' own time: 17.7 us -> 0 us
  between operations: 16.5 us -> 0.67 us
    reduce_scatter x5 -> x0, waiting for transfers between devices: 417 us -> none  [the longest x2 170 us: layer_backward(): lax.psum_scatter(key_terms.astype(jnp.bfloat16), 'blk', scatter_dimension...]
    unnamed x14 -> x0, waiting for transfers between devices: 213 us -> none
    dot_general x82 -> x0, matrix products: 157 us -> none  [the longest x16 29.2 us: block_scores(): jnp.einsum('qhd,khd->hqk', queries, keys_part, preferred_element_type=jnp...]
    pallas_call x0 -> x2, Pallas kernels: none -> 154 us  [the longest x1 151 us: fast_body(): pl.pallas_call(layers_kernel, out_shape=(shape((LAYERS, 4, CHUNK, 128), B...]
    all_gather x2 -> x0, waiting for transfers between devices: 145 us -> none  [layer_forward(): whole = lax.all_gather(key_value, 'blk', axis=0, tiled=True)]
    psum x1 -> x0, waiting for transfers between devices: 34.3 us -> none  [reduce_all(): lax.psum(shares[0].astype(jnp.bfloat16), 'grp').astype(jnp.float32)]
    slice x27 -> x0, local copies, waits for them, and re-layouts: 29.7 us -> none  [the longest x16 18.9 us: key_block(): keys_part = key_piece[:, :half_width].reshape(block_rows, head_count, -1)]
    reduce_sum x14 -> x0, other arithmetic: 29.5 us -> none  [the longest x8 24.4 us: statistics(): totals = totals * jnp.exp(largest - newest) + jnp.sum(weights, axis=2)]
  transfers between devices with their start and end apart: 11 -> 0, of which waited for: 11 -> 0; matrix products, arithmetic and copies ran while one was open for 3% -> 0% of each run, Pallas kernels for 0% -> 0%
where the time goes in v2:
time: 159 us; the launch traced here: 158 us
  Pallas kernels  154 us (97%)
  local copies, waits for them, and re-layouts  3.97 us (2%)
    pallas_call x1, Pallas kernels, fast_body(): pl.pallas_call(layers_kernel, out_shape=(shape((LAYERS, 4, CHUNK, 128), B...  151 us
    unnamed x8, local copies, waits for them, and re-layouts  3.97 us

profile of v2, /device:TPU:0, one launch (start us, length us, event | category | flops | bytes accessed | tf_op | source)
XLA Modules:
  0.0 158.4 jit_solution(641309073106130053)
XLA Ops:
  0.6 151.5 %layers.1 = (bf16[2,4,768,128]{3,2,1,0:T(8,128)(2,1)}, bf16[256,512]{1,0:T(8,128)(2,1)}, bf16[256,512]{1,0:T(8,128)(2,1)}, f32[2,512]{1,0:T(2,128)}) custom-call(bf16[256,512]{1,0:T(8,128)(2,1)} %tokens.1, s32[1,4]{1,0:T(1,128)} %seq_len.1, f32[2,2]{1,0:T(2,128)} %alphas.1, f32[2,2048]{1,0:T(2,128)} %up_bias.1, f32[2,512]{1,0:T(2,128)} %down_bias.1, ...), custom_call_target="tpu_custom_call" | custom-call | tf_op jit(solution)/shard_map/layers/pallas_call | solution.py:762
  152.1 0.0 copy-start
  152.1 1.4 copy-done
  153.5 0.0 copy-start.1
  153.5 0.9 copy-done.1
  154.5 0.0 copy-start.2
  154.5 0.9 copy-done.2
  155.4 0.0 copy-start.3
  155.4 0.7 copy-done.3
  156.1 2.3 %results.1 = (bf16[256,512]{1,0:T(8,128)(2,1)}, f32[256,512]{1,0:T(8,128)}, f32[2,64,1536]{2,1,0:T(8,128)}, f32[2,64,512]{2,1,0:T(8,128)}, f32[2,64,2048]{2,1,0:...) custom-call(bf16[2,4,768,128]{3,2,1,0:T(8,128)(2,1)S(1)} %copy-done, ...), custom_call_target="tpu_custom_call" | custom-call | tf_op jit(solution)/shard_map/results/pallas_call | solution.py:853
Async XLA Ops:
  152.1 1.4 copy-start
  153.5 0.9 copy-start.1
  154.5 0.9 copy-start.2
  155.4 0.7 copy-start.3

commit v3 on v2

--- a/solution.py
+++ b/solution.py
@@ -26,8 +26,19 @@
 PACK = HALF + DIM
 CHUNK = 768
 SMALL = FF + WIDTH + 128
-ROWS = (((192, 288), (480, 288)), ((0, 96), (96, 96)))
-SPAN = ((192, 576), (0, 192))
+UP, DOWN, LATE = 256, 512, 0
+PART = 256
+ORDERS = ((0, 128), (128, 128))
+
+SLOPE_AT = 0.28
+TAIL = (
+    0.11652077851573843,
+    0.06749675579450809,
+    0.2689101589486142,
+    -0.23699347299932225,
+    0.3898740127620002,
+    -0.10580824228351815,
+)
 
 
 def nn(a, b):
@@ -252,8 +263,14 @@
         for step in range(FF // CUT):
             cut = slice(CUT * step, CUT * step + CUT)
             gate = nn(entered, wup[layer, :, cut]) + up_bias[layer : layer + 1, cut]
-            risen = 0.5 * (1.0 + lax.erf(gate * (0.5 ** 0.5)))
-            slope[layer, half, :, cut] = risen + gate * jnp.exp(-0.5 * gate * gate) * 0.3989422804014327
+            bell = jnp.exp(gate * gate * -0.5)
+            near = pl.reciprocal(1.0 + SLOPE_AT * jnp.abs(gate), approx=True)
+            tail = jnp.full_like(gate, TAIL[5])
+            for factor in TAIL[4::-1]:
+                tail = tail * near + factor
+            tail = bell * (tail * near)
+            risen = jnp.where(gate > 0.0, 1.0 - tail, tail)
+            slope[layer, half, :, cut] = risen + gate * bell * 0.3989422804014327
             active = (gate * risen).astype(BF16)
             act_t[layer, cut, rows] = active.T
             total = total + nn(active, wdown[layer, cut, :])
@@ -285,7 +302,7 @@
             column == 0, alpha_first, jnp.where(column == 1, alpha_second, 0.0)
         )
         mixed = (alphas[layer, 0] * middle).astype(BF16)
-        da[rows, :] = mixed
+        da[layer, rows, :] = mixed
         spread = nt(wout[layer], mixed).astype(BF16)
         left(*((1, 1) if layer == 1 else (2, 1)), half, head_out)
         for head in range(RUNS):
@@ -356,21 +373,25 @@
                     DIM * run : DIM * run + DIM, 128 * quarter : 128 * quarter + 128
                 ].astype(BF16)
 
-    def early_grads(layer):
-        scatter_rows(layer, nn(attn_t[layer], da[...]), 192)
+    def up_grads(layer):
         for step in range(FF // CUT):
             cut = slice(CUT * step, CUT * step + CUT)
-            scatter_rows(layer, nn(ent_t[layer], du[:, cut]), 256 + DIM * step)
+            scatter_rows(layer, nn(ent_t[layer], du[:, cut]), UP + DIM * step)
+
+    def down_grads(layer):
         for run in range(RUNS):
             result = nn(act_t[layer, TILE * run : TILE * run + TILE, :], dz[...])
             for quarter in range(4):
-                parts[layer, quarter, run // 2, run % 2, 512:768, :] = result[
+                parts[layer, quarter, run // 2, run % 2, DOWN : DOWN + PART, :] = result[
                     :, 128 * quarter : 128 * quarter + 128
                 ].astype(BF16)
 
     def late_grads(layer):
+        scatter_rows(layer, nn(attn_t[layer], da[layer]), LATE + 192)
         for step in range(3):
-            scatter_rows(layer, nn(hid_t[layer], dqkv[:, WIDTH * step : WIDTH * step + WIDTH]), DIM * step)
+            scatter_rows(
+                layer, nn(hid_t[layer], dqkv[:, WIDTH * step : WIDTH * step + WIDTH]), LATE + DIM * step
+            )
 
     def remote(source, target, send, recv, peer):
         return pltpu.make_async_remote_copy(
@@ -385,147 +406,121 @@
     def credit(semaphore, peer):
         pl.semaphore_signal(semaphore, inc=1, device_id=peer, device_id_type=MESH)
 
+    def rows_in(part, order):
+        return pl.ds(part + ORDERS[order][0], ORDERS[order][1])
+
     def core_copy(layer, part, across):
-        rows = pl.ds(*SPAN[part])
+        rows = pl.ds(part, PART)
+        which = (layer, part // PART, across)
         return remote(
             parts.at[layer, 2 * across + 1 - core, :, :, rows],
             core_in.at[across, :, :, rows],
-            core_send.at[layer, part, across],
-            core_recv.at[layer, part, across],
+            core_send.at[which],
+            core_recv.at[which],
             core_peer,
         )
 
     def x_copy(layer, part, order):
-        rows = pl.ds(*ROWS[part][order])
-        which = (x_send.at[layer, part, order], x_recv.at[layer, part, order], x_peer)
+        rows = rows_in(part, order)
+        which = (layer, part // PART, order)
+        ends = (x_send.at[which], x_recv.at[which], x_peer)
         if order == 0:
-            return remote(parts.at[layer, far_side, :, :, rows], x_in.at[:, :, rows], *which)
-        return remote(parts.at[layer, far_side, :, yy, rows], x_in.at[:, 0, rows], *which)
+            return remote(parts.at[layer, far_side, :, :, rows], x_in.at[:, :, rows], *ends)
+        return remote(parts.at[layer, far_side, :, yy, rows], x_in.at[:, 0, rows], *ends)
 
     def y_copy(layer, part, order, across):
-        rows = pl.ds(*ROWS[part][order])
-        which = (y_send.at[layer, part, order, across], y_recv.at[layer, part, order, across], y_peer)
+        rows = rows_in(part, order)
+        which = (layer, part // PART, order, across)
+        ends = (y_send.at[which], y_recv.at[which], y_peer)
         quarter = grp if order == 0 else 2 * across + core
-        return remote(parts.at[layer, quarter, :, 1 - yy, rows], y_in.at[across, :, rows], *which)
+        return remote(parts.at[layer, quarter, :, 1 - yy, rows], y_in.at[across, :, rows], *ends)
 
     def z_copy(layer, part, order, step):
-        rows = pl.ds(*ROWS[part][order])
+        rows = rows_in(part, order)
         peer = lax.rem(zz + step, 4)
         return remote(
             parts.at[layer, grp, peer, yy, rows],
             z_in.at[layer, 4 - step, rows],
-            z_send.at[layer, part, order, step],
-            z_recv.at[layer, part, order, 4 - step],
+            z_send.at[layer, part // PART, order, step],
+            z_recv.at[layer, part // PART, order, 4 - step],
             place(core, side, peer, yy),
         )
 
     def final_copy(layer, part, which):
-        rows = pl.ds(*SPAN[part])
+        rows = pl.ds(part, PART)
         quarter = far_side if which == 2 else grp
         block = final.at[layer, quarter, rows]
         return remote(
             block,
             block,
-            fin_send.at[layer, part, which],
-            fin_recv.at[layer, part, which],
+            fin_send.at[layer, part // PART, which],
+            fin_recv.at[layer, part // PART, which],
             x_peer if which == 0 else core_peer,
         )
 
     def core_start(layer, part):
         if layer == 0:
-            pl.semaphore_wait(core_free.at[part], 1)
+            pl.semaphore_wait(core_free.at[part // PART], 1)
         for across in range(2):
             core_copy(layer, part, across).start()
 
     def core_done(layer, part):
-        rows = pl.ds(*SPAN[part])
+        rows = pl.ds(part, PART)
         for across in range(2):
             core_copy(layer, part, across).wait()
-        for turn in range(2):
-            across = 1 - side if turn == 0 else side
-            quarter = 2 * across + core
-
-            def add(z, carry):
-                for y in range(2):
-                    own = parts[layer, quarter, z, y, rows, :].astype(F32)
-                    own = own + core_in[across, z, y, rows, :].astype(F32)
-                    parts[layer, quarter, z, y, rows, :] = own.astype(BF16)
-                return carry
-
-            lax.fori_loop(0, 4, add, 0)
-            if turn == 0:
-                if layer == 0:
-                    pl.semaphore_wait(x_free.at[part, 0], 1)
+        if layer == 0:
+            pl.semaphore_wait(x_free.at[part // PART, 0], 1)
+            pl.semaphore_wait(y_free.at[part // PART, 1], 1)
+        for across in (1 - side, side):
+            parts[layer, 2 * across + core, :, :, rows, :] += core_in[across, :, :, rows, :]
+            if across is not side:
                 x_copy(layer, part, 0).start()
+            y_copy(layer, part, 1, across).start()
         if layer == 1:
-            credit(core_free.at[part], core_peer)
-        else:
-            pl.semaphore_wait(y_free.at[part, 1], 1)
-        for across in range(2):
-            y_copy(layer, part, 1, across).start()
+            credit(core_free.at[part // PART], core_peer)
 
     def first_done(layer, part):
-        rows = pl.ds(*ROWS[part][1])
-        for across in range(2):
+        rows = rows_in(part, 1)
+        for across in (1 - side, side):
             y_copy(layer, part, 1, across).wait()
-        for turn in range(2):
-            across = 1 - side if turn == 0 else side
-            quarter = 2 * across + core
-
-            def add(z, carry):
-                own = parts[layer, quarter, z, yy, rows, :].astype(F32)
-                own = own + y_in[across, z, rows, :].astype(F32)
-                parts[layer, quarter, z, yy, rows, :] = own.astype(BF16)
-                return carry
-
-            lax.fori_loop(0, 4, add, 0)
-            if turn == 0:
-                if layer == 0:
-                    pl.semaphore_wait(x_free.at[part, 1], 1)
+        if layer == 0:
+            pl.semaphore_wait(x_free.at[part // PART, 1], 1)
+            pl.semaphore_wait(y_free.at[part // PART, 0], 1)
+        for across in (1 - side, side):
+            parts[layer, 2 * across + core, :, yy, rows, :] += y_in[across, :, rows, :]
+            if across is not side:
                 x_copy(layer, part, 1).start()
         if layer == 1:
-            credit(y_free.at[part, 1], y_peer)
-
-        rows = pl.ds(*ROWS[part][0])
+            credit(y_free.at[part // PART, 1], y_peer)
+
+        rows = rows_in(part, 0)
         x_copy(layer, part, 0).wait()
-        for turn in range(2):
-            y = 1 - yy if turn == 0 else yy
-
-            def add(z, carry):
-                own = parts[layer, grp, z, y, rows, :].astype(F32) + x_in[z, y, rows, :].astype(F32)
-                parts[layer, grp, z, y, rows, :] = own.astype(BF16)
-                return carry
-
-            lax.fori_loop(0, 4, add, 0)
-            if turn == 0:
-                if layer == 0:
-                    pl.semaphore_wait(y_free.at[part, 0], 1)
+        for y in (1 - yy, yy):
+            parts[layer, grp, :, y, rows, :] += x_in[:, y, rows, :]
+            if y is not yy:
                 y_copy(layer, part, 0, 0).start()
         if layer == 1:
-            credit(x_free.at[part, 0], x_peer)
+            credit(x_free.at[part // PART, 0], x_peer)
 
     def second_done(layer, part):
         for order in (1, 0):
-            rows = pl.ds(*ROWS[part][order])
-            (y_copy(layer, part, 0, 0) if order == 0 else x_copy(layer, part, 1)).wait()
-
-            def add(z, carry):
-                arrival = y_in[0, z, rows, :] if order == 0 else x_in[z, 0, rows, :]
-                own = parts[layer, grp, z, yy, rows, :].astype(F32) + arrival.astype(F32)
-                parts[layer, grp, z, yy, rows, :] = own.astype(BF16)
-                return carry
-
-            lax.fori_loop(0, 4, add, 0)
+            rows = rows_in(part, order)
+            if order == 0:
+                y_copy(layer, part, 0, 0).wait()
+                parts[layer, grp, :, yy, rows, :] += y_in[0, :, rows, :]
+            else:
+                x_copy(layer, part, 1).wait()
+                parts[layer, grp, :, yy, rows, :] += x_in[:, 0, rows, :]
+            for step in range(1, 4):
+                z_copy(layer, part, order, step).start()
             if layer == 1:
                 if order == 0:
-                    credit(y_free.at[part, 0], y_peer)
+                    credit(y_free.at[part // PART, 0], y_peer)
                 else:
-                    credit(x_free.at[part, 1], x_peer)
-            for step in range(1, 4):
-                z_copy(layer, part, order, step).start()
+                    credit(x_free.at[part // PART, 1], x_peer)
 
     def z_done(layer, part):
-        rows = pl.ds(*SPAN[part])
+        rows = pl.ds(part, PART)
         for order in (1, 0):
             for step in range(1, 4):
                 z_copy(layer, part, order, step).wait()
@@ -541,9 +536,9 @@
         final_copy(layer, part, 2).start()
 
     def final_out(layer, part):
-        rows = pl.ds(*SPAN[part])
+        rows = pl.ds(part, PART)
         return pltpu.make_async_copy(
-            final.at[layer, :, rows], final_hbm.at[layer, :, rows], out_sem.at[layer, part]
+            final.at[layer, :, rows], final_hbm.at[layer, :, rows], out_sem.at[layer, part // PART]
         )
 
     def final_done(layer, part):
@@ -649,43 +644,65 @@
     halves(functools.partial(feed, 1), finish)
 
     halves(turn_round, functools.partial(feed_back, 1), backward=True)
-    early_grads(1)
-    core_start(1, 0)
+    up_grads(1)
+    core_start(1, UP)
     attend_back(1, 1)
+    core_done(1, UP)
+    down_grads(1)
+    core_start(1, DOWN)
     attend_back(1, 0)
-    core_done(1, 0)
-    halves(functools.partial(project_back, 1), functools.partial(feed_back, 0), backward=True)
+    core_done(1, DOWN)
+
+    def once(half):
+        @pl.when(half == 1)
+        def _():
+            first_done(1, UP)
+
+    halves(functools.partial(project_back, 1), functools.partial(feed_back, 0), once, backward=True)
+    up_grads(0)
+    core_start(0, UP)
     small_start()
+    first_done(1, DOWN)
+    second_done(1, UP)
+    attend_back(0, 1)
+    core_done(0, UP)
     late_grads(1)
-    core_start(1, 1)
-    early_grads(0)
-    core_start(0, 0)
-    attend_back(0, 1)
+    core_start(1, LATE)
+    down_grads(0)
+    core_start(0, DOWN)
     small_next(0)
-    core_done(1, 1)
     attend_back(0, 0)
+    core_done(1, LATE)
+    core_done(0, DOWN)
     small_next(1)
-    first_done(1, 0)
-    core_done(0, 0)
-    halves(functools.partial(project_back, 0), hand_back, backward=True)
+    second_done(1, DOWN)
+    z_done(1, UP)
+
+    def twice(half):
+        @pl.when(half == 1)
+        def _():
+            first_done(0, UP)
+            first_done(1, LATE)
+
+    halves(functools.partial(project_back, 0), hand_back, twice, backward=True)
     late_grads(0)
-    core_start(0, 1)
+    core_start(0, LATE)
     small_next(2)
-    first_done(1, 1)
-    second_done(1, 0)
-    core_done(0, 1)
-    first_done(0, 0)
-    second_done(1, 1)
-    z_done(1, 0)
-    first_done(0, 1)
-    second_done(0, 0)
+    first_done(0, DOWN)
+    z_done(1, DOWN)
+    second_done(0, UP)
+    second_done(1, LATE)
+    core_done(0, LATE)
+    final_pass(1, UP)
+    final_pass(1, DOWN)
     small_done()
-    z_done(1, 1)
-    final_pass(1, 0)
-    second_done(0, 1)
-    final_pass(1, 1)
-    final_done(1, 0)
-    final_done(1, 1)
+    second_done(0, DOWN)
+    first_done(0, LATE)
+    z_done(0, UP)
+    z_done(1, LATE)
+    second_done(0, LATE)
+    final_done(1, UP)
+    final_done(1, DOWN)
     results = []
     for half in range(2):
         rows = pl.ds(HALF * half, HALF)
@@ -695,12 +712,16 @@
         results.append(pltpu.make_async_copy(grad_in.at[half], input_grad_hbm.at[rows], out_sem.at[3, half]))
     for copy in results:
         copy.start()
-    z_done(0, 0)
-    z_done(0, 1)
-    final_pass(0, 0)
-    final_pass(0, 1)
-    final_done(0, 0)
-    final_done(0, 1)
+    z_done(0, DOWN)
+    final_pass(1, LATE)
+    final_pass(0, UP)
+    z_done(0, LATE)
+    final_pass(0, DOWN)
+    final_done(1, LATE)
+    final_done(0, UP)
+    final_pass(0, LATE)
+    final_done(0, DOWN)
+    final_done(0, LATE)
 
     for half in range(2):
         left(2, 0, half, head_out)
@@ -713,20 +734,28 @@
     for copy in results:
         copy.wait()
     for layer in range(LAYERS):
-        for part in range(2):
+        for part in (UP, DOWN, LATE):
             final_out(layer, part).wait()
 
 
 def results_kernel(
-    final, out_block, grad_block, small,
+    final_hbm, out_hbm, grad_hbm, small,
     output, input_grad, qkv_grad, out_grad, up_grad, up_bias_grad, down_grad, down_bias_grad, alpha_grad,
+    final, grad_block, sem,
 ):
-    output[...] = out_block[...]
-    input_grad[...] = grad_block[...].astype(F32)
+    moves = [
+        pltpu.make_async_copy(final_hbm.at[1], final.at[1], sem.at[0]),
+        pltpu.make_async_copy(final_hbm.at[0], final.at[0], sem.at[1]),
+        pltpu.make_async_copy(grad_hbm, grad_block, sem.at[2]),
+        pltpu.make_async_copy(out_hbm, output, sem.at[3]),
+    ]
+    for move in moves:
+        move.start()
     up_bias_grad[...] = small[:, 0:256]
     down_bias_grad[...] = small[:, 256 : 256 + DIM]
     alpha_grad[...] = small[:, 384:386]
-    for layer in range(LAYERS):
+    for layer in (1, 0):
+        moves[1 - layer].wait()
         for quarter in range(4):
 
             def block(first, count):
@@ -739,8 +768,11 @@
                 qkv_grad[layer, :, columns(step)] = block(DIM * step, DIM)
             out_grad[layer, :, columns(0)] = block(192, DIM)
             for step in range(4):
-                up_grad[layer, :, columns(step)] = block(256 + DIM * step, DIM)
-            down_grad[layer, :, columns(0)] = block(512, 256)
+                up_grad[layer, :, columns(step)] = block(UP + DIM * step, DIM)
+            down_grad[layer, :, columns(0)] = block(DOWN, PART)
+    moves[2].wait()
+    input_grad[...] = grad_block[...].astype(F32)
+    moves[3].wait()
 
 
 def fast_body(
@@ -792,7 +824,7 @@
             wide(LAYERS, 2, HALF, WIDTH),
             vmem(2 * HALF, WIDTH),
             vmem(2 * HALF, FF),
-            vmem(2 * HALF, WIDTH),
+            vmem(LAYERS, 2 * HALF, WIDTH),
             vmem(2 * HALF, 3 * WIDTH),
             vmem(2, TEAM, OWN, PACK, 128),
             vmem(2, TEAM, OWN, DIM, 128),
@@ -824,22 +856,22 @@
             dma((5, 2)),
             dma((4, LAYERS, 2)),
             dma((4, LAYERS, 2)),
-            dma((LAYERS, 2, 2)),
-            dma((LAYERS, 2, 2)),
-            dma((LAYERS, 2, 2)),
-            dma((LAYERS, 2, 2)),
-            dma((LAYERS, 2, 2, 2)),
-            dma((LAYERS, 2, 2, 2)),
-            dma((LAYERS, 2, 2, 4)),
-            dma((LAYERS, 2, 2, 4)),
-            dma((LAYERS, 2, 3)),
-            dma((LAYERS, 2, 3)),
+            dma((LAYERS, 3, 2)),
+            dma((LAYERS, 3, 2)),
+            dma((LAYERS, 3, 2)),
+            dma((LAYERS, 3, 2)),
+            dma((LAYERS, 3, 2, 2)),
+            dma((LAYERS, 3, 2, 2)),
+            dma((LAYERS, 3, 2, 4)),
+            dma((LAYERS, 3, 2, 4)),
+            dma((LAYERS, 3, 3)),
+            dma((LAYERS, 3, 3)),
             dma((6,)),
             dma((6,)),
-            dma((4, 2)),
-            pltpu.SemaphoreType.REGULAR((2,)),
-            pltpu.SemaphoreType.REGULAR((2, 2)),
-            pltpu.SemaphoreType.REGULAR((2, 2)),
+            dma((4, 3)),
+            pltpu.SemaphoreType.REGULAR((3,)),
+            pltpu.SemaphoreType.REGULAR((3, 2)),
+            pltpu.SemaphoreType.REGULAR((3, 2)),
         ],
         compiler_params=pltpu.CompilerParams(
             collective_id=0, has_side_effects=True, vmem_limit_bytes=63 * 1024 * 1024
@@ -863,9 +895,10 @@
                 shape((LAYERS, DIM), F32),
                 shape((LAYERS, 2), F32),
             ),
-            in_specs=[whole] * 4,
-            out_specs=(whole,) * 9,
-            compiler_params=pltpu.CompilerParams(vmem_limit_bytes=24 * 1024 * 1024),
+            in_specs=[far, far, far, whole],
+            out_specs=(far,) + (whole,) * 8,
+            scratch_shapes=[vmem(LAYERS, 4, CHUNK, 128), vmem(2 * HALF, WIDTH), dma((4,))],
+            compiler_params=pltpu.CompilerParams(vmem_limit_bytes=60 * 1024 * 1024),
             name="results",
         )(final, out_block, grad_block, small)
     )

time: 159 us -> 160 us (level)
  Pallas kernels: 154 us -> 159 us
  local copies, waits for them, and re-layouts: 3.97 us -> 0 us
    pallas_call x1, Pallas kernels: 2.26 us -> 11.6 us  [fast_body(): pl.pallas_call(results_kernel, out_shape=(shape((2 * HALF, WIDTH), BF16),...]
    unnamed x8 -> x0, local copies, waits for them, and re-layouts: 3.97 us -> none
    pallas_call x1, Pallas kernels: 151 us -> 148 us  [fast_body(): pl.pallas_call(layers_kernel, out_shape=(shape((LAYERS, 4, CHUNK, 128), B...]
where the time goes in v3:
time: 160 us
  Pallas kernels  159 us (99%)
    pallas_call x1, Pallas kernels, fast_body(): pl.pallas_call(layers_kernel, out_shape=(shape((LAYERS, 4, CHUNK, 128), B...  148 us
    pallas_call x1, Pallas kernels, fast_body(): pl.pallas_call(results_kernel, out_shape=(shape((2 * HALF, WIDTH), BF16),...  11.6 us

profile of v3, /device:TPU:0, one launch (start us, length us, event | category | flops | bytes accessed | tf_op | source)
XLA Modules:
  0.0 160.2 jit_solution(11328473100713583292)
XLA Ops:
  0.6 147.8 %layers.1 = (bf16[2,4,768,128]{3,2,1,0:T(8,128)(2,1)}, bf16[256,512]{1,0:T(8,128)(2,1)}, bf16[256,512]{1,0:T(8,128)(2,1)}, f32[2,512]{1,0:T(2,128)}) custom-call(bf16[256,512]{1,0:T(8,128)(2,1)} %tokens.1, s32[1,4]{1,0:T(1,128)} %seq_len.1, f32[2,2]{1,0:T(2,128)} %alphas.1, f32[2,2048]{1,0:T(2,128)} %up_bias.1, f32[2,512]{1,0:T(2,128)} %down_bias.1, ...), custom_call_target="tpu_custom_call" | custom-call | tf_op jit(solution)/shard_map/layers/pallas_call | solution.py:794
  148.5 11.6 %results.1 = (bf16[256,512]{1,0:T(8,128)(2,1)}, f32[256,512]{1,0:T(8,128)}, f32[2,64,1536]{2,1,0:T(8,128)}, f32[2,64,512]{2,1,0:T(8,128)}, f32[2,64,2048]{2,1,0:...) custom-call(bf16[2,4,768,128]{3,2,1,0:T(8,128)(2,1)} %get-tuple-element.13.final_hbm, ...), custom_call_target="tpu_custom_call" | custom-call | tf_op jit(solution)/shard_map/results/pallas_call | solution.py:885

commit v4 on v3

--- a/solution.py
+++ b/solution.py
@@ -28,7 +28,8 @@
 SMALL = FF + WIDTH + 128
 UP, DOWN, LATE = 256, 512, 0
 PART = 256
-ORDERS = ((0, 128), (128, 128))
+ORDERS = ((0, 144), (144, 48), (192, 64))
+THIRD = ORDERS[2][1]
 
 SLOPE_AT = 0.28
 TAIL = (
@@ -58,9 +59,9 @@
     dz, du, da, dqkv,
     pack_out, head_out, qkv_in, o_in, do_in, dqkv_in,
     kv, kv_t, rq, ro, o_t, lse, acc, dq_t, bias,
-    parts, core_in, x_in, y_in, z_in, final, small, small_in, small_z, small_sum,
+    parts, core_in, x_in, y_in, z_in, third_z, third_x, third_y, final, small, small_in, small_z, small_sum,
     w_sem, move_send, move_recv, a2a_send, a2a_recv, core_send, core_recv, x_send, x_recv, y_send, y_recv,
-    z_send, z_recv, fin_send, fin_recv, small_send, small_recv, out_sem, core_free, x_free, y_free,
+    z_send, z_recv, tz_send, tz_recv, tx_send, tx_recv, ty_send, ty_recv, fin_send, fin_recv, small_send, small_recv, out_sem, core_free, x_free, y_free,
 ):
     grp = lax.axis_index("grp")
     blk = lax.axis_index("blk")
@@ -284,8 +285,9 @@
     def feed_back(layer, half):
         rows = rows_of(half)
         start = grad[half]
-        scaled = (alphas[layer, 1] * start).astype(BF16)
-        dz[rows, :] = scaled
+        if layer == 0:
+            dz[rows, :] = (alphas[layer, 1] * start).astype(BF16)
+        scaled = dz[rows, :]
         alpha_second = total_of(start * second[layer, half])
         small[half, layer : layer + 1, FF : FF + WIDTH] = jnp.sum(scaled.astype(F32), axis=0, keepdims=True)
         middle = start
@@ -446,6 +448,37 @@
             place(core, side, peer, yy),
         )
 
+    def third_z_copy(layer, part, across, step):
+        peer = lax.rem(zz + step, 4)
+        which = (layer, part // PART, across)
+        return remote(
+            parts.at[layer, 2 * across + core, peer, :, rows_in(part, 2)],
+            third_z.at[layer, part // PART, across, 4 - step],
+            tz_send.at[(*which, step)],
+            tz_recv.at[(*which, 4 - step)],
+            place(core, side, peer, yy),
+        )
+
+    def third_x_copy(layer, part):
+        which = (layer, part // PART)
+        return remote(
+            parts.at[layer, far_side, zz, :, rows_in(part, 2)],
+            third_x.at[which],
+            tx_send.at[which],
+            tx_recv.at[which],
+            x_peer,
+        )
+
+    def third_y_copy(layer, part):
+        which = (layer, part // PART)
+        return remote(
+            parts.at[layer, grp, zz, 1 - yy, rows_in(part, 2)],
+            third_y.at[which],
+            ty_send.at[which],
+            ty_recv.at[which],
+            y_peer,
+        )
+
     def final_copy(layer, part, which):
         rows = pl.ds(part, PART)
         quarter = far_side if which == 2 else grp
@@ -476,6 +509,8 @@
             if across is not side:
                 x_copy(layer, part, 0).start()
             y_copy(layer, part, 1, across).start()
+            for step in range(1, 4):
+                third_z_copy(layer, part, across, step).start()
         if layer == 1:
             credit(core_free.at[part // PART], core_peer)
 
@@ -501,6 +536,17 @@
                 y_copy(layer, part, 0, 0).start()
         if layer == 1:
             credit(x_free.at[part // PART, 0], x_peer)
+
+        rows = rows_in(part, 2)
+        for across in (1 - side, side):
+            for step in range(1, 4):
+                third_z_copy(layer, part, across, step).wait()
+            total = parts[layer, 2 * across + core, zz, :, rows, :].astype(F32)
+            for slot in range(1, 4):
+                total = total + third_z[layer, part // PART, across, slot].astype(F32)
+            parts[layer, 2 * across + core, zz, :, rows, :] = total.astype(BF16)
+            if across is not side:
+                third_x_copy(layer, part).start()
 
     def second_done(layer, part):
         for order in (1, 0):
@@ -518,16 +564,25 @@
                     credit(y_free.at[part // PART, 0], y_peer)
                 else:
                     credit(x_free.at[part // PART, 1], x_peer)
+        rows = rows_in(part, 2)
+        third_x_copy(layer, part).wait()
+        for y in (1 - yy, yy):
+            parts[layer, grp, zz, y, rows, :] += third_x[layer, part // PART, y]
+            if y is not yy:
+                third_y_copy(layer, part).start()
 
     def z_done(layer, part):
-        rows = pl.ds(part, PART)
         for order in (1, 0):
             for step in range(1, 4):
                 z_copy(layer, part, order, step).wait()
+        rows = pl.ds(part, ORDERS[2][0])
         total = parts[layer, grp, zz, yy, rows, :].astype(F32)
         for slot in range(1, 4):
             total = total + z_in[layer, slot, rows, :].astype(F32)
         final[layer, grp, rows, :] = total.astype(BF16)
+        rows = rows_in(part, 2)
+        third_y_copy(layer, part).wait()
+        final[layer, grp, rows, :] = parts[layer, grp, zz, yy, rows, :] + third_y[layer, part // PART]
         for which in range(2):
             final_copy(layer, part, which).start()
 
@@ -601,9 +656,10 @@
         back_out[0, half] = hidden[half].astype(BF16)
         to_owner(3, half, back_out.at[0, half], out_in)
 
-    def turn_round(half):
+    def turn_round(layer, half):
         move_arrived(2, half, cot_in)
         grad[half] = cot_in[half].astype(F32)
+        dz[rows_of(half), :] = (alphas[layer, 1] * grad[half]).astype(BF16)
 
     def hand_back(half):
         back_out[1, half] = grad[half].astype(BF16)
@@ -643,27 +699,28 @@
     attend(1, 1)
     halves(functools.partial(feed, 1), finish)
 
-    halves(turn_round, functools.partial(feed_back, 1), backward=True)
+    halves(functools.partial(turn_round, 1))
+    down_grads(1)
+    core_start(1, DOWN)
+    halves(functools.partial(feed_back, 1), backward=True)
+    core_done(1, DOWN)
     up_grads(1)
     core_start(1, UP)
     attend_back(1, 1)
     core_done(1, UP)
-    down_grads(1)
-    core_start(1, DOWN)
     attend_back(1, 0)
-    core_done(1, DOWN)
 
     def once(half):
         @pl.when(half == 1)
         def _():
-            first_done(1, UP)
+            first_done(1, DOWN)
 
     halves(functools.partial(project_back, 1), functools.partial(feed_back, 0), once, backward=True)
     up_grads(0)
     core_start(0, UP)
     small_start()
-    first_done(1, DOWN)
-    second_done(1, UP)
+    first_done(1, UP)
+    second_done(1, DOWN)
     attend_back(0, 1)
     core_done(0, UP)
     late_grads(1)
@@ -675,8 +732,8 @@
     core_done(1, LATE)
     core_done(0, DOWN)
     small_next(1)
-    second_done(1, DOWN)
-    z_done(1, UP)
+    second_done(1, UP)
+    z_done(1, DOWN)
 
     def twice(half):
         @pl.when(half == 1)
@@ -689,7 +746,7 @@
     core_start(0, LATE)
     small_next(2)
     first_done(0, DOWN)
-    z_done(1, DOWN)
+    z_done(1, UP)
     second_done(0, UP)
     second_done(1, LATE)
     core_done(0, LATE)
@@ -741,13 +798,13 @@
 def results_kernel(
     final_hbm, out_hbm, grad_hbm, small,
     output, input_grad, qkv_grad, out_grad, up_grad, up_bias_grad, down_grad, down_bias_grad, alpha_grad,
-    final, grad_block, sem,
+    final, grad_block, out_block, sem,
 ):
     moves = [
         pltpu.make_async_copy(final_hbm.at[1], final.at[1], sem.at[0]),
         pltpu.make_async_copy(final_hbm.at[0], final.at[0], sem.at[1]),
         pltpu.make_async_copy(grad_hbm, grad_block, sem.at[2]),
-        pltpu.make_async_copy(out_hbm, output, sem.at[3]),
+        pltpu.make_async_copy(out_hbm, out_block, sem.at[3]),
     ]
     for move in moves:
         move.start()
@@ -773,6 +830,7 @@
     moves[2].wait()
     input_grad[...] = grad_block[...].astype(F32)
     moves[3].wait()
+    output[...] = out_block[...]
 
 
 def fast_body(
@@ -846,6 +904,9 @@
             vmem(4, 2, CHUNK, 128),
             vmem(2, 4, CHUNK, 128),
             vmem(LAYERS, 4, CHUNK, 128),
+            vmem(LAYERS, 3, 2, 4, 2, THIRD, 128),
+            vmem(LAYERS, 3, 2, THIRD, 128),
+            vmem(LAYERS, 3, THIRD, 128),
             vmem(LAYERS, 4, CHUNK, 128),
             wide(2, LAYERS, SMALL),
             wide(3, LAYERS, SMALL),
@@ -864,6 +925,12 @@
             dma((LAYERS, 3, 2, 2)),
             dma((LAYERS, 3, 2, 4)),
             dma((LAYERS, 3, 2, 4)),
+            dma((LAYERS, 3, 2, 4)),
+            dma((LAYERS, 3, 2, 4)),
+            dma((LAYERS, 3)),
+            dma((LAYERS, 3)),
+            dma((LAYERS, 3)),
+            dma((LAYERS, 3)),
             dma((LAYERS, 3, 3)),
             dma((LAYERS, 3, 3)),
             dma((6,)),
@@ -896,8 +963,10 @@
                 shape((LAYERS, 2), F32),
             ),
             in_specs=[far, far, far, whole],
-            out_specs=(far,) + (whole,) * 8,
-            scratch_shapes=[vmem(LAYERS, 4, CHUNK, 128), vmem(2 * HALF, WIDTH), dma((4,))],
+            out_specs=(whole,) * 9,
+            scratch_shapes=[
+                vmem(LAYERS, 4, CHUNK, 128), vmem(2 * HALF, WIDTH), vmem(2 * HALF, WIDTH), dma((4,))
+            ],
             compiler_params=pltpu.CompilerParams(vmem_limit_bytes=60 * 1024 * 1024),
             name="results",
         )(final, out_block, grad_block, small)

time: 160 us -> 146 us (0.912)
  Pallas kernels: 159 us -> 145 us
    pallas_call x1, Pallas kernels: 11.6 us -> 4.26 us  [fast_body(): pl.pallas_call(results_kernel, out_shape=(shape((2 * HALF, WIDTH), BF16),...]
    pallas_call x1, Pallas kernels: 148 us -> 141 us  [fast_body(): pl.pallas_call(layers_kernel, out_shape=(shape((LAYERS, 4, CHUNK, 128), B...]
where the time goes in v4:
time: 146 us
  Pallas kernels  145 us (99%)
    pallas_call x1, Pallas kernels, fast_body(): pl.pallas_call(layers_kernel, out_shape=(shape((LAYERS, 4, CHUNK, 128), B...  141 us
    pallas_call x1, Pallas kernels, fast_body(): pl.pallas_call(results_kernel, out_shape=(shape((2 * HALF, WIDTH), BF16),...  4.26 us

profile of v4, /device:TPU:0, one launch (start us, length us, event | category | flops | bytes accessed | tf_op | source)
XLA Modules:
  0.0 146.0 jit_solution(15186956008369892862)
XLA Ops:
  0.6 140.9 %layers.1 = (bf16[2,4,768,128]{3,2,1,0:T(8,128)(2,1)}, bf16[256,512]{1,0:T(8,128)(2,1)}, bf16[256,512]{1,0:T(8,128)(2,1)}, f32[2,512]{1,0:T(2,128)}) custom-call(bf16[256,512]{1,0:T(8,128)(2,1)} %tokens.1, s32[1,4]{1,0:T(1,128)} %seq_len.1, f32[2,2]{1,0:T(2,128)} %alphas.1, f32[2,2048]{1,0:T(2,128)} %up_bias.1, f32[2,512]{1,0:T(2,128)} %down_bias.1, ...), custom_call_target="tpu_custom_call" | custom-call | tf_op jit(solution)/shard_map/layers/pallas_call | solution.py:852
  141.6 4.3 %results.1 = (bf16[256,512]{1,0:T(8,128)(2,1)}, f32[256,512]{1,0:T(8,128)}, f32[2,64,1536]{2,1,0:T(8,128)}, f32[2,64,512]{2,1,0:T(8,128)}, f32[2,64,2048]{2,1,0:...) custom-call(bf16[2,4,768,128]{3,2,1,0:T(8,128)(2,1)} %get-tuple-element.13.final_hbm, ...), custom_call_target="tpu_custom_call" | custom-call | tf_op jit(solution)/shard_map/results/pallas_call | solution.py:952

commit v5 on v4

--- a/solution.py
+++ b/solution.py
@@ -23,6 +23,7 @@
 FF = 2048
 CUT = 512
 TILE = 256
+TILES = HALF * RUNS // TILE
 PACK = HALF + DIM
 CHUNK = 768
 SMALL = FF + WIDTH + 128
@@ -57,7 +58,7 @@
     tok_in, cot_in, flag_out, flag_in, back_out, out_in, grad_in,
     hidden, grad, hid_t, attn_t, ent_t, act_t, branch, slope, second,
     dz, du, da, dqkv,
-    pack_out, head_out, qkv_in, o_in, do_in, dqkv_in,
+    pack_out, head_out, pack_in, o_in, do_in,
     kv, kv_t, rq, ro, o_t, lse, acc, dq_t, bias,
     parts, core_in, x_in, y_in, z_in, third_z, third_x, third_y, final, small, small_in, small_z, small_sum,
     w_sem, move_send, move_recv, a2a_send, a2a_recv, core_send, core_recv, x_send, x_recv, y_send, y_recv,
@@ -163,12 +164,12 @@
         return lax.rem(other + TEAM - member, TEAM)
 
     def exchange(kind, layer, half, outgoing, incoming):
-        incoming[layer, half, 0] = outgoing[half, member]
+        incoming[half, 0] = outgoing[half, member]
         for step in range(1, TEAM):
             peer = lax.rem(member + step, TEAM)
             pltpu.make_async_remote_copy(
                 src_ref=outgoing.at[half, peer],
-                dst_ref=incoming.at[layer, half, TEAM - step],
+                dst_ref=incoming.at[half, TEAM - step],
                 send_sem=a2a_send.at[kind, layer, half],
                 recv_sem=a2a_recv.at[kind, layer, half],
                 device_id=place(lax.div(peer, 2), side, zz, lax.rem(peer, 2)),
@@ -176,7 +177,7 @@
             ).start()
 
     def arrived(kind, layer, half, incoming):
-        whole = incoming.at[layer, half, pl.ds(1, TEAM - 1)]
+        whole = incoming.at[half, pl.ds(1, TEAM - 1)]
         pltpu.make_async_copy(whole, whole, a2a_recv.at[kind, layer, half]).wait()
 
     def left(kind, layer, half, outgoing):
@@ -202,10 +203,10 @@
             pack_out[half, pair, 1, 0:HALF, :] = other.astype(BF16)
         for head in range(RUNS):
             pack_out[half, head // 2, head % 2, HALF:, :] = queries_t[DIM * head : DIM * head + DIM, :]
-        exchange(0, layer, half, pack_out, qkv_in)
+        exchange(0, layer, half, pack_out, pack_in)
 
     def attend(layer, chunk):
-        arrived(0, layer, chunk, qkv_in)
+        arrived(0, layer, chunk, pack_in)
         if layer == 1:
             left(1, 0, chunk, head_out)
 
@@ -214,28 +215,19 @@
                 slot = slot_of(other)
                 start = HALF * (TEAM * chunk + other)
                 span = slice(start, start + HALF)
-                block = qkv_in[layer, chunk, slot, head, 0:HALF, :]
+                block = pack_in[chunk, slot, head, 0:HALF, :]
                 kv[layer, head, span, :] = block
                 kv_t[layer, head, :, span] = block.T
-                rq[layer, head, 0:DIM, span] = qkv_in[layer, chunk, slot, head, HALF:, :]
+                rq[layer, head, 0:DIM, span] = pack_in[chunk, slot, head, HALF:, :]
             for i in (2 * chunk, 2 * chunk + 1):
                 columns = slice(TILE * i, TILE * i + TILE)
                 query_tile = rq[layer, head, :, columns]
-                scores = []
-                for j in range(i + 1):
-                    tile = nn(kv[layer, head, TILE * j : TILE * j + TILE, :], query_tile)
-                    scores.append(tile + bias[1 if j == i else 0])
-                largest = functools.reduce(
-                    jnp.maximum, [jnp.max(tile, axis=0, keepdims=True) for tile in scores]
-                )
-                total = jnp.zeros((1, TILE), F32)
-                summed = jnp.zeros((DIM, TILE), F32)
-                for j in range(i + 1):
-                    weight = jnp.exp(scores[j] - largest)
-                    total = total + jnp.sum(weight, axis=0, keepdims=True)
-                    summed = summed + nn(
-                        kv_t[layer, head, DIM:, TILE * j : TILE * j + TILE], weight.astype(BF16)
-                    )
+                count = TILE * (i + 1)
+                scores = nn(kv[layer, head, 0:count, :], query_tile) + bias[TILE * TILES - count :, :]
+                largest = jnp.max(scores, axis=0, keepdims=True)
+                weight = jnp.exp(scores - largest)
+                total = jnp.sum(weight, axis=0, keepdims=True)
+                summed = nn(kv_t[layer, head, DIM:, 0:count], weight.astype(BF16))
                 summed = summed / total
                 o_t[layer, head, :, columns] = summed
                 lse[layer, head, :, columns] = largest + jnp.log(total)
@@ -246,14 +238,15 @@
                     ]
             return carry
 
-        lax.fori_loop(0, OWN, one_head, 0)
+        for head in range(OWN):
+            one_head(head, 0)
         exchange(1, layer, chunk, head_out, o_in)
 
     def feed(layer, half):
         rows = rows_of(half)
         arrived(1, layer, half, o_in)
         for head in range(RUNS):
-            attn_t[layer, DIM * head : DIM * head + DIM, rows] = o_in[layer, half, slot_of(head // 2), head % 2]
+            attn_t[layer, DIM * head : DIM * head + DIM, rows] = o_in[half, slot_of(head // 2), head % 2]
         attn = attn_t[layer, :, rows].T
         grown = nn(attn, wout[layer])
         branch[layer, half] = grown
@@ -318,7 +311,7 @@
         def one_head(head, carry):
             for other in range(TEAM):
                 start = HALF * (TEAM * chunk + other)
-                ro[head, DIM:, start : start + HALF] = do_in[layer, chunk, slot_of(other), head]
+                ro[head, DIM:, start : start + HALF] = do_in[chunk, slot_of(other), head]
             for i in (2 * chunk, 2 * chunk + 1):
                 columns = slice(TILE * i, TILE * i + TILE)
                 query_tile = rq[layer, head, :, columns]
@@ -329,39 +322,41 @@
                     axis=0,
                     keepdims=True,
                 )
-                query_grad = jnp.zeros((DIM, TILE), F32)
-                for j in range(i + 1):
-                    span = slice(TILE * j, TILE * j + TILE)
-                    keys = kv[layer, head, span, :]
-                    weight = jnp.exp(nn(keys, query_tile) + bias[1 if j == i else 0] - log_total)
-                    scored = (weight * (nn(keys, grad_tile) - delta)).astype(BF16)
-                    term = nt(scored, query_tile) + nt(weight.astype(BF16), grad_tile)
-                    if chunk == 1 and (i == 2 or j == i):
-                        acc[head, span, :] = term
-                    else:
-                        acc[head, span, :] += term
-                    query_grad = query_grad + nn(kv_t[layer, head, 0:DIM, span], scored)
-                dq_t[:, columns] = query_grad * (DIM ** -0.5)
+                count = TILE * (i + 1)
+                keys = kv[layer, head, 0:count, :]
+                weight = jnp.exp(nn(keys, query_tile) + bias[TILE * TILES - count :, :] - log_total)
+                scored = (weight * (nn(keys, grad_tile) - delta)).astype(BF16)
+                term = nt(scored, query_tile) + nt(weight.astype(BF16), grad_tile)
+                if chunk == 1 and i == 2:
+                    acc[head, 0:count, :] = term
+                elif chunk == 1:
+                    acc[head, 0 : count - TILE, :] += term[0 : count - TILE, :]
+                    acc[head, count - TILE : count, :] = term[count - TILE :, :]
+                else:
+                    acc[head, 0:count, :] += term
+                query_grad = nn(kv_t[layer, head, 0:DIM, 0:count], scored)
+                dq_t[head, :, columns] = query_grad * (DIM ** -0.5)
             for other in range(TEAM):
                 start = HALF * (TEAM * chunk + other)
                 span = slice(start, start + HALF)
                 pack_out[chunk, other, head, 0:HALF, :] = acc[head, span, :].astype(BF16)
-                pack_out[chunk, other, head, HALF:, :] = dq_t[:, span].astype(BF16)
+                pack_out[chunk, other, head, HALF:, :] = dq_t[head, :, span].astype(BF16)
             return carry
 
-        lax.fori_loop(0, OWN, one_head, 0)
-        exchange(3, layer, chunk, pack_out, dqkv_in)
+        for head in range(OWN):
+            one_head(head, 0)
+        exchange(3, layer, chunk, pack_out, pack_in)
 
     def project_back(layer, half):
         rows = rows_of(half)
-        arrived(3, layer, half, dqkv_in)
+        arrived(3, layer, half, pack_in)
         turned = jnp.concatenate(
-            [dqkv_in[layer, half, slot_of(head // 2), head % 2, HALF:, :] for head in range(RUNS)], axis=0
+            [pack_in[half, slot_of(head // 2), head % 2, HALF:, :] for head in range(RUNS)], axis=0
         )
         dqkv[rows, 0:WIDTH] = turned.T
         for pair in range(RUNS // 2):
-            first = dqkv_in[layer, half, slot_of(pair), 0, 0:HALF, :].astype(F32)
-            other = dqkv_in[layer, half, slot_of(pair), 1, 0:HALF, :].astype(F32)
+            first = pack_in[half, slot_of(pair), 0, 0:HALF, :].astype(F32)
+            other = pack_in[half, slot_of(pair), 1, 0:HALF, :].astype(F32)
             k_pair = jnp.where(low, first, pltpu.roll(other, DIM, 1))
             v_pair = jnp.where(low, pltpu.roll(first, DIM, 1), other)
             dqkv[rows, WIDTH + 128 * pair : WIDTH + 128 * pair + 128] = k_pair.astype(BF16)
@@ -684,8 +679,9 @@
     key_sub = lax.rem(key_row, HALF).astype(F32) >= border
     query_sub = lax.rem(query_col, HALF).astype(F32) >= border
     apart = jnp.logical_xor(key_sub, query_sub)
-    bias[0] = jnp.where(apart, NEGATIVE, 0.0)
-    bias[1] = jnp.where(jnp.logical_or(later, apart), NEGATIVE, 0.0)
+    for tile in range(TILES - 1):
+        bias[TILE * tile : TILE * tile + TILE, :] = jnp.where(apart, NEGATIVE, 0.0)
+    bias[TILE * (TILES - 1) :, :] = jnp.where(jnp.logical_or(later, apart), NEGATIVE, 0.0)
 
     for number in range(1, 4):
         weight_copies[0, number].wait()
@@ -886,10 +882,9 @@
             vmem(2 * HALF, 3 * WIDTH),
             vmem(2, TEAM, OWN, PACK, 128),
             vmem(2, TEAM, OWN, DIM, 128),
-            vmem(LAYERS, 2, TEAM, OWN, PACK, 128),
-            vmem(LAYERS, 2, TEAM, OWN, DIM, 128),
-            vmem(LAYERS, 2, TEAM, OWN, DIM, 128),
-            vmem(LAYERS, 2, TEAM, OWN, PACK, 128),
+            vmem(2, TEAM, OWN, PACK, 128),
+            vmem(2, TEAM, OWN, DIM, 128),
+            vmem(2, TEAM, OWN, DIM, 128),
             vmem(LAYERS, OWN, rows, 128),
             vmem(LAYERS, OWN, 128, rows),
             vmem(LAYERS, OWN, 128, rows),
@@ -897,8 +892,8 @@
             wide(LAYERS, OWN, DIM, rows),
             wide(LAYERS, OWN, 1, rows),
             wide(OWN, rows, 128),
-            wide(DIM, rows),
-            wide(2, TILE, TILE),
+            wide(OWN, DIM, rows),
+            wide(rows, TILE),
             vmem(LAYERS, 4, 4, 2, CHUNK, 128),
             vmem(2, 4, 2, CHUNK, 128),
             vmem(4, 2, CHUNK, 128),

time: 146 us -> 146 us (level)
  no operation moved by 1% of the time
where the time goes in v5:
time: 146 us; the launch traced here: 145 us
  Pallas kernels  144 us (99%)
    pallas_call x1, Pallas kernels, fast_body(): pl.pallas_call(layers_kernel, out_shape=(shape((LAYERS, 4, CHUNK, 128), B...  140 us
    pallas_call x1, Pallas kernels, fast_body(): pl.pallas_call(results_kernel, out_shape=(shape((2 * HALF, WIDTH), BF16),...  4.26 us

profile of v5, /device:TPU:0, one launch (start us, length us, event | category | flops | bytes accessed | tf_op | source)
XLA Modules:
  0.0 145.3 jit_solution(8057339347640822536)
XLA Ops:
  0.6 140.2 %layers.1 = (bf16[2,4,768,128]{3,2,1,0:T(8,128)(2,1)}, bf16[256,512]{1,0:T(8,128)(2,1)}, bf16[256,512]{1,0:T(8,128)(2,1)}, f32[2,512]{1,0:T(2,128)}) custom-call(bf16[256,512]{1,0:T(8,128)(2,1)} %tokens.1, s32[1,4]{1,0:T(1,128)} %seq_len.1, f32[2,2]{1,0:T(2,128)} %alphas.1, f32[2,2048]{1,0:T(2,128)} %up_bias.1, f32[2,512]{1,0:T(2,128)} %down_bias.1, ...), custom_call_target="tpu_custom_call" | custom-call | tf_op jit(solution)/shard_map/layers/pallas_call | solution.py:848
  140.9 4.3 %results.1 = (bf16[256,512]{1,0:T(8,128)(2,1)}, f32[256,512]{1,0:T(8,128)}, f32[2,64,1536]{2,1,0:T(8,128)}, f32[2,64,512]{2,1,0:T(8,128)}, f32[2,64,2048]{2,1,0:...) custom-call(bf16[2,4,768,128]{3,2,1,0:T(8,128)(2,1)} %get-tuple-element.13.final_hbm, ...), custom_call_target="tpu_custom_call" | custom-call | tf_op jit(solution)/shard_map/results/pallas_call | solution.py:947

commit v6 on v5

--- a/solution.py
+++ b/solution.py
@@ -25,12 +25,25 @@
 TILE = 256
 TILES = HALF * RUNS // TILE
 PACK = HALF + DIM
-CHUNK = 768
+CHUNK = 576
 SMALL = FF + WIDTH + 128
-UP, DOWN, LATE = 256, 512, 0
-PART = 256
-ORDERS = ((0, 144), (144, 48), (192, 64))
-THIRD = ORDERS[2][1]
+UP, DOWN = 0, 1
+PARTS = ((0, 320), (320, 256))
+SHARES = {(1, UP): (176, 0, 144), (1, DOWN): (144, 32, 80), (0, UP): (112, 160, 48), (0, DOWN): (112, 144, 0)}
+
+
+def spans():
+    places, totals = {}, [0, 0, 0]
+    for key, counts in SHARES.items():
+        first = PARTS[key[1]][0]
+        for route, count in enumerate(counts):
+            places[(*key, route)] = (first, totals[route], count)
+            first += count
+            totals[route] += count
+    return places, totals
+
+
+SPANS, TOTALS = spans()
 
 SLOPE_AT = 0.28
 TAIL = (
@@ -53,16 +66,18 @@
 
 def layers_kernel(
     tokens, seq_len, alphas, up_bias, down_bias, cotangent, qkv_hbm, out_hbm, up_hbm, down_hbm,
-    final_hbm, output_hbm, input_grad_hbm, small_final,
+    final_hbm, heads_hbm, output_hbm, input_grad_hbm, small_final,
     wqkv, wout, wup, wdown,
     tok_in, cot_in, flag_out, flag_in, back_out, out_in, grad_in,
-    hidden, grad, hid_t, attn_t, ent_t, act_t, branch, slope, second,
+    hidden, grad, hid_all, attn_t, ent_t, act_t, branch, slope, second,
     dz, du, da, dqkv,
     pack_out, head_out, pack_in, o_in, do_in,
     kv, kv_t, rq, ro, o_t, lse, acc, dq_t, bias,
-    parts, core_in, x_in, y_in, z_in, third_z, third_x, third_y, final, small, small_in, small_z, small_sum,
+    parts, core_in, xa_in, xb_in, ya_in, yb_in, z_in, third_z, third_x, third_y, final,
+    heads_out, heads_x, heads_z, heads_sum, heads_all, small, small_in, small_z, small_sum,
     w_sem, move_send, move_recv, a2a_send, a2a_recv, core_send, core_recv, x_send, x_recv, y_send, y_recv,
-    z_send, z_recv, tz_send, tz_recv, tx_send, tx_recv, ty_send, ty_recv, fin_send, fin_recv, small_send, small_recv, out_sem, core_free, x_free, y_free,
+    z_send, z_recv, tz_send, tz_recv, fin_send, fin_recv, hid_send, hid_recv, hx_send, hx_recv, hz_send, hz_recv, hf_send, hf_recv,
+    small_send, small_recv, out_sem, core_free,
 ):
     grp = lax.axis_index("grp")
     blk = lax.axis_index("blk")
@@ -102,9 +117,13 @@
         )
     pl.semaphore_signal(barrier, inc=1, device_id=x_peer, device_id_type=MESH)
     pl.semaphore_signal(barrier, inc=1, device_id=y_peer, device_id_type=MESH)
-    pl.semaphore_signal(
-        barrier, inc=1, device_id=place(1 - core, side, zz, 1 - yy), device_id_type=MESH
-    )
+    for peer in (
+        place(1 - core, side, zz, 1 - yy),
+        place(1 - core, 1 - side, zz, yy),
+        place(core, 1 - side, zz, 1 - yy),
+        place(1 - core, 1 - side, zz, 1 - yy),
+    ):
+        pl.semaphore_signal(barrier, inc=1, device_id=peer, device_id_type=MESH)
 
     end_second = lax.div(seq_len[0, 0] + seq_len[0, 1], RUNS)
     flag_out[...] = jnp.full((8, 128), end_second.astype(F32), F32)
@@ -113,6 +132,19 @@
             rq[layer, head, DIM:, :] = jnp.zeros((DIM, HALF * RUNS), BF16)
     for head in range(OWN):
         ro[head, 0:DIM, :] = jnp.zeros((DIM, HALF * RUNS), BF16)
+
+    def remote(source, target, send, recv, peer):
+        return pltpu.make_async_remote_copy(
+            src_ref=source,
+            dst_ref=target,
+            send_sem=send,
+            recv_sem=recv,
+            device_id=peer,
+            device_id_type=MESH,
+        )
+
+    def credit(semaphore, peer):
+        pl.semaphore_signal(semaphore, inc=1, device_id=peer, device_id_type=MESH)
 
     def moved(kind, slot, source, target, at, core_at, z_at):
         here = jnp.logical_and(core_at == core, z_at == zz)
@@ -163,31 +195,58 @@
     def slot_of(other):
         return lax.rem(other + TEAM - member, TEAM)
 
-    def exchange(kind, layer, half, outgoing, incoming):
-        incoming[half, 0] = outgoing[half, member]
+    def exchange(kind, layer, half, head, outgoing, incoming):
+        incoming[half, 0, head] = outgoing[half, member, head]
         for step in range(1, TEAM):
             peer = lax.rem(member + step, TEAM)
             pltpu.make_async_remote_copy(
-                src_ref=outgoing.at[half, peer],
-                dst_ref=incoming.at[half, TEAM - step],
-                send_sem=a2a_send.at[kind, layer, half],
-                recv_sem=a2a_recv.at[kind, layer, half],
+                src_ref=outgoing.at[half, peer, head],
+                dst_ref=incoming.at[half, TEAM - step, head],
+                send_sem=a2a_send.at[kind, layer, half, head],
+                recv_sem=a2a_recv.at[kind, layer, half, head],
                 device_id=place(lax.div(peer, 2), side, zz, lax.rem(peer, 2)),
                 device_id_type=MESH,
             ).start()
 
-    def arrived(kind, layer, half, incoming):
-        whole = incoming.at[half, pl.ds(1, TEAM - 1)]
-        pltpu.make_async_copy(whole, whole, a2a_recv.at[kind, layer, half]).wait()
+    def arrived(kind, layer, half, head, incoming):
+        whole = incoming.at[half, pl.ds(1, TEAM - 1), head]
+        pltpu.make_async_copy(whole, whole, a2a_recv.at[kind, layer, half, head]).wait()
 
     def left(kind, layer, half, outgoing):
-        whole = outgoing.at[half, pl.ds(1, TEAM - 1)]
-        pltpu.make_async_copy(whole, whole, a2a_send.at[kind, layer, half]).wait()
+        for head in range(OWN):
+            whole = outgoing.at[half, pl.ds(1, TEAM - 1), head]
+            pltpu.make_async_copy(whole, whole, a2a_send.at[kind, layer, half, head]).wait()
+
+    def tokens_of(chunk, other):
+        return pl.ds(pl.multiple_of(HALF * (TEAM * chunk + other), HALF), HALF)
+
+    def hidden_copy(layer, chunk, which):
+        whose = 2 * core + 1 - yy if which == 2 else member
+        block = hid_all.at[layer, :, tokens_of(chunk, whose)]
+        return remote(
+            block,
+            block,
+            hid_send.at[layer, chunk, which],
+            hid_recv.at[layer, chunk, which],
+            y_peer if which == 0 else core_peer,
+        )
+
+    def hidden_start(layer, chunk):
+        for which in range(2):
+            hidden_copy(layer, chunk, which).start()
+
+    def hidden_pass(layer, chunk):
+        hidden_copy(layer, chunk, 0).wait()
+        hidden_copy(layer, chunk, 2).start()
+
+    def hidden_done(layer, chunk):
+        for which in range(1, 3):
+            hidden_copy(layer, chunk, which).wait()
 
     def project(layer, half):
         rows = rows_of(half)
         rounded = hidden[half].astype(BF16)
-        hid_t[layer, :, rows] = rounded.T
+        hid_all[layer, :, tokens_of(half, member)] = rounded.T
         if layer == 1:
             left(0, 0, half, pack_out)
         queries = nn(rounded, wqkv[layer, :, 0:WIDTH]) * (DIM ** -0.5)
@@ -203,14 +262,15 @@
             pack_out[half, pair, 1, 0:HALF, :] = other.astype(BF16)
         for head in range(RUNS):
             pack_out[half, head // 2, head % 2, HALF:, :] = queries_t[DIM * head : DIM * head + DIM, :]
-        exchange(0, layer, half, pack_out, pack_in)
+        for head in range(OWN):
+            exchange(0, layer, half, head, pack_out, pack_in)
 
     def attend(layer, chunk):
-        arrived(0, layer, chunk, pack_in)
         if layer == 1:
             left(1, 0, chunk, head_out)
 
         def one_head(head, carry):
+            arrived(0, layer, chunk, head, pack_in)
             for other in range(TEAM):
                 slot = slot_of(other)
                 start = HALF * (TEAM * chunk + other)
@@ -236,15 +296,16 @@
                     head_out[chunk, 2 * (i - 2 * chunk) + part, head] = rounded[
                         :, HALF * part : HALF * part + HALF
                     ]
+            exchange(1, layer, chunk, head, head_out, o_in)
             return carry
 
         for head in range(OWN):
             one_head(head, 0)
-        exchange(1, layer, chunk, head_out, o_in)
 
     def feed(layer, half):
         rows = rows_of(half)
-        arrived(1, layer, half, o_in)
+        for head in range(OWN):
+            arrived(1, layer, half, head, o_in)
         for head in range(RUNS):
             attn_t[layer, DIM * head : DIM * head + DIM, rows] = o_in[half, slot_of(head // 2), head % 2]
         attn = attn_t[layer, :, rows].T
@@ -297,18 +358,19 @@
             column == 0, alpha_first, jnp.where(column == 1, alpha_second, 0.0)
         )
         mixed = (alphas[layer, 0] * middle).astype(BF16)
-        da[layer, rows, :] = mixed
+        da[rows, :] = mixed
         spread = nt(wout[layer], mixed).astype(BF16)
         left(*((1, 1) if layer == 1 else (2, 1)), half, head_out)
         for head in range(RUNS):
             head_out[half, head // 2, head % 2] = spread[DIM * head : DIM * head + DIM, :]
-        exchange(2, layer, half, head_out, do_in)
+        for head in range(OWN):
+            exchange(2, layer, half, head, head_out, do_in)
 
     def attend_back(layer, chunk):
-        arrived(2, layer, chunk, do_in)
         left(*((0, 1) if layer == 1 else (3, 1)), chunk, pack_out)
 
         def one_head(head, carry):
+            arrived(2, layer, chunk, head, do_in)
             for other in range(TEAM):
                 start = HALF * (TEAM * chunk + other)
                 ro[head, DIM:, start : start + HALF] = do_in[chunk, slot_of(other), head]
@@ -341,27 +403,27 @@
                 span = slice(start, start + HALF)
                 pack_out[chunk, other, head, 0:HALF, :] = acc[head, span, :].astype(BF16)
                 pack_out[chunk, other, head, HALF:, :] = dq_t[head, :, span].astype(BF16)
+            exchange(3, layer, chunk, head, pack_out, pack_in)
             return carry
 
         for head in range(OWN):
             one_head(head, 0)
-        exchange(3, layer, chunk, pack_out, pack_in)
 
     def project_back(layer, half):
-        rows = rows_of(half)
-        arrived(3, layer, half, pack_in)
+        for head in range(OWN):
+            arrived(3, layer, half, head, pack_in)
         turned = jnp.concatenate(
             [pack_in[half, slot_of(head // 2), head % 2, HALF:, :] for head in range(RUNS)], axis=0
         )
-        dqkv[rows, 0:WIDTH] = turned.T
+        dqkv[:, 0:WIDTH] = turned.T
         for pair in range(RUNS // 2):
             first = pack_in[half, slot_of(pair), 0, 0:HALF, :].astype(F32)
             other = pack_in[half, slot_of(pair), 1, 0:HALF, :].astype(F32)
             k_pair = jnp.where(low, first, pltpu.roll(other, DIM, 1))
             v_pair = jnp.where(low, pltpu.roll(first, DIM, 1), other)
-            dqkv[rows, WIDTH + 128 * pair : WIDTH + 128 * pair + 128] = k_pair.astype(BF16)
-            dqkv[rows, 2 * WIDTH + 128 * pair : 2 * WIDTH + 128 * pair + 128] = v_pair.astype(BF16)
-        grad[half] = grad[half] + nt(dqkv[rows, :], wqkv[layer])
+            dqkv[:, WIDTH + 128 * pair : WIDTH + 128 * pair + 128] = k_pair.astype(BF16)
+            dqkv[:, 2 * WIDTH + 128 * pair : 2 * WIDTH + 128 * pair + 128] = v_pair.astype(BF16)
+        grad[half] = grad[half] + nt(dqkv[...], wqkv[layer])
 
     def scatter_rows(layer, result, first_row):
         for run in range(RUNS):
@@ -373,211 +435,278 @@
     def up_grads(layer):
         for step in range(FF // CUT):
             cut = slice(CUT * step, CUT * step + CUT)
-            scatter_rows(layer, nn(ent_t[layer], du[:, cut]), UP + DIM * step)
+            scatter_rows(layer, nn(ent_t[layer], du[:, cut]), DIM * step)
+        scatter_rows(layer, nn(attn_t[layer], da[...]), 256)
+        core_start(layer, UP)
 
     def down_grads(layer):
         for run in range(RUNS):
             result = nn(act_t[layer, TILE * run : TILE * run + TILE, :], dz[...])
             for quarter in range(4):
-                parts[layer, quarter, run // 2, run % 2, DOWN : DOWN + PART, :] = result[
+                parts[layer, quarter, run // 2, run % 2, 320:576, :] = result[
                     :, 128 * quarter : 128 * quarter + 128
                 ].astype(BF16)
-
-    def late_grads(layer):
-        scatter_rows(layer, nn(attn_t[layer], da[layer]), LATE + 192)
-        for step in range(3):
-            scatter_rows(
-                layer, nn(hid_t[layer], dqkv[:, WIDTH * step : WIDTH * step + WIDTH]), LATE + DIM * step
-            )
-
-    def remote(source, target, send, recv, peer):
-        return pltpu.make_async_remote_copy(
-            src_ref=source,
-            dst_ref=target,
-            send_sem=send,
-            recv_sem=recv,
-            device_id=peer,
-            device_id_type=MESH,
-        )
-
-    def credit(semaphore, peer):
-        pl.semaphore_signal(semaphore, inc=1, device_id=peer, device_id_type=MESH)
-
-    def rows_in(part, order):
-        return pl.ds(part + ORDERS[order][0], ORDERS[order][1])
+        core_start(layer, DOWN)
+
+    def heads_grads(layer):
+        for chunk in range(2):
+            hidden_done(layer, chunk)
+        blocks = [(run // TEAM, run % TEAM) for run in range(RUNS)]
+        keys_values = jnp.concatenate(
+            [
+                jnp.concatenate([pack_out[chunk, other, head, 0:HALF, :] for chunk, other in blocks], axis=0)
+                for head in range(OWN)
+            ],
+            axis=1,
+        )
+        queries = jnp.concatenate(
+            [
+                jnp.concatenate([pack_out[chunk, other, head, HALF:, :] for chunk, other in blocks], axis=1)
+                for head in range(OWN)
+            ],
+            axis=0,
+        )
+        both = nn(hid_all[layer], keys_values)
+        q_part = nt(hid_all[layer], queries)
+        first, other = both[:, 0:128], both[:, 128:256]
+        left_half = lax.broadcasted_iota(jnp.int32, (WIDTH, 128), 1) < DIM
+        k_part = jnp.where(left_half, first, pltpu.roll(other, DIM, 1))
+        v_part = jnp.where(left_half, pltpu.roll(first, DIM, 1), other)
+        for number, values in enumerate((q_part, k_part, v_part)):
+            for run in range(RUNS):
+                heads_out[layer, run // 2, run % 2, :, 128 * number : 128 * number + 128] = values[
+                    DIM * run : DIM * run + DIM, :
+                ].astype(BF16)
+        heads_x_copy(layer).start()
+
+    def half_rows(which):
+        return pl.ds(pl.multiple_of(32 * which, 32), 32)
+
+    def heads_x_copy(layer):
+        return remote(
+            heads_out.at[layer, :, :, half_rows(1 - side)],
+            heads_x.at[layer],
+            hx_send.at[layer],
+            hx_recv.at[layer],
+            x_peer,
+        )
+
+    def heads_z_copy(layer, step):
+        peer = lax.rem(zz + step, 4)
+        return remote(
+            heads_out.at[layer, peer, :, half_rows(side)],
+            heads_z.at[layer, 4 - step],
+            hz_send.at[layer, step],
+            hz_recv.at[layer, 4 - step],
+            place(core, side, peer, yy),
+        )
+
+    def heads_last_copy(layer, number):
+        x, c, y = number // 4, number // 2 % 2, number % 2
+        return remote(
+            heads_sum.at[layer, 1 - yy if y else yy],
+            heads_all.at[layer, side, member],
+            hf_send.at[layer, number],
+            hf_recv.at[layer, number],
+            place(1 - core if c else core, 1 - side if x else side, zz, 1 - yy if y else yy),
+        )
+
+    def heads_second(layer):
+        heads_x_copy(layer).wait()
+        heads_out[layer, :, :, half_rows(side), :] += heads_x[layer]
+        for step in range(1, 4):
+            heads_z_copy(layer, step).start()
+
+    def heads_third(layer):
+        for step in range(1, 4):
+            heads_z_copy(layer, step).wait()
+        total = heads_out[layer, zz, :, half_rows(side), :].astype(F32)
+        for slot in range(1, 4):
+            total = total + heads_z[layer, slot].astype(F32)
+        heads_sum[layer] = total.astype(BF16)
+        heads_all[layer, side, member] = heads_sum[layer, yy]
+        for number in range(1, 8):
+            heads_last_copy(layer, number).start()
+
+    def heads_copy_out(layer):
+        return pltpu.make_async_copy(heads_all.at[layer], heads_hbm.at[layer], out_sem.at[1, layer])
+
+    def heads_done(layer):
+        for number in range(1, 8):
+            heads_last_copy(layer, number).wait()
+        heads_copy_out(layer).start()
+
+    def chunk_rows(layer, part, route):
+        first, _, count = SPANS[layer, part, route]
+        return pl.ds(first, count)
+
+    def route_rows(layer, part, route):
+        _, first, count = SPANS[layer, part, route]
+        return pl.ds(first, count)
+
+    def rows_in(layer, part, route):
+        return chunk_rows(layer, part, route), route_rows(layer, part, route)
+
+    def used(layer, part, route):
+        return SHARES[layer, part][route] > 0
 
     def core_copy(layer, part, across):
-        rows = pl.ds(part, PART)
-        which = (layer, part // PART, across)
+        rows = pl.ds(*PARTS[part])
         return remote(
             parts.at[layer, 2 * across + 1 - core, :, :, rows],
             core_in.at[across, :, :, rows],
-            core_send.at[which],
-            core_recv.at[which],
+            core_send.at[layer, part, across],
+            core_recv.at[layer, part, across],
             core_peer,
         )
 
-    def x_copy(layer, part, order):
-        rows = rows_in(part, order)
-        which = (layer, part // PART, order)
-        ends = (x_send.at[which], x_recv.at[which], x_peer)
-        if order == 0:
-            return remote(parts.at[layer, far_side, :, :, rows], x_in.at[:, :, rows], *ends)
-        return remote(parts.at[layer, far_side, :, yy, rows], x_in.at[:, 0, rows], *ends)
-
-    def y_copy(layer, part, order, across):
-        rows = rows_in(part, order)
-        which = (layer, part // PART, order, across)
+    def x_copy(layer, part, route):
+        rows, room = rows_in(layer, part, route)
+        ends = (x_send.at[layer, part, route], x_recv.at[layer, part, route], x_peer)
+        if route == 0:
+            return remote(parts.at[layer, far_side, :, :, rows], xa_in.at[:, :, room], *ends)
+        if route == 1:
+            return remote(parts.at[layer, far_side, :, yy, rows], xb_in.at[:, room], *ends)
+        return remote(parts.at[layer, far_side, zz, :, rows], third_x.at[:, room], *ends)
+
+    def y_copy(layer, part, route, across=0):
+        rows, room = rows_in(layer, part, route)
+        which = (layer, part, route + across)
+        if route == 2:
+            which = (layer, part, 3)
         ends = (y_send.at[which], y_recv.at[which], y_peer)
-        quarter = grp if order == 0 else 2 * across + core
-        return remote(parts.at[layer, quarter, :, 1 - yy, rows], y_in.at[across, :, rows], *ends)
-
-    def z_copy(layer, part, order, step):
-        rows = rows_in(part, order)
+        if route == 0:
+            return remote(parts.at[layer, grp, :, 1 - yy, rows], ya_in.at[:, room], *ends)
+        if route == 1:
+            return remote(parts.at[layer, 2 * across + core, :, 1 - yy, rows], yb_in.at[across, :, room], *ends)
+        return remote(parts.at[layer, grp, zz, 1 - yy, rows], third_y.at[room], *ends)
+
+    def z_copy(layer, part, route, step):
+        rows = chunk_rows(layer, part, route)
         peer = lax.rem(zz + step, 4)
         return remote(
             parts.at[layer, grp, peer, yy, rows],
             z_in.at[layer, 4 - step, rows],
-            z_send.at[layer, part // PART, order, step],
-            z_recv.at[layer, part // PART, order, 4 - step],
+            z_send.at[layer, part, route, step],
+            z_recv.at[layer, part, route, 4 - step],
             place(core, side, peer, yy),
         )
 
     def third_z_copy(layer, part, across, step):
+        rows, room = rows_in(layer, part, 2)
         peer = lax.rem(zz + step, 4)
-        which = (layer, part // PART, across)
         return remote(
-            parts.at[layer, 2 * across + core, peer, :, rows_in(part, 2)],
-            third_z.at[layer, part // PART, across, 4 - step],
-            tz_send.at[(*which, step)],
-            tz_recv.at[(*which, 4 - step)],
+            parts.at[layer, 2 * across + core, peer, :, rows],
+            third_z.at[across, 4 - step, :, room],
+            tz_send.at[layer, part, across, step],
+            tz_recv.at[layer, part, across, 4 - step],
             place(core, side, peer, yy),
         )
 
-    def third_x_copy(layer, part):
-        which = (layer, part // PART)
-        return remote(
-            parts.at[layer, far_side, zz, :, rows_in(part, 2)],
-            third_x.at[which],
-            tx_send.at[which],
-            tx_recv.at[which],
-            x_peer,
-        )
-
-    def third_y_copy(layer, part):
-        which = (layer, part // PART)
-        return remote(
-            parts.at[layer, grp, zz, 1 - yy, rows_in(part, 2)],
-            third_y.at[which],
-            ty_send.at[which],
-            ty_recv.at[which],
-            y_peer,
-        )
-
     def final_copy(layer, part, which):
-        rows = pl.ds(part, PART)
-        quarter = far_side if which == 2 else grp
-        block = final.at[layer, quarter, rows]
+        block = final.at[layer, far_side if which == 2 else grp, pl.ds(*PARTS[part])]
         return remote(
             block,
             block,
-            fin_send.at[layer, part // PART, which],
-            fin_recv.at[layer, part // PART, which],
+            fin_send.at[layer, part, which],
+            fin_recv.at[layer, part, which],
             x_peer if which == 0 else core_peer,
         )
 
     def core_start(layer, part):
         if layer == 0:
-            pl.semaphore_wait(core_free.at[part // PART], 1)
+            pl.semaphore_wait(core_free.at[part], 1)
         for across in range(2):
             core_copy(layer, part, across).start()
 
     def core_done(layer, part):
-        rows = pl.ds(part, PART)
+        rows = pl.ds(*PARTS[part])
         for across in range(2):
             core_copy(layer, part, across).wait()
-        if layer == 0:
-            pl.semaphore_wait(x_free.at[part // PART, 0], 1)
-            pl.semaphore_wait(y_free.at[part // PART, 1], 1)
         for across in (1 - side, side):
             parts[layer, 2 * across + core, :, :, rows, :] += core_in[across, :, :, rows, :]
-            if across is not side:
+            if used(layer, part, 0) and across is not side:
                 x_copy(layer, part, 0).start()
-            y_copy(layer, part, 1, across).start()
+            if used(layer, part, 1):
+                y_copy(layer, part, 1, across).start()
+            if used(layer, part, 2):
+                for step in range(1, 4):
+                    third_z_copy(layer, part, across, step).start()
+        if layer == 1:
+            credit(core_free.at[part], core_peer)
+
+    def first_x(layer, part):
+        if used(layer, part, 0):
+            rows, room = rows_in(layer, part, 0)
+            x_copy(layer, part, 0).wait()
+            for y in (1 - yy, yy):
+                parts[layer, grp, :, y, rows, :] += xa_in[:, y, room, :]
+                if y is not yy:
+                    y_copy(layer, part, 0).start()
+
+    def first_y(layer, part):
+        if used(layer, part, 1):
+            rows, room = rows_in(layer, part, 1)
+            for across in (1 - side, side):
+                y_copy(layer, part, 1, across).wait()
+            for across in (1 - side, side):
+                parts[layer, 2 * across + core, :, yy, rows, :] += yb_in[across, :, room, :]
+                if across is not side:
+                    x_copy(layer, part, 1).start()
+
+    def first_z(layer, part):
+        if used(layer, part, 2):
+            rows, room = rows_in(layer, part, 2)
+            for across in (1 - side, side):
+                for step in range(1, 4):
+                    third_z_copy(layer, part, across, step).wait()
+                total = parts[layer, 2 * across + core, zz, :, rows, :].astype(F32)
+                for slot in range(1, 4):
+                    total = total + third_z[across, slot, :, room, :].astype(F32)
+                parts[layer, 2 * across + core, zz, :, rows, :] = total.astype(BF16)
+                if across is not side:
+                    x_copy(layer, part, 2).start()
+
+    def second_x(layer, part):
+        if used(layer, part, 0):
+            rows, room = rows_in(layer, part, 0)
+            y_copy(layer, part, 0).wait()
+            parts[layer, grp, :, yy, rows, :] += ya_in[:, room, :]
             for step in range(1, 4):
-                third_z_copy(layer, part, across, step).start()
-        if layer == 1:
-            credit(core_free.at[part // PART], core_peer)
-
-    def first_done(layer, part):
-        rows = rows_in(part, 1)
-        for across in (1 - side, side):
-            y_copy(layer, part, 1, across).wait()
-        if layer == 0:
-            pl.semaphore_wait(x_free.at[part // PART, 1], 1)
-            pl.semaphore_wait(y_free.at[part // PART, 0], 1)
-        for across in (1 - side, side):
-            parts[layer, 2 * across + core, :, yy, rows, :] += y_in[across, :, rows, :]
-            if across is not side:
-                x_copy(layer, part, 1).start()
-        if layer == 1:
-            credit(y_free.at[part // PART, 1], y_peer)
-
-        rows = rows_in(part, 0)
-        x_copy(layer, part, 0).wait()
-        for y in (1 - yy, yy):
-            parts[layer, grp, :, y, rows, :] += x_in[:, y, rows, :]
-            if y is not yy:
-                y_copy(layer, part, 0, 0).start()
-        if layer == 1:
-            credit(x_free.at[part // PART, 0], x_peer)
-
-        rows = rows_in(part, 2)
-        for across in (1 - side, side):
+                z_copy(layer, part, 0, step).start()
+
+    def second_y(layer, part):
+        if used(layer, part, 1):
+            rows, room = rows_in(layer, part, 1)
+            x_copy(layer, part, 1).wait()
+            parts[layer, grp, :, yy, rows, :] += xb_in[:, room, :]
             for step in range(1, 4):
-                third_z_copy(layer, part, across, step).wait()
-            total = parts[layer, 2 * across + core, zz, :, rows, :].astype(F32)
-            for slot in range(1, 4):
-                total = total + third_z[layer, part // PART, across, slot].astype(F32)
-            parts[layer, 2 * across + core, zz, :, rows, :] = total.astype(BF16)
-            if across is not side:
-                third_x_copy(layer, part).start()
-
-    def second_done(layer, part):
-        for order in (1, 0):
-            rows = rows_in(part, order)
-            if order == 0:
-                y_copy(layer, part, 0, 0).wait()
-                parts[layer, grp, :, yy, rows, :] += y_in[0, :, rows, :]
+                z_copy(layer, part, 1, step).start()
+
+    def second_z(layer, part):
+        if used(layer, part, 2):
+            rows, room = rows_in(layer, part, 2)
+            x_copy(layer, part, 2).wait()
+            for y in (1 - yy, yy):
+                parts[layer, grp, zz, y, rows, :] += third_x[y, room, :]
+                if y is not yy:
+                    y_copy(layer, part, 2).start()
+
+    def third_done(layer, part):
+        for route in range(3):
+            if not used(layer, part, route):
+                continue
+            rows, room = rows_in(layer, part, route)
+            if route == 2:
+                y_copy(layer, part, 2).wait()
+                final[layer, grp, rows, :] = parts[layer, grp, zz, yy, rows, :] + third_y[room, :]
             else:
-                x_copy(layer, part, 1).wait()
-                parts[layer, grp, :, yy, rows, :] += x_in[:, 0, rows, :]
-            for step in range(1, 4):
-                z_copy(layer, part, order, step).start()
-            if layer == 1:
-                if order == 0:
-                    credit(y_free.at[part // PART, 0], y_peer)
-                else:
-                    credit(x_free.at[part // PART, 1], x_peer)
-        rows = rows_in(part, 2)
-        third_x_copy(layer, part).wait()
-        for y in (1 - yy, yy):
-            parts[layer, grp, zz, y, rows, :] += third_x[layer, part // PART, y]
-            if y is not yy:
-                third_y_copy(layer, part).start()
-
-    def z_done(layer, part):
-        for order in (1, 0):
-            for step in range(1, 4):
-                z_copy(layer, part, order, step).wait()
-        rows = pl.ds(part, ORDERS[2][0])
-        total = parts[layer, grp, zz, yy, rows, :].astype(F32)
-        for slot in range(1, 4):
-            total = total + z_in[layer, slot, rows, :].astype(F32)
-        final[layer, grp, rows, :] = total.astype(BF16)
-        rows = rows_in(part, 2)
-        third_y_copy(layer, part).wait()
-        final[layer, grp, rows, :] = parts[layer, grp, zz, yy, rows, :] + third_y[layer, part // PART]
+                for step in range(1, 4):
+                    z_copy(layer, part, route, step).wait()
+                total = parts[layer, grp, zz, yy, rows, :].astype(F32)
+                for slot in range(1, 4):
+                    total = total + z_in[layer, slot, rows, :].astype(F32)
+                final[layer, grp, rows, :] = total.astype(BF16)
         for which in range(2):
             final_copy(layer, part, which).start()
 
@@ -586,9 +715,9 @@
         final_copy(layer, part, 2).start()
 
     def final_out(layer, part):
-        rows = pl.ds(part, PART)
+        rows = pl.ds(*PARTS[part])
         return pltpu.make_async_copy(
-            final.at[layer, :, rows], final_hbm.at[layer, :, rows], out_sem.at[layer, part // PART]
+            final.at[layer, :, rows], final_hbm.at[layer, :, rows], out_sem.at[0, 2 * layer + part]
         )
 
     def final_done(layer, part):
@@ -660,7 +789,7 @@
         back_out[1, half] = grad[half].astype(BF16)
         to_owner(4, half, back_out.at[1, half], grad_in)
 
-    pl.semaphore_wait(barrier, 10)
+    pl.semaphore_wait(barrier, 13)
     for half in range(2):
         to_team(0, half, half_of(tokens, half), tok_in)
     for half in range(2):
@@ -687,75 +816,83 @@
         weight_copies[0, number].wait()
     attend(0, 0)
     attend(0, 1)
+    hidden_start(0, 0)
     weight_copies[1, 0].wait()
     halves(functools.partial(feed, 0), functools.partial(project, 1))
     for number in range(1, 4):
         weight_copies[1, number].wait()
     attend(1, 0)
     attend(1, 1)
+    hidden_pass(0, 0)
+    hidden_start(1, 0)
     halves(functools.partial(feed, 1), finish)
+    hidden_start(0, 1)
+    hidden_start(1, 1)
+    hidden_pass(1, 0)
 
     halves(functools.partial(turn_round, 1))
     down_grads(1)
-    core_start(1, DOWN)
-    halves(functools.partial(feed_back, 1), backward=True)
+    feed_back(1, 1)
+    hidden_pass(0, 1)
+    hidden_pass(1, 1)
+    feed_back(1, 0)
     core_done(1, DOWN)
     up_grads(1)
-    core_start(1, UP)
     attend_back(1, 1)
+    first_y(1, DOWN)
     core_done(1, UP)
     attend_back(1, 0)
-
-    def once(half):
-        @pl.when(half == 1)
-        def _():
-            first_done(1, DOWN)
-
-    halves(functools.partial(project_back, 1), functools.partial(feed_back, 0), once, backward=True)
-    up_grads(0)
-    core_start(0, UP)
+    first_z(1, DOWN)
+    first_y(1, UP)
+    heads_grads(1)
+    project_back(1, 1)
+    feed_back(0, 1)
+    second_y(1, DOWN)
+    first_x(1, DOWN)
+    second_y(1, UP)
+    project_back(1, 0)
+    feed_back(0, 0)
     small_start()
-    first_done(1, UP)
-    second_done(1, DOWN)
     attend_back(0, 1)
-    core_done(0, UP)
-    late_grads(1)
-    core_start(1, LATE)
-    down_grads(0)
-    core_start(0, DOWN)
+    second_x(1, DOWN)
+    first_z(1, UP)
+    first_x(1, UP)
     small_next(0)
     attend_back(0, 0)
-    core_done(1, LATE)
+    heads_second(1)
+    up_grads(0)
+    heads_grads(0)
+    small_next(1)
+    project_back(0, 1)
+    hand_back(1)
+    down_grads(0)
+    core_done(0, UP)
+    heads_second(0)
     core_done(0, DOWN)
-    small_next(1)
-    second_done(1, UP)
-    z_done(1, DOWN)
-
-    def twice(half):
-        @pl.when(half == 1)
-        def _():
-            first_done(0, UP)
-            first_done(1, LATE)
-
-    halves(functools.partial(project_back, 0), hand_back, twice, backward=True)
-    late_grads(0)
-    core_start(0, LATE)
+    second_x(1, UP)
+    first_y(0, UP)
     small_next(2)
-    first_done(0, DOWN)
-    z_done(1, UP)
-    second_done(0, UP)
-    second_done(1, LATE)
-    core_done(0, LATE)
-    final_pass(1, UP)
+    project_back(0, 0)
+    hand_back(0)
+    second_z(1, DOWN)
+    first_z(0, UP)
+    first_x(0, UP)
+    heads_third(1)
+    second_z(1, UP)
+    second_y(0, UP)
+    first_y(0, DOWN)
+    third_done(1, DOWN)
+    first_z(0, DOWN)
+    second_z(0, DOWN)
+    second_z(0, UP)
+    first_x(0, DOWN)
+    small_done()
+    second_x(0, UP)
+    second_y(0, DOWN)
+    heads_third(0)
+    third_done(1, UP)
     final_pass(1, DOWN)
-    small_done()
-    second_done(0, DOWN)
-    first_done(0, LATE)
-    z_done(0, UP)
-    z_done(1, LATE)
-    second_done(0, LATE)
-    final_done(1, UP)
-    final_done(1, DOWN)
+    second_x(0, DOWN)
     results = []
     for half in range(2):
         rows = pl.ds(HALF * half, HALF)
@@ -765,16 +902,17 @@
         results.append(pltpu.make_async_copy(grad_in.at[half], input_grad_hbm.at[rows], out_sem.at[3, half]))
     for copy in results:
         copy.start()
-    z_done(0, DOWN)
-    final_pass(1, LATE)
+    third_done(0, UP)
+    third_done(0, DOWN)
     final_pass(0, UP)
-    z_done(0, LATE)
+    heads_done(1)
+    final_done(1, DOWN)
+    final_pass(1, UP)
+    final_done(1, UP)
+    heads_done(0)
     final_pass(0, DOWN)
-    final_done(1, LATE)
     final_done(0, UP)
-    final_pass(0, LATE)
     final_done(0, DOWN)
-    final_done(0, LATE)
 
     for half in range(2):
         left(2, 0, half, head_out)
@@ -787,20 +925,22 @@
     for copy in results:
         copy.wait()
     for layer in range(LAYERS):
-        for part in (UP, DOWN, LATE):
+        for part in (UP, DOWN):
             final_out(layer, part).wait()
+        heads_copy_out(layer).wait()
 
 
 def results_kernel(
-    final_hbm, out_hbm, grad_hbm, small,
+    final_hbm, heads_hbm, out_hbm, grad_hbm, small,
     output, input_grad, qkv_grad, out_grad, up_grad, up_bias_grad, down_grad, down_bias_grad, alpha_grad,
-    final, grad_block, out_block, sem,
+    final, heads, grad_block, out_block, sem,
 ):
     moves = [
         pltpu.make_async_copy(final_hbm.at[1], final.at[1], sem.at[0]),
         pltpu.make_async_copy(final_hbm.at[0], final.at[0], sem.at[1]),
         pltpu.make_async_copy(grad_hbm, grad_block, sem.at[2]),
         pltpu.make_async_copy(out_hbm, out_block, sem.at[3]),
+        pltpu.make_async_copy(heads_hbm, heads, sem.at[4]),
     ]
     for move in moves:
         move.start()
@@ -817,12 +957,19 @@
             def columns(step):
                 return slice(WIDTH * step + 128 * quarter, WIDTH * step + 128 * quarter + 128)
 
-            for step in range(3):
-                qkv_grad[layer, :, columns(step)] = block(DIM * step, DIM)
-            out_grad[layer, :, columns(0)] = block(192, DIM)
             for step in range(4):
-                up_grad[layer, :, columns(step)] = block(UP + DIM * step, DIM)
-            down_grad[layer, :, columns(0)] = block(DOWN, PART)
+                up_grad[layer, :, columns(step)] = block(DIM * step, DIM)
+            out_grad[layer, :, columns(0)] = block(256, DIM)
+            down_grad[layer, :, columns(0)] = block(320, 256)
+    moves[4].wait()
+    for layer in range(LAYERS):
+        for side in range(2):
+            for member in range(TEAM):
+                for step in range(3):
+                    at = WIDTH * step + 128 * member
+                    qkv_grad[layer, 32 * side : 32 * side + 32, at : at + 128] = heads[
+                        layer, side, member, :, 128 * step : 128 * step + 128
+                    ].astype(F32)
     moves[2].wait()
     input_grad[...] = grad_block[...].astype(F32)
     moves[3].wait()
@@ -845,16 +992,17 @@
         return pltpu.VMEM(dims, F32)
 
     dma = pltpu.SemaphoreType.DMA
-    final, out_block, grad_block, small = pl.pallas_call(
+    final, heads, out_block, grad_block, small = pl.pallas_call(
         layers_kernel,
         out_shape=(
             shape((LAYERS, 4, CHUNK, 128), BF16),
+            shape((LAYERS, 2, TEAM, DIM // 2, 3 * 128), BF16),
             shape((2 * HALF, WIDTH), BF16),
             shape((2 * HALF, WIDTH), BF16),
             shape((LAYERS, WIDTH), F32),
         ),
         in_specs=[whole, scalar, scalar, whole, whole, whole, far, far, far, far],
-        out_specs=(far, far, far, whole),
+        out_specs=(far, far, far, far, whole),
         scratch_shapes=[
             vmem(LAYERS, WIDTH, 3 * WIDTH),
             vmem(LAYERS, WIDTH, WIDTH),
@@ -869,7 +1017,7 @@
             vmem(2, HALF, WIDTH),
             wide(2, HALF, WIDTH),
             wide(2, HALF, WIDTH),
-            vmem(LAYERS, WIDTH, 2 * HALF),
+            vmem(LAYERS, WIDTH, rows),
             vmem(LAYERS, WIDTH, 2 * HALF),
             vmem(LAYERS, WIDTH, 2 * HALF),
             vmem(LAYERS, FF, 2 * HALF),
@@ -878,8 +1026,8 @@
             wide(LAYERS, 2, HALF, WIDTH),
             vmem(2 * HALF, WIDTH),
             vmem(2 * HALF, FF),
-            vmem(LAYERS, 2 * HALF, WIDTH),
-            vmem(2 * HALF, 3 * WIDTH),
+            vmem(2 * HALF, WIDTH),
+            vmem(HALF, 3 * WIDTH),
             vmem(2, TEAM, OWN, PACK, 128),
             vmem(2, TEAM, OWN, DIM, 128),
             vmem(2, TEAM, OWN, PACK, 128),
@@ -896,13 +1044,20 @@
             wide(rows, TILE),
             vmem(LAYERS, 4, 4, 2, CHUNK, 128),
             vmem(2, 4, 2, CHUNK, 128),
-            vmem(4, 2, CHUNK, 128),
-            vmem(2, 4, CHUNK, 128),
+            vmem(4, 2, TOTALS[0], 128),
+            vmem(4, TOTALS[1], 128),
+            vmem(4, TOTALS[0], 128),
+            vmem(2, 4, TOTALS[1], 128),
             vmem(LAYERS, 4, CHUNK, 128),
-            vmem(LAYERS, 3, 2, 4, 2, THIRD, 128),
-            vmem(LAYERS, 3, 2, THIRD, 128),
-            vmem(LAYERS, 3, THIRD, 128),
+            vmem(2, 4, 2, TOTALS[2], 128),
+            vmem(2, TOTALS[2], 128),
+            vmem(TOTALS[2], 128),
             vmem(LAYERS, 4, CHUNK, 128),
+            vmem(LAYERS, 4, 2, DIM, 3 * 128),
+            vmem(LAYERS, 4, 2, DIM // 2, 3 * 128),
+            vmem(LAYERS, 4, 2, DIM // 2, 3 * 128),
+            vmem(LAYERS, 2, DIM // 2, 3 * 128),
+            vmem(LAYERS, 2, TEAM, DIM // 2, 3 * 128),
             wide(2, LAYERS, SMALL),
             wide(3, LAYERS, SMALL),
             wide(4, LAYERS, SMALL),
@@ -910,30 +1065,32 @@
             dma((LAYERS, 4)),
             dma((5, 2)),
             dma((5, 2)),
-            dma((4, LAYERS, 2)),
-            dma((4, LAYERS, 2)),
-            dma((LAYERS, 3, 2)),
-            dma((LAYERS, 3, 2)),
-            dma((LAYERS, 3, 2)),
-            dma((LAYERS, 3, 2)),
-            dma((LAYERS, 3, 2, 2)),
-            dma((LAYERS, 3, 2, 2)),
-            dma((LAYERS, 3, 2, 4)),
-            dma((LAYERS, 3, 2, 4)),
-            dma((LAYERS, 3, 2, 4)),
-            dma((LAYERS, 3, 2, 4)),
-            dma((LAYERS, 3)),
-            dma((LAYERS, 3)),
-            dma((LAYERS, 3)),
-            dma((LAYERS, 3)),
-            dma((LAYERS, 3, 3)),
-            dma((LAYERS, 3, 3)),
+            dma((4, LAYERS, 2, OWN)),
+            dma((4, LAYERS, 2, OWN)),
+            dma((LAYERS, 2, 2)),
+            dma((LAYERS, 2, 2)),
+            dma((LAYERS, 2, 3)),
+            dma((LAYERS, 2, 3)),
+            dma((LAYERS, 2, 4)),
+            dma((LAYERS, 2, 4)),
+            dma((LAYERS, 2, 2, 4)),
+            dma((LAYERS, 2, 2, 4)),
+            dma((LAYERS, 2, 2, 4)),
+            dma((LAYERS, 2, 2, 4)),
+            dma((LAYERS, 2, 3)),
+            dma((LAYERS, 2, 3)),
+            dma((LAYERS, 2, 3)),
+            dma((LAYERS, 2, 3)),
+            dma((LAYERS,)),
+            dma((LAYERS,)),
+            dma((LAYERS, 4)),
+            dma((LAYERS, 4)),
+            dma((LAYERS, 8)),
+            dma((LAYERS, 8)),
             dma((6,)),
             dma((6,)),
-            dma((4, 3)),
-            pltpu.SemaphoreType.REGULAR((3,)),
-            pltpu.SemaphoreType.REGULAR((3, 2)),
-            pltpu.SemaphoreType.REGULAR((3, 2)),
+            dma((4, 4)),
+            pltpu.SemaphoreType.REGULAR((2,)),
         ],
         compiler_params=pltpu.CompilerParams(
             collective_id=0, has_side_effects=True, vmem_limit_bytes=63 * 1024 * 1024
@@ -957,14 +1114,18 @@
                 shape((LAYERS, DIM), F32),
                 shape((LAYERS, 2), F32),
             ),
-            in_specs=[far, far, far, whole],
+            in_specs=[far, far, far, far, whole],
             out_specs=(whole,) * 9,
             scratch_shapes=[
-                vmem(LAYERS, 4, CHUNK, 128), vmem(2 * HALF, WIDTH), vmem(2 * HALF, WIDTH), dma((4,))
+                vmem(LAYERS, 4, CHUNK, 128),
+                vmem(LAYERS, 2, TEAM, DIM // 2, 3 * 128),
+                vmem(2 * HALF, WIDTH),
+                vmem(2 * HALF, WIDTH),
+                dma((6,)),
             ],
             compiler_params=pltpu.CompilerParams(vmem_limit_bytes=60 * 1024 * 1024),
             name="results",
-        )(final, out_block, grad_block, small)
+        )(final, heads, out_block, grad_block, small)
     )
 
 

time: 146 us -> 132 us (0.904)
  Pallas kernels: 144 us -> 131 us
    pallas_call x1, Pallas kernels: 140 us -> 126 us  [fast_body(): pl.pallas_call(layers_kernel, out_shape=(shape((LAYERS, 4, CHUNK, 128), B...]
where the time goes in v6:
time: 132 us; the launch traced here: 131 us
  Pallas kernels  131 us (99%)
    pallas_call x1, Pallas kernels, fast_body(): pl.pallas_call(layers_kernel, out_shape=(shape((LAYERS, 4, CHUNK, 128), B...  126 us
    pallas_call x1, Pallas kernels, fast_body(): pl.pallas_call(results_kernel, out_shape=(shape((2 * HALF, WIDTH), BF16),...  4.27 us

profile of v6, /device:TPU:0, one launch (start us, length us, event | category | flops | bytes accessed | tf_op | source)
XLA Modules:
  0.0 131.5 jit_solution(7733706979743203254)
XLA Ops:
  0.6 126.4 %layers.1 = (bf16[2,4,576,128]{3,2,1,0:T(8,128)(2,1)}, bf16[2,2,4,32,384]{4,3,2,1,0:T(8,128)(2,1)}, bf16[256,512]{1,0:T(8,128)(2,1)}, bf16[256,512]{1,0:T(8,128)(2,1)}, f32[2,512]{1,0:T(2,128)}) custom-call(bf16[256,512]{1,0:T(8,128)(2,1)} %tokens.1, s32[1,4]{1,0:T(1,128)} %seq_len.1, f32[2,2]{1,0:T(2,128)} %alphas.1, f32[2,2048]{1,0:T(2,128)} %up_bias.1, ...), custom_call_target="tpu_custom_call" | custom-call | tf_op jit(solution)/shard_map/layers/pallas_call | solution.py:995
  127.0 4.3 %results.1 = (bf16[256,512]{1,0:T(8,128)(2,1)}, f32[256,512]{1,0:T(8,128)}, f32[2,64,1536]{2,1,0:T(8,128)}, f32[2,64,512]{2,1,0:T(8,128)}, f32[2,64,2048]{2,1,0:...) custom-call(bf16[2,4,576,128]{3,2,1,0:T(8,128)(2,1)} %get-tuple-element.14.final_hbm, ...), custom_call_target="tpu_custom_call" | custom-call | tf_op jit(solution)/shard_map/results/pallas_call | solution.py:1104

commit v7 on v6

--- a/solution.py
+++ b/solution.py
@@ -29,7 +29,7 @@
 SMALL = FF + WIDTH + 128
 UP, DOWN = 0, 1
 PARTS = ((0, 320), (320, 256))
-SHARES = {(1, UP): (176, 0, 144), (1, DOWN): (144, 32, 80), (0, UP): (112, 160, 48), (0, DOWN): (112, 144, 0)}
+SHARES = {(1, UP): (192, 0, 128), (1, DOWN): (160, 16, 80), (0, UP): (160, 112, 48), (0, DOWN): (128, 96, 32)}
 
 
 def spans():
@@ -187,7 +187,7 @@
         move_left(kind, chunk, source, lax.rem(zz, 2), core + 2 * chunk)
 
     def half_of(ref, half):
-        return ref.at[pl.ds(HALF * half, HALF)]
+        return ref.at[pl.ds(pl.multiple_of(HALF * half, HALF), HALF)]
 
     def rows_of(half):
         return pl.ds(pl.multiple_of(half * HALF, HALF), HALF)
@@ -245,7 +245,7 @@
 
     def project(layer, half):
         rows = rows_of(half)
-        rounded = hidden[half].astype(BF16)
+        rounded = hidden[rows, :].astype(BF16)
         hid_all[layer, :, tokens_of(half, member)] = rounded.T
         if layer == 1:
             left(0, 0, half, pack_out)
@@ -310,8 +310,8 @@
             attn_t[layer, DIM * head : DIM * head + DIM, rows] = o_in[half, slot_of(head // 2), head % 2]
         attn = attn_t[layer, :, rows].T
         grown = nn(attn, wout[layer])
-        branch[layer, half] = grown
-        middle = hidden[half] + alphas[layer, 0] * grown
+        branch[layer, rows, :] = grown
+        middle = hidden[rows, :] + alphas[layer, 0] * grown
         entered = middle.astype(BF16)
         ent_t[layer, :, rows] = entered.T
         total = jnp.zeros((HALF, WIDTH), F32)
@@ -325,46 +325,48 @@
                 tail = tail * near + factor
             tail = bell * (tail * near)
             risen = jnp.where(gate > 0.0, 1.0 - tail, tail)
-            slope[layer, half, :, cut] = risen + gate * bell * 0.3989422804014327
+            slope[layer, rows, cut] = risen + gate * bell * 0.3989422804014327
             active = (gate * risen).astype(BF16)
             act_t[layer, cut, rows] = active.T
             total = total + nn(active, wdown[layer, cut, :])
         total = total + down_bias[layer : layer + 1, :]
-        second[layer, half] = total
-        hidden[half] = middle + alphas[layer, 1] * total
+        second[layer, rows, :] = total
+        hidden[rows, :] = middle + alphas[layer, 1] * total
 
     def total_of(values):
         return jnp.sum(jnp.sum(values, axis=0, keepdims=True), axis=1, keepdims=True)
 
-    def feed_back(layer, half):
-        rows = rows_of(half)
-        start = grad[half]
+    def feed_back(layer):
+        start = grad[...]
         if layer == 0:
-            dz[rows, :] = (alphas[layer, 1] * start).astype(BF16)
-        scaled = dz[rows, :]
-        alpha_second = total_of(start * second[layer, half])
-        small[half, layer : layer + 1, FF : FF + WIDTH] = jnp.sum(scaled.astype(F32), axis=0, keepdims=True)
+            dz[...] = (alphas[layer, 1] * start).astype(BF16)
+        scaled = dz[...]
+        alpha_second = total_of(start * second[layer])
+        small[layer : layer + 1, FF : FF + WIDTH] = jnp.sum(scaled.astype(F32), axis=0, keepdims=True)
         middle = start
         for step in range(FF // CUT):
             cut = slice(CUT * step, CUT * step + CUT)
-            gate = (nt(scaled, wdown[layer, cut, :]) * slope[layer, half, :, cut]).astype(BF16)
-            du[rows, cut] = gate
-            small[half, layer : layer + 1, cut] = jnp.sum(gate.astype(F32), axis=0, keepdims=True)
+            gate = (nt(scaled, wdown[layer, cut, :]) * slope[layer, :, cut]).astype(BF16)
+            du[:, cut] = gate
+            small[layer : layer + 1, cut] = jnp.sum(gate.astype(F32), axis=0, keepdims=True)
             middle = middle + nt(gate, wup[layer, :, cut])
-        grad[half] = middle
-        alpha_first = total_of(middle * branch[layer, half])
+        grad[...] = middle
+        mixed = (alphas[layer, 0] * middle).astype(BF16)
+        da[...] = mixed
+        spread = nt(wout[layer], mixed).astype(BF16)
+        for chunk in (1, 0):
+            left(*((1, 1) if layer == 1 else (2, 1)), chunk, head_out)
+            for head in range(RUNS):
+                head_out[chunk, head // 2, head % 2] = spread[
+                    DIM * head : DIM * head + DIM, HALF * chunk : HALF * chunk + HALF
+                ]
+            for head in range(OWN):
+                exchange(2, layer, chunk, head, head_out, do_in)
+        alpha_first = total_of(middle * branch[layer])
         column = lax.broadcasted_iota(jnp.int32, (1, 128), 1)
-        small[half, layer : layer + 1, FF + WIDTH :] = jnp.where(
+        small[layer : layer + 1, FF + WIDTH :] = jnp.where(
             column == 0, alpha_first, jnp.where(column == 1, alpha_second, 0.0)
         )
-        mixed = (alphas[layer, 0] * middle).astype(BF16)
-        da[rows, :] = mixed
-        spread = nt(wout[layer], mixed).astype(BF16)
-        left(*((1, 1) if layer == 1 else (2, 1)), half, head_out)
-        for head in range(RUNS):
-            head_out[half, head // 2, head % 2] = spread[DIM * head : DIM * head + DIM, :]
-        for head in range(OWN):
-            exchange(2, layer, half, head, head_out, do_in)
 
     def attend_back(layer, chunk):
         left(*((0, 1) if layer == 1 else (3, 1)), chunk, pack_out)
@@ -423,7 +425,8 @@
             v_pair = jnp.where(low, pltpu.roll(first, DIM, 1), other)
             dqkv[:, WIDTH + 128 * pair : WIDTH + 128 * pair + 128] = k_pair.astype(BF16)
             dqkv[:, 2 * WIDTH + 128 * pair : 2 * WIDTH + 128 * pair + 128] = v_pair.astype(BF16)
-        grad[half] = grad[half] + nt(dqkv[...], wqkv[layer])
+        rows = rows_of(half)
+        grad[rows, :] = grad[rows, :] + nt(dqkv[...], wqkv[layer])
 
     def scatter_rows(layer, result, first_row):
         for run in range(RUNS):
@@ -741,7 +744,7 @@
         )
 
     def small_start():
-        small_sum[0] = small[0] + small[1]
+        small_sum[0] = small[...]
         small_copy(0).start()
 
     def small_next(stage):
@@ -764,40 +767,42 @@
         small_final[:, 256:384] = jnp.where(yy == 1, pltpu.roll(pair, DIM, 1), pair)
         small_final[:, 384:512] = small_sum[0, :, FF + WIDTH :]
 
-    def halves(*phases, backward=False):
+    def halves(*phases, first=0):
         def both(step, carry):
             for phase in phases:
-                phase(1 - step if backward else step)
+                phase(lax.rem(step + first, 2))
             return carry
 
         lax.fori_loop(0, 2, both, 0)
 
     def begin(half):
         move_arrived(0, half, tok_in)
-        hidden[half] = tok_in[half].astype(F32)
+        hidden[rows_of(half), :] = tok_in[half].astype(F32)
 
     def finish(half):
-        back_out[0, half] = hidden[half].astype(BF16)
+        back_out[0, half] = hidden[rows_of(half), :].astype(BF16)
         to_owner(3, half, back_out.at[0, half], out_in)
 
     def turn_round(layer, half):
         move_arrived(2, half, cot_in)
-        grad[half] = cot_in[half].astype(F32)
-        dz[rows_of(half), :] = (alphas[layer, 1] * grad[half]).astype(BF16)
+        rows = rows_of(half)
+        grad[rows, :] = cot_in[half].astype(F32)
+        dz[rows, :] = (alphas[layer, 1] * grad[rows, :]).astype(BF16)
 
     def hand_back(half):
-        back_out[1, half] = grad[half].astype(BF16)
+        back_out[1, half] = grad[rows_of(half), :].astype(BF16)
         to_owner(4, half, back_out.at[1, half], grad_in)
 
     pl.semaphore_wait(barrier, 13)
-    for half in range(2):
+    upper = lax.div(zz, 2)
+    for half in (1 - upper, upper):
         to_team(0, half, half_of(tokens, half), tok_in)
-    for half in range(2):
+    for half in (1 - upper, upper):
         to_team(1, half, flag_out, flag_in)
-    for half in range(2):
+    weight_copies[0, 0].wait()
+    halves(begin, functools.partial(project, 0), first=upper)
+    for half in (1 - upper, upper):
         to_team(2, half, half_of(cotangent, half), cot_in)
-    weight_copies[0, 0].wait()
-    halves(begin, functools.partial(project, 0))
 
     move_arrived(1, 0, flag_in)
     move_arrived(1, 1, flag_in)
@@ -832,67 +837,71 @@
 
     halves(functools.partial(turn_round, 1))
     down_grads(1)
-    feed_back(1, 1)
+    feed_back(1)
     hidden_pass(0, 1)
     hidden_pass(1, 1)
-    feed_back(1, 0)
     core_done(1, DOWN)
     up_grads(1)
     attend_back(1, 1)
     first_y(1, DOWN)
     core_done(1, UP)
     attend_back(1, 0)
+    second_y(1, DOWN)
+    first_y(1, UP)
+    first_x(1, DOWN)
+    project_back(1, 1)
+    heads_grads(1)
     first_z(1, DOWN)
-    first_y(1, UP)
-    heads_grads(1)
-    project_back(1, 1)
-    feed_back(0, 1)
-    second_y(1, DOWN)
-    first_x(1, DOWN)
+    project_back(1, 0)
+    feed_back(0)
+    small_start()
+    second_x(1, DOWN)
     second_y(1, UP)
-    project_back(1, 0)
-    feed_back(0, 0)
-    small_start()
+    up_grads(0)
+    first_x(1, UP)
+    heads_second(1)
+    first_z(1, UP)
     attend_back(0, 1)
-    second_x(1, DOWN)
-    first_z(1, UP)
-    first_x(1, UP)
     small_next(0)
+    core_done(0, UP)
+    second_x(1, UP)
+    down_grads(0)
     attend_back(0, 0)
-    heads_second(1)
-    up_grads(0)
-    heads_grads(0)
     small_next(1)
     project_back(0, 1)
     hand_back(1)
-    down_grads(0)
-    core_done(0, UP)
+    first_z(0, UP)
+    heads_grads(0)
+    small_next(2)
+    first_x(0, UP)
+    core_done(0, DOWN)
+    first_y(0, UP)
     heads_second(0)
-    core_done(0, DOWN)
-    second_x(1, UP)
-    first_y(0, UP)
-    small_next(2)
+    small_done()
+    first_z(0, DOWN)
+    second_x(0, UP)
+    first_x(0, DOWN)
+    second_z(0, UP)
+    second_z(1, UP)
+    heads_third(1)
+    second_z(1, DOWN)
+    first_y(0, DOWN)
+    heads_third(0)
+    second_y(0, UP)
+    second_x(0, DOWN)
+    second_z(0, DOWN)
+    third_done(1, UP)
+    third_done(0, UP)
+    second_y(0, DOWN)
     project_back(0, 0)
     hand_back(0)
-    second_z(1, DOWN)
-    first_z(0, UP)
-    first_x(0, UP)
-    heads_third(1)
-    second_z(1, UP)
-    second_y(0, UP)
-    first_y(0, DOWN)
+    heads_done(1)
     third_done(1, DOWN)
-    first_z(0, DOWN)
-    second_z(0, DOWN)
-    second_z(0, UP)
-    first_x(0, DOWN)
-    small_done()
-    second_x(0, UP)
-    second_y(0, DOWN)
-    heads_third(0)
-    third_done(1, UP)
+    third_done(0, DOWN)
+    final_pass(1, UP)
+    final_pass(0, UP)
     final_pass(1, DOWN)
-    second_x(0, DOWN)
+    final_pass(0, DOWN)
     results = []
     for half in range(2):
         rows = pl.ds(HALF * half, HALF)
@@ -902,16 +911,10 @@
         results.append(pltpu.make_async_copy(grad_in.at[half], input_grad_hbm.at[rows], out_sem.at[3, half]))
     for copy in results:
         copy.start()
-    third_done(0, UP)
-    third_done(0, DOWN)
-    final_pass(0, UP)
-    heads_done(1)
+    final_done(0, UP)
     final_done(1, DOWN)
-    final_pass(1, UP)
+    heads_done(0)
     final_done(1, UP)
-    heads_done(0)
-    final_pass(0, DOWN)
-    final_done(0, UP)
     final_done(0, DOWN)
 
     for half in range(2):
@@ -933,22 +936,29 @@
 def results_kernel(
     final_hbm, heads_hbm, out_hbm, grad_hbm, small,
     output, input_grad, qkv_grad, out_grad, up_grad, up_bias_grad, down_grad, down_bias_grad, alpha_grad,
-    final, heads, grad_block, out_block, sem,
+    final, heads, grad_block, out_block, grad_wide, qkv_wide, out_wide, up_wide, down_wide, sem, out_sem,
 ):
-    moves = [
-        pltpu.make_async_copy(final_hbm.at[1], final.at[1], sem.at[0]),
-        pltpu.make_async_copy(final_hbm.at[0], final.at[0], sem.at[1]),
-        pltpu.make_async_copy(grad_hbm, grad_block, sem.at[2]),
-        pltpu.make_async_copy(out_hbm, out_block, sem.at[3]),
-        pltpu.make_async_copy(heads_hbm, heads, sem.at[4]),
-    ]
-    for move in moves:
+    order = [(layer, part) for layer in (1, 0) for part in (UP, DOWN)]
+    pieces = []
+    for number, (layer, part) in enumerate(order):
+        rows = pl.ds(*PARTS[part])
+        pieces.append(pltpu.make_async_copy(final_hbm.at[layer, :, rows], final.at[layer, :, rows], sem.at[number]))
+    grad_move = pltpu.make_async_copy(grad_hbm, grad_block, sem.at[4])
+    out_move = pltpu.make_async_copy(out_hbm, out_block, sem.at[5])
+    heads_move = pltpu.make_async_copy(heads_hbm, heads, sem.at[6])
+    for move in (*pieces, grad_move, heads_move, out_move):
         move.start()
+    ends = []
+
+    def write(source, target):
+        ends.append(pltpu.make_async_copy(source, target, out_sem.at[len(ends)]))
+        ends[-1].start()
+
     up_bias_grad[...] = small[:, 0:256]
     down_bias_grad[...] = small[:, 256 : 256 + DIM]
     alpha_grad[...] = small[:, 384:386]
-    for layer in (1, 0):
-        moves[1 - layer].wait()
+    for (layer, part), piece in zip(order, pieces):
+        piece.wait()
         for quarter in range(4):
 
             def block(first, count):
@@ -957,23 +967,34 @@
             def columns(step):
                 return slice(WIDTH * step + 128 * quarter, WIDTH * step + 128 * quarter + 128)
 
-            for step in range(4):
-                up_grad[layer, :, columns(step)] = block(DIM * step, DIM)
-            out_grad[layer, :, columns(0)] = block(256, DIM)
-            down_grad[layer, :, columns(0)] = block(320, 256)
-    moves[4].wait()
+            if part == UP:
+                for step in range(4):
+                    up_wide[layer, :, columns(step)] = block(DIM * step, DIM)
+                out_wide[layer, :, columns(0)] = block(256, DIM)
+            else:
+                down_wide[layer, :, columns(0)] = block(320, 256)
+        if part == UP:
+            write(up_wide.at[layer], up_grad.at[layer])
+            write(out_wide.at[layer], out_grad.at[layer])
+        else:
+            write(down_wide.at[layer], down_grad.at[layer])
+    grad_move.wait()
+    grad_wide[...] = grad_block[...].astype(F32)
+    write(grad_wide, input_grad)
+    heads_move.wait()
     for layer in range(LAYERS):
         for side in range(2):
             for member in range(TEAM):
                 for step in range(3):
                     at = WIDTH * step + 128 * member
-                    qkv_grad[layer, 32 * side : 32 * side + 32, at : at + 128] = heads[
+                    qkv_wide[layer, 32 * side : 32 * side + 32, at : at + 128] = heads[
                         layer, side, member, :, 128 * step : 128 * step + 128
                     ].astype(F32)
-    moves[2].wait()
-    input_grad[...] = grad_block[...].astype(F32)
-    moves[3].wait()
-    output[...] = out_block[...]
+        write(qkv_wide.at[layer], qkv_grad.at[layer])
+    out_move.wait()
+    write(out_block, output)
+    for end in ends:
+        end.wait()
 
 
 def fast_body(
@@ -1001,7 +1022,7 @@
             shape((2 * HALF, WIDTH), BF16),
             shape((LAYERS, WIDTH), F32),
         ),
-        in_specs=[whole, scalar, scalar, whole, whole, whole, far, far, far, far],
+        in_specs=[far, scalar, scalar, whole, whole, far, far, far, far, far],
         out_specs=(far, far, far, far, whole),
         scratch_shapes=[
             vmem(LAYERS, WIDTH, 3 * WIDTH),
@@ -1015,15 +1036,15 @@
             vmem(2, 2, HALF, WIDTH),
             vmem(2, HALF, WIDTH),
             vmem(2, HALF, WIDTH),
-            wide(2, HALF, WIDTH),
-            wide(2, HALF, WIDTH),
+            wide(2 * HALF, WIDTH),
+            wide(2 * HALF, WIDTH),
             vmem(LAYERS, WIDTH, rows),
             vmem(LAYERS, WIDTH, 2 * HALF),
             vmem(LAYERS, WIDTH, 2 * HALF),
             vmem(LAYERS, FF, 2 * HALF),
-            wide(LAYERS, 2, HALF, WIDTH),
-            wide(LAYERS, 2, HALF, FF),
-            wide(LAYERS, 2, HALF, WIDTH),
+            wide(LAYERS, 2 * HALF, WIDTH),
+            wide(LAYERS, 2 * HALF, FF),
+            wide(LAYERS, 2 * HALF, WIDTH),
             vmem(2 * HALF, WIDTH),
             vmem(2 * HALF, FF),
             vmem(2 * HALF, WIDTH),
@@ -1058,7 +1079,7 @@
             vmem(LAYERS, 4, 2, DIM // 2, 3 * 128),
             vmem(LAYERS, 2, DIM // 2, 3 * 128),
             vmem(LAYERS, 2, TEAM, DIM // 2, 3 * 128),
-            wide(2, LAYERS, SMALL),
+            wide(LAYERS, SMALL),
             wide(3, LAYERS, SMALL),
             wide(4, LAYERS, SMALL),
             wide(3, LAYERS, SMALL),
@@ -1115,13 +1136,19 @@
                 shape((LAYERS, 2), F32),
             ),
             in_specs=[far, far, far, far, whole],
-            out_specs=(whole,) * 9,
+            out_specs=(far, far, far, far, far, whole, far, whole, whole),
             scratch_shapes=[
                 vmem(LAYERS, 4, CHUNK, 128),
                 vmem(LAYERS, 2, TEAM, DIM // 2, 3 * 128),
                 vmem(2 * HALF, WIDTH),
                 vmem(2 * HALF, WIDTH),
-                dma((6,)),
+                wide(2 * HALF, WIDTH),
+                wide(LAYERS, DIM, 3 * WIDTH),
+                wide(LAYERS, DIM, WIDTH),
+                wide(LAYERS, DIM, FF),
+                wide(LAYERS, FF // RUNS, WIDTH),
+                dma((7,)),
+                dma((10,)),
             ],
             compiler_params=pltpu.CompilerParams(vmem_limit_bytes=60 * 1024 * 1024),
             name="results",

time: 132 us -> 132 us (level)
  no operation moved by 1% of the time
where the time goes in v7:
time: 132 us
  Pallas kernels  131 us (99%)
    pallas_call x1, Pallas kernels, fast_body(): pl.pallas_call(layers_kernel, out_shape=(shape((LAYERS, 4, CHUNK, 128), B...  127 us
    pallas_call x1, Pallas kernels, fast_body(): pl.pallas_call(results_kernel, out_shape=(shape((2 * HALF, WIDTH), BF16),...  4.35 us

profile of v7, /device:TPU:0, one launch (start us, length us, event | category | flops | bytes accessed | tf_op | source)
XLA Modules:
  0.0 132.0 jit_solution(11123373271965375336)
XLA Ops:
  0.6 126.9 %layers.1 = (bf16[2,4,576,128]{3,2,1,0:T(8,128)(2,1)}, bf16[2,2,4,32,384]{4,3,2,1,0:T(8,128)(2,1)}, bf16[256,512]{1,0:T(8,128)(2,1)}, bf16[256,512]{1,0:T(8,128)(2,1)}, f32[2,512]{1,0:T(2,128)}) custom-call(bf16[256,512]{1,0:T(8,128)(2,1)} %tokens.1, s32[1,4]{1,0:T(1,128)} %seq_len.1, f32[2,2]{1,0:T(2,128)} %alphas.1, f32[2,2048]{1,0:T(2,128)} %up_bias.1, ...), custom_call_target="tpu_custom_call" | custom-call | tf_op jit(solution)/shard_map/layers/pallas_call | solution.py:1016
  127.5 4.4 %results.1 = (bf16[256,512]{1,0:T(8,128)(2,1)}, f32[256,512]{1,0:T(8,128)}, f32[2,64,1536]{2,1,0:T(8,128)}, f32[2,64,512]{2,1,0:T(8,128)}, f32[2,64,2048]{2,1,0:...) custom-call(bf16[2,4,576,128]{3,2,1,0:T(8,128)(2,1)} %get-tuple-element.14.final_hbm, ...), custom_call_target="tpu_custom_call" | custom-call | tf_op jit(solution)/shard_map/results/pallas_call | solution.py:1125

commit v8 on v7

--- a/solution.py
+++ b/solution.py
@@ -66,18 +66,18 @@
 
 def layers_kernel(
     tokens, seq_len, alphas, up_bias, down_bias, cotangent, qkv_hbm, out_hbm, up_hbm, down_hbm,
-    final_hbm, heads_hbm, output_hbm, input_grad_hbm, small_final,
+    final, heads_all, out_in, grad_in, small_final,
     wqkv, wout, wup, wdown,
-    tok_in, cot_in, flag_out, flag_in, back_out, out_in, grad_in,
-    hidden, grad, hid_all, attn_t, ent_t, act_t, branch, slope, second,
+    tok_in, cot_in, flag_out, flag_in, back_out,
+    hidden, grad, hid_all, attn_t, entered, act, branch, slope, second,
     dz, du, da, dqkv,
     pack_out, head_out, pack_in, o_in, do_in,
     kv, kv_t, rq, ro, o_t, lse, acc, dq_t, bias,
-    parts, core_in, xa_in, xb_in, ya_in, yb_in, z_in, third_z, third_x, third_y, final,
-    heads_out, heads_x, heads_z, heads_sum, heads_all, small, small_in, small_z, small_sum,
+    parts, core_in, xa_in, xb_in, ya_in, yb_in, z_in, third_z, third_x, third_y,
+    heads_out, heads_x, heads_z, heads_sum, small, small_in, small_z, small_sum,
     w_sem, move_send, move_recv, a2a_send, a2a_recv, core_send, core_recv, x_send, x_recv, y_send, y_recv,
     z_send, z_recv, tz_send, tz_recv, fin_send, fin_recv, hid_send, hid_recv, hx_send, hx_recv, hz_send, hz_recv, hf_send, hf_recv,
-    small_send, small_recv, out_sem, core_free,
+    small_send, small_recv, core_free,
 ):
     grp = lax.axis_index("grp")
     blk = lax.axis_index("blk")
@@ -246,7 +246,6 @@
     def project(layer, half):
         rows = rows_of(half)
         rounded = hidden[rows, :].astype(BF16)
-        hid_all[layer, :, tokens_of(half, member)] = rounded.T
         if layer == 1:
             left(0, 0, half, pack_out)
         queries = nn(rounded, wqkv[layer, :, 0:WIDTH]) * (DIM ** -0.5)
@@ -264,6 +263,7 @@
             pack_out[half, head // 2, head % 2, HALF:, :] = queries_t[DIM * head : DIM * head + DIM, :]
         for head in range(OWN):
             exchange(0, layer, half, head, pack_out, pack_in)
+        hid_all[layer, :, tokens_of(half, member)] = rounded.T
 
     def attend(layer, chunk):
         if layer == 1:
@@ -279,11 +279,17 @@
                 kv[layer, head, span, :] = block
                 kv_t[layer, head, :, span] = block.T
                 rq[layer, head, 0:DIM, span] = pack_in[chunk, slot, head, HALF:, :]
+
+            def scores_of(i):
+                count = TILE * (i + 1)
+                tile = rq[layer, head, :, TILE * i : TILE * i + TILE]
+                return nn(kv[layer, head, 0:count, :], tile) + bias[TILE * TILES - count :, :]
+
+            ahead = [scores_of(i) for i in (2 * chunk, 2 * chunk + 1)]
             for i in (2 * chunk, 2 * chunk + 1):
                 columns = slice(TILE * i, TILE * i + TILE)
-                query_tile = rq[layer, head, :, columns]
                 count = TILE * (i + 1)
-                scores = nn(kv[layer, head, 0:count, :], query_tile) + bias[TILE * TILES - count :, :]
+                scores = ahead[i - 2 * chunk]
                 largest = jnp.max(scores, axis=0, keepdims=True)
                 weight = jnp.exp(scores - largest)
                 total = jnp.sum(weight, axis=0, keepdims=True)
@@ -312,12 +318,20 @@
         grown = nn(attn, wout[layer])
         branch[layer, rows, :] = grown
         middle = hidden[rows, :] + alphas[layer, 0] * grown
-        entered = middle.astype(BF16)
-        ent_t[layer, :, rows] = entered.T
+        rounded = middle.astype(BF16)
+        entered[layer, rows, :] = rounded
         total = jnp.zeros((HALF, WIDTH), F32)
+
+        def gate_of(step):
+            cut = slice(CUT * step, CUT * step + CUT)
+            return nn(rounded, wup[layer, :, cut]) + up_bias[layer : layer + 1, cut]
+
+        coming = gate_of(0)
         for step in range(FF // CUT):
             cut = slice(CUT * step, CUT * step + CUT)
-            gate = nn(entered, wup[layer, :, cut]) + up_bias[layer : layer + 1, cut]
+            gate = coming
+            if step + 1 < FF // CUT:
+                coming = gate_of(step + 1)
             bell = jnp.exp(gate * gate * -0.5)
             near = pl.reciprocal(1.0 + SLOPE_AT * jnp.abs(gate), approx=True)
             tail = jnp.full_like(gate, TAIL[5])
@@ -327,7 +341,7 @@
             risen = jnp.where(gate > 0.0, 1.0 - tail, tail)
             slope[layer, rows, cut] = risen + gate * bell * 0.3989422804014327
             active = (gate * risen).astype(BF16)
-            act_t[layer, cut, rows] = active.T
+            act[layer, rows, cut] = active
             total = total + nn(active, wdown[layer, cut, :])
         total = total + down_bias[layer : layer + 1, :]
         second[layer, rows, :] = total
@@ -344,9 +358,13 @@
         alpha_second = total_of(start * second[layer])
         small[layer : layer + 1, FF : FF + WIDTH] = jnp.sum(scaled.astype(F32), axis=0, keepdims=True)
         middle = start
+        coming = nt(scaled, wdown[layer, 0:CUT, :])
         for step in range(FF // CUT):
             cut = slice(CUT * step, CUT * step + CUT)
-            gate = (nt(scaled, wdown[layer, cut, :]) * slope[layer, :, cut]).astype(BF16)
+            raw = coming
+            if step + 1 < FF // CUT:
+                coming = nt(scaled, wdown[layer, CUT * (step + 1) : CUT * (step + 2), :])
+            gate = (raw * slope[layer, :, cut]).astype(BF16)
             du[:, cut] = gate
             small[layer : layer + 1, cut] = jnp.sum(gate.astype(F32), axis=0, keepdims=True)
             middle = middle + nt(gate, wup[layer, :, cut])
@@ -436,15 +454,16 @@
                 ].astype(BF16)
 
     def up_grads(layer):
+        turned = entered[layer].T
         for step in range(FF // CUT):
             cut = slice(CUT * step, CUT * step + CUT)
-            scatter_rows(layer, nn(ent_t[layer], du[:, cut]), DIM * step)
+            scatter_rows(layer, nn(turned, du[:, cut]), DIM * step)
         scatter_rows(layer, nn(attn_t[layer], da[...]), 256)
         core_start(layer, UP)
 
     def down_grads(layer):
         for run in range(RUNS):
-            result = nn(act_t[layer, TILE * run : TILE * run + TILE, :], dz[...])
+            result = nn(act[layer, :, TILE * run : TILE * run + TILE].T, dz[...])
             for quarter in range(4):
                 parts[layer, quarter, run // 2, run % 2, 320:576, :] = result[
                     :, 128 * quarter : 128 * quarter + 128
@@ -531,13 +550,9 @@
         for number in range(1, 8):
             heads_last_copy(layer, number).start()
 
-    def heads_copy_out(layer):
-        return pltpu.make_async_copy(heads_all.at[layer], heads_hbm.at[layer], out_sem.at[1, layer])
-
     def heads_done(layer):
         for number in range(1, 8):
             heads_last_copy(layer, number).wait()
-        heads_copy_out(layer).start()
 
     def chunk_rows(layer, part, route):
         first, _, count = SPANS[layer, part, route]
@@ -717,16 +732,9 @@
         final_copy(layer, part, 0).wait()
         final_copy(layer, part, 2).start()
 
-    def final_out(layer, part):
-        rows = pl.ds(*PARTS[part])
-        return pltpu.make_async_copy(
-            final.at[layer, :, rows], final_hbm.at[layer, :, rows], out_sem.at[0, 2 * layer + part]
-        )
-
     def final_done(layer, part):
         for which in range(1, 3):
             final_copy(layer, part, which).wait()
-        final_out(layer, part).start()
 
     def small_copy(stage):
         peer = (core_peer, x_peer, y_peer)[stage]
@@ -902,15 +910,9 @@
     final_pass(0, UP)
     final_pass(1, DOWN)
     final_pass(0, DOWN)
-    results = []
     for half in range(2):
-        rows = pl.ds(HALF * half, HALF)
         move_arrived(3, half, out_in)
-        results.append(pltpu.make_async_copy(out_in.at[half], output_hbm.at[rows], out_sem.at[2, half]))
         move_arrived(4, half, grad_in)
-        results.append(pltpu.make_async_copy(grad_in.at[half], input_grad_hbm.at[rows], out_sem.at[3, half]))
-    for copy in results:
-        copy.start()
     final_done(0, UP)
     final_done(1, DOWN)
     heads_done(0)
@@ -925,29 +927,13 @@
         to_team_left(2, half, half_of(cotangent, half))
         to_owner_left(3, half, back_out.at[0, half])
         to_owner_left(4, half, back_out.at[1, half])
-    for copy in results:
-        copy.wait()
-    for layer in range(LAYERS):
-        for part in (UP, DOWN):
-            final_out(layer, part).wait()
-        heads_copy_out(layer).wait()
 
 
 def results_kernel(
-    final_hbm, heads_hbm, out_hbm, grad_hbm, small,
+    final, heads, out_block, grad_block, small,
     output, input_grad, qkv_grad, out_grad, up_grad, up_bias_grad, down_grad, down_bias_grad, alpha_grad,
-    final, heads, grad_block, out_block, grad_wide, qkv_wide, out_wide, up_wide, down_wide, sem, out_sem,
+    out_flat, grad_wide, qkv_wide, out_wide, up_wide, down_wide, out_sem,
 ):
-    order = [(layer, part) for layer in (1, 0) for part in (UP, DOWN)]
-    pieces = []
-    for number, (layer, part) in enumerate(order):
-        rows = pl.ds(*PARTS[part])
-        pieces.append(pltpu.make_async_copy(final_hbm.at[layer, :, rows], final.at[layer, :, rows], sem.at[number]))
-    grad_move = pltpu.make_async_copy(grad_hbm, grad_block, sem.at[4])
-    out_move = pltpu.make_async_copy(out_hbm, out_block, sem.at[5])
-    heads_move = pltpu.make_async_copy(heads_hbm, heads, sem.at[6])
-    for move in (*pieces, grad_move, heads_move, out_move):
-        move.start()
     ends = []
 
     def write(source, target):
@@ -957,8 +943,7 @@
     up_bias_grad[...] = small[:, 0:256]
     down_bias_grad[...] = small[:, 256 : 256 + DIM]
     alpha_grad[...] = small[:, 384:386]
-    for (layer, part), piece in zip(order, pieces):
-        piece.wait()
+    for layer, part in [(layer, part) for layer in range(LAYERS) for part in (UP, DOWN)]:
         for quarter in range(4):
 
             def block(first, count):
@@ -978,10 +963,12 @@
             write(out_wide.at[layer], out_grad.at[layer])
         else:
             write(down_wide.at[layer], down_grad.at[layer])
-    grad_move.wait()
-    grad_wide[...] = grad_block[...].astype(F32)
+    for half in range(2):
+        rows = slice(HALF * half, HALF * half + HALF)
+        grad_wide[rows, :] = grad_block[half].astype(F32)
+        out_flat[rows, :] = out_block[half]
     write(grad_wide, input_grad)
-    heads_move.wait()
+    write(out_flat, output)
     for layer in range(LAYERS):
         for side in range(2):
             for member in range(TEAM):
@@ -991,8 +978,6 @@
                         layer, side, member, :, 128 * step : 128 * step + 128
                     ].astype(F32)
         write(qkv_wide.at[layer], qkv_grad.at[layer])
-    out_move.wait()
-    write(out_block, output)
     for end in ends:
         end.wait()
 
@@ -1016,14 +1001,14 @@
     final, heads, out_block, grad_block, small = pl.pallas_call(
         layers_kernel,
         out_shape=(
-            shape((LAYERS, 4, CHUNK, 128), BF16),
-            shape((LAYERS, 2, TEAM, DIM // 2, 3 * 128), BF16),
-            shape((2 * HALF, WIDTH), BF16),
-            shape((2 * HALF, WIDTH), BF16),
-            shape((LAYERS, WIDTH), F32),
+            vmem(LAYERS, 4, CHUNK, 128),
+            vmem(LAYERS, 2, TEAM, DIM // 2, 3 * 128),
+            vmem(2, HALF, WIDTH),
+            vmem(2, HALF, WIDTH),
+            wide(LAYERS, WIDTH),
         ),
         in_specs=[far, scalar, scalar, whole, whole, far, far, far, far, far],
-        out_specs=(far, far, far, far, whole),
+        out_specs=(whole,) * 5,
         scratch_shapes=[
             vmem(LAYERS, WIDTH, 3 * WIDTH),
             vmem(LAYERS, WIDTH, WIDTH),
@@ -1034,14 +1019,12 @@
             wide(8, 128),
             wide(2, 8, 128),
             vmem(2, 2, HALF, WIDTH),
-            vmem(2, HALF, WIDTH),
-            vmem(2, HALF, WIDTH),
             wide(2 * HALF, WIDTH),
             wide(2 * HALF, WIDTH),
             vmem(LAYERS, WIDTH, rows),
             vmem(LAYERS, WIDTH, 2 * HALF),
-            vmem(LAYERS, WIDTH, 2 * HALF),
-            vmem(LAYERS, FF, 2 * HALF),
+            vmem(LAYERS, 2 * HALF, WIDTH),
+            vmem(LAYERS, 2 * HALF, FF),
             wide(LAYERS, 2 * HALF, WIDTH),
             wide(LAYERS, 2 * HALF, FF),
             wide(LAYERS, 2 * HALF, WIDTH),
@@ -1073,12 +1056,10 @@
             vmem(2, 4, 2, TOTALS[2], 128),
             vmem(2, TOTALS[2], 128),
             vmem(TOTALS[2], 128),
-            vmem(LAYERS, 4, CHUNK, 128),
             vmem(LAYERS, 4, 2, DIM, 3 * 128),
             vmem(LAYERS, 4, 2, DIM // 2, 3 * 128),
             vmem(LAYERS, 4, 2, DIM // 2, 3 * 128),
             vmem(LAYERS, 2, DIM // 2, 3 * 128),
-            vmem(LAYERS, 2, TEAM, DIM // 2, 3 * 128),
             wide(LAYERS, SMALL),
             wide(3, LAYERS, SMALL),
             wide(4, LAYERS, SMALL),
@@ -1110,11 +1091,10 @@
             dma((LAYERS, 8)),
             dma((6,)),
             dma((6,)),
-            dma((4, 4)),
             pltpu.SemaphoreType.REGULAR((2,)),
         ],
         compiler_params=pltpu.CompilerParams(
-            collective_id=0, has_side_effects=True, vmem_limit_bytes=63 * 1024 * 1024
+            collective_id=0, has_side_effects=True, vmem_limit_bytes=61 * 1024 * 1024
         ),
         name="layers",
     )(
@@ -1135,22 +1115,18 @@
                 shape((LAYERS, DIM), F32),
                 shape((LAYERS, 2), F32),
             ),
-            in_specs=[far, far, far, far, whole],
+            in_specs=[whole] * 5,
             out_specs=(far, far, far, far, far, whole, far, whole, whole),
             scratch_shapes=[
-                vmem(LAYERS, 4, CHUNK, 128),
-                vmem(LAYERS, 2, TEAM, DIM // 2, 3 * 128),
-                vmem(2 * HALF, WIDTH),
                 vmem(2 * HALF, WIDTH),
                 wide(2 * HALF, WIDTH),
                 wide(LAYERS, DIM, 3 * WIDTH),
                 wide(LAYERS, DIM, WIDTH),
                 wide(LAYERS, DIM, FF),
                 wide(LAYERS, FF // RUNS, WIDTH),
-                dma((7,)),
                 dma((10,)),
             ],
-            compiler_params=pltpu.CompilerParams(vmem_limit_bytes=60 * 1024 * 1024),
+            compiler_params=pltpu.CompilerParams(vmem_limit_bytes=24 * 1024 * 1024),
             name="results",
         )(final, heads, out_block, grad_block, small)
     )

time: 132 us -> 128 us (0.970)
  Pallas kernels: 131 us -> 127 us
    pallas_call x1, Pallas kernels: 127 us -> 124 us  [fast_body(): pl.pallas_call(layers_kernel, out_shape=(vmem(LAYERS, 4, CHUNK, 128), vme...]
    pallas_call x1, Pallas kernels: 4.35 us -> 2.64 us  [fast_body(): pl.pallas_call(results_kernel, out_shape=(shape((2 * HALF, WIDTH), BF16),...]
where the time goes in v8:
time: 128 us
  Pallas kernels  127 us (99%)
    pallas_call x1, Pallas kernels, fast_body(): pl.pallas_call(layers_kernel, out_shape=(vmem(LAYERS, 4, CHUNK, 128), vme...  124 us
    pallas_call x1, Pallas kernels, fast_body(): pl.pallas_call(results_kernel, out_shape=(shape((2 * HALF, WIDTH), BF16),...  2.64 us

profile of v8, /device:TPU:0, one launch (start us, length us, event | category | flops | bytes accessed | tf_op | source)
XLA Modules:
  0.0 127.6 jit_solution(17850754931200758511)
XLA Ops:
  0.6 124.1 %layers.1 = (bf16[2,4,576,128]{3,2,1,0:T(8,128)(2,1)S(1)}, bf16[2,2,4,32,384]{4,3,2,1,0:T(8,128)(2,1)S(1)}, bf16[2,128,512]{2,1,0:T(8,128)(2,1)S(1)}, bf16[2,128,512]{2,1,0:T(8,128)(2,1)S(1)}, f32[2,512]{1,0:T(2,128)S(1)}) custom-call(bf16[256,512]{1,0:T(8,128)(2,1)} %tokens.1, s32[1,4]{1,0:T(1,128)} %seq_len.1, f32[2,2]{1,0:T(2,128)} %alphas.1, ...), custom_call_target="tpu_custom_call" | custom-call | tf_op jit(solution)/shard_map/layers/pallas_call | solution.py:1001
  124.7 2.6 %results.1 = (bf16[256,512]{1,0:T(8,128)(2,1)}, f32[256,512]{1,0:T(8,128)}, f32[2,64,1536]{2,1,0:T(8,128)}, f32[2,64,512]{2,1,0:T(8,128)}, f32[2,64,2048]{2,1,0:...) custom-call(bf16[2,4,576,128]{3,2,1,0:T(8,128)(2,1)S(1)} %get-tuple-element.14.final, ...), custom_call_target="tpu_custom_call" | custom-call | tf_op jit(solution)/shard_map/results/pallas_call | solution.py:1105

commit v9 on v8

--- a/solution.py
+++ b/solution.py
@@ -27,17 +27,16 @@
 PACK = HALF + DIM
 CHUNK = 576
 SMALL = FF + WIDTH + 128
-UP, DOWN = 0, 1
-PARTS = ((0, 320), (320, 256))
-SHARES = {(1, UP): (192, 0, 128), (1, DOWN): (160, 16, 80), (0, UP): (160, 112, 48), (0, DOWN): (128, 96, 32)}
+PARTS = ((1, 0, 320), (1, 320, 256), (0, 0, 128), (0, 128, 192), (0, 320, 128), (0, 448, 128))
+SHARES = ((176, 0, 144), (176, 0, 80), (64, 0, 64), (128, 64, 0), (128, 0, 0), (0, 128, 0))
 
 
 def spans():
     places, totals = {}, [0, 0, 0]
-    for key, counts in SHARES.items():
-        first = PARTS[key[1]][0]
+    for part, counts in enumerate(SHARES):
+        first = PARTS[part][1]
         for route, count in enumerate(counts):
-            places[(*key, route)] = (first, totals[route], count)
+            places[part, route] = (first, totals[route], count)
             first += count
             totals[route] += count
     return places, totals
@@ -65,9 +64,9 @@
 
 
 def layers_kernel(
-    tokens, seq_len, alphas, up_bias, down_bias, cotangent, qkv_hbm, out_hbm, up_hbm, down_hbm,
+    tokens, seq_len, alphas, up_bias_hbm, down_bias_hbm, cotangent, qkv_hbm, out_hbm, up_hbm, down_hbm,
     final, heads_all, out_in, grad_in, small_final,
-    wqkv, wout, wup, wdown,
+    wqkv, wout, wup, wdown, up_bias, down_bias,
     tok_in, cot_in, flag_out, flag_in, back_out,
     hidden, grad, hid_all, attn_t, entered, act, branch, slope, second,
     dz, du, da, dqkv,
@@ -76,7 +75,7 @@
     parts, core_in, xa_in, xb_in, ya_in, yb_in, z_in, third_z, third_x, third_y,
     heads_out, heads_x, heads_z, heads_sum, small, small_in, small_z, small_sum,
     w_sem, move_send, move_recv, a2a_send, a2a_recv, core_send, core_recv, x_send, x_recv, y_send, y_recv,
-    z_send, z_recv, tz_send, tz_recv, fin_send, fin_recv, hid_send, hid_recv, hx_send, hx_recv, hz_send, hz_recv, hf_send, hf_recv,
+    z_send, z_recv, fin_send, fin_recv, hid_send, hid_recv, hx_send, hx_recv, hz_send, hz_recv, hf_send, hf_recv,
     small_send, small_recv, core_free,
 ):
     grp = lax.axis_index("grp")
@@ -96,43 +95,6 @@
     x_peer = place(core, 1 - side, zz, yy)
     y_peer = place(core, side, zz, 1 - yy)
 
-    weight_copies = {}
-    for layer in range(LAYERS):
-        for number, (source, target) in enumerate(
-            ((qkv_hbm, wqkv), (out_hbm, wout), (up_hbm, wup), (down_hbm, wdown))
-        ):
-            weight_copies[layer, number] = pltpu.make_async_copy(
-                source.at[layer], target.at[layer], w_sem.at[layer, number]
-            )
-            weight_copies[layer, number].start()
-
-    barrier = pltpu.get_barrier_semaphore()
-    for step in range(1, 4):
-        pl.semaphore_signal(
-            barrier, inc=1, device_id=place(core, side, lax.rem(zz + step, 4), yy), device_id_type=MESH
-        )
-    for step in range(4):
-        pl.semaphore_signal(
-            barrier, inc=1, device_id=place(1 - core, side, lax.rem(zz + step, 4), yy), device_id_type=MESH
-        )
-    pl.semaphore_signal(barrier, inc=1, device_id=x_peer, device_id_type=MESH)
-    pl.semaphore_signal(barrier, inc=1, device_id=y_peer, device_id_type=MESH)
-    for peer in (
-        place(1 - core, side, zz, 1 - yy),
-        place(1 - core, 1 - side, zz, yy),
-        place(core, 1 - side, zz, 1 - yy),
-        place(1 - core, 1 - side, zz, 1 - yy),
-    ):
-        pl.semaphore_signal(barrier, inc=1, device_id=peer, device_id_type=MESH)
-
-    end_second = lax.div(seq_len[0, 0] + seq_len[0, 1], RUNS)
-    flag_out[...] = jnp.full((8, 128), end_second.astype(F32), F32)
-    for layer in range(LAYERS):
-        for head in range(OWN):
-            rq[layer, head, DIM:, :] = jnp.zeros((DIM, HALF * RUNS), BF16)
-    for head in range(OWN):
-        ro[head, 0:DIM, :] = jnp.zeros((DIM, HALF * RUNS), BF16)
-
     def remote(source, target, send, recv, peer):
         return pltpu.make_async_remote_copy(
             src_ref=source,
@@ -143,8 +105,8 @@
             device_id_type=MESH,
         )
 
-    def credit(semaphore, peer):
-        pl.semaphore_signal(semaphore, inc=1, device_id=peer, device_id_type=MESH)
+    def credit(semaphore, peer, count=1):
+        pl.semaphore_signal(semaphore, inc=count, device_id=peer, device_id_type=MESH)
 
     def moved(kind, slot, source, target, at, core_at, z_at):
         here = jnp.logical_and(core_at == core, z_at == zz)
@@ -195,27 +157,29 @@
     def slot_of(other):
         return lax.rem(other + TEAM - member, TEAM)
 
-    def exchange(kind, layer, half, head, outgoing, incoming):
-        incoming[half, 0, head] = outgoing[half, member, head]
+    def exchange(kind, layer, half, outgoing, incoming, head=None):
+        at = () if head is None else (head,)
+        incoming[(half, 0, *at)] = outgoing[(half, member, *at)]
         for step in range(1, TEAM):
             peer = lax.rem(member + step, TEAM)
-            pltpu.make_async_remote_copy(
-                src_ref=outgoing.at[half, peer, head],
-                dst_ref=incoming.at[half, TEAM - step, head],
-                send_sem=a2a_send.at[kind, layer, half, head],
-                recv_sem=a2a_recv.at[kind, layer, half, head],
-                device_id=place(lax.div(peer, 2), side, zz, lax.rem(peer, 2)),
-                device_id_type=MESH,
+            remote(
+                outgoing.at[(half, peer, *at)],
+                incoming.at[(half, TEAM - step, *at)],
+                a2a_send.at[kind, layer, half, head or 0],
+                a2a_recv.at[kind, layer, half, head or 0],
+                place(lax.div(peer, 2), side, zz, lax.rem(peer, 2)),
             ).start()
 
-    def arrived(kind, layer, half, head, incoming):
-        whole = incoming.at[half, pl.ds(1, TEAM - 1), head]
-        pltpu.make_async_copy(whole, whole, a2a_recv.at[kind, layer, half, head]).wait()
+    def arrived(kind, layer, half, incoming, head=None):
+        at = () if head is None else (head,)
+        whole = incoming.at[(half, pl.ds(1, TEAM - 1), *at)]
+        pltpu.make_async_copy(whole, whole, a2a_recv.at[kind, layer, half, head or 0]).wait()
 
     def left(kind, layer, half, outgoing):
-        for head in range(OWN):
-            whole = outgoing.at[half, pl.ds(1, TEAM - 1), head]
-            pltpu.make_async_copy(whole, whole, a2a_send.at[kind, layer, half, head]).wait()
+        for head in range(OWN) if kind in (0, 3) else (None,):
+            at = () if head is None else (head,)
+            whole = outgoing.at[(half, pl.ds(1, TEAM - 1), *at)]
+            pltpu.make_async_copy(whole, whole, a2a_send.at[kind, layer, half, head or 0]).wait()
 
     def tokens_of(chunk, other):
         return pl.ds(pl.multiple_of(HALF * (TEAM * chunk + other), HALF), HALF)
@@ -262,7 +226,7 @@
         for head in range(RUNS):
             pack_out[half, head // 2, head % 2, HALF:, :] = queries_t[DIM * head : DIM * head + DIM, :]
         for head in range(OWN):
-            exchange(0, layer, half, head, pack_out, pack_in)
+            exchange(0, layer, half, pack_out, pack_in, head)
         hid_all[layer, :, tokens_of(half, member)] = rounded.T
 
     def attend(layer, chunk):
@@ -270,7 +234,7 @@
             left(1, 0, chunk, head_out)
 
         def one_head(head, carry):
-            arrived(0, layer, chunk, head, pack_in)
+            arrived(0, layer, chunk, pack_in, head)
             for other in range(TEAM):
                 slot = slot_of(other)
                 start = HALF * (TEAM * chunk + other)
@@ -302,16 +266,15 @@
                     head_out[chunk, 2 * (i - 2 * chunk) + part, head] = rounded[
                         :, HALF * part : HALF * part + HALF
                     ]
-            exchange(1, layer, chunk, head, head_out, o_in)
             return carry
 
         for head in range(OWN):
             one_head(head, 0)
+        exchange(1, layer, chunk, head_out, o_in)
 
     def feed(layer, half):
         rows = rows_of(half)
-        for head in range(OWN):
-            arrived(1, layer, half, head, o_in)
+        arrived(1, layer, half, o_in)
         for head in range(RUNS):
             attn_t[layer, DIM * head : DIM * head + DIM, rows] = o_in[half, slot_of(head // 2), head % 2]
         attn = attn_t[layer, :, rows].T
@@ -378,8 +341,7 @@
                 head_out[chunk, head // 2, head % 2] = spread[
                     DIM * head : DIM * head + DIM, HALF * chunk : HALF * chunk + HALF
                 ]
-            for head in range(OWN):
-                exchange(2, layer, chunk, head, head_out, do_in)
+            exchange(2, layer, chunk, head_out, do_in)
         alpha_first = total_of(middle * branch[layer])
         column = lax.broadcasted_iota(jnp.int32, (1, 128), 1)
         small[layer : layer + 1, FF + WIDTH :] = jnp.where(
@@ -387,10 +349,10 @@
         )
 
     def attend_back(layer, chunk):
+        arrived(2, layer, chunk, do_in)
         left(*((0, 1) if layer == 1 else (3, 1)), chunk, pack_out)
 
         def one_head(head, carry):
-            arrived(2, layer, chunk, head, do_in)
             for other in range(TEAM):
                 start = HALF * (TEAM * chunk + other)
                 ro[head, DIM:, start : start + HALF] = do_in[chunk, slot_of(other), head]
@@ -423,7 +385,7 @@
                 span = slice(start, start + HALF)
                 pack_out[chunk, other, head, 0:HALF, :] = acc[head, span, :].astype(BF16)
                 pack_out[chunk, other, head, HALF:, :] = dq_t[head, :, span].astype(BF16)
-            exchange(3, layer, chunk, head, pack_out, pack_in)
+            exchange(3, layer, chunk, pack_out, pack_in, head)
             return carry
 
         for head in range(OWN):
@@ -431,7 +393,7 @@
 
     def project_back(layer, half):
         for head in range(OWN):
-            arrived(3, layer, half, head, pack_in)
+            arrived(3, layer, half, pack_in, head)
         turned = jnp.concatenate(
             [pack_in[half, slot_of(head // 2), head % 2, HALF:, :] for head in range(RUNS)], axis=0
         )
@@ -449,26 +411,30 @@
     def scatter_rows(layer, result, first_row):
         for run in range(RUNS):
             for quarter in range(4):
-                parts[layer, quarter, run // 2, run % 2, first_row : first_row + DIM, :] = result[
+                parts[layer, quarter % 2, quarter // 2, run // 2, run % 2, first_row : first_row + DIM, :] = result[
                     DIM * run : DIM * run + DIM, 128 * quarter : 128 * quarter + 128
                 ].astype(BF16)
 
-    def up_grads(layer):
-        turned = entered[layer].T
-        for step in range(FF // CUT):
-            cut = slice(CUT * step, CUT * step + CUT)
-            scatter_rows(layer, nn(turned, du[:, cut]), DIM * step)
-        scatter_rows(layer, nn(attn_t[layer], da[...]), 256)
-        core_start(layer, UP)
-
-    def down_grads(layer):
-        for run in range(RUNS):
-            result = nn(act[layer, :, TILE * run : TILE * run + TILE].T, dz[...])
-            for quarter in range(4):
-                parts[layer, quarter, run // 2, run % 2, 320:576, :] = result[
-                    :, 128 * quarter : 128 * quarter + 128
-                ].astype(BF16)
-        core_start(layer, DOWN)
+    def make(part):
+        layer, first, count = PARTS[part]
+        if first < 256:
+            turned = entered[layer].T
+        for row in range(first, min(first + count, 256), DIM):
+            step = row // DIM
+            scatter_rows(layer, nn(turned, du[:, CUT * step : CUT * step + CUT]), row)
+        if first <= 256 < first + count:
+            scatter_rows(layer, nn(attn_t[layer], da[...]), 256)
+        if first >= 320:
+            for run in range(RUNS):
+                at = TILE * run + first - 320
+                result = nn(act[layer, :, at : at + count].T, dz[...])
+                for quarter in range(4):
+                    parts[layer, quarter % 2, quarter // 2, run // 2, run % 2, first : first + count, :] = result[
+                        :, 128 * quarter : 128 * quarter + 128
+                    ].astype(BF16)
+        if layer == 0:
+            pl.semaphore_wait(core_free.at[0 if first < 320 else 1], 1)
+        core_copy(part).start()
 
     def heads_grads(layer):
         for chunk in range(2):
@@ -554,187 +520,172 @@
         for number in range(1, 8):
             heads_last_copy(layer, number).wait()
 
-    def chunk_rows(layer, part, route):
-        first, _, count = SPANS[layer, part, route]
-        return pl.ds(first, count)
-
-    def route_rows(layer, part, route):
-        _, first, count = SPANS[layer, part, route]
-        return pl.ds(first, count)
-
-    def rows_in(layer, part, route):
-        return chunk_rows(layer, part, route), route_rows(layer, part, route)
-
-    def used(layer, part, route):
-        return SHARES[layer, part][route] > 0
-
-    def core_copy(layer, part, across):
-        rows = pl.ds(*PARTS[part])
+    def rows_in(part, route):
+        first, room, count = SPANS[part, route]
+        return pl.ds(first, count), pl.ds(room, count)
+
+    def used(part, route):
+        return SHARES[part][route] > 0
+
+    def core_copy(part):
+        layer, first, count = PARTS[part]
+        rows = pl.ds(first, count)
         return remote(
-            parts.at[layer, 2 * across + 1 - core, :, :, rows],
-            core_in.at[across, :, :, rows],
-            core_send.at[layer, part, across],
-            core_recv.at[layer, part, across],
+            parts.at[layer, 1 - core, :, :, :, rows],
+            core_in.at[:, :, :, rows],
+            core_send.at[part],
+            core_recv.at[part],
             core_peer,
         )
 
-    def x_copy(layer, part, route):
-        rows, room = rows_in(layer, part, route)
-        ends = (x_send.at[layer, part, route], x_recv.at[layer, part, route], x_peer)
+    def x_copy(part, route):
+        layer = PARTS[part][0]
+        rows, room = rows_in(part, route)
+        ends = (x_send.at[part, route], x_recv.at[part, route], x_peer)
+        mine = parts.at[layer, core, 1 - side]
         if route == 0:
-            return remote(parts.at[layer, far_side, :, :, rows], xa_in.at[:, :, room], *ends)
+            return remote(mine.at[:, :, rows], xa_in.at[:, :, room], *ends)
         if route == 1:
-            return remote(parts.at[layer, far_side, :, yy, rows], xb_in.at[:, room], *ends)
-        return remote(parts.at[layer, far_side, zz, :, rows], third_x.at[:, room], *ends)
-
-    def y_copy(layer, part, route, across=0):
-        rows, room = rows_in(layer, part, route)
-        which = (layer, part, route + across)
+            return remote(mine.at[:, yy, rows], xb_in.at[:, room], *ends)
+        return remote(mine.at[zz, :, rows], third_x.at[:, room], *ends)
+
+    def y_copy(part, route):
+        layer = PARTS[part][0]
+        rows, room = rows_in(part, route)
+        ends = (y_send.at[part, route], y_recv.at[part, route], y_peer)
+        mine = parts.at[layer, core]
+        if route == 0:
+            return remote(mine.at[side, :, 1 - yy, rows], ya_in.at[:, room], *ends)
+        if route == 1:
+            return remote(mine.at[:, :, 1 - yy, rows], yb_in.at[:, :, room], *ends)
+        return remote(mine.at[side, zz, 1 - yy, rows], third_y.at[room], *ends)
+
+    def z_copy(part, route, step):
+        layer = PARTS[part][0]
+        rows, room = rows_in(part, route)
+        peer = lax.rem(zz + step, 4)
+        ends = (z_send.at[part, route, step], z_recv.at[part, route, 4 - step], place(core, side, peer, yy))
         if route == 2:
-            which = (layer, part, 3)
-        ends = (y_send.at[which], y_recv.at[which], y_peer)
-        if route == 0:
-            return remote(parts.at[layer, grp, :, 1 - yy, rows], ya_in.at[:, room], *ends)
-        if route == 1:
-            return remote(parts.at[layer, 2 * across + core, :, 1 - yy, rows], yb_in.at[across, :, room], *ends)
-        return remote(parts.at[layer, grp, zz, 1 - yy, rows], third_y.at[room], *ends)
-
-    def z_copy(layer, part, route, step):
-        rows = chunk_rows(layer, part, route)
-        peer = lax.rem(zz + step, 4)
-        return remote(
-            parts.at[layer, grp, peer, yy, rows],
-            z_in.at[layer, 4 - step, rows],
-            z_send.at[layer, part, route, step],
-            z_recv.at[layer, part, route, 4 - step],
-            place(core, side, peer, yy),
-        )
-
-    def third_z_copy(layer, part, across, step):
-        rows, room = rows_in(layer, part, 2)
-        peer = lax.rem(zz + step, 4)
-        return remote(
-            parts.at[layer, 2 * across + core, peer, :, rows],
-            third_z.at[across, 4 - step, :, room],
-            tz_send.at[layer, part, across, step],
-            tz_recv.at[layer, part, across, 4 - step],
-            place(core, side, peer, yy),
-        )
-
-    def final_copy(layer, part, which):
-        block = final.at[layer, far_side if which == 2 else grp, pl.ds(*PARTS[part])]
+            return remote(parts.at[layer, core, :, peer, :, rows], third_z.at[4 - step, :, :, room], *ends)
+        return remote(parts.at[layer, core, side, peer, yy, rows], z_in.at[layer, 4 - step, rows], *ends)
+
+    def final_copy(part, which):
+        layer, first, count = PARTS[part]
+        block = final.at[layer, far_side if which == 2 else grp, pl.ds(first, count)]
         return remote(
             block,
             block,
-            fin_send.at[layer, part, which],
-            fin_recv.at[layer, part, which],
+            fin_send.at[part, which],
+            fin_recv.at[part, which],
             x_peer if which == 0 else core_peer,
         )
 
-    def core_start(layer, part):
-        if layer == 0:
-            pl.semaphore_wait(core_free.at[part], 1)
-        for across in range(2):
-            core_copy(layer, part, across).start()
-
-    def core_done(layer, part):
-        rows = pl.ds(*PARTS[part])
-        for across in range(2):
-            core_copy(layer, part, across).wait()
+    def core_done(part):
+        layer, first, count = PARTS[part]
+        rows = pl.ds(first, count)
+        core_copy(part).wait()
         for across in (1 - side, side):
-            parts[layer, 2 * across + core, :, :, rows, :] += core_in[across, :, :, rows, :]
-            if used(layer, part, 0) and across is not side:
-                x_copy(layer, part, 0).start()
-            if used(layer, part, 1):
-                y_copy(layer, part, 1, across).start()
-            if used(layer, part, 2):
-                for step in range(1, 4):
-                    third_z_copy(layer, part, across, step).start()
+            parts[layer, core, across, :, :, rows, :] += core_in[across, :, :, rows, :]
+            if used(part, 0) and across is not side:
+                x_copy(part, 0).start()
+        if used(part, 1):
+            y_copy(part, 1).start()
+        if used(part, 2):
+            for step in range(1, 4):
+                z_copy(part, 2, step).start()
         if layer == 1:
-            credit(core_free.at[part], core_peer)
-
-    def first_x(layer, part):
-        if used(layer, part, 0):
-            rows, room = rows_in(layer, part, 0)
-            x_copy(layer, part, 0).wait()
+            freed = 0 if first < 320 else 1
+            followers = [1 for other in PARTS if other[0] == 0 and (other[1] >= 320) == (freed == 1)]
+            credit(core_free.at[freed], core_peer, len(followers))
+
+    def first_x(part):
+        if used(part, 0):
+            layer = PARTS[part][0]
+            rows, room = rows_in(part, 0)
+            x_copy(part, 0).wait()
             for y in (1 - yy, yy):
-                parts[layer, grp, :, y, rows, :] += xa_in[:, y, room, :]
+                parts[layer, core, side, :, y, rows, :] += xa_in[:, y, room, :]
                 if y is not yy:
-                    y_copy(layer, part, 0).start()
-
-    def first_y(layer, part):
-        if used(layer, part, 1):
-            rows, room = rows_in(layer, part, 1)
+                    y_copy(part, 0).start()
+
+    def first_y(part):
+        if used(part, 1):
+            layer = PARTS[part][0]
+            rows, room = rows_in(part, 1)
+            y_copy(part, 1).wait()
             for across in (1 - side, side):
-                y_copy(layer, part, 1, across).wait()
+                parts[layer, core, across, :, yy, rows, :] += yb_in[across, :, room, :]
+                if across is not side:
+                    x_copy(part, 1).start()
+
+    def first_z(part):
+        if used(part, 2):
+            layer = PARTS[part][0]
+            rows, room = rows_in(part, 2)
+            for step in range(1, 4):
+                z_copy(part, 2, step).wait()
             for across in (1 - side, side):
-                parts[layer, 2 * across + core, :, yy, rows, :] += yb_in[across, :, room, :]
+                total = parts[layer, core, across, zz, :, rows, :].astype(F32)
+                for slot in range(1, 4):
+                    total = total + third_z[slot, across, :, room, :].astype(F32)
+                parts[layer, core, across, zz, :, rows, :] = total.astype(BF16)
                 if across is not side:
-                    x_copy(layer, part, 1).start()
-
-    def first_z(layer, part):
-        if used(layer, part, 2):
-            rows, room = rows_in(layer, part, 2)
-            for across in (1 - side, side):
-                for step in range(1, 4):
-                    third_z_copy(layer, part, across, step).wait()
-                total = parts[layer, 2 * across + core, zz, :, rows, :].astype(F32)
-                for slot in range(1, 4):
-                    total = total + third_z[across, slot, :, room, :].astype(F32)
-                parts[layer, 2 * across + core, zz, :, rows, :] = total.astype(BF16)
-                if across is not side:
-                    x_copy(layer, part, 2).start()
-
-    def second_x(layer, part):
-        if used(layer, part, 0):
-            rows, room = rows_in(layer, part, 0)
-            y_copy(layer, part, 0).wait()
-            parts[layer, grp, :, yy, rows, :] += ya_in[:, room, :]
+                    x_copy(part, 2).start()
+
+    def second_x(part):
+        if used(part, 0):
+            layer = PARTS[part][0]
+            rows, room = rows_in(part, 0)
+            y_copy(part, 0).wait()
+            parts[layer, core, side, :, yy, rows, :] += ya_in[:, room, :]
             for step in range(1, 4):
-                z_copy(layer, part, 0, step).start()
-
-    def second_y(layer, part):
-        if used(layer, part, 1):
-            rows, room = rows_in(layer, part, 1)
-            x_copy(layer, part, 1).wait()
-            parts[layer, grp, :, yy, rows, :] += xb_in[:, room, :]
+                z_copy(part, 0, step).start()
+
+    def second_y(part):
+        if used(part, 1):
+            layer = PARTS[part][0]
+            rows, room = rows_in(part, 1)
+            x_copy(part, 1).wait()
+            parts[layer, core, side, :, yy, rows, :] += xb_in[:, room, :]
             for step in range(1, 4):
-                z_copy(layer, part, 1, step).start()
-
-    def second_z(layer, part):
-        if used(layer, part, 2):
-            rows, room = rows_in(layer, part, 2)
-            x_copy(layer, part, 2).wait()
+                z_copy(part, 1, step).start()
+
+    def second_z(part):
+        if used(part, 2):
+            layer = PARTS[part][0]
+            rows, room = rows_in(part, 2)
+            x_copy(part, 2).wait()
             for y in (1 - yy, yy):
-                parts[layer, grp, zz, y, rows, :] += third_x[y, room, :]
+                parts[layer, core, side, zz, y, rows, :] += third_x[y, room, :]
                 if y is not yy:
-                    y_copy(layer, part, 2).start()
-
-    def third_done(layer, part):
+                    y_copy(part, 2).start()
+
+    def third_done(part):
+        layer = PARTS[part][0]
         for route in range(3):
-            if not used(layer, part, route):
+            if not used(part, route):
                 continue
-            rows, room = rows_in(layer, part, route)
+            rows, room = rows_in(part, route)
             if route == 2:
-                y_copy(layer, part, 2).wait()
-                final[layer, grp, rows, :] = parts[layer, grp, zz, yy, rows, :] + third_y[room, :]
+                y_copy(part, 2).wait()
+                final[layer, grp, rows, :] = parts[layer, core, side, zz, yy, rows, :] + third_y[room, :]
             else:
                 for step in range(1, 4):
-                    z_copy(layer, part, route, step).wait()
-                total = parts[layer, grp, zz, yy, rows, :].astype(F32)
+                    z_copy(part, route, step).wait()
+                total = parts[layer, core, side, zz, yy, rows, :].astype(F32)
                 for slot in range(1, 4):
                     total = total + z_in[layer, slot, rows, :].astype(F32)
                 final[layer, grp, rows, :] = total.astype(BF16)
         for which in range(2):
-            final_copy(layer, part, which).start()
-
-    def final_pass(layer, part):
-        final_copy(layer, part, 0).wait()
-        final_copy(layer, part, 2).start()
-
-    def final_done(layer, part):
+            final_copy(part, which).start()
+
+    def final_pass(part):
+        final_copy(part, 0).wait()
+        final_copy(part, 2).start()
+
+    def final_done(part):
         for which in range(1, 3):
-            final_copy(layer, part, which).wait()
+            final_copy(part, which).wait()
 
     def small_copy(stage):
         peer = (core_peer, x_peer, y_peer)[stage]
@@ -801,12 +752,49 @@
         back_out[1, half] = grad[rows_of(half), :].astype(BF16)
         to_owner(4, half, back_out.at[1, half], grad_in)
 
+    barrier = pltpu.get_barrier_semaphore()
+    for step in range(1, 4):
+        credit(barrier, place(core, side, lax.rem(zz + step, 4), yy))
+    for step in range(4):
+        credit(barrier, place(1 - core, side, lax.rem(zz + step, 4), yy))
+    for peer in (
+        x_peer,
+        y_peer,
+        place(1 - core, side, zz, 1 - yy),
+        place(1 - core, 1 - side, zz, yy),
+        place(core, 1 - side, zz, 1 - yy),
+        place(1 - core, 1 - side, zz, 1 - yy),
+    ):
+        credit(barrier, peer)
+
+    weight_copies = {}
+    for layer in range(LAYERS):
+        for number, (source, target) in enumerate(
+            ((qkv_hbm, wqkv), (out_hbm, wout), (up_hbm, wup), (down_hbm, wdown))
+        ):
+            weight_copies[layer, number] = pltpu.make_async_copy(
+                source.at[layer], target.at[layer], w_sem.at[layer, number]
+            )
+    bias_copies = [
+        pltpu.make_async_copy(up_bias_hbm, up_bias, w_sem.at[2, 0]),
+        pltpu.make_async_copy(down_bias_hbm, down_bias, w_sem.at[2, 1]),
+    ]
+    weight_copies[0, 0].start()
     pl.semaphore_wait(barrier, 13)
     upper = lax.div(zz, 2)
     for half in (1 - upper, upper):
         to_team(0, half, half_of(tokens, half), tok_in)
+    for copy in (*list(weight_copies.values())[1:], *bias_copies):
+        copy.start()
+    end_second = lax.div(seq_len[0, 0] + seq_len[0, 1], RUNS)
+    flag_out[...] = jnp.full((8, 128), end_second.astype(F32), F32)
     for half in (1 - upper, upper):
         to_team(1, half, flag_out, flag_in)
+    for layer in range(LAYERS):
+        for head in range(OWN):
+            rq[layer, head, DIM:, :] = jnp.zeros((DIM, HALF * RUNS), BF16)
+    for head in range(OWN):
+        ro[head, 0:DIM, :] = jnp.zeros((DIM, HALF * RUNS), BF16)
     weight_copies[0, 0].wait()
     halves(begin, functools.partial(project, 0), first=upper)
     for half in (1 - upper, upper):
@@ -825,8 +813,8 @@
         bias[TILE * tile : TILE * tile + TILE, :] = jnp.where(apart, NEGATIVE, 0.0)
     bias[TILE * (TILES - 1) :, :] = jnp.where(jnp.logical_or(later, apart), NEGATIVE, 0.0)
 
-    for number in range(1, 4):
-        weight_copies[0, number].wait()
+    for copy in (*bias_copies, *(weight_copies[0, number] for number in range(1, 4))):
+        copy.wait()
     attend(0, 0)
     attend(0, 1)
     hidden_start(0, 0)
@@ -844,80 +832,86 @@
     hidden_pass(1, 0)
 
     halves(functools.partial(turn_round, 1))
-    down_grads(1)
+    make(1)
     feed_back(1)
     hidden_pass(0, 1)
     hidden_pass(1, 1)
-    core_done(1, DOWN)
-    up_grads(1)
+    core_done(1)
+    make(0)
     attend_back(1, 1)
-    first_y(1, DOWN)
-    core_done(1, UP)
+    core_done(0)
     attend_back(1, 0)
-    second_y(1, DOWN)
-    first_y(1, UP)
-    first_x(1, DOWN)
     project_back(1, 1)
+    first_x(1)
     heads_grads(1)
-    first_z(1, DOWN)
     project_back(1, 0)
     feed_back(0)
     small_start()
-    second_x(1, DOWN)
-    second_y(1, UP)
-    up_grads(0)
-    first_x(1, UP)
+    make(4)
+    second_x(1)
+    make(5)
+    first_x(0)
+    first_z(1)
+    make(2)
+    core_done(4)
+    core_done(5)
+    make(3)
+    core_done(2)
+    core_done(3)
     heads_second(1)
-    first_z(1, UP)
+    second_x(0)
+    first_x(4)
     attend_back(0, 1)
     small_next(0)
-    core_done(0, UP)
-    second_x(1, UP)
-    down_grads(0)
+    first_y(3)
+    first_y(5)
+    first_x(2)
+    first_z(2)
+    first_z(0)
+    second_x(4)
+    first_x(3)
     attend_back(0, 0)
     small_next(1)
+    second_y(3)
+    heads_grads(0)
+    small_next(2)
+    second_y(5)
+    second_z(1)
+    second_z(0)
+    second_x(2)
+    second_x(3)
+    third_done(5)
+    second_z(2)
+    heads_third(1)
+    heads_second(0)
+    small_done()
+    third_done(1)
+    third_done(4)
     project_back(0, 1)
     hand_back(1)
-    first_z(0, UP)
-    heads_grads(0)
-    small_next(2)
-    first_x(0, UP)
-    core_done(0, DOWN)
-    first_y(0, UP)
-    heads_second(0)
-    small_done()
-    first_z(0, DOWN)
-    second_x(0, UP)
-    first_x(0, DOWN)
-    second_z(0, UP)
-    second_z(1, UP)
-    heads_third(1)
-    second_z(1, DOWN)
-    first_y(0, DOWN)
-    heads_third(0)
-    second_y(0, UP)
-    second_x(0, DOWN)
-    second_z(0, DOWN)
-    third_done(1, UP)
-    third_done(0, UP)
-    second_y(0, DOWN)
+    third_done(2)
+    third_done(0)
+    third_done(3)
     project_back(0, 0)
     hand_back(0)
+    heads_third(0)
+    final_pass(2)
+    final_pass(4)
+    final_pass(5)
+    final_pass(3)
+    final_done(4)
+    final_pass(0)
+    final_pass(1)
+    heads_done(0)
     heads_done(1)
-    third_done(1, DOWN)
-    third_done(0, DOWN)
-    final_pass(1, UP)
-    final_pass(0, UP)
-    final_pass(1, DOWN)
-    final_pass(0, DOWN)
+    final_done(2)
+    final_done(0)
+    final_done(1)
+    final_done(3)
+    final_done(5)
     for half in range(2):
         move_arrived(3, half, out_in)
         move_arrived(4, half, grad_in)
-    final_done(0, UP)
-    final_done(1, DOWN)
-    heads_done(0)
-    final_done(1, UP)
-    final_done(0, DOWN)
 
     for half in range(2):
         left(2, 0, half, head_out)
@@ -943,7 +937,7 @@
     up_bias_grad[...] = small[:, 0:256]
     down_bias_grad[...] = small[:, 256 : 256 + DIM]
     alpha_grad[...] = small[:, 384:386]
-    for layer, part in [(layer, part) for layer in range(LAYERS) for part in (UP, DOWN)]:
+    for layer in range(LAYERS):
         for quarter in range(4):
 
             def block(first, count):
@@ -952,17 +946,13 @@
             def columns(step):
                 return slice(WIDTH * step + 128 * quarter, WIDTH * step + 128 * quarter + 128)
 
-            if part == UP:
-                for step in range(4):
-                    up_wide[layer, :, columns(step)] = block(DIM * step, DIM)
-                out_wide[layer, :, columns(0)] = block(256, DIM)
-            else:
-                down_wide[layer, :, columns(0)] = block(320, 256)
-        if part == UP:
-            write(up_wide.at[layer], up_grad.at[layer])
-            write(out_wide.at[layer], out_grad.at[layer])
-        else:
-            write(down_wide.at[layer], down_grad.at[layer])
+            for step in range(4):
+                up_wide[layer, :, columns(step)] = block(DIM * step, DIM)
+            out_wide[layer, :, columns(0)] = block(256, DIM)
+            down_wide[layer, :, columns(0)] = block(320, 256)
+        write(up_wide.at[layer], up_grad.at[layer])
+        write(out_wide.at[layer], out_grad.at[layer])
+        write(down_wide.at[layer], down_grad.at[layer])
     for half in range(2):
         rows = slice(HALF * half, HALF * half + HALF)
         grad_wide[rows, :] = grad_block[half].astype(F32)
@@ -1007,13 +997,15 @@
             vmem(2, HALF, WIDTH),
             wide(LAYERS, WIDTH),
         ),
-        in_specs=[far, scalar, scalar, whole, whole, far, far, far, far, far],
+        in_specs=[far, scalar, scalar, far, far, far, far, far, far, far],
         out_specs=(whole,) * 5,
         scratch_shapes=[
             vmem(LAYERS, WIDTH, 3 * WIDTH),
             vmem(LAYERS, WIDTH, WIDTH),
             vmem(LAYERS, WIDTH, FF),
             vmem(LAYERS, FF, WIDTH),
+            wide(LAYERS, FF),
+            wide(LAYERS, WIDTH),
             vmem(2, HALF, WIDTH),
             vmem(2, HALF, WIDTH),
             wide(8, 128),
@@ -1046,14 +1038,14 @@
             wide(OWN, rows, 128),
             wide(OWN, DIM, rows),
             wide(rows, TILE),
-            vmem(LAYERS, 4, 4, 2, CHUNK, 128),
+            vmem(LAYERS, 2, 2, 4, 2, CHUNK, 128),
             vmem(2, 4, 2, CHUNK, 128),
             vmem(4, 2, TOTALS[0], 128),
             vmem(4, TOTALS[1], 128),
             vmem(4, TOTALS[0], 128),
             vmem(2, 4, TOTALS[1], 128),
             vmem(LAYERS, 4, CHUNK, 128),
-            vmem(2, 4, 2, TOTALS[2], 128),
+            vmem(4, 2, 2, TOTALS[2], 128),
             vmem(2, TOTALS[2], 128),
             vmem(TOTALS[2], 128),
             vmem(LAYERS, 4, 2, DIM, 3 * 128),
@@ -1064,23 +1056,21 @@
             wide(3, LAYERS, SMALL),
             wide(4, LAYERS, SMALL),
             wide(3, LAYERS, SMALL),
-            dma((LAYERS, 4)),
+            dma((LAYERS + 1, 4)),
             dma((5, 2)),
             dma((5, 2)),
             dma((4, LAYERS, 2, OWN)),
             dma((4, LAYERS, 2, OWN)),
-            dma((LAYERS, 2, 2)),
-            dma((LAYERS, 2, 2)),
-            dma((LAYERS, 2, 3)),
-            dma((LAYERS, 2, 3)),
-            dma((LAYERS, 2, 4)),
-            dma((LAYERS, 2, 4)),
-            dma((LAYERS, 2, 2, 4)),
-            dma((LAYERS, 2, 2, 4)),
-            dma((LAYERS, 2, 2, 4)),
-            dma((LAYERS, 2, 2, 4)),
-            dma((LAYERS, 2, 3)),
-            dma((LAYERS, 2, 3)),
+            dma((len(PARTS),)),
+            dma((len(PARTS),)),
+            dma((len(PARTS), 3)),
+            dma((len(PARTS), 3)),
+            dma((len(PARTS), 3)),
+            dma((len(PARTS), 3)),
+            dma((len(PARTS), 3, 4)),
+            dma((len(PARTS), 3, 4)),
+            dma((len(PARTS), 3)),
+            dma((len(PARTS), 3)),
             dma((LAYERS, 2, 3)),
             dma((LAYERS, 2, 3)),
             dma((LAYERS,)),

time: 128 us -> 129 us (level)
  no operation moved by 1% of the time
where the time goes in v9:
time: 129 us
  Pallas kernels  128 us (99%)
    pallas_call x1, Pallas kernels, fast_body(): pl.pallas_call(layers_kernel, out_shape=(vmem(LAYERS, 4, CHUNK, 128), vme...  125 us
    pallas_call x1, Pallas kernels, fast_body(): pl.pallas_call(results_kernel, out_shape=(shape((2 * HALF, WIDTH), BF16),...  2.64 us

profile of v9, /device:TPU:0, one launch (start us, length us, event | category | flops | bytes accessed | tf_op | source)
XLA Modules:
  0.0 128.8 jit_solution(10495982645791478253)
XLA Ops:
  0.6 125.3 %layers.1 = (bf16[2,4,576,128]{3,2,1,0:T(8,128)(2,1)S(1)}, bf16[2,2,4,32,384]{4,3,2,1,0:T(8,128)(2,1)S(1)}, bf16[2,128,512]{2,1,0:T(8,128)(2,1)S(1)}, bf16[2,128,512]{2,1,0:T(8,128)(2,1)S(1)}, f32[2,512]{1,0:T(2,128)S(1)}) custom-call(bf16[256,512]{1,0:T(8,128)(2,1)} %tokens.1, s32[1,4]{1,0:T(1,128)} %seq_len.1, f32[2,2]{1,0:T(2,128)} %alphas.1, ...), custom_call_target="tpu_custom_call" | custom-call | tf_op jit(solution)/shard_map/layers/pallas_call | solution.py:991
  126.0 2.6 %results.1 = (bf16[256,512]{1,0:T(8,128)(2,1)}, f32[256,512]{1,0:T(8,128)}, f32[2,64,1536]{2,1,0:T(8,128)}, f32[2,64,512]{2,1,0:T(8,128)}, f32[2,64,2048]{2,1,0:...) custom-call(bf16[2,4,576,128]{3,2,1,0:T(8,128)(2,1)S(1)} %get-tuple-element.14.final, ...), custom_call_target="tpu_custom_call" | custom-call | tf_op jit(solution)/shard_map/results/pallas_call | solution.py:1095

commit v10 on v9

--- a/solution.py
+++ b/solution.py
@@ -27,8 +27,8 @@
 PACK = HALF + DIM
 CHUNK = 576
 SMALL = FF + WIDTH + 128
-PARTS = ((1, 0, 320), (1, 320, 256), (0, 0, 128), (0, 128, 192), (0, 320, 128), (0, 448, 128))
-SHARES = ((176, 0, 144), (176, 0, 80), (64, 0, 64), (128, 64, 0), (128, 0, 0), (0, 128, 0))
+PARTS = ((1, 0, 320), (1, 320, 256), (0, 0, 320), (0, 320, 256))
+SHARES = ((192, 0, 128), (160, 16, 80), (160, 112, 48), (128, 96, 32))
 
 
 def spans():
@@ -839,76 +839,68 @@
     core_done(1)
     make(0)
     attend_back(1, 1)
+    first_y(1)
     core_done(0)
     attend_back(1, 0)
+    second_y(1)
+    first_x(1)
     project_back(1, 1)
-    first_x(1)
     heads_grads(1)
+    first_z(1)
     project_back(1, 0)
     feed_back(0)
     small_start()
-    make(4)
     second_x(1)
-    make(5)
+    make(2)
     first_x(0)
-    first_z(1)
-    make(2)
-    core_done(4)
-    core_done(5)
-    make(3)
-    core_done(2)
-    core_done(3)
     heads_second(1)
-    second_x(0)
-    first_x(4)
+    first_z(0)
     attend_back(0, 1)
     small_next(0)
-    first_y(3)
-    first_y(5)
-    first_x(2)
-    first_z(2)
-    first_z(0)
-    second_x(4)
-    first_x(3)
+    core_done(2)
+    second_x(0)
+    make(3)
     attend_back(0, 0)
     small_next(1)
-    second_y(3)
+    project_back(0, 1)
+    hand_back(1)
+    first_z(2)
     heads_grads(0)
     small_next(2)
-    second_y(5)
-    second_z(1)
-    second_z(0)
-    second_x(2)
-    second_x(3)
-    third_done(5)
-    second_z(2)
-    heads_third(1)
+    first_x(2)
+    core_done(3)
+    first_y(2)
     heads_second(0)
     small_done()
-    third_done(1)
-    third_done(4)
-    project_back(0, 1)
-    hand_back(1)
+    first_z(3)
+    second_x(2)
+    first_x(3)
+    second_z(2)
+    second_z(0)
+    heads_third(1)
+    second_z(1)
+    first_y(3)
+    heads_third(0)
+    second_y(2)
+    second_x(3)
+    second_z(3)
+    third_done(0)
     third_done(2)
-    third_done(0)
-    third_done(3)
+    second_y(3)
     project_back(0, 0)
     hand_back(0)
-    heads_third(0)
+    heads_done(1)
+    third_done(1)
+    third_done(3)
+    final_pass(0)
     final_pass(2)
-    final_pass(4)
-    final_pass(5)
+    final_pass(1)
     final_pass(3)
-    final_done(4)
-    final_pass(0)
-    final_pass(1)
+    final_done(2)
+    final_done(1)
     heads_done(0)
-    heads_done(1)
-    final_done(2)
     final_done(0)
-    final_done(1)
     final_done(3)
-    final_done(5)
     for half in range(2):
         move_arrived(3, half, out_in)
         move_arrived(4, half, grad_in)

time: 129 us -> 128 us (level)
  Pallas kernels: 128 us -> 126 us
    pallas_call x1, Pallas kernels: 125 us -> 124 us  [fast_body(): pl.pallas_call(layers_kernel, out_shape=(vmem(LAYERS, 4, CHUNK, 128), vme...]
where the time goes in v10:
time: 128 us; the launch traced here: 127 us
  Pallas kernels  126 us (98%)
    pallas_call x1, Pallas kernels, fast_body(): pl.pallas_call(layers_kernel, out_shape=(vmem(LAYERS, 4, CHUNK, 128), vme...  124 us
    pallas_call x1, Pallas kernels, fast_body(): pl.pallas_call(results_kernel, out_shape=(shape((2 * HALF, WIDTH), BF16),...  2.64 us

profile of v10, /device:TPU:0, one launch (start us, length us, event | category | flops | bytes accessed | tf_op | source)
XLA Modules:
  0.0 127.3 jit_solution(8646615024479637310)
XLA Ops:
  0.6 123.8 %layers.1 = (bf16[2,4,576,128]{3,2,1,0:T(8,128)(2,1)S(1)}, bf16[2,2,4,32,384]{4,3,2,1,0:T(8,128)(2,1)S(1)}, bf16[2,128,512]{2,1,0:T(8,128)(2,1)S(1)}, bf16[2,128,512]{2,1,0:T(8,128)(2,1)S(1)}, f32[2,512]{1,0:T(2,128)S(1)}) custom-call(bf16[256,512]{1,0:T(8,128)(2,1)} %tokens.1, s32[1,4]{1,0:T(1,128)} %seq_len.1, f32[2,2]{1,0:T(2,128)} %alphas.1, ...), custom_call_target="tpu_custom_call" | custom-call | tf_op jit(solution)/shard_map/layers/pallas_call | solution.py:983
  124.5 2.6 %results.1 = (bf16[256,512]{1,0:T(8,128)(2,1)}, f32[256,512]{1,0:T(8,128)}, f32[2,64,1536]{2,1,0:T(8,128)}, f32[2,64,512]{2,1,0:T(8,128)}, f32[2,64,2048]{2,1,0:...) custom-call(bf16[2,4,576,128]{3,2,1,0:T(8,128)(2,1)S(1)} %get-tuple-element.14.final, ...), custom_call_target="tpu_custom_call" | custom-call | tf_op jit(solution)/shard_map/results/pallas_call | solution.py:1087

commit v11 on v10

--- a/solution.py
+++ b/solution.py
@@ -425,13 +425,15 @@
         if first <= 256 < first + count:
             scatter_rows(layer, nn(attn_t[layer], da[...]), 256)
         if first >= 320:
-            for run in range(RUNS):
-                at = TILE * run + first - 320
-                result = nn(act[layer, :, at : at + count].T, dz[...])
-                for quarter in range(4):
-                    parts[layer, quarter % 2, quarter // 2, run // 2, run % 2, first : first + count, :] = result[
-                        :, 128 * quarter : 128 * quarter + 128
-                    ].astype(BF16)
+            turned = dz[...].T
+            for step in range(FF // CUT):
+                result = nn(turned, act[layer, :, CUT * step : CUT * step + CUT])
+                for block in range(CUT // 128):
+                    run, row = 2 * step + block // 2, 320 + 128 * (block % 2)
+                    for quarter in range(4):
+                        parts[layer, quarter % 2, quarter // 2, run // 2, run % 2, row : row + 128, :] = result[
+                            128 * quarter : 128 * quarter + 128, 128 * block : 128 * block + 128
+                        ].astype(BF16)
         if layer == 0:
             pl.semaphore_wait(core_free.at[0 if first < 320 else 1], 1)
         core_copy(part).start()
@@ -676,6 +678,9 @@
                 for slot in range(1, 4):
                     total = total + z_in[layer, slot, rows, :].astype(F32)
                 final[layer, grp, rows, :] = total.astype(BF16)
+        if PARTS[part][1] >= 320:
+            for row in (320, 448):
+                final[layer, grp, row : row + 128, :] = final[layer, grp, row : row + 128, :].T
         for which in range(2):
             final_copy(part, which).start()
 
@@ -785,7 +790,7 @@
     for half in (1 - upper, upper):
         to_team(0, half, half_of(tokens, half), tok_in)
     for copy in (*list(weight_copies.values())[1:], *bias_copies):
-        copy.start()
+        copy.start(priority=1)
     end_second = lax.div(seq_len[0, 0] + seq_len[0, 1], RUNS)
     flag_out[...] = jnp.full((8, 128), end_second.astype(F32), F32)
     for half in (1 - upper, upper):

time: 128 us -> 126 us (0.984)
    pallas_call x1, Pallas kernels: 124 us -> 122 us  [fast_body(): pl.pallas_call(layers_kernel, out_shape=(vmem(LAYERS, 4, CHUNK, 128), vme...]
where the time goes in v11:
time: 126 us
  Pallas kernels  125 us (99%)
    pallas_call x1, Pallas kernels, fast_body(): pl.pallas_call(layers_kernel, out_shape=(vmem(LAYERS, 4, CHUNK, 128), vme...  122 us
    pallas_call x1, Pallas kernels, fast_body(): pl.pallas_call(results_kernel, out_shape=(shape((2 * HALF, WIDTH), BF16),...  2.64 us

profile of v11, /device:TPU:0, one launch (start us, length us, event | category | flops | bytes accessed | tf_op | source)
XLA Modules:
  0.0 125.6 jit_solution(13518412131777872474)
XLA Ops:
  0.6 122.1 %layers.1 = (bf16[2,4,576,128]{3,2,1,0:T(8,128)(2,1)S(1)}, bf16[2,2,4,32,384]{4,3,2,1,0:T(8,128)(2,1)S(1)}, bf16[2,128,512]{2,1,0:T(8,128)(2,1)S(1)}, bf16[2,128,512]{2,1,0:T(8,128)(2,1)S(1)}, f32[2,512]{1,0:T(2,128)S(1)}) custom-call(bf16[256,512]{1,0:T(8,128)(2,1)} %tokens.1, s32[1,4]{1,0:T(1,128)} %seq_len.1, f32[2,2]{1,0:T(2,128)} %alphas.1, ...), custom_call_target="tpu_custom_call" | custom-call | tf_op jit(solution)/shard_map/layers/pallas_call | solution.py:988
  122.8 2.6 %results.1 = (bf16[256,512]{1,0:T(8,128)(2,1)}, f32[256,512]{1,0:T(8,128)}, f32[2,64,1536]{2,1,0:T(8,128)}, f32[2,64,512]{2,1,0:T(8,128)}, f32[2,64,2048]{2,1,0:...) custom-call(bf16[2,4,576,128]{3,2,1,0:T(8,128)(2,1)S(1)} %get-tuple-element.14.final, ...), custom_call_target="tpu_custom_call" | custom-call | tf_op jit(solution)/shard_map/results/pallas_call | solution.py:1092

commit v12 on v11

--- a/solution.py
+++ b/solution.py
@@ -24,7 +24,6 @@
 CUT = 512
 TILE = 256
 TILES = HALF * RUNS // TILE
-PACK = HALF + DIM
 CHUNK = 576
 SMALL = FF + WIDTH + 128
 PARTS = ((1, 0, 320), (1, 320, 256), (0, 0, 320), (0, 320, 256))
@@ -71,7 +70,7 @@
     hidden, grad, hid_all, attn_t, entered, act, branch, slope, second,
     dz, du, da, dqkv,
     pack_out, head_out, pack_in, o_in, do_in,
-    kv, kv_t, rq, ro, o_t, lse, acc, dq_t, bias,
+    kp, kt, vp, vt, rq, ro, o_t, lse, acc_k, acc_v, dq_t, bias,
     parts, core_in, xa_in, xb_in, ya_in, yb_in, z_in, third_z, third_x, third_y,
     heads_out, heads_x, heads_z, heads_sum, small, small_in, small_z, small_sum,
     w_sem, move_send, move_recv, a2a_send, a2a_recv, core_send, core_recv, x_send, x_recv, y_send, y_recv,
@@ -86,7 +85,6 @@
     zz = lax.div(blk, 2)
     member = 2 * core + yy
     far_side = 2 * (1 - side) + core
-    low = lax.broadcasted_iota(jnp.int32, (HALF, 128), 1) < DIM
 
     def place(c, x, z, y):
         return (2 * x + c, 2 * z + y)
@@ -157,29 +155,40 @@
     def slot_of(other):
         return lax.rem(other + TEAM - member, TEAM)
 
-    def exchange(kind, layer, half, outgoing, incoming, head=None):
-        at = () if head is None else (head,)
-        incoming[(half, 0, *at)] = outgoing[(half, member, *at)]
+    def exchange(kind, layer, half, outgoing, incoming, blocks=()):
+        incoming[(half, 0, *blocks)] = outgoing[(half, member, *blocks)]
         for step in range(1, TEAM):
             peer = lax.rem(member + step, TEAM)
             remote(
-                outgoing.at[(half, peer, *at)],
-                incoming.at[(half, TEAM - step, *at)],
-                a2a_send.at[kind, layer, half, head or 0],
-                a2a_recv.at[kind, layer, half, head or 0],
+                outgoing.at[(half, peer, *blocks)],
+                incoming.at[(half, TEAM - step, *blocks)],
+                a2a_send.at[kind, layer, half],
+                a2a_recv.at[kind, layer, half],
                 place(lax.div(peer, 2), side, zz, lax.rem(peer, 2)),
             ).start()
 
-    def arrived(kind, layer, half, incoming, head=None):
-        at = () if head is None else (head,)
-        whole = incoming.at[(half, pl.ds(1, TEAM - 1), *at)]
-        pltpu.make_async_copy(whole, whole, a2a_recv.at[kind, layer, half, head or 0]).wait()
-
-    def left(kind, layer, half, outgoing):
-        for head in range(OWN) if kind in (0, 3) else (None,):
-            at = () if head is None else (head,)
-            whole = outgoing.at[(half, pl.ds(1, TEAM - 1), *at)]
-            pltpu.make_async_copy(whole, whole, a2a_send.at[kind, layer, half, head or 0]).wait()
+    def give(kind, layer, half, outgoing, incoming, peer):
+        @pl.when(member == peer)
+        def _():
+            incoming[half, 0] = outgoing[half, peer]
+
+        @pl.when(member != peer)
+        def _():
+            remote(
+                outgoing.at[half, peer],
+                incoming.at[half, lax.rem(member + TEAM - peer, TEAM)],
+                a2a_send.at[kind, layer, half],
+                a2a_recv.at[kind, layer, half],
+                place(peer // 2, side, zz, peer % 2),
+            ).start()
+
+    def arrived(kind, layer, half, incoming, blocks=()):
+        whole = incoming.at[(half, pl.ds(1, TEAM - 1), *blocks)]
+        pltpu.make_async_copy(whole, whole, a2a_recv.at[kind, layer, half]).wait()
+
+    def left(kind, layer, half, outgoing, blocks=()):
+        whole = outgoing.at[(half, pl.ds(1, TEAM - 1), *blocks)]
+        pltpu.make_async_copy(whole, whole, a2a_send.at[kind, layer, half]).wait()
 
     def tokens_of(chunk, other):
         return pl.ds(pl.multiple_of(HALF * (TEAM * chunk + other), HALF), HALF)
@@ -207,70 +216,75 @@
         for which in range(1, 3):
             hidden_copy(layer, chunk, which).wait()
 
+    keys_queries, only_values = (pl.ds(0, 2),), (2,)
+
     def project(layer, half):
         rows = rows_of(half)
         rounded = hidden[rows, :].astype(BF16)
         if layer == 1:
-            left(0, 0, half, pack_out)
-        queries = nn(rounded, wqkv[layer, :, 0:WIDTH]) * (DIM ** -0.5)
-        queries_t = queries.T.astype(BF16)
-        keys = nn(rounded, wqkv[layer, :, WIDTH : 2 * WIDTH])
-        values = nn(rounded, wqkv[layer, :, 2 * WIDTH : 3 * WIDTH])
-        for pair in range(RUNS // 2):
-            k_pair = keys[:, 128 * pair : 128 * pair + 128]
-            v_pair = values[:, 128 * pair : 128 * pair + 128]
-            first = jnp.where(low, k_pair, pltpu.roll(v_pair, DIM, 1))
-            other = jnp.where(low, pltpu.roll(k_pair, DIM, 1), v_pair)
-            pack_out[half, pair, 0, 0:HALF, :] = first.astype(BF16)
-            pack_out[half, pair, 1, 0:HALF, :] = other.astype(BF16)
-        for head in range(RUNS):
-            pack_out[half, head // 2, head % 2, HALF:, :] = queries_t[DIM * head : DIM * head + DIM, :]
-        for head in range(OWN):
-            exchange(0, layer, half, pack_out, pack_in, head)
+            left(0, 0, half, pack_out, keys_queries)
+            left(4, 0, half, pack_out, only_values)
+        queries = (nn(rounded, wqkv[layer, :, 0:WIDTH]) * (DIM ** -0.5)).astype(BF16).T
+        keys = nn(rounded, wqkv[layer, :, WIDTH : 2 * WIDTH]).astype(BF16)
+        for pair in range(TEAM):
+            pack_out[half, pair, 0] = keys[:, 128 * pair : 128 * pair + 128]
+            pack_out[half, pair, 1] = queries[128 * pair : 128 * pair + 128, :]
+        exchange(0, layer, half, pack_out, pack_in, keys_queries)
+        values = nn(rounded, wqkv[layer, :, 2 * WIDTH : 3 * WIDTH]).astype(BF16)
+        for pair in range(TEAM):
+            pack_out[half, pair, 2] = values[:, 128 * pair : 128 * pair + 128]
+        exchange(4, layer, half, pack_out, pack_in, only_values)
         hid_all[layer, :, tokens_of(half, member)] = rounded.T
+
+    def span_of(chunk, other):
+        start = HALF * (TEAM * chunk + other)
+        return slice(start, start + HALF)
 
     def attend(layer, chunk):
         if layer == 1:
             left(1, 0, chunk, head_out)
-
-        def one_head(head, carry):
-            arrived(0, layer, chunk, pack_in, head)
-            for other in range(TEAM):
-                slot = slot_of(other)
-                start = HALF * (TEAM * chunk + other)
-                span = slice(start, start + HALF)
-                block = pack_in[chunk, slot, head, 0:HALF, :]
-                kv[layer, head, span, :] = block
-                kv_t[layer, head, :, span] = block.T
-                rq[layer, head, 0:DIM, span] = pack_in[chunk, slot, head, HALF:, :]
-
-            def scores_of(i):
-                count = TILE * (i + 1)
-                tile = rq[layer, head, :, TILE * i : TILE * i + TILE]
-                return nn(kv[layer, head, 0:count, :], tile) + bias[TILE * TILES - count :, :]
-
-            ahead = [scores_of(i) for i in (2 * chunk, 2 * chunk + 1)]
-            for i in (2 * chunk, 2 * chunk + 1):
-                columns = slice(TILE * i, TILE * i + TILE)
-                count = TILE * (i + 1)
-                scores = ahead[i - 2 * chunk]
-                largest = jnp.max(scores, axis=0, keepdims=True)
-                weight = jnp.exp(scores - largest)
-                total = jnp.sum(weight, axis=0, keepdims=True)
-                summed = nn(kv_t[layer, head, DIM:, 0:count], weight.astype(BF16))
-                summed = summed / total
-                o_t[layer, head, :, columns] = summed
-                lse[layer, head, :, columns] = largest + jnp.log(total)
-                rounded = summed.astype(BF16)
-                for part in range(2):
-                    head_out[chunk, 2 * (i - 2 * chunk) + part, head] = rounded[
-                        :, HALF * part : HALF * part + HALF
-                    ]
-            return carry
-
-        for head in range(OWN):
-            one_head(head, 0)
+        arrived(0, layer, chunk, pack_in, keys_queries)
+        for other in range(TEAM):
+            slot, span = slot_of(other), span_of(chunk, other)
+            kp[layer, span, :] = pack_in[chunk, slot, 0]
+            for head in range(OWN):
+                lanes = slice(DIM * head, DIM * head + DIM)
+                rq[layer, head, lanes, span] = pack_in[chunk, slot, 1, lanes, :]
+
+        def scores_of(head, i):
+            count = TILE * (i + 1)
+            tile = rq[layer, head, :, TILE * i : TILE * i + TILE]
+            return nn(kp[layer, 0:count, :], tile) + bias[TILE * TILES - count :, :]
+
+        order = [(head, i) for head in range(OWN) for i in (2 * chunk, 2 * chunk + 1)]
+        coming = scores_of(*order[0])
+        arrived(4, layer, chunk, pack_in, only_values)
+        for other in range(TEAM):
+            span = span_of(chunk, other)
+            block = pack_in[chunk, slot_of(other), 2]
+            vp[layer, span, :] = block
+            vt[layer, :, span] = block.T
+        for number, (head, i) in enumerate(order):
+            lanes = slice(DIM * head, DIM * head + DIM)
+            columns = slice(TILE * i, TILE * i + TILE)
+            scores = coming
+            if number + 1 < len(order):
+                coming = scores_of(*order[number + 1])
+            largest = jnp.max(scores, axis=0, keepdims=True)
+            weight = jnp.exp(scores - largest)
+            total = jnp.sum(weight, axis=0, keepdims=True)
+            summed = nn(vt[layer, lanes, 0 : TILE * (i + 1)], weight.astype(BF16)) / total
+            o_t[layer, head, :, columns] = summed
+            lse[layer, head, :, columns] = largest + jnp.log(total)
+            rounded = summed.astype(BF16)
+            for part in range(2):
+                head_out[chunk, 2 * (i - 2 * chunk) + part, head] = rounded[
+                    :, HALF * part : HALF * part + HALF
+                ]
         exchange(1, layer, chunk, head_out, o_in)
+        for other in range(TEAM):
+            span = span_of(chunk, other)
+            kt[layer, :, span] = kp[layer, span, :].T
 
     def feed(layer, half):
         rows = rows_of(half)
@@ -350,61 +364,54 @@
 
     def attend_back(layer, chunk):
         arrived(2, layer, chunk, do_in)
-        left(*((0, 1) if layer == 1 else (3, 1)), chunk, pack_out)
-
-        def one_head(head, carry):
-            for other in range(TEAM):
-                start = HALF * (TEAM * chunk + other)
-                ro[head, DIM:, start : start + HALF] = do_in[chunk, slot_of(other), head]
-            for i in (2 * chunk, 2 * chunk + 1):
-                columns = slice(TILE * i, TILE * i + TILE)
+        if layer == 1:
+            left(0, 1, chunk, pack_out, keys_queries)
+            left(4, 1, chunk, pack_out, only_values)
+        else:
+            left(3, 1, chunk, pack_out)
+        for other in range(TEAM):
+            for head in range(OWN):
+                lanes = slice(DIM * head, DIM * head + DIM)
+                ro[head, lanes, span_of(chunk, other)] = do_in[chunk, slot_of(other), head]
+        for i in (2 * chunk + 1, 2 * chunk):
+            columns = slice(TILE * i, TILE * i + TILE)
+            count = TILE * (i + 1)
+            for head in range(OWN):
+                lanes = slice(DIM * head, DIM * head + DIM)
                 query_tile = rq[layer, head, :, columns]
                 grad_tile = ro[head, :, columns]
-                log_total = lse[layer, head, :, columns]
                 delta = jnp.sum(
-                    ro[head, DIM:, columns].astype(F32) * o_t[layer, head, :, columns],
+                    ro[head, lanes, columns].astype(F32) * o_t[layer, head, :, columns],
                     axis=0,
                     keepdims=True,
                 )
-                count = TILE * (i + 1)
-                keys = kv[layer, head, 0:count, :]
-                weight = jnp.exp(nn(keys, query_tile) + bias[TILE * TILES - count :, :] - log_total)
-                scored = (weight * (nn(keys, grad_tile) - delta)).astype(BF16)
-                term = nt(scored, query_tile) + nt(weight.astype(BF16), grad_tile)
-                if chunk == 1 and i == 2:
-                    acc[head, 0:count, :] = term
-                elif chunk == 1:
-                    acc[head, 0 : count - TILE, :] += term[0 : count - TILE, :]
-                    acc[head, count - TILE : count, :] = term[count - TILE :, :]
+                scores = nn(kp[layer, 0:count, :], query_tile) + bias[TILE * TILES - count :, :]
+                weight = jnp.exp(scores - lse[layer, head, :, columns])
+                scored = (weight * (nn(vp[layer, 0:count, :], grad_tile) - delta)).astype(BF16)
+                key_term = nt(scored, query_tile)
+                value_term = nt(weight.astype(BF16), grad_tile)
+                if i == TILES - 1 and head == 0:
+                    acc_k[...] = key_term
+                    acc_v[...] = value_term
                 else:
-                    acc[head, 0:count, :] += term
-                query_grad = nn(kv_t[layer, head, 0:DIM, 0:count], scored)
-                dq_t[head, :, columns] = query_grad * (DIM ** -0.5)
-            for other in range(TEAM):
-                start = HALF * (TEAM * chunk + other)
-                span = slice(start, start + HALF)
-                pack_out[chunk, other, head, 0:HALF, :] = acc[head, span, :].astype(BF16)
-                pack_out[chunk, other, head, HALF:, :] = dq_t[head, :, span].astype(BF16)
-            exchange(3, layer, chunk, pack_out, pack_in, head)
-            return carry
-
-        for head in range(OWN):
-            one_head(head, 0)
+                    acc_k[0:count, :] += key_term
+                    acc_v[0:count, :] += value_term
+                dq_t[lanes, columns] = nn(kt[layer, lanes, 0:count], scored) * (DIM ** -0.5)
+            for run in (2 * i, 2 * i + 1):
+                span = slice(HALF * run, HALF * run + HALF)
+                pack_out[chunk, run % TEAM, 0] = acc_k[span, :].astype(BF16)
+                pack_out[chunk, run % TEAM, 1] = dq_t[:, span].astype(BF16)
+                pack_out[chunk, run % TEAM, 2] = acc_v[span, :].astype(BF16)
+                give(3, layer, chunk, pack_out, pack_in, run % TEAM)
 
     def project_back(layer, half):
-        for head in range(OWN):
-            arrived(3, layer, half, pack_in, head)
-        turned = jnp.concatenate(
-            [pack_in[half, slot_of(head // 2), head % 2, HALF:, :] for head in range(RUNS)], axis=0
-        )
+        arrived(3, layer, half, pack_in)
+        turned = jnp.concatenate([pack_in[half, slot_of(other), 1] for other in range(TEAM)], axis=0)
         dqkv[:, 0:WIDTH] = turned.T
-        for pair in range(RUNS // 2):
-            first = pack_in[half, slot_of(pair), 0, 0:HALF, :].astype(F32)
-            other = pack_in[half, slot_of(pair), 1, 0:HALF, :].astype(F32)
-            k_pair = jnp.where(low, first, pltpu.roll(other, DIM, 1))
-            v_pair = jnp.where(low, pltpu.roll(first, DIM, 1), other)
-            dqkv[:, WIDTH + 128 * pair : WIDTH + 128 * pair + 128] = k_pair.astype(BF16)
-            dqkv[:, 2 * WIDTH + 128 * pair : 2 * WIDTH + 128 * pair + 128] = v_pair.astype(BF16)
+        for other in range(TEAM):
+            at = WIDTH + 128 * other
+            dqkv[:, at : at + 128] = pack_in[half, slot_of(other), 0]
+            dqkv[:, WIDTH + at : WIDTH + at + 128] = pack_in[half, slot_of(other), 2]
         rows = rows_of(half)
         grad[rows, :] = grad[rows, :] + nt(dqkv[...], wqkv[layer])
 
@@ -444,24 +451,15 @@
         blocks = [(run // TEAM, run % TEAM) for run in range(RUNS)]
         keys_values = jnp.concatenate(
             [
-                jnp.concatenate([pack_out[chunk, other, head, 0:HALF, :] for chunk, other in blocks], axis=0)
-                for head in range(OWN)
+                jnp.concatenate([pack_out[chunk, other, number] for chunk, other in blocks], axis=0)
+                for number in (0, 2)
             ],
             axis=1,
         )
-        queries = jnp.concatenate(
-            [
-                jnp.concatenate([pack_out[chunk, other, head, HALF:, :] for chunk, other in blocks], axis=1)
-                for head in range(OWN)
-            ],
-            axis=0,
-        )
+        queries = jnp.concatenate([pack_out[chunk, other, 1] for chunk, other in blocks], axis=1)
         both = nn(hid_all[layer], keys_values)
         q_part = nt(hid_all[layer], queries)
-        first, other = both[:, 0:128], both[:, 128:256]
-        left_half = lax.broadcasted_iota(jnp.int32, (WIDTH, 128), 1) < DIM
-        k_part = jnp.where(left_half, first, pltpu.roll(other, DIM, 1))
-        v_part = jnp.where(left_half, pltpu.roll(first, DIM, 1), other)
+        k_part, v_part = both[:, 0:128], both[:, 128:256]
         for number, values in enumerate((q_part, k_part, v_part)):
             for run in range(RUNS):
                 heads_out[layer, run // 2, run % 2, :, 128 * number : 128 * number + 128] = values[
@@ -795,11 +793,11 @@
     flag_out[...] = jnp.full((8, 128), end_second.astype(F32), F32)
     for half in (1 - upper, upper):
         to_team(1, half, flag_out, flag_in)
-    for layer in range(LAYERS):
-        for head in range(OWN):
-            rq[layer, head, DIM:, :] = jnp.zeros((DIM, HALF * RUNS), BF16)
     for head in range(OWN):
-        ro[head, 0:DIM, :] = jnp.zeros((DIM, HALF * RUNS), BF16)
+        other = slice(DIM * (1 - head), DIM * (1 - head) + DIM)
+        for layer in range(LAYERS):
+            rq[layer, head, other, :] = jnp.zeros((DIM, HALF * RUNS), BF16)
+        ro[head, other, :] = jnp.zeros((DIM, HALF * RUNS), BF16)
     weight_copies[0, 0].wait()
     halves(begin, functools.partial(project, 0), first=upper)
     for half in (1 - upper, upper):
@@ -1021,19 +1019,22 @@
             vmem(2 * HALF, FF),
             vmem(2 * HALF, WIDTH),
             vmem(HALF, 3 * WIDTH),
-            vmem(2, TEAM, OWN, PACK, 128),
+            vmem(2, TEAM, 3, 128, 128),
             vmem(2, TEAM, OWN, DIM, 128),
-            vmem(2, TEAM, OWN, PACK, 128),
+            vmem(2, TEAM, 3, 128, 128),
             vmem(2, TEAM, OWN, DIM, 128),
             vmem(2, TEAM, OWN, DIM, 128),
-            vmem(LAYERS, OWN, rows, 128),
-            vmem(LAYERS, OWN, 128, rows),
+            vmem(LAYERS, rows, 128),
+            vmem(LAYERS, 128, rows),
+            vmem(LAYERS, rows, 128),
+            vmem(LAYERS, 128, rows),
             vmem(LAYERS, OWN, 128, rows),
             vmem(OWN, 128, rows),
             wide(LAYERS, OWN, DIM, rows),
             wide(LAYERS, OWN, 1, rows),
-            wide(OWN, rows, 128),
-            wide(OWN, DIM, rows),
+            wide(rows, 128),
+            wide(rows, 128),
+            wide(128, rows),
             wide(rows, TILE),
             vmem(LAYERS, 2, 2, 4, 2, CHUNK, 128),
             vmem(2, 4, 2, CHUNK, 128),
@@ -1056,8 +1057,8 @@
             dma((LAYERS + 1, 4)),
             dma((5, 2)),
             dma((5, 2)),
-            dma((4, LAYERS, 2, OWN)),
-            dma((4, LAYERS, 2, OWN)),
+            dma((5, LAYERS, 2)),
+            dma((5, LAYERS, 2)),
             dma((len(PARTS),)),
             dma((len(PARTS),)),
             dma((len(PARTS), 3)),

time: 126 us -> 127 us (level)
    pallas_call x1, Pallas kernels: 122 us -> 124 us  [fast_body(): pl.pallas_call(layers_kernel, out_shape=(vmem(LAYERS, 4, CHUNK, 128), vme...]
where the time goes in v12:
time: 127 us
  Pallas kernels  126 us (99%)
    pallas_call x1, Pallas kernels, fast_body(): pl.pallas_call(layers_kernel, out_shape=(vmem(LAYERS, 4, CHUNK, 128), vme...  124 us
    pallas_call x1, Pallas kernels, fast_body(): pl.pallas_call(results_kernel, out_shape=(shape((2 * HALF, WIDTH), BF16),...  2.64 us

profile of v12, /device:TPU:0, one launch (start us, length us, event | category | flops | bytes accessed | tf_op | source)
XLA Modules:
  0.0 127.0 jit_solution(2989914078140104149)
XLA Ops:
  0.6 123.6 %layers.1 = (bf16[2,4,576,128]{3,2,1,0:T(8,128)(2,1)S(1)}, bf16[2,2,4,32,384]{4,3,2,1,0:T(8,128)(2,1)S(1)}, bf16[2,128,512]{2,1,0:T(8,128)(2,1)S(1)}, bf16[2,128,512]{2,1,0:T(8,128)(2,1)S(1)}, f32[2,512]{1,0:T(2,128)S(1)}) custom-call(bf16[256,512]{1,0:T(8,128)(2,1)} %tokens.1, s32[1,4]{1,0:T(1,128)} %seq_len.1, f32[2,2]{1,0:T(2,128)} %alphas.1, ...), custom_call_target="tpu_custom_call" | custom-call | tf_op jit(solution)/shard_map/layers/pallas_call | solution.py:986
  124.2 2.6 %results.1 = (bf16[256,512]{1,0:T(8,128)(2,1)}, f32[256,512]{1,0:T(8,128)}, f32[2,64,1536]{2,1,0:T(8,128)}, f32[2,64,512]{2,1,0:T(8,128)}, f32[2,64,2048]{2,1,0:...) custom-call(bf16[2,4,576,128]{3,2,1,0:T(8,128)(2,1)S(1)} %get-tuple-element.14.final, ...), custom_call_target="tpu_custom_call" | custom-call | tf_op jit(solution)/shard_map/results/pallas_call | solution.py:1093

commit v13 on v11

--- a/solution.py
+++ b/solution.py
@@ -61,6 +61,14 @@
 
 def nt(a, b):
     return lax.dot_general(a, b, (((1,), (1,)), ((), ())), preferred_element_type=F32)
+
+
+def beside(first, other):
+    low = lax.broadcasted_iota(jnp.int32, first.shape, 1) < DIM
+    return (
+        jnp.where(low, first, pltpu.roll(other, DIM, 1)),
+        jnp.where(low, pltpu.roll(first, DIM, 1), other),
+    )
 
 
 def layers_kernel(
@@ -86,7 +94,6 @@
     zz = lax.div(blk, 2)
     member = 2 * core + yy
     far_side = 2 * (1 - side) + core
-    low = lax.broadcasted_iota(jnp.int32, (HALF, 128), 1) < DIM
 
     def place(c, x, z, y):
         return (2 * x + c, 2 * z + y)
@@ -212,19 +219,16 @@
         rounded = hidden[rows, :].astype(BF16)
         if layer == 1:
             left(0, 0, half, pack_out)
-        queries = nn(rounded, wqkv[layer, :, 0:WIDTH]) * (DIM ** -0.5)
-        queries_t = queries.T.astype(BF16)
-        keys = nn(rounded, wqkv[layer, :, WIDTH : 2 * WIDTH])
-        values = nn(rounded, wqkv[layer, :, 2 * WIDTH : 3 * WIDTH])
-        for pair in range(RUNS // 2):
-            k_pair = keys[:, 128 * pair : 128 * pair + 128]
-            v_pair = values[:, 128 * pair : 128 * pair + 128]
-            first = jnp.where(low, k_pair, pltpu.roll(v_pair, DIM, 1))
-            other = jnp.where(low, pltpu.roll(k_pair, DIM, 1), v_pair)
-            pack_out[half, pair, 0, 0:HALF, :] = first.astype(BF16)
-            pack_out[half, pair, 1, 0:HALF, :] = other.astype(BF16)
+        queries = (nn(rounded, wqkv[layer, :, 0:WIDTH]) * (DIM ** -0.5)).astype(BF16).T
         for head in range(RUNS):
-            pack_out[half, head // 2, head % 2, HALF:, :] = queries_t[DIM * head : DIM * head + DIM, :]
+            pack_out[half, head // 2, head % 2, HALF:, :] = queries[DIM * head : DIM * head + DIM, :]
+        for step in range(2):
+            at = WIDTH * (step + 1)
+            keys_values = nn(rounded, wqkv[layer, :, at : at + WIDTH]).astype(BF16)
+            for head in range(4):
+                pack_out[half, 2 * step + head // 2, head % 2, 0:HALF, :] = keys_values[
+                    :, 128 * head : 128 * head + 128
+                ]
         for head in range(OWN):
             exchange(0, layer, half, pack_out, pack_in, head)
         hid_all[layer, :, tokens_of(half, member)] = rounded.T
@@ -398,13 +402,9 @@
             [pack_in[half, slot_of(head // 2), head % 2, HALF:, :] for head in range(RUNS)], axis=0
         )
         dqkv[:, 0:WIDTH] = turned.T
-        for pair in range(RUNS // 2):
-            first = pack_in[half, slot_of(pair), 0, 0:HALF, :].astype(F32)
-            other = pack_in[half, slot_of(pair), 1, 0:HALF, :].astype(F32)
-            k_pair = jnp.where(low, first, pltpu.roll(other, DIM, 1))
-            v_pair = jnp.where(low, pltpu.roll(first, DIM, 1), other)
-            dqkv[:, WIDTH + 128 * pair : WIDTH + 128 * pair + 128] = k_pair.astype(BF16)
-            dqkv[:, 2 * WIDTH + 128 * pair : 2 * WIDTH + 128 * pair + 128] = v_pair.astype(BF16)
+        for head in range(RUNS):
+            at = WIDTH + 128 * head
+            dqkv[:, at : at + 128] = pack_in[half, slot_of(head // 2), head % 2, 0:HALF, :]
         rows = rows_of(half)
         grad[rows, :] = grad[rows, :] + nt(dqkv[...], wqkv[layer])
 
@@ -458,11 +458,7 @@
         )
         both = nn(hid_all[layer], keys_values)
         q_part = nt(hid_all[layer], queries)
-        first, other = both[:, 0:128], both[:, 128:256]
-        left_half = lax.broadcasted_iota(jnp.int32, (WIDTH, 128), 1) < DIM
-        k_part = jnp.where(left_half, first, pltpu.roll(other, DIM, 1))
-        v_part = jnp.where(left_half, pltpu.roll(first, DIM, 1), other)
-        for number, values in enumerate((q_part, k_part, v_part)):
+        for number, values in enumerate((q_part, both[:, 0:128], both[:, 128:256])):
             for run in range(RUNS):
                 heads_out[layer, run // 2, run % 2, :, 128 * number : 128 * number + 128] = values[
                     DIM * run : DIM * run + DIM, :
@@ -789,7 +785,9 @@
     upper = lax.div(zz, 2)
     for half in (1 - upper, upper):
         to_team(0, half, half_of(tokens, half), tok_in)
-    for copy in (*list(weight_copies.values())[1:], *bias_copies):
+    for layer, number in ((1, 0), (0, 1), (0, 2), (0, 3), (1, 1), (1, 2), (1, 3)):
+        weight_copies[layer, number].start(priority=1)
+    for copy in bias_copies:
         copy.start(priority=1)
     end_second = lax.div(seq_len[0, 0] + seq_len[0, 1], RUNS)
     flag_out[...] = jnp.full((8, 128), end_second.astype(F32), F32)
@@ -800,7 +798,18 @@
             rq[layer, head, DIM:, :] = jnp.zeros((DIM, HALF * RUNS), BF16)
     for head in range(OWN):
         ro[head, 0:DIM, :] = jnp.zeros((DIM, HALF * RUNS), BF16)
-    weight_copies[0, 0].wait()
+    for layer in range(LAYERS):
+        weight_copies[layer, 0].wait()
+        pairs = [
+            beside(
+                wqkv[layer, :, WIDTH + 128 * pair : WIDTH + 128 * pair + 128].astype(F32),
+                wqkv[layer, :, 2 * WIDTH + 128 * pair : 2 * WIDTH + 128 * pair + 128].astype(F32),
+            )
+            for pair in range(TEAM)
+        ]
+        for head in range(RUNS):
+            at = WIDTH + 128 * head
+            wqkv[layer, :, at : at + 128] = pairs[head // 2][head % 2].astype(BF16)
     halves(begin, functools.partial(project, 0), first=upper)
     for half in (1 - upper, upper):
         to_team(2, half, half_of(cotangent, half), cot_in)
@@ -823,7 +832,6 @@
     attend(0, 0)
     attend(0, 1)
     hidden_start(0, 0)
-    weight_copies[1, 0].wait()
     halves(functools.partial(feed, 0), functools.partial(project, 1))
     for number in range(1, 4):
         weight_copies[1, number].wait()
@@ -959,11 +967,11 @@
     for layer in range(LAYERS):
         for side in range(2):
             for member in range(TEAM):
+                block = heads[layer, side, member].astype(F32)
+                columns = (block[:, 0:128], *beside(block[:, 128:256], block[:, 256:384]))
                 for step in range(3):
                     at = WIDTH * step + 128 * member
-                    qkv_wide[layer, 32 * side : 32 * side + 32, at : at + 128] = heads[
-                        layer, side, member, :, 128 * step : 128 * step + 128
-                    ].astype(F32)
+                    qkv_wide[layer, 32 * side : 32 * side + 32, at : at + 128] = columns[step]
         write(qkv_wide.at[layer], qkv_grad.at[layer])
     for end in ends:
         end.wait()

time: 126 us -> 126 us (level)
  no operation moved by 1% of the time
where the time goes in v13:
time: 126 us
  Pallas kernels  125 us (99%)
    pallas_call x1, Pallas kernels, fast_body(): pl.pallas_call(layers_kernel, out_shape=(vmem(LAYERS, 4, CHUNK, 128), vme...  122 us
    pallas_call x1, Pallas kernels, fast_body(): pl.pallas_call(results_kernel, out_shape=(shape((2 * HALF, WIDTH), BF16),...  2.68 us

profile of v13, /device:TPU:0, one launch (start us, length us, event | category | flops | bytes accessed | tf_op | source)
XLA Modules:
  0.0 125.6 jit_solution(4472017256413448307)
XLA Ops:
  0.6 122.1 %layers.1 = (bf16[2,4,576,128]{3,2,1,0:T(8,128)(2,1)S(1)}, bf16[2,2,4,32,384]{4,3,2,1,0:T(8,128)(2,1)S(1)}, bf16[2,128,512]{2,1,0:T(8,128)(2,1)S(1)}, bf16[2,128,512]{2,1,0:T(8,128)(2,1)S(1)}, f32[2,512]{1,0:T(2,128)S(1)}) custom-call(bf16[256,512]{1,0:T(8,128)(2,1)} %tokens.1, s32[1,4]{1,0:T(1,128)} %seq_len.1, f32[2,2]{1,0:T(2,128)} %alphas.1, ...), custom_call_target="tpu_custom_call" | custom-call | tf_op jit(solution)/shard_map/layers/pallas_call | solution.py:996
  122.8 2.7 %results.1 = (bf16[256,512]{1,0:T(8,128)(2,1)}, f32[256,512]{1,0:T(8,128)}, f32[2,64,1536]{2,1,0:T(8,128)}, f32[2,64,512]{2,1,0:T(8,128)}, f32[2,64,2048]{2,1,0:...) custom-call(bf16[2,4,576,128]{3,2,1,0:T(8,128)(2,1)S(1)} %get-tuple-element.14.final, ...), custom_call_target="tpu_custom_call" | custom-call | tf_op jit(solution)/shard_map/results/pallas_call | solution.py:1100

commit v14 on v13

--- a/solution.py
+++ b/solution.py
@@ -28,7 +28,7 @@
 CHUNK = 576
 SMALL = FF + WIDTH + 128
 PARTS = ((1, 0, 320), (1, 320, 256), (0, 0, 320), (0, 320, 256))
-SHARES = ((192, 0, 128), (160, 16, 80), (160, 112, 48), (128, 96, 32))
+SHARES = ((192, 64, 64), (160, 64, 32), (176, 112, 32), (144, 96, 16))
 
 
 def spans():
@@ -856,6 +856,7 @@
     core_done(0)
     attend_back(1, 0)
     second_y(1)
+    first_y(0)
     first_x(1)
     project_back(1, 1)
     heads_grads(1)
@@ -864,6 +865,7 @@
     feed_back(0)
     small_start()
     second_x(1)
+    second_y(0)
     make(2)
     first_x(0)
     heads_second(1)

time: 126 us -> 130 us (1.032)
  Pallas kernels: 125 us -> 129 us
    pallas_call x1, Pallas kernels: 122 us -> 126 us  [fast_body(): pl.pallas_call(layers_kernel, out_shape=(vmem(LAYERS, 4, CHUNK, 128), vme...]
where the time goes in v14:
time: 130 us
  Pallas kernels  129 us (99%)
    pallas_call x1, Pallas kernels, fast_body(): pl.pallas_call(layers_kernel, out_shape=(vmem(LAYERS, 4, CHUNK, 128), vme...  126 us
    pallas_call x1, Pallas kernels, fast_body(): pl.pallas_call(results_kernel, out_shape=(shape((2 * HALF, WIDTH), BF16),...  2.68 us

profile of v14, /device:TPU:0, one launch (start us, length us, event | category | flops | bytes accessed | tf_op | source)
XLA Modules:
  0.0 129.6 jit_solution(4523505278851373390)
XLA Ops:
  0.6 126.0 %layers.1 = (bf16[2,4,576,128]{3,2,1,0:T(8,128)(2,1)S(1)}, bf16[2,2,4,32,384]{4,3,2,1,0:T(8,128)(2,1)S(1)}, bf16[2,128,512]{2,1,0:T(8,128)(2,1)S(1)}, bf16[2,128,512]{2,1,0:T(8,128)(2,1)S(1)}, f32[2,512]{1,0:T(2,128)S(1)}) custom-call(bf16[256,512]{1,0:T(8,128)(2,1)} %tokens.1, s32[1,4]{1,0:T(1,128)} %seq_len.1, f32[2,2]{1,0:T(2,128)} %alphas.1, ...), custom_call_target="tpu_custom_call" | custom-call | tf_op jit(solution)/shard_map/layers/pallas_call | solution.py:998
  126.7 2.7 %results.1 = (bf16[256,512]{1,0:T(8,128)(2,1)}, f32[256,512]{1,0:T(8,128)}, f32[2,64,1536]{2,1,0:T(8,128)}, f32[2,64,512]{2,1,0:T(8,128)}, f32[2,64,2048]{2,1,0:...) custom-call(bf16[2,4,576,128]{3,2,1,0:T(8,128)(2,1)S(1)} %get-tuple-element.14.final, ...), custom_call_target="tpu_custom_call" | custom-call | tf_op jit(solution)/shard_map/results/pallas_call | solution.py:1102

commit v15 on v13

--- a/solution.py
+++ b/solution.py
@@ -28,7 +28,7 @@
 CHUNK = 576
 SMALL = FF + WIDTH + 128
 PARTS = ((1, 0, 320), (1, 320, 256), (0, 0, 320), (0, 320, 256))
-SHARES = ((192, 0, 128), (160, 16, 80), (160, 112, 48), (128, 96, 32))
+SHARES = ((160, 0, 160), (128, 16, 112), (144, 80, 96), (112, 80, 64))
 
 
 def spans():

time: 126 us -> 140 us (1.11)
  Pallas kernels: 125 us -> 139 us
    pallas_call x1, Pallas kernels: 122 us -> 136 us  [fast_body(): pl.pallas_call(layers_kernel, out_shape=(vmem(LAYERS, 4, CHUNK, 128), vme...]
where the time goes in v15:
time: 140 us
  Pallas kernels  139 us (99%)
    pallas_call x1, Pallas kernels, fast_body(): pl.pallas_call(layers_kernel, out_shape=(vmem(LAYERS, 4, CHUNK, 128), vme...  136 us

profile of v15, /device:TPU:0, one launch (start us, length us, event | category | flops | bytes accessed | tf_op | source)
XLA Modules:
  0.0 139.6 jit_solution(4158226029643423977)
XLA Ops:
  0.6 136.1 %layers.1 = (bf16[2,4,576,128]{3,2,1,0:T(8,128)(2,1)S(1)}, bf16[2,2,4,32,384]{4,3,2,1,0:T(8,128)(2,1)S(1)}, bf16[2,128,512]{2,1,0:T(8,128)(2,1)S(1)}, bf16[2,128,512]{2,1,0:T(8,128)(2,1)S(1)}, f32[2,512]{1,0:T(2,128)S(1)}) custom-call(bf16[256,512]{1,0:T(8,128)(2,1)} %tokens.1, s32[1,4]{1,0:T(1,128)} %seq_len.1, f32[2,2]{1,0:T(2,128)} %alphas.1, ...), custom_call_target="tpu_custom_call" | custom-call | tf_op jit(solution)/shard_map/layers/pallas_call | solution.py:996
  136.7 2.7 %results.1 = (bf16[256,512]{1,0:T(8,128)(2,1)}, f32[256,512]{1,0:T(8,128)}, f32[2,64,1536]{2,1,0:T(8,128)}, f32[2,64,512]{2,1,0:T(8,128)}, f32[2,64,2048]{2,1,0:...) custom-call(bf16[2,4,576,128]{3,2,1,0:T(8,128)(2,1)S(1)} %get-tuple-element.14.final, ...), custom_call_target="tpu_custom_call" | custom-call | tf_op jit(solution)/shard_map/results/pallas_call | solution.py:1100

commit v16 on v15

--- a/solution.py
+++ b/solution.py
@@ -28,7 +28,7 @@
 CHUNK = 576
 SMALL = FF + WIDTH + 128
 PARTS = ((1, 0, 320), (1, 320, 256), (0, 0, 320), (0, 320, 256))
-SHARES = ((160, 0, 160), (128, 16, 112), (144, 80, 96), (112, 80, 64))
+SHARES = ((208, 0, 112), (176, 16, 64), (192, 80, 48), (160, 80, 16))
 
 
 def spans():

time: 140 us -> 127 us (0.907)
  Pallas kernels: 139 us -> 126 us
    pallas_call x1, Pallas kernels: 136 us -> 124 us  [fast_body(): pl.pallas_call(layers_kernel, out_shape=(vmem(LAYERS, 4, CHUNK, 128), vme...]
where the time goes in v16:
time: 127 us
  Pallas kernels  126 us (99%)
    pallas_call x1, Pallas kernels, fast_body(): pl.pallas_call(layers_kernel, out_shape=(vmem(LAYERS, 4, CHUNK, 128), vme...  124 us
    pallas_call x1, Pallas kernels, fast_body(): pl.pallas_call(results_kernel, out_shape=(shape((2 * HALF, WIDTH), BF16),...  2.68 us

profile of v16, /device:TPU:0, one launch (start us, length us, event | category | flops | bytes accessed | tf_op | source)
XLA Modules:
  0.0 127.0 jit_solution(399352360803472750)
XLA Ops:
  0.6 123.5 %layers.1 = (bf16[2,4,576,128]{3,2,1,0:T(8,128)(2,1)S(1)}, bf16[2,2,4,32,384]{4,3,2,1,0:T(8,128)(2,1)S(1)}, bf16[2,128,512]{2,1,0:T(8,128)(2,1)S(1)}, bf16[2,128,512]{2,1,0:T(8,128)(2,1)S(1)}, f32[2,512]{1,0:T(2,128)S(1)}) custom-call(bf16[256,512]{1,0:T(8,128)(2,1)} %tokens.1, s32[1,4]{1,0:T(1,128)} %seq_len.1, f32[2,2]{1,0:T(2,128)} %alphas.1, ...), custom_call_target="tpu_custom_call" | custom-call | tf_op jit(solution)/shard_map/layers/pallas_call | solution.py:996
  124.2 2.7 %results.1 = (bf16[256,512]{1,0:T(8,128)(2,1)}, f32[256,512]{1,0:T(8,128)}, f32[2,64,1536]{2,1,0:T(8,128)}, f32[2,64,512]{2,1,0:T(8,128)}, f32[2,64,2048]{2,1,0:...) custom-call(bf16[2,4,576,128]{3,2,1,0:T(8,128)(2,1)S(1)} %get-tuple-element.14.final, ...), custom_call_target="tpu_custom_call" | custom-call | tf_op jit(solution)/shard_map/results/pallas_call | solution.py:1100

commit v17 on v16

--- a/solution.py
+++ b/solution.py
@@ -28,7 +28,7 @@
 CHUNK = 576
 SMALL = FF + WIDTH + 128
 PARTS = ((1, 0, 320), (1, 320, 256), (0, 0, 320), (0, 320, 256))
-SHARES = ((208, 0, 112), (176, 16, 64), (192, 80, 48), (160, 80, 16))
+SHARES = ((160, 0, 160), (96, 32, 128), (96, 144, 80), (128, 64, 64))
 
 
 def spans():
@@ -80,7 +80,7 @@
     dz, du, da, dqkv,
     pack_out, head_out, pack_in, o_in, do_in,
     kv, kv_t, rq, ro, o_t, lse, acc, dq_t, bias,
-    parts, core_in, xa_in, xb_in, ya_in, yb_in, z_in, third_z, third_x, third_y,
+    parts, core_in, xa_in, xb_in, ya_in, yb_in, near_in, far_in, third_near, third_far, third_x, third_y,
     heads_out, heads_x, heads_z, heads_sum, small, small_in, small_z, small_sum,
     w_sem, move_send, move_recv, a2a_send, a2a_recv, core_send, core_recv, x_send, x_recv, y_send, y_recv,
     z_send, z_recv, fin_send, fin_recv, hid_send, hid_recv, hx_send, hx_recv, hz_send, hz_recv, hf_send, hf_recv,
@@ -101,6 +101,9 @@
     core_peer = place(1 - core, side, zz, yy)
     x_peer = place(core, 1 - side, zz, yy)
     y_peer = place(core, side, zz, 1 - yy)
+    high, odd = lax.div(zz, 2), lax.rem(zz, 2)
+    near_peer = place(core, side, 2 * high + 1 - odd, yy)
+    far_peer = place(core, side, 2 * (1 - high) + odd, yy)
 
     def remote(source, target, send, recv, peer):
         return pltpu.make_async_remote_copy(
@@ -411,7 +414,7 @@
     def scatter_rows(layer, result, first_row):
         for run in range(RUNS):
             for quarter in range(4):
-                parts[layer, quarter % 2, quarter // 2, run // 2, run % 2, first_row : first_row + DIM, :] = result[
+                parts[layer, quarter % 2, quarter // 2, run // 4, run // 2 % 2, run % 2, first_row : first_row + DIM, :] = result[
                     DIM * run : DIM * run + DIM, 128 * quarter : 128 * quarter + 128
                 ].astype(BF16)
 
@@ -431,7 +434,7 @@
                 for block in range(CUT // 128):
                     run, row = 2 * step + block // 2, 320 + 128 * (block % 2)
                     for quarter in range(4):
-                        parts[layer, quarter % 2, quarter // 2, run // 2, run % 2, row : row + 128, :] = result[
+                        parts[layer, quarter % 2, quarter // 2, run // 4, run // 2 % 2, run % 2, row : row + 128, :] = result[
                             128 * quarter : 128 * quarter + 128, 128 * block : 128 * block + 128
                         ].astype(BF16)
         if layer == 0:
@@ -529,8 +532,8 @@
         layer, first, count = PARTS[part]
         rows = pl.ds(first, count)
         return remote(
-            parts.at[layer, 1 - core, :, :, :, rows],
-            core_in.at[:, :, :, rows],
+            parts.at[layer, 1 - core, :, :, :, :, rows],
+            core_in.at[:, :, :, :, rows],
             core_send.at[part],
             core_recv.at[part],
             core_peer,
@@ -542,10 +545,10 @@
         ends = (x_send.at[part, route], x_recv.at[part, route], x_peer)
         mine = parts.at[layer, core, 1 - side]
         if route == 0:
-            return remote(mine.at[:, :, rows], xa_in.at[:, :, room], *ends)
+            return remote(mine.at[:, :, :, rows], xa_in.at[:, :, :, room], *ends)
         if route == 1:
-            return remote(mine.at[:, yy, rows], xb_in.at[:, room], *ends)
-        return remote(mine.at[zz, :, rows], third_x.at[:, room], *ends)
+            return remote(mine.at[:, :, yy, rows], xb_in.at[:, :, room], *ends)
+        return remote(mine.at[high, odd, :, rows], third_x.at[:, room], *ends)
 
     def y_copy(part, route):
         layer = PARTS[part][0]
@@ -553,19 +556,28 @@
         ends = (y_send.at[part, route], y_recv.at[part, route], y_peer)
         mine = parts.at[layer, core]
         if route == 0:
-            return remote(mine.at[side, :, 1 - yy, rows], ya_in.at[:, room], *ends)
+            return remote(mine.at[side, :, :, 1 - yy, rows], ya_in.at[:, :, room], *ends)
         if route == 1:
-            return remote(mine.at[:, :, 1 - yy, rows], yb_in.at[:, :, room], *ends)
-        return remote(mine.at[side, zz, 1 - yy, rows], third_y.at[room], *ends)
-
-    def z_copy(part, route, step):
+            return remote(mine.at[:, :, :, 1 - yy, rows], yb_in.at[:, :, :, room], *ends)
+        return remote(mine.at[side, high, odd, 1 - yy, rows], third_y.at[room], *ends)
+
+    def near_copy(part, route):
         layer = PARTS[part][0]
         rows, room = rows_in(part, route)
-        peer = lax.rem(zz + step, 4)
-        ends = (z_send.at[part, route, step], z_recv.at[part, route, 4 - step], place(core, side, peer, yy))
+        ends = (z_send.at[part, route, 0], z_recv.at[part, route, 0], near_peer)
+        mine = parts.at[layer, core]
         if route == 2:
-            return remote(parts.at[layer, core, :, peer, :, rows], third_z.at[4 - step, :, :, room], *ends)
-        return remote(parts.at[layer, core, side, peer, yy, rows], z_in.at[layer, 4 - step, rows], *ends)
+            return remote(mine.at[:, :, 1 - odd, :, rows], third_near.at[:, :, :, room], *ends)
+        return remote(mine.at[side, :, 1 - odd, yy, rows], near_in.at[layer, :, rows], *ends)
+
+    def far_copy(part, route):
+        layer = PARTS[part][0]
+        rows, room = rows_in(part, route)
+        ends = (z_send.at[part, route, 1], z_recv.at[part, route, 1], far_peer)
+        mine = parts.at[layer, core]
+        if route == 2:
+            return remote(mine.at[:, 1 - high, odd, :, rows], third_far.at[:, :, room], *ends)
+        return remote(mine.at[side, 1 - high, odd, yy, rows], far_in.at[layer, rows], *ends)
 
     def final_copy(part, which):
         layer, first, count = PARTS[part]
@@ -583,80 +595,95 @@
         rows = pl.ds(first, count)
         core_copy(part).wait()
         for across in (1 - side, side):
-            parts[layer, core, across, :, :, rows, :] += core_in[across, :, :, rows, :]
+            parts[layer, core, across, :, :, :, rows, :] += core_in[across, :, :, :, rows, :]
             if used(part, 0) and across is not side:
                 x_copy(part, 0).start()
         if used(part, 1):
             y_copy(part, 1).start()
         if used(part, 2):
-            for step in range(1, 4):
-                z_copy(part, 2, step).start()
+            near_copy(part, 2).start()
         if layer == 1:
             freed = 0 if first < 320 else 1
             followers = [1 for other in PARTS if other[0] == 0 and (other[1] >= 320) == (freed == 1)]
             credit(core_free.at[freed], core_peer, len(followers))
 
     def first_x(part):
-        if used(part, 0):
-            layer = PARTS[part][0]
-            rows, room = rows_in(part, 0)
-            x_copy(part, 0).wait()
-            for y in (1 - yy, yy):
-                parts[layer, core, side, :, y, rows, :] += xa_in[:, y, room, :]
-                if y is not yy:
-                    y_copy(part, 0).start()
+        layer = PARTS[part][0]
+        rows, room = rows_in(part, 0)
+        x_copy(part, 0).wait()
+        for y in (1 - yy, yy):
+            parts[layer, core, side, :, :, y, rows, :] += xa_in[:, :, y, room, :]
+            if y is not yy:
+                y_copy(part, 0).start()
 
     def first_y(part):
-        if used(part, 1):
-            layer = PARTS[part][0]
-            rows, room = rows_in(part, 1)
-            y_copy(part, 1).wait()
-            for across in (1 - side, side):
-                parts[layer, core, across, :, yy, rows, :] += yb_in[across, :, room, :]
-                if across is not side:
-                    x_copy(part, 1).start()
+        layer = PARTS[part][0]
+        rows, room = rows_in(part, 1)
+        y_copy(part, 1).wait()
+        for across in (1 - side, side):
+            parts[layer, core, across, :, :, yy, rows, :] += yb_in[across, :, :, room, :]
+            if across is not side:
+                x_copy(part, 1).start()
+
+    def far_z(part):
+        layer = PARTS[part][0]
+        rows, room = rows_in(part, 2)
+        near_copy(part, 2).wait()
+        for half in (1 - high, high):
+            parts[layer, core, :, half, odd, :, rows, :] += third_near[:, half, :, room, :]
+            if half is not high:
+                far_copy(part, 2).start()
 
     def first_z(part):
-        if used(part, 2):
-            layer = PARTS[part][0]
-            rows, room = rows_in(part, 2)
-            for step in range(1, 4):
-                z_copy(part, 2, step).wait()
-            for across in (1 - side, side):
-                total = parts[layer, core, across, zz, :, rows, :].astype(F32)
-                for slot in range(1, 4):
-                    total = total + third_z[slot, across, :, room, :].astype(F32)
-                parts[layer, core, across, zz, :, rows, :] = total.astype(BF16)
-                if across is not side:
-                    x_copy(part, 2).start()
+        layer = PARTS[part][0]
+        rows, room = rows_in(part, 2)
+        far_copy(part, 2).wait()
+        for across in (1 - side, side):
+            parts[layer, core, across, high, odd, :, rows, :] += third_far[across, :, room, :]
+            if across is not side:
+                x_copy(part, 2).start()
 
     def second_x(part):
-        if used(part, 0):
-            layer = PARTS[part][0]
-            rows, room = rows_in(part, 0)
-            y_copy(part, 0).wait()
-            parts[layer, core, side, :, yy, rows, :] += ya_in[:, room, :]
-            for step in range(1, 4):
-                z_copy(part, 0, step).start()
+        layer = PARTS[part][0]
+        rows, room = rows_in(part, 0)
+        y_copy(part, 0).wait()
+        for z in (1 - odd, odd):
+            parts[layer, core, side, :, z, yy, rows, :] += ya_in[:, z, room, :]
+            if z is not odd:
+                near_copy(part, 0).start()
 
     def second_y(part):
-        if used(part, 1):
-            layer = PARTS[part][0]
-            rows, room = rows_in(part, 1)
-            x_copy(part, 1).wait()
-            parts[layer, core, side, :, yy, rows, :] += xb_in[:, room, :]
-            for step in range(1, 4):
-                z_copy(part, 1, step).start()
+        layer = PARTS[part][0]
+        rows, room = rows_in(part, 1)
+        x_copy(part, 1).wait()
+        for z in (1 - odd, odd):
+            parts[layer, core, side, :, z, yy, rows, :] += xb_in[:, z, room, :]
+            if z is not odd:
+                near_copy(part, 1).start()
 
     def second_z(part):
-        if used(part, 2):
-            layer = PARTS[part][0]
-            rows, room = rows_in(part, 2)
-            x_copy(part, 2).wait()
-            for y in (1 - yy, yy):
-                parts[layer, core, side, zz, y, rows, :] += third_x[y, room, :]
-                if y is not yy:
-                    y_copy(part, 2).start()
+        layer = PARTS[part][0]
+        rows, room = rows_in(part, 2)
+        x_copy(part, 2).wait()
+        for y in (1 - yy, yy):
+            parts[layer, core, side, high, odd, y, rows, :] += third_x[y, room, :]
+            if y is not yy:
+                y_copy(part, 2).start()
+
+    def far_of(part, route):
+        layer = PARTS[part][0]
+        rows, room = rows_in(part, route)
+        near_copy(part, route).wait()
+        for half in (1 - high, high):
+            parts[layer, core, side, half, odd, yy, rows, :] += near_in[layer, half, rows, :]
+            if half is not high:
+                far_copy(part, route).start()
+
+    def far_x(part):
+        far_of(part, 0)
+
+    def far_y(part):
+        far_of(part, 1)
 
     def third_done(part):
         layer = PARTS[part][0]
@@ -666,14 +693,11 @@
             rows, room = rows_in(part, route)
             if route == 2:
                 y_copy(part, 2).wait()
-                final[layer, grp, rows, :] = parts[layer, core, side, zz, yy, rows, :] + third_y[room, :]
+                last = third_y[room, :]
             else:
-                for step in range(1, 4):
-                    z_copy(part, route, step).wait()
-                total = parts[layer, core, side, zz, yy, rows, :].astype(F32)
-                for slot in range(1, 4):
-                    total = total + z_in[layer, slot, rows, :].astype(F32)
-                final[layer, grp, rows, :] = total.astype(BF16)
+                far_copy(part, route).wait()
+                last = far_in[layer, rows, :]
+            final[layer, grp, rows, :] = parts[layer, core, side, high, odd, yy, rows, :] + last
         if PARTS[part][1] >= 320:
             for row in (320, 448):
                 final[layer, grp, row : row + 128, :] = final[layer, grp, row : row + 128, :].T
@@ -852,68 +876,79 @@
     core_done(1)
     make(0)
     attend_back(1, 1)
-    first_y(1)
     core_done(0)
     attend_back(1, 0)
-    second_y(1)
     first_x(1)
     project_back(1, 1)
     heads_grads(1)
-    first_z(1)
+    far_z(1)
+    first_y(1)
     project_back(1, 0)
+    first_x(0)
+    far_z(0)
     feed_back(0)
     small_start()
-    second_x(1)
+    make(3)
+    second_x(0)
+    first_z(1)
     make(2)
-    first_x(0)
+    first_z(0)
     heads_second(1)
-    first_z(0)
+    second_y(1)
+    core_done(3)
+    core_done(2)
     attend_back(0, 1)
     small_next(0)
-    core_done(2)
-    second_x(0)
-    make(3)
+    second_x(1)
+    far_y(1)
+    first_x(3)
+    far_z(3)
+    first_y(3)
+    far_x(0)
+    far_z(2)
+    first_x(2)
+    first_y(2)
+    second_z(0)
+    far_x(1)
+    second_z(1)
     attend_back(0, 0)
     small_next(1)
+    second_y(3)
+    heads_grads(0)
+    small_next(2)
+    second_y(2)
+    first_z(3)
+    far_y(3)
+    first_z(2)
+    second_x(3)
+    far_y(2)
+    second_x(2)
+    third_done(1)
+    far_x(3)
+    heads_second(0)
+    small_done()
+    second_z(3)
+    third_done(0)
+    heads_third(1)
+    far_x(2)
+    second_z(2)
+    third_done(3)
     project_back(0, 1)
     hand_back(1)
-    first_z(2)
-    heads_grads(0)
-    small_next(2)
-    first_x(2)
-    core_done(3)
-    first_y(2)
-    heads_second(0)
-    small_done()
-    first_z(3)
-    second_x(2)
-    first_x(3)
-    second_z(2)
-    second_z(0)
-    heads_third(1)
-    second_z(1)
-    first_y(3)
-    heads_third(0)
-    second_y(2)
-    second_x(3)
-    second_z(3)
-    third_done(0)
-    third_done(2)
-    second_y(3)
     project_back(0, 0)
     hand_back(0)
-    heads_done(1)
-    third_done(1)
-    third_done(3)
-    final_pass(0)
-    final_pass(2)
+    third_done(2)
     final_pass(1)
     final_pass(3)
+    heads_third(0)
+    final_done(1)
+    final_pass(2)
+    final_done(3)
+    final_pass(0)
+    heads_done(1)
     final_done(2)
-    final_done(1)
+    final_done(0)
     heads_done(0)
-    final_done(0)
-    final_done(3)
     for half in range(2):
         move_arrived(3, half, out_in)
         move_arrived(4, half, grad_in)
@@ -1043,14 +1078,16 @@
             wide(OWN, rows, 128),
             wide(OWN, DIM, rows),
             wide(rows, TILE),
-            vmem(LAYERS, 2, 2, 4, 2, CHUNK, 128),
-            vmem(2, 4, 2, CHUNK, 128),
-            vmem(4, 2, TOTALS[0], 128),
-            vmem(4, TOTALS[1], 128),
-            vmem(4, TOTALS[0], 128),
-            vmem(2, 4, TOTALS[1], 128),
-            vmem(LAYERS, 4, CHUNK, 128),
-            vmem(4, 2, 2, TOTALS[2], 128),
+            vmem(LAYERS, 2, 2, 2, 2, 2, CHUNK, 128),
+            vmem(2, 2, 2, 2, CHUNK, 128),
+            vmem(2, 2, 2, TOTALS[0], 128),
+            vmem(2, 2, TOTALS[1], 128),
+            vmem(2, 2, TOTALS[0], 128),
+            vmem(2, 2, 2, TOTALS[1], 128),
+            vmem(LAYERS, 2, CHUNK, 128),
+            vmem(LAYERS, CHUNK, 128),
+            vmem(2, 2, 2, TOTALS[2], 128),
+            vmem(2, 2, TOTALS[2], 128),
             vmem(2, TOTALS[2], 128),
             vmem(TOTALS[2], 128),
             vmem(LAYERS, 4, 2, DIM, 3 * 128),
@@ -1072,8 +1109,8 @@
             dma((len(PARTS), 3)),
             dma((len(PARTS), 3)),
             dma((len(PARTS), 3)),
-            dma((len(PARTS), 3, 4)),
-            dma((len(PARTS), 3, 4)),
+            dma((len(PARTS), 3, 2)),
+            dma((len(PARTS), 3, 2)),
             dma((len(PARTS), 3)),
             dma((len(PARTS), 3)),
             dma((LAYERS, 2, 3)),

time: 127 us -> 133 us (1.047); the launches traced: 127 us -> 130 us
  Pallas kernels: 126 us -> 130 us
    pallas_call x1, Pallas kernels: 124 us -> 127 us  [fast_body(): pl.pallas_call(layers_kernel, out_shape=(vmem(LAYERS, 4, CHUNK, 128), vme...]
where the time goes in v17:
time: 133 us; the launch traced here: 130 us
  Pallas kernels  130 us (98%)
    pallas_call x1, Pallas kernels, fast_body(): pl.pallas_call(layers_kernel, out_shape=(vmem(LAYERS, 4, CHUNK, 128), vme...  127 us
    pallas_call x1, Pallas kernels, fast_body(): pl.pallas_call(results_kernel, out_shape=(shape((2 * HALF, WIDTH), BF16),...  2.68 us

profile of v17, /device:TPU:0, one launch (start us, length us, event | category | flops | bytes accessed | tf_op | source)
XLA Modules:
  0.0 130.4 jit_solution(6758514733834424143)
XLA Ops:
  0.6 126.9 %layers.1 = (bf16[2,4,576,128]{3,2,1,0:T(8,128)(2,1)S(1)}, bf16[2,2,4,32,384]{4,3,2,1,0:T(8,128)(2,1)S(1)}, bf16[2,128,512]{2,1,0:T(8,128)(2,1)S(1)}, bf16[2,128,512]{2,1,0:T(8,128)(2,1)S(1)}, f32[2,512]{1,0:T(2,128)S(1)}) custom-call(bf16[256,512]{1,0:T(8,128)(2,1)} %tokens.1, s32[1,4]{1,0:T(1,128)} %seq_len.1, f32[2,2]{1,0:T(2,128)} %alphas.1, ...), custom_call_target="tpu_custom_call" | custom-call | tf_op jit(solution)/shard_map/layers/pallas_call | solution.py:1031
  127.6 2.7 %results.1 = (bf16[256,512]{1,0:T(8,128)(2,1)}, f32[256,512]{1,0:T(8,128)}, f32[2,64,1536]{2,1,0:T(8,128)}, f32[2,64,512]{2,1,0:T(8,128)}, f32[2,64,2048]{2,1,0:...) custom-call(bf16[2,4,576,128]{3,2,1,0:T(8,128)(2,1)S(1)} %get-tuple-element.14.final, ...), custom_call_target="tpu_custom_call" | custom-call | tf_op jit(solution)/shard_map/results/pallas_call | solution.py:1137

commit v18 on v17

--- a/solution.py
+++ b/solution.py
@@ -28,7 +28,7 @@
 CHUNK = 576
 SMALL = FF + WIDTH + 128
 PARTS = ((1, 0, 320), (1, 320, 256), (0, 0, 320), (0, 320, 256))
-SHARES = ((160, 0, 160), (96, 32, 128), (96, 144, 80), (128, 64, 64))
+SHARES = ((192, 0, 128), (176, 0, 80), (128, 96, 96), (80, 128, 48))
 
 
 def spans():
@@ -876,79 +876,76 @@
     core_done(1)
     make(0)
     attend_back(1, 1)
+    far_z(1)
     core_done(0)
     attend_back(1, 0)
     first_x(1)
     project_back(1, 1)
     heads_grads(1)
-    far_z(1)
-    first_y(1)
+    first_z(1)
     project_back(1, 0)
-    first_x(0)
     far_z(0)
     feed_back(0)
     small_start()
-    make(3)
-    second_x(0)
-    first_z(1)
+    second_x(1)
     make(2)
+    first_x(0)
+    heads_second(1)
     first_z(0)
-    heads_second(1)
-    second_y(1)
-    core_done(3)
-    core_done(2)
     attend_back(0, 1)
     small_next(0)
-    second_x(1)
-    far_y(1)
-    first_x(3)
-    far_z(3)
-    first_y(3)
-    far_x(0)
-    far_z(2)
-    first_x(2)
-    first_y(2)
-    second_z(0)
-    far_x(1)
-    second_z(1)
+    core_done(2)
+    second_x(0)
+    make(3)
+    core_done(3)
     attend_back(0, 0)
     small_next(1)
-    second_y(3)
+    far_x(1)
+    first_y(2)
+    first_x(2)
+    far_z(2)
     heads_grads(0)
     small_next(2)
+    far_x(0)
+    project_back(0, 1)
+    hand_back(1)
+    second_z(1)
+    far_z(3)
+    first_x(3)
     second_y(2)
-    first_z(3)
-    far_y(3)
+    second_z(0)
     first_z(2)
-    second_x(3)
-    far_y(2)
-    second_x(2)
-    third_done(1)
-    far_x(3)
+    first_y(3)
     heads_second(0)
     small_done()
+    heads_third(1)
+    second_x(2)
+    first_z(3)
+    third_done(1)
+    second_y(3)
+    far_y(2)
+    second_z(2)
+    second_x(3)
+    heads_third(0)
+    third_done(0)
+    far_x(2)
+    final_pass(1)
     second_z(3)
-    third_done(0)
-    heads_third(1)
-    far_x(2)
-    second_z(2)
-    third_done(3)
-    project_back(0, 1)
-    hand_back(1)
+    far_y(3)
+    far_x(3)
+    third_done(2)
+    heads_done(1)
     project_back(0, 0)
     hand_back(0)
-    third_done(2)
-    final_pass(1)
+    final_pass(0)
+    third_done(3)
+    final_pass(2)
     final_pass(3)
-    heads_third(0)
     final_done(1)
-    final_pass(2)
     final_done(3)
-    final_pass(0)
-    heads_done(1)
+    heads_done(0)
+    final_done(0)
     final_done(2)
-    final_done(0)
-    heads_done(0)
     for half in range(2):
         move_arrived(3, half, out_in)
         move_arrived(4, half, grad_in)

time: 133 us -> 131 us (0.985)
  no operation moved by 1% of the time
where the time goes in v18:
time: 131 us; the launch traced here: 129 us
  Pallas kernels  129 us (98%)
    pallas_call x1, Pallas kernels, fast_body(): pl.pallas_call(layers_kernel, out_shape=(vmem(LAYERS, 4, CHUNK, 128), vme...  126 us
    pallas_call x1, Pallas kernels, fast_body(): pl.pallas_call(results_kernel, out_shape=(shape((2 * HALF, WIDTH), BF16),...  2.68 us

profile of v18, /device:TPU:0, one launch (start us, length us, event | category | flops | bytes accessed | tf_op | source)
XLA Modules:
  0.0 129.5 jit_solution(16935231686897042473)
XLA Ops:
  0.6 125.9 %layers.1 = (bf16[2,4,576,128]{3,2,1,0:T(8,128)(2,1)S(1)}, bf16[2,2,4,32,384]{4,3,2,1,0:T(8,128)(2,1)S(1)}, bf16[2,128,512]{2,1,0:T(8,128)(2,1)S(1)}, bf16[2,128,512]{2,1,0:T(8,128)(2,1)S(1)}, f32[2,512]{1,0:T(2,128)S(1)}) custom-call(bf16[256,512]{1,0:T(8,128)(2,1)} %tokens.1, s32[1,4]{1,0:T(1,128)} %seq_len.1, f32[2,2]{1,0:T(2,128)} %alphas.1, ...), custom_call_target="tpu_custom_call" | custom-call | tf_op jit(solution)/shard_map/layers/pallas_call | solution.py:1028
  126.6 2.7 %results.1 = (bf16[256,512]{1,0:T(8,128)(2,1)}, f32[256,512]{1,0:T(8,128)}, f32[2,64,1536]{2,1,0:T(8,128)}, f32[2,64,512]{2,1,0:T(8,128)}, f32[2,64,2048]{2,1,0:...) custom-call(bf16[2,4,576,128]{3,2,1,0:T(8,128)(2,1)S(1)} %get-tuple-element.14.final, ...), custom_call_target="tpu_custom_call" | custom-call | tf_op jit(solution)/shard_map/results/pallas_call | solution.py:1134

commit v19 on v14

--- a/solution.py
+++ b/solution.py
@@ -28,7 +28,7 @@
 CHUNK = 576
 SMALL = FF + WIDTH + 128
 PARTS = ((1, 0, 320), (1, 320, 256), (0, 0, 320), (0, 320, 256))
-SHARES = ((192, 64, 64), (160, 64, 32), (176, 112, 32), (144, 96, 16))
+SHARES = ((192, 16, 112), (160, 16, 80), (160, 112, 48), (128, 96, 32))
 
 
 def spans():
@@ -798,7 +798,7 @@
             rq[layer, head, DIM:, :] = jnp.zeros((DIM, HALF * RUNS), BF16)
     for head in range(OWN):
         ro[head, 0:DIM, :] = jnp.zeros((DIM, HALF * RUNS), BF16)
-    for layer in range(LAYERS):
+    def reorder(layer):
         weight_copies[layer, 0].wait()
         pairs = [
             beside(
@@ -810,10 +810,13 @@
         for head in range(RUNS):
             at = WIDTH + 128 * head
             wqkv[layer, :, at : at + 128] = pairs[head // 2][head % 2].astype(BF16)
+
+    reorder(0)
     halves(begin, functools.partial(project, 0), first=upper)
     for half in (1 - upper, upper):
         to_team(2, half, half_of(cotangent, half), cot_in)
 
+    reorder(1)
     move_arrived(1, 0, flag_in)
     move_arrived(1, 1, flag_in)
     border = jnp.concatenate([flag_in[0, 0:1, :]] * 2, axis=1) - (HALF * lax.div(zz, 2)).astype(F32)
@@ -838,22 +841,22 @@
     attend(1, 0)
     attend(1, 1)
     hidden_pass(0, 0)
+    hidden_start(0, 1)
     hidden_start(1, 0)
     halves(functools.partial(feed, 1), finish)
-    hidden_start(0, 1)
-    hidden_start(1, 1)
+    hidden_pass(0, 1)
     hidden_pass(1, 0)
 
     halves(functools.partial(turn_round, 1))
     make(1)
     feed_back(1)
-    hidden_pass(0, 1)
-    hidden_pass(1, 1)
+    hidden_start(1, 1)
     core_done(1)
     make(0)
     attend_back(1, 1)
     first_y(1)
     core_done(0)
+    hidden_pass(1, 1)
     attend_back(1, 0)
     second_y(1)
     first_y(0)

time: 130 us -> 128 us (0.985)
  Pallas kernels: 129 us -> 127 us
    pallas_call x1, Pallas kernels: 126 us -> 124 us  [fast_body(): pl.pallas_call(layers_kernel, out_shape=(vmem(LAYERS, 4, CHUNK, 128), vme...]
where the time goes in v19:
time: 128 us
  Pallas kernels  127 us (99%)
    pallas_call x1, Pallas kernels, fast_body(): pl.pallas_call(layers_kernel, out_shape=(vmem(LAYERS, 4, CHUNK, 128), vme...  124 us
    pallas_call x1, Pallas kernels, fast_body(): pl.pallas_call(results_kernel, out_shape=(shape((2 * HALF, WIDTH), BF16),...  2.68 us

profile of v19, /device:TPU:0, one launch (start us, length us, event | category | flops | bytes accessed | tf_op | source)
XLA Modules:
  0.0 127.8 jit_solution(1048309470956710745)
XLA Ops:
  0.6 124.3 %layers.1 = (bf16[2,4,576,128]{3,2,1,0:T(8,128)(2,1)S(1)}, bf16[2,2,4,32,384]{4,3,2,1,0:T(8,128)(2,1)S(1)}, bf16[2,128,512]{2,1,0:T(8,128)(2,1)S(1)}, bf16[2,128,512]{2,1,0:T(8,128)(2,1)S(1)}, f32[2,512]{1,0:T(2,128)S(1)}) custom-call(bf16[256,512]{1,0:T(8,128)(2,1)} %tokens.1, s32[1,4]{1,0:T(1,128)} %seq_len.1, f32[2,2]{1,0:T(2,128)} %alphas.1, ...), custom_call_target="tpu_custom_call" | custom-call | tf_op jit(solution)/shard_map/layers/pallas_call | solution.py:1001
  124.9 2.7 %results.1 = (bf16[256,512]{1,0:T(8,128)(2,1)}, f32[256,512]{1,0:T(8,128)}, f32[2,64,1536]{2,1,0:T(8,128)}, f32[2,64,512]{2,1,0:T(8,128)}, f32[2,64,2048]{2,1,0:...) custom-call(bf16[2,4,576,128]{3,2,1,0:T(8,128)(2,1)S(1)} %get-tuple-element.14.final, ...), custom_call_target="tpu_custom_call" | custom-call | tf_op jit(solution)/shard_map/results/pallas_call | solution.py:1105

commit v20 on v16

--- a/solution.py
+++ b/solution.py
@@ -28,7 +28,7 @@
 CHUNK = 576
 SMALL = FF + WIDTH + 128
 PARTS = ((1, 0, 320), (1, 320, 256), (0, 0, 320), (0, 320, 256))
-SHARES = ((208, 0, 112), (176, 16, 64), (192, 80, 48), (160, 80, 16))
+SHARES = ((192, 0, 128), (160, 16, 80), (160, 128, 32), (128, 96, 32))
 
 
 def spans():
@@ -72,9 +72,9 @@
 
 
 def layers_kernel(
-    tokens, seq_len, alphas, up_bias_hbm, down_bias_hbm, cotangent, qkv_hbm, out_hbm, up_hbm, down_hbm,
+    tokens, seq_len_hbm, alphas_hbm, up_bias_hbm, down_bias_hbm, cotangent, qkv_hbm, out_hbm, up_hbm, down_hbm,
     final, heads_all, out_in, grad_in, small_final,
-    wqkv, wout, wup, wdown, up_bias, down_bias,
+    seq_len, alphas, wqkv, wout, wup, wdown, up_bias, down_bias,
     tok_in, cot_in, flag_out, flag_in, back_out,
     hidden, grad, hid_all, attn_t, entered, act, branch, slope, second,
     dz, du, da, dqkv,
@@ -779,7 +779,10 @@
     bias_copies = [
         pltpu.make_async_copy(up_bias_hbm, up_bias, w_sem.at[2, 0]),
         pltpu.make_async_copy(down_bias_hbm, down_bias, w_sem.at[2, 1]),
+        pltpu.make_async_copy(alphas_hbm, alphas, w_sem.at[2, 2]),
     ]
+    length_copy = pltpu.make_async_copy(seq_len_hbm, seq_len, w_sem.at[2, 3])
+    length_copy.start()
     weight_copies[0, 0].start()
     pl.semaphore_wait(barrier, 13)
     upper = lax.div(zz, 2)
@@ -789,6 +792,7 @@
         weight_copies[layer, number].start(priority=1)
     for copy in bias_copies:
         copy.start(priority=1)
+    length_copy.wait()
     end_second = lax.div(seq_len[0, 0] + seq_len[0, 1], RUNS)
     flag_out[...] = jnp.full((8, 128), end_second.astype(F32), F32)
     for half in (1 - upper, upper):
@@ -931,7 +935,7 @@
 def results_kernel(
     final, heads, out_block, grad_block, small,
     output, input_grad, qkv_grad, out_grad, up_grad, up_bias_grad, down_grad, down_bias_grad, alpha_grad,
-    out_flat, grad_wide, qkv_wide, out_wide, up_wide, down_wide, out_sem,
+    grad_wide, qkv_wide, out_wide, up_wide, down_wide, up_bias, down_bias, alpha, out_sem,
 ):
     ends = []
 
@@ -939,9 +943,14 @@
         ends.append(pltpu.make_async_copy(source, target, out_sem.at[len(ends)]))
         ends[-1].start()
 
-    up_bias_grad[...] = small[:, 0:256]
-    down_bias_grad[...] = small[:, 256 : 256 + DIM]
-    alpha_grad[...] = small[:, 384:386]
+    for half in range(2):
+        write(out_block.at[half], output.at[pl.ds(HALF * half, HALF)])
+    up_bias[...] = small[:, 0:256]
+    write(up_bias, up_bias_grad)
+    down_bias[...] = small[:, 256 : 256 + DIM]
+    write(down_bias, down_bias_grad)
+    alpha[...] = small[:, 384:386]
+    write(alpha, alpha_grad)
     for layer in range(LAYERS):
         for quarter in range(4):
 
@@ -961,9 +970,7 @@
     for half in range(2):
         rows = slice(HALF * half, HALF * half + HALF)
         grad_wide[rows, :] = grad_block[half].astype(F32)
-        out_flat[rows, :] = out_block[half]
     write(grad_wide, input_grad)
-    write(out_flat, output)
     for layer in range(LAYERS):
         for side in range(2):
             for member in range(TEAM):
@@ -981,7 +988,6 @@
     tokens, seq_len, qkv_weight, out_weight, up_weight, up_bias, down_weight, down_bias, alphas, cotangent
 ):
     whole = pl.BlockSpec(memory_space=pltpu.VMEM)
-    scalar = pl.BlockSpec(memory_space=pltpu.SMEM)
     far = pl.BlockSpec(memory_space=pl.ANY)
     shape = jax.ShapeDtypeStruct
     rows = HALF * RUNS
@@ -1002,9 +1008,11 @@
             vmem(2, HALF, WIDTH),
             wide(LAYERS, WIDTH),
         ),
-        in_specs=[far, scalar, scalar, far, far, far, far, far, far, far],
+        in_specs=[far, far, far, far, far, far, far, far, far, far],
         out_specs=(whole,) * 5,
         scratch_shapes=[
+            pltpu.SMEM((1, 4), jnp.int32),
+            pltpu.SMEM((LAYERS, 2), F32),
             vmem(LAYERS, WIDTH, 3 * WIDTH),
             vmem(LAYERS, WIDTH, WIDTH),
             vmem(LAYERS, WIDTH, FF),
@@ -1111,15 +1119,17 @@
                 shape((LAYERS, 2), F32),
             ),
             in_specs=[whole] * 5,
-            out_specs=(far, far, far, far, far, whole, far, whole, whole),
+            out_specs=(far,) * 9,
             scratch_shapes=[
-                vmem(2 * HALF, WIDTH),
                 wide(2 * HALF, WIDTH),
                 wide(LAYERS, DIM, 3 * WIDTH),
                 wide(LAYERS, DIM, WIDTH),
                 wide(LAYERS, DIM, FF),
                 wide(LAYERS, FF // RUNS, WIDTH),
-                dma((10,)),
+                wide(LAYERS, FF // RUNS),
+                wide(LAYERS, DIM),
+                wide(LAYERS, 2),
+                dma((14,)),
             ],
             compiler_params=pltpu.CompilerParams(vmem_limit_bytes=24 * 1024 * 1024),
             name="results",

time: 127 us -> 125 us (0.984)
  Pallas kernels: 126 us -> 124 us
    pallas_call x1, Pallas kernels: 124 us -> 122 us  [fast_body(): pl.pallas_call(layers_kernel, out_shape=(vmem(LAYERS, 4, CHUNK, 128), vme...]
where the time goes in v20:
time: 125 us
  Pallas kernels  124 us (99%)
    pallas_call x1, Pallas kernels, fast_body(): pl.pallas_call(layers_kernel, out_shape=(vmem(LAYERS, 4, CHUNK, 128), vme...  122 us

profile of v20, /device:TPU:0, one launch (start us, length us, event | category | flops | bytes accessed | tf_op | source)
XLA Modules:
  0.0 124.7 jit_solution(5008704350398211448)
XLA Ops:
  0.6 121.9 %layers.1 = (bf16[2,4,576,128]{3,2,1,0:T(8,128)(2,1)S(1)}, bf16[2,2,4,32,384]{4,3,2,1,0:T(8,128)(2,1)S(1)}, bf16[2,128,512]{2,1,0:T(8,128)(2,1)S(1)}, bf16[2,128,512]{2,1,0:T(8,128)(2,1)S(1)}, f32[2,512]{1,0:T(2,128)S(1)}) custom-call(bf16[256,512]{1,0:T(8,128)(2,1)} %tokens.1, s32[1,4]{1,0:T(1,128)} %seq_len_hbm.1, f32[2,2]{1,0:T(2,128)} %alphas_hbm.1, ...), custom_call_target="tpu_custom_call" | custom-call | tf_op jit(solution)/shard_map/layers/pallas_call | solution.py:1002
  122.5 2.0 %results.1 = (bf16[256,512]{1,0:T(8,128)(2,1)}, f32[256,512]{1,0:T(8,128)}, f32[2,64,1536]{2,1,0:T(8,128)}, f32[2,64,512]{2,1,0:T(8,128)}, f32[2,64,2048]{2,1,0:...) custom-call(bf16[2,4,576,128]{3,2,1,0:T(8,128)(2,1)S(1)} %get-tuple-element.14.final, ...), custom_call_target="tpu_custom_call" | custom-call | tf_op jit(solution)/shard_map/results/pallas_call | solution.py:1108

commit v21 on v20

--- a/solution.py
+++ b/solution.py
@@ -79,7 +79,7 @@
     hidden, grad, hid_all, attn_t, entered, act, branch, slope, second,
     dz, du, da, dqkv,
     pack_out, head_out, pack_in, o_in, do_in,
-    kv, kv_t, rq, ro, o_t, lse, acc, dq_t, bias,
+    kv, kv_t, rq, ro, o_t, probs, acc, dq_t, bias,
     parts, core_in, xa_in, xb_in, ya_in, yb_in, z_in, third_z, third_x, third_y,
     heads_out, heads_x, heads_z, heads_sum, small, small_in, small_z, small_sum,
     w_sem, move_send, move_recv, a2a_send, a2a_recv, core_send, core_recv, x_send, x_recv, y_send, y_recv,
@@ -233,6 +233,9 @@
             exchange(0, layer, half, pack_out, pack_in, head)
         hid_all[layer, :, tokens_of(half, member)] = rounded.T
 
+    def rows_before(i):
+        return TILE * i * (i + 1) // 2
+
     def attend(layer, chunk):
         if layer == 1:
             left(1, 0, chunk, head_out)
@@ -261,10 +264,10 @@
                 largest = jnp.max(scores, axis=0, keepdims=True)
                 weight = jnp.exp(scores - largest)
                 total = jnp.sum(weight, axis=0, keepdims=True)
-                summed = nn(kv_t[layer, head, DIM:, 0:count], weight.astype(BF16))
-                summed = summed / total
+                share = (weight * (1.0 / total)).astype(BF16)
+                probs[layer, head, rows_before(i) : rows_before(i) + count, :] = share
+                summed = nn(kv_t[layer, head, DIM:, 0:count], share)
                 o_t[layer, head, :, columns] = summed
-                lse[layer, head, :, columns] = largest + jnp.log(total)
                 rounded = summed.astype(BF16)
                 for part in range(2):
                     head_out[chunk, 2 * (i - 2 * chunk) + part, head] = rounded[
@@ -364,7 +367,6 @@
                 columns = slice(TILE * i, TILE * i + TILE)
                 query_tile = rq[layer, head, :, columns]
                 grad_tile = ro[head, :, columns]
-                log_total = lse[layer, head, :, columns]
                 delta = jnp.sum(
                     ro[head, DIM:, columns].astype(F32) * o_t[layer, head, :, columns],
                     axis=0,
@@ -372,9 +374,9 @@
                 )
                 count = TILE * (i + 1)
                 keys = kv[layer, head, 0:count, :]
-                weight = jnp.exp(nn(keys, query_tile) + bias[TILE * TILES - count :, :] - log_total)
-                scored = (weight * (nn(keys, grad_tile) - delta)).astype(BF16)
-                term = nt(scored, query_tile) + nt(weight.astype(BF16), grad_tile)
+                share = probs[layer, head, rows_before(i) : rows_before(i) + count, :]
+                scored = (share.astype(F32) * (nn(keys, grad_tile) - delta)).astype(BF16)
+                term = nt(scored, query_tile) + nt(share, grad_tile)
                 if chunk == 1 and i == 2:
                     acc[head, 0:count, :] = term
                 elif chunk == 1:
@@ -1047,7 +1049,7 @@
             vmem(LAYERS, OWN, 128, rows),
             vmem(OWN, 128, rows),
             wide(LAYERS, OWN, DIM, rows),
-            wide(LAYERS, OWN, 1, rows),
+            vmem(LAYERS, OWN, TILE * TILES * (TILES + 1) // 2, TILE),
             wide(OWN, rows, 128),
             wide(OWN, DIM, rows),
             wide(rows, TILE),

time: 125 us -> 125 us (level)
  no operation moved by 1% of the time
where the time goes in v21:
time: 125 us
  Pallas kernels  124 us (99%)
    pallas_call x1, Pallas kernels, fast_body(): pl.pallas_call(layers_kernel, out_shape=(vmem(LAYERS, 4, CHUNK, 128), vme...  122 us

profile of v21, /device:TPU:0, one launch (start us, length us, event | category | flops | bytes accessed | tf_op | source)
XLA Modules:
  0.0 125.0 jit_solution(15960749805928841260)
XLA Ops:
  0.6 122.1 %layers.1 = (bf16[2,4,576,128]{3,2,1,0:T(8,128)(2,1)S(1)}, bf16[2,2,4,32,384]{4,3,2,1,0:T(8,128)(2,1)S(1)}, bf16[2,128,512]{2,1,0:T(8,128)(2,1)S(1)}, bf16[2,128,512]{2,1,0:T(8,128)(2,1)S(1)}, f32[2,512]{1,0:T(2,128)S(1)}) custom-call(bf16[256,512]{1,0:T(8,128)(2,1)} %tokens.1, s32[1,4]{1,0:T(1,128)} %seq_len_hbm.1, f32[2,2]{1,0:T(2,128)} %alphas_hbm.1, ...), custom_call_target="tpu_custom_call" | custom-call | tf_op jit(solution)/shard_map/layers/pallas_call | solution.py:1004
  122.7 2.0 %results.1 = (bf16[256,512]{1,0:T(8,128)(2,1)}, f32[256,512]{1,0:T(8,128)}, f32[2,64,1536]{2,1,0:T(8,128)}, f32[2,64,512]{2,1,0:T(8,128)}, f32[2,64,2048]{2,1,0:...) custom-call(bf16[2,4,576,128]{3,2,1,0:T(8,128)(2,1)S(1)} %get-tuple-element.14.final, ...), custom_call_target="tpu_custom_call" | custom-call | tf_op jit(solution)/shard_map/results/pallas_call | solution.py:1110

commit v22 on v21

--- a/solution.py
+++ b/solution.py
@@ -865,60 +865,60 @@
     first_x(1)
     project_back(1, 1)
     heads_grads(1)
-    first_z(1)
     project_back(1, 0)
     feed_back(0)
     small_start()
     second_x(1)
+    first_z(1)
     make(2)
     first_x(0)
-    heads_second(1)
-    first_z(0)
     attend_back(0, 1)
     small_next(0)
     core_done(2)
+    heads_second(1)
+    make(3)
     second_x(0)
-    make(3)
     attend_back(0, 0)
     small_next(1)
+    first_z(0)
+    heads_grads(0)
+    core_done(3)
     project_back(0, 1)
     hand_back(1)
+    small_next(2)
+    second_z(1)
+    first_x(2)
+    first_y(2)
     first_z(2)
-    heads_grads(0)
-    small_next(2)
-    first_x(2)
-    core_done(3)
-    first_y(2)
     heads_second(0)
     small_done()
-    first_z(3)
+    second_z(0)
+    heads_third(1)
     second_x(2)
     first_x(3)
+    first_z(3)
     second_z(2)
-    second_z(0)
-    heads_third(1)
-    second_z(1)
     first_y(3)
     heads_third(0)
     second_y(2)
+    project_back(0, 0)
+    hand_back(0)
     second_x(3)
     second_z(3)
     third_done(0)
+    third_done(1)
     third_done(2)
     second_y(3)
-    project_back(0, 0)
-    hand_back(0)
     heads_done(1)
-    third_done(1)
     third_done(3)
     final_pass(0)
+    final_pass(1)
     final_pass(2)
-    final_pass(1)
     final_pass(3)
+    final_done(0)
+    final_done(1)
     final_done(2)
-    final_done(1)
     heads_done(0)
-    final_done(0)
     final_done(3)
     for half in range(2):
         move_arrived(3, half, out_in)

time: 125 us -> 127 us (1.016)
  Pallas kernels: 124 us -> 126 us
    pallas_call x1, Pallas kernels: 122 us -> 124 us  [fast_body(): pl.pallas_call(layers_kernel, out_shape=(vmem(LAYERS, 4, CHUNK, 128), vme...]
where the time goes in v22:
time: 127 us
  Pallas kernels  126 us (99%)
    pallas_call x1, Pallas kernels, fast_body(): pl.pallas_call(layers_kernel, out_shape=(vmem(LAYERS, 4, CHUNK, 128), vme...  124 us

profile of v22, /device:TPU:0, one launch (start us, length us, event | category | flops | bytes accessed | tf_op | source)
XLA Modules:
  0.0 127.3 jit_solution(130578458466525578)
XLA Ops:
  0.6 124.4 %layers.1 = (bf16[2,4,576,128]{3,2,1,0:T(8,128)(2,1)S(1)}, bf16[2,2,4,32,384]{4,3,2,1,0:T(8,128)(2,1)S(1)}, bf16[2,128,512]{2,1,0:T(8,128)(2,1)S(1)}, bf16[2,128,512]{2,1,0:T(8,128)(2,1)S(1)}, f32[2,512]{1,0:T(2,128)S(1)}) custom-call(bf16[256,512]{1,0:T(8,128)(2,1)} %tokens.1, s32[1,4]{1,0:T(1,128)} %seq_len_hbm.1, f32[2,2]{1,0:T(2,128)} %alphas_hbm.1, ...), custom_call_target="tpu_custom_call" | custom-call | tf_op jit(solution)/shard_map/layers/pallas_call | solution.py:1004
  125.0 2.0 %results.1 = (bf16[256,512]{1,0:T(8,128)(2,1)}, f32[256,512]{1,0:T(8,128)}, f32[2,64,1536]{2,1,0:T(8,128)}, f32[2,64,512]{2,1,0:T(8,128)}, f32[2,64,2048]{2,1,0:...) custom-call(bf16[2,4,576,128]{3,2,1,0:T(8,128)(2,1)S(1)} %get-tuple-element.14.final, ...), custom_call_target="tpu_custom_call" | custom-call | tf_op jit(solution)/shard_map/results/pallas_call | solution.py:1110

commit v23 on v21

--- a/solution.py
+++ b/solution.py
@@ -838,14 +838,18 @@
     attend(0, 0)
     attend(0, 1)
     hidden_start(0, 0)
-    halves(functools.partial(feed, 0), functools.partial(project, 1))
+    for half in range(2):
+        feed(0, half)
+        project(1, half)
     for number in range(1, 4):
         weight_copies[1, number].wait()
     attend(1, 0)
     attend(1, 1)
     hidden_pass(0, 0)
     hidden_start(1, 0)
-    halves(functools.partial(feed, 1), finish)
+    for half in range(2):
+        feed(1, half)
+        finish(half)
     hidden_start(0, 1)
     hidden_start(1, 1)
     hidden_pass(1, 0)

time: 125 us -> 125 us (level)
  no operation moved by 1% of the time
where the time goes in v23:
time: 125 us
  Pallas kernels  124 us (99%)
    pallas_call x1, Pallas kernels, fast_body(): pl.pallas_call(layers_kernel, out_shape=(vmem(LAYERS, 4, CHUNK, 128), vme...  122 us

profile of v23, /device:TPU:0, one launch (start us, length us, event | category | flops | bytes accessed | tf_op | source)
XLA Modules:
  0.0 124.9 jit_solution(11896689510619229889)
XLA Ops:
  0.6 122.0 %layers.1 = (bf16[2,4,576,128]{3,2,1,0:T(8,128)(2,1)S(1)}, bf16[2,2,4,32,384]{4,3,2,1,0:T(8,128)(2,1)S(1)}, bf16[2,128,512]{2,1,0:T(8,128)(2,1)S(1)}, bf16[2,128,512]{2,1,0:T(8,128)(2,1)S(1)}, f32[2,512]{1,0:T(2,128)S(1)}) custom-call(bf16[256,512]{1,0:T(8,128)(2,1)} %tokens.1, s32[1,4]{1,0:T(1,128)} %seq_len_hbm.1, f32[2,2]{1,0:T(2,128)} %alphas_hbm.1, ...), custom_call_target="tpu_custom_call" | custom-call | tf_op jit(solution)/shard_map/layers/pallas_call | solution.py:1008
  122.7 2.0 %results.1 = (bf16[256,512]{1,0:T(8,128)(2,1)}, f32[256,512]{1,0:T(8,128)}, f32[2,64,1536]{2,1,0:T(8,128)}, f32[2,64,512]{2,1,0:T(8,128)}, f32[2,64,2048]{2,1,0:...) custom-call(bf16[2,4,576,128]{3,2,1,0:T(8,128)(2,1)S(1)} %get-tuple-element.14.final, ...), custom_call_target="tpu_custom_call" | custom-call | tf_op jit(solution)/shard_map/results/pallas_call | solution.py:1114

commit v24 on v21

--- a/solution.py
+++ b/solution.py
@@ -865,26 +865,26 @@
     first_x(1)
     project_back(1, 1)
     heads_grads(1)
-    first_z(1)
     project_back(1, 0)
     feed_back(0)
+    first_z(1)
     small_start()
     second_x(1)
     make(2)
     first_x(0)
     heads_second(1)
+    attend_back(0, 1)
     first_z(0)
-    attend_back(0, 1)
     small_next(0)
     core_done(2)
     second_x(0)
     make(3)
     attend_back(0, 0)
+    heads_grads(0)
     small_next(1)
     project_back(0, 1)
     hand_back(1)
     first_z(2)
-    heads_grads(0)
     small_next(2)
     first_x(2)
     core_done(3)

time: 125 us -> 125 us (level)
  no operation moved by 1% of the time
where the time goes in v24:
time: 125 us
  Pallas kernels  124 us (99%)
    pallas_call x1, Pallas kernels, fast_body(): pl.pallas_call(layers_kernel, out_shape=(vmem(LAYERS, 4, CHUNK, 128), vme...  122 us

profile of v24, /device:TPU:0, one launch (start us, length us, event | category | flops | bytes accessed | tf_op | source)
XLA Modules:
  0.0 124.7 jit_solution(274463430404357958)
XLA Ops:
  0.6 121.8 %layers.1 = (bf16[2,4,576,128]{3,2,1,0:T(8,128)(2,1)S(1)}, bf16[2,2,4,32,384]{4,3,2,1,0:T(8,128)(2,1)S(1)}, bf16[2,128,512]{2,1,0:T(8,128)(2,1)S(1)}, bf16[2,128,512]{2,1,0:T(8,128)(2,1)S(1)}, f32[2,512]{1,0:T(2,128)S(1)}) custom-call(bf16[256,512]{1,0:T(8,128)(2,1)} %tokens.1, s32[1,4]{1,0:T(1,128)} %seq_len_hbm.1, f32[2,2]{1,0:T(2,128)} %alphas_hbm.1, ...), custom_call_target="tpu_custom_call" | custom-call | tf_op jit(solution)/shard_map/layers/pallas_call | solution.py:1004
  122.5 2.0 %results.1 = (bf16[256,512]{1,0:T(8,128)(2,1)}, f32[256,512]{1,0:T(8,128)}, f32[2,64,1536]{2,1,0:T(8,128)}, f32[2,64,512]{2,1,0:T(8,128)}, f32[2,64,2048]{2,1,0:...) custom-call(bf16[2,4,576,128]{3,2,1,0:T(8,128)(2,1)S(1)} %get-tuple-element.14.final, ...), custom_call_target="tpu_custom_call" | custom-call | tf_op jit(solution)/shard_map/results/pallas_call | solution.py:1110

commit v25 on v24

--- a/solution.py
+++ b/solution.py
@@ -28,7 +28,7 @@
 CHUNK = 576
 SMALL = FF + WIDTH + 128
 PARTS = ((1, 0, 320), (1, 320, 256), (0, 0, 320), (0, 320, 256))
-SHARES = ((192, 0, 128), (160, 16, 80), (160, 128, 32), (128, 96, 32))
+SHARES = ((192, 0, 128), (176, 0, 80), (160, 128, 32), (128, 96, 32))
 
 
 def spans():
@@ -858,10 +858,8 @@
     core_done(1)
     make(0)
     attend_back(1, 1)
-    first_y(1)
     core_done(0)
     attend_back(1, 0)
-    second_y(1)
     first_x(1)
     project_back(1, 1)
     heads_grads(1)
@@ -891,9 +889,9 @@
     first_y(2)
     heads_second(0)
     small_done()
-    first_z(3)
     second_x(2)
     first_x(3)
+    first_z(3)
     second_z(2)
     second_z(0)
     heads_third(1)
@@ -903,11 +901,11 @@
     second_y(2)
     second_x(3)
     second_z(3)
-    third_done(0)
     third_done(2)
     second_y(3)
     project_back(0, 0)
     hand_back(0)
+    third_done(0)
     heads_done(1)
     third_done(1)
     third_done(3)

time: 125 us -> 125 us (level)
  no operation moved by 1% of the time
where the time goes in v25:
time: 125 us
  Pallas kernels  124 us (99%)
    pallas_call x1, Pallas kernels, fast_body(): pl.pallas_call(layers_kernel, out_shape=(vmem(LAYERS, 4, CHUNK, 128), vme...  122 us

profile of v25, /device:TPU:0, one launch (start us, length us, event | category | flops | bytes accessed | tf_op | source)
XLA Modules:
  0.0 124.8 jit_solution(5161486169412928389)
XLA Ops:
  0.6 121.9 %layers.1 = (bf16[2,4,576,128]{3,2,1,0:T(8,128)(2,1)S(1)}, bf16[2,2,4,32,384]{4,3,2,1,0:T(8,128)(2,1)S(1)}, bf16[2,128,512]{2,1,0:T(8,128)(2,1)S(1)}, bf16[2,128,512]{2,1,0:T(8,128)(2,1)S(1)}, f32[2,512]{1,0:T(2,128)S(1)}) custom-call(bf16[256,512]{1,0:T(8,128)(2,1)} %tokens.1, s32[1,4]{1,0:T(1,128)} %seq_len_hbm.1, f32[2,2]{1,0:T(2,128)} %alphas_hbm.1, ...), custom_call_target="tpu_custom_call" | custom-call | tf_op jit(solution)/shard_map/layers/pallas_call | solution.py:1002
  122.6 2.0 %results.1 = (bf16[256,512]{1,0:T(8,128)(2,1)}, f32[256,512]{1,0:T(8,128)}, f32[2,64,1536]{2,1,0:T(8,128)}, f32[2,64,512]{2,1,0:T(8,128)}, f32[2,64,2048]{2,1,0:...) custom-call(bf16[2,4,576,128]{3,2,1,0:T(8,128)(2,1)S(1)} %get-tuple-element.14.final, ...), custom_call_target="tpu_custom_call" | custom-call | tf_op jit(solution)/shard_map/results/pallas_call | solution.py:1108

commit v26 on v24

--- a/solution.py
+++ b/solution.py
@@ -884,11 +884,11 @@
     small_next(1)
     project_back(0, 1)
     hand_back(1)
-    first_z(2)
     small_next(2)
     first_x(2)
     core_done(3)
     first_y(2)
+    first_z(2)
     heads_second(0)
     small_done()
     first_z(3)

time: 125 us -> 126 us (level)
    pallas_call x1, Pallas kernels: 122 us -> 123 us  [fast_body(): pl.pallas_call(layers_kernel, out_shape=(vmem(LAYERS, 4, CHUNK, 128), vme...]
where the time goes in v26:
time: 126 us
  Pallas kernels  125 us (99%)
    pallas_call x1, Pallas kernels, fast_body(): pl.pallas_call(layers_kernel, out_shape=(vmem(LAYERS, 4, CHUNK, 128), vme...  123 us

profile of v26, /device:TPU:0, one launch (start us, length us, event | category | flops | bytes accessed | tf_op | source)
XLA Modules:
  0.0 126.2 jit_solution(12103426360463707213)
XLA Ops:
  0.6 123.4 %layers.1 = (bf16[2,4,576,128]{3,2,1,0:T(8,128)(2,1)S(1)}, bf16[2,2,4,32,384]{4,3,2,1,0:T(8,128)(2,1)S(1)}, bf16[2,128,512]{2,1,0:T(8,128)(2,1)S(1)}, bf16[2,128,512]{2,1,0:T(8,128)(2,1)S(1)}, f32[2,512]{1,0:T(2,128)S(1)}) custom-call(bf16[256,512]{1,0:T(8,128)(2,1)} %tokens.1, s32[1,4]{1,0:T(1,128)} %seq_len_hbm.1, f32[2,2]{1,0:T(2,128)} %alphas_hbm.1, ...), custom_call_target="tpu_custom_call" | custom-call | tf_op jit(solution)/shard_map/layers/pallas_call | solution.py:1004
  124.0 2.0 %results.1 = (bf16[256,512]{1,0:T(8,128)(2,1)}, f32[256,512]{1,0:T(8,128)}, f32[2,64,1536]{2,1,0:T(8,128)}, f32[2,64,512]{2,1,0:T(8,128)}, f32[2,64,2048]{2,1,0:...) custom-call(bf16[2,4,576,128]{3,2,1,0:T(8,128)(2,1)S(1)} %get-tuple-element.14.final, ...), custom_call_target="tpu_custom_call" | custom-call | tf_op jit(solution)/shard_map/results/pallas_call | solution.py:1110

commit v27 on v26

--- a/solution.py
+++ b/solution.py
@@ -881,6 +881,7 @@
     make(3)
     attend_back(0, 0)
     heads_grads(0)
+    first_z(2)
     small_next(1)
     project_back(0, 1)
     hand_back(1)
@@ -888,7 +889,6 @@
     first_x(2)
     core_done(3)
     first_y(2)
-    first_z(2)
     heads_second(0)
     small_done()
     first_z(3)

time: 126 us -> 125 us (level)
    pallas_call x1, Pallas kernels: 123 us -> 122 us  [fast_body(): pl.pallas_call(layers_kernel, out_shape=(vmem(LAYERS, 4, CHUNK, 128), vme...]
where the time goes in v27:
time: 125 us
  Pallas kernels  124 us (99%)
    pallas_call x1, Pallas kernels, fast_body(): pl.pallas_call(layers_kernel, out_shape=(vmem(LAYERS, 4, CHUNK, 128), vme...  122 us

profile of v27, /device:TPU:0, one launch (start us, length us, event | category | flops | bytes accessed | tf_op | source)
XLA Modules:
  0.0 124.7 jit_solution(8001098776769426995)
XLA Ops:
  0.6 121.8 %layers.1 = (bf16[2,4,576,128]{3,2,1,0:T(8,128)(2,1)S(1)}, bf16[2,2,4,32,384]{4,3,2,1,0:T(8,128)(2,1)S(1)}, bf16[2,128,512]{2,1,0:T(8,128)(2,1)S(1)}, bf16[2,128,512]{2,1,0:T(8,128)(2,1)S(1)}, f32[2,512]{1,0:T(2,128)S(1)}) custom-call(bf16[256,512]{1,0:T(8,128)(2,1)} %tokens.1, s32[1,4]{1,0:T(1,128)} %seq_len_hbm.1, f32[2,2]{1,0:T(2,128)} %alphas_hbm.1, ...), custom_call_target="tpu_custom_call" | custom-call | tf_op jit(solution)/shard_map/layers/pallas_call | solution.py:1004
  122.5 2.0 %results.1 = (bf16[256,512]{1,0:T(8,128)(2,1)}, f32[256,512]{1,0:T(8,128)}, f32[2,64,1536]{2,1,0:T(8,128)}, f32[2,64,512]{2,1,0:T(8,128)}, f32[2,64,2048]{2,1,0:...) custom-call(bf16[2,4,576,128]{3,2,1,0:T(8,128)(2,1)S(1)} %get-tuple-element.14.final, ...), custom_call_target="tpu_custom_call" | custom-call | tf_op jit(solution)/shard_map/results/pallas_call | solution.py:1110
